TPU v7x, 32 devices: a whole 2x2x4 slice. The times are simulated.
32 devices in a mesh: leaf: 8 (over z, x), rows: 4 (over y, core).
Axes of the slice: x: 2, y: 2, z: 4, core: 2. Of those that a mesh axis runs over, the one named last changes fastest.
Arguments:
- loads_first: bfloat16 [49152, 256], P(('leaf', 'rows')), may hold values from -6 to 6
- loads_second: bfloat16 [24576, 256], P(('leaf', 'rows')), may hold values from -6 to 6
- loads_third: bfloat16 [12288, 256], P(('leaf', 'rows')), may hold values from -6 to 6
- loads_fourth: bfloat16 [6144, 256], P(('leaf', 'rows')), may hold values from -6 to 6
- inverse_first: bfloat16 [49152, 6144], P(('leaf', 'rows')), as said below
- inverse_second: bfloat16 [24576, 6144], P(('leaf', 'rows')), as said below
- inverse_third: bfloat16 [12288, 6144], P(('leaf', 'rows')), as said below
- inverse_fourth: bfloat16 [6144, 6144], P(('leaf', 'rows')), as said below
- panel_first: bfloat16 [1536, 49152], P(None, ('leaf', 'rows')), may hold values from -0.078125 to 0.078125
- panel_second: bfloat16 [1536, 24576], P(None, ('leaf', 'rows')), may hold values from -0.078125 to 0.078125
- panel_third: bfloat16 [1536, 12288], P(None, ('leaf', 'rows')), may hold values from -0.078125 to 0.078125
- panel_fourth: bfloat16 [1536, 6144], P(None, ('leaf', 'rows')), may hold values from -0.078125 to 0.078125
- blocks_first: int32 [8, 12], replicated, may hold values from 0 to 47, as said below
- blocks_second: int32 [4, 12], replicated, may hold values from 0 to 47, as said below
- blocks_third: int32 [2, 12], replicated, may hold values from 0 to 47, as said below
Outputs:
- solved_first: bfloat16 [49152, 256], P(('leaf', 'rows'))
- solved_second: bfloat16 [24576, 256], P(('leaf', 'rows'))
- solved_third: bfloat16 [12288, 256], P(('leaf', 'rows'))
- solved_fourth: bfloat16 [6144, 256], P(('leaf', 'rows'))
- ancestor_update: float32 [1536, 256], P(('leaf', 'rows'))
Inputs may be any that keep to these rules, and one draw needn't show every extreme that they name: `blocks_first`: each row lists 12 distinct block numbers in increasing order. `blocks_second`: each row lists 12 distinct block numbers in increasing order. `blocks_third`: each row lists 12 distinct block numbers in increasing order. `inverse_first`: each block of 6144 rows is lower triangular with a positive diagonal. `inverse_second`: each block of 6144 rows is lower triangular with a positive diagonal. `inverse_third`: each block of 6144 rows is lower triangular with a positive diagonal. `inverse_fourth`: each block of 6144 rows is lower triangular with a positive diagonal.
All inputs are finite; a program needn't handle non-finite values.
Results may differ from a plain program's by a relative error of at most 0.015.
Values may be sent and summed in bfloat16 or wider, within the bound.
No kernel may reach another device: no remote copies, remote signals or barrier semaphores. Data moves between devices by JAX's collectives and lax.ppermute only.
A program may use at most 128 MiB of HBM per device.

v0:
```python
import jax
import jax.numpy as jnp
from jax import lax
from jax.sharding import PartitionSpec as P

S = 6144
BLK = 128


def partner_2(value, axis, apart):
    return lax.ppermute(value, axis, [(i, i ^ 1 << apart) for i in range(lax.axis_size(axis))])


def stack_group(local_rows, level_index):
    gathered = lax.all_gather(local_rows, "rows", axis=0, tiled=True)
    leaf_index = lax.axis_index("leaf")
    for bit_number in range(level_index):
        partner = partner_2(gathered, "leaf", bit_number)
        is_upper = leaf_index >> bit_number & 1 == 1
        lower_part = jnp.where(is_upper, partner, gathered)
        upper_part = jnp.where(is_upper, gathered, partner)
        gathered = jnp.concatenate([lower_part, upper_part], 0)
    return gathered


def reduce_sliced(partial_value, level_index, sibling):
    slice_part = lax.psum_scatter(partial_value, "rows", scatter_dimension=0, tiled=True)
    for bit_number in range(level_index):
        slice_part = slice_part + partner_2(
            slice_part.astype(jnp.bfloat16), "leaf", bit_number
        ).astype(slice_part.dtype)
    if sibling:
        partner = partner_2(slice_part, "leaf", level_index)
        own_full, sibling_full = (
            lax.all_gather(slice_part, "rows", axis=0, tiled=True),
            lax.all_gather(partner, "rows", axis=0, tiled=True),
        )
        return (own_full, sibling_full)
    return (
        lax.all_gather(slice_part.astype(jnp.bfloat16), "rows", axis=0, tiled=True).astype(
            slice_part.dtype
        ),
        None,
    )


def place_rows(update, table_row):
    columns = update.shape[1]
    selector = (table_row[:, None] == jnp.arange(S // BLK, dtype=jnp.int32)[None, :]).astype(
        jnp.float32
    )
    blocks = update.reshape(table_row.shape[0], BLK, columns)
    spread = jnp.einsum("us,ubn->sbn", selector, blocks, precision=lax.Precision.HIGHEST)
    return spread.reshape(S, columns)


def per_device(
    loads_first,
    loads_second,
    loads_third,
    loads_fourth,
    inverse_first,
    inverse_second,
    inverse_third,
    inverse_fourth,
    panel_first,
    panel_second,
    panel_third,
    panel_fourth,
    blocks_first,
    blocks_second,
    blocks_third,
):
    load_list = [loads_first, loads_second, loads_third, loads_fourth]
    inverse_list = [inverse_first, inverse_second, inverse_third, inverse_fourth]
    panel_list = [panel_first, panel_second, panel_third, panel_fourth]
    table_list = [blocks_first, blocks_second, blocks_third]
    leaf_index = lax.axis_index("leaf")
    own_up = None
    sib_up = None
    solved_list = []
    for level_index in range(4):
        gathered = stack_group(load_list[level_index], level_index)
        if level_index == 0:
            prepared = gathered
        else:
            row_table = table_list[level_index - 1]
            child_index = leaf_index >> level_index - 1
            own_row = lax.dynamic_index_in_dim(row_table, child_index, 0, keepdims=False)
            sib_row = lax.dynamic_index_in_dim(row_table, child_index ^ 1, 0, keepdims=False)
            assembled = (
                gathered.astype(jnp.float32)
                - place_rows(own_up, own_row)
                - place_rows(sib_up, sib_row)
            )
            prepared = assembled.astype(jnp.bfloat16)
        solved = jnp.dot(
            inverse_list[level_index], prepared, preferred_element_type=jnp.float32
        ).astype(jnp.bfloat16)
        solved_list.append(solved)
        partial_value = jnp.dot(panel_list[level_index], solved, preferred_element_type=jnp.float32)
        sibling = level_index < 3
        own_up, sib_up = reduce_sliced(partial_value, level_index, sibling)
    row_count = own_up.shape[0] // (8 * lax.axis_size("rows"))
    position = leaf_index % 8 * lax.axis_size("rows") + lax.axis_index("rows")
    ancestor = lax.dynamic_slice_in_dim(own_up, position * row_count, row_count, 0)
    return (solved_list[0], solved_list[1], solved_list[2], solved_list[3], ancestor)


def solution(mesh):
    in_specs = (
        P(("leaf", "rows"), None),
        P(("leaf", "rows"), None),
        P(("leaf", "rows"), None),
        P(("leaf", "rows"), None),
        P(("leaf", "rows"), None),
        P(("leaf", "rows"), None),
        P(("leaf", "rows"), None),
        P(("leaf", "rows"), None),
        P(None, ("leaf", "rows")),
        P(None, ("leaf", "rows")),
        P(None, ("leaf", "rows")),
        P(None, ("leaf", "rows")),
        P(),
        P(),
        P(),
    )
    out_specs = (
        P(("leaf", "rows"), None),
        P(("leaf", "rows"), None),
        P(("leaf", "rows"), None),
        P(("leaf", "rows"), None),
        P(("leaf", "rows"), None),
    )
    return jax.shard_map(
        per_device, mesh=mesh, in_specs=in_specs, out_specs=out_specs, check_vma=False
    )
```

profile of v0, /device:TPU:0, one launch (start us, length us, event | category | flops | bytes accessed | tf_op | source)
XLA Modules:
  0.0 602.0 jit_solution(15014248640843321858)
XLA Ops:
  8.0 32.9 %all-gather.9.cloned.1.call-done = bf16[6144,256]{1,0:T(8,128)(2,1)} async-done(((bf16[1536,256]{1,0:T(8,128)(2,1)}), bf16[6144,256]{1,0:T(8,128)(2,1)}) %all-gather.9.cloned.1.call-update) | async-done | bytes 3145744 | tf_op jit(solution)/shard_map/all_gather | solution.py:15
  40.8 9.9 %convolution_convert_fusion = bf16[1536,256]{1,0:T(8,128)(2,1)S(1)} fusion(bf16[1536,6144]{1,0:T(8,128)(2,1)} %param.19, bf16[6144,256]{1,0:T(8,128)(2,1)} %all-gather.9.cloned.1.call-done), kind=kOutput, calls=%fused_computation.13 | convolution fusion | flops 4832231424 | bytes 22806528 | tf_op jit(solution)/shard_map/dot_general | solution.py:97
  51.6 4.9 convolution_bitcast_fusion.3
  57.3 27.6 %reduce-scatter.5.cloned.1.call-done = f32[384,256]{0,1:T(8,128)} async-done(((f32[1536,256]{0,1:T(8,128)}), f32[384,256]{0,1:T(8,128)}) %reduce-scatter.5.cloned.1.call-update) | async-done | bytes 393232 | tf_op jit(solution)/shard_map/reduce_scatter | solution.py:27
  85.0 21.3 %all-gather.11.cloned.1.call-done = bf16[3072,256]{1,0:T(8,128)(2,1)} async-done(((bf16[768,256]{1,0:T(8,128)(2,1)}), bf16[3072,256]{1,0:T(8,128)(2,1)}) %all-gather.11.cloned.1.call-update) | async-done | bytes 1572880 | tf_op jit(solution)/shard_map/all_gather | solution.py:15
  108.3 43.1 %collective-permute-done.1 = f32[384,256]{0,1:T(8,128)S(1)} collective-permute-done((f32[384,256]{0,1:T(8,128)}, f32[384,256]{0,1:T(8,128)S(1)}, u32[]{:S(2)}, u32[]{:S(2)}) %collective-permute-start.1) | collective-permute-done | bytes 393248 | tf_op jit(solution)/shard_map/ppermute | solution.py:11
  153.3 3.8 broadcast_select_fusion.5
  160.2 4.6 fusion.13
  164.9 6.3 %copy.31 = f32[48,128,256]{2,1,0:T(8,128)} copy(f32[48,128,256]{2,0,1:T(8,128)S(1)} %fusion.13) | data formatting | bytes 12582912 | tf_op jit(solution)/shard_map/us,ubn->sbn/dot_general | solution.py:53
  175.1 4.8 fusion.11
  179.9 4.2 copy.34
  191.1 28.3 %reduce-scatter.7.cloned.1.call-done = f32[384,256]{0,1:T(8,128)} async-done(((f32[1536,256]{0,1:T(8,128)}), f32[384,256]{0,1:T(8,128)}) %reduce-scatter.7.cloned.1.call-update) | async-done | bytes 393232 | tf_op jit(solution)/shard_map/reduce_scatter | solution.py:27
  221.9 5.2 collective-permute-done.4
  228.9 7.6 %all_gather.37 = bf16[1536,256]{1,0:T(8,128)(2,1)S(1)} all-gather(bf16[384,256]{1,0:T(8,128)(2,1)S(1)} %copy-done.20), channel_id=1, replica_groups=mesh['leaf'=8,'rows'=4] {'rows'}, dimensions={0}, use_global_device_ids=true | all-gather | bytes 983040 | tf_op jit(solution)/shard_map/all_gather | solution.py:15
  238.1 18.3 %collective-permute-done.2 = bf16[1536,256]{1,0:T(8,128)(2,1)S(1)} collective-permute-done((bf16[1536,256]{1,0:T(8,128)(2,1)S(1)}, bf16[1536,256]{1,0:T(8,128)(2,1)S(1)}, u32[]{:S(2)}, u32[]{:S(2)}) %collective-permute-start.2) | collective-permute-done | bytes 786464 | tf_op jit(solution)/shard_map/ppermute | solution.py:11
  259.8 42.5 %collective-permute-done.5 = f32[384,256]{0,1:T(8,128)S(1)} collective-permute-done((f32[384,256]{0,1:T(8,128)S(1)}, f32[384,256]{0,1:T(8,128)S(1)}, u32[]{:S(2)}, u32[]{:S(2)}) %collective-permute-start.5) | collective-permute-done | bytes 393248 | tf_op jit(solution)/shard_map/ppermute | solution.py:11
  303.4 3.6 broadcast_select_fusion.3
  312.1 6.3 %copy.37 = f32[48,128,256]{2,1,0:T(8,128)} copy(f32[48,128,256]{2,0,1:T(8,128)S(1)} %fusion.9) | data formatting | bytes 12582912 | tf_op jit(solution)/shard_map/us,ubn->sbn/dot_general | solution.py:53
  318.4 5.5 all-gather.19.cloned.1.call-done
  329.1 3.9 copy.40
  338.9 28.3 %reduce-scatter.9.cloned.1.call-done = f32[384,256]{0,1:T(8,128)} async-done(((f32[1536,256]{0,1:T(8,128)}), f32[384,256]{0,1:T(8,128)}) %reduce-scatter.9.cloned.1.call-update) | async-done | bytes 393232 | tf_op jit(solution)/shard_map/reduce_scatter | solution.py:27
  369.8 6.1 %all_gather.40 = bf16[768,256]{1,0:T(8,128)(2,1)S(1)} all-gather(bf16[192,256]{1,0:T(8,128)(2,1)S(1)} %copy-done.21), channel_id=1, replica_groups=mesh['leaf'=8,'rows'=4] {'rows'}, dimensions={0}, use_global_device_ids=true | all-gather | bytes 491520 | tf_op jit(solution)/shard_map/all_gather | solution.py:15
  379.1 8.2 %collective-permute-done.6 = bf16[768,256]{1,0:T(8,128)(2,1)S(1)} collective-permute-done((bf16[768,256]{1,0:T(8,128)(2,1)S(1)}, bf16[768,256]{1,0:T(8,128)(2,1)S(1)}, u32[]{:S(2)}, u32[]{:S(2)}) %collective-permute-start.6) | collective-permute-done | bytes 393248 | tf_op jit(solution)/shard_map/ppermute | solution.py:11
  389.8 17.5 %collective-permute-done.7 = bf16[1536,256]{1,0:T(8,128)(2,1)S(1)} collective-permute-done((bf16[1536,256]{1,0:T(8,128)(2,1)S(1)}, bf16[1536,256]{1,0:T(8,128)(2,1)S(1)}, u32[]{:S(2)}, u32[]{:S(2)}) %collective-permute-start.7) | collective-permute-done | bytes 786464 | tf_op jit(solution)/shard_map/ppermute | solution.py:11
  411.9 83.8 %collective-permute-done.11 = f32[384,256]{0,1:T(8,128)S(1)} collective-permute-done((f32[384,256]{0,1:T(8,128)S(1)}, f32[384,256]{0,1:T(8,128)S(1)}, u32[]{:S(2)}, u32[]{:S(2)}) %collective-permute-start.11) | collective-permute-done | bytes 393248 | tf_op jit(solution)/shard_map/ppermute | solution.py:11
  505.8 6.3 %copy.43 = f32[48,128,256]{2,1,0:T(8,128)} copy(f32[48,128,256]{2,0,1:T(8,128)S(1)} %fusion.5) | data formatting | bytes 12582912 | tf_op jit(solution)/shard_map/us,ubn->sbn/dot_general | solution.py:53
  520.8 3.8 copy.46
  529.2 28.3 %reduce-scatter.11.cloned.1.call-done = f32[384,256]{0,1:T(8,128)} async-done(((f32[1536,256]{0,1:T(8,128)}), f32[384,256]{0,1:T(8,128)}) %reduce-scatter.11.cloned.1.call-update) | async-done | bytes 393232 | tf_op jit(solution)/shard_map/reduce_scatter | solution.py:27
  560.1 5.2 collective-permute-done.12
  568.1 4.3 collective-permute-done.13
  578.9 6.1 %collective-permute-done.14 = bf16[384,256]{0,1:T(8,128)(2,1)} collective-permute-done((bf16[384,256]{0,1:T(8,128)(2,1)}, bf16[384,256]{0,1:T(8,128)(2,1)}, u32[]{:S(2)}, u32[]{:S(2)}) %collective-permute-start.14) | collective-permute-done | bytes 196640 | tf_op jit(solution)/shard_map/ppermute | solution.py:11
  586.2 8.0 %all_gather.43 = bf16[1536,256]{0,1:T(8,128)(2,1)S(1)} all-gather(bf16[384,256]{0,1:T(8,128)(2,1)S(1)} %add_convert_fusion), channel_id=1, replica_groups=mesh['leaf'=8,'rows'=4] {'rows'}, dimensions={0}, use_global_device_ids=true | all-gather | bytes 983040 | tf_op jit(solution)/shard_map/all_gather | solution.py:40
  (168 shorter events, 96.7 us)
Async XLA Ops:
  7.2 181.9 %copy-start = (bf16[1536,768]{1,0:T(8,128)(2,1)S(1)}, bf16[1536,768]{1,0:T(8,128)(2,1)}, u32[]{:S(2)}) copy-start(bf16[1536,768]{1,0:T(8,128)(2,1)} %param.24) | copy-start | bytes 7077892
  7.2 33.7 %all-gather.9.cloned.1.call-start = ((), (), s32[]{:S(2)}) async-start(), calls=%async_computation.4 | async-start | bytes 3932160 | tf_op jit(solution)/shard_map/all_gather | solution.py:15
  7.9 77.0 %reduce-scatter.5.cloned.1.call-start = ((), (), s32[]{:S(2)}) async-start(), calls=%async_computation.6 | async-start | bytes 1966080 | tf_op jit(solution)/shard_map/reduce_scatter | solution.py:27
  56.6 49.7 %all-gather.11.cloned.1.call-start = ((), (), s32[]{:S(2)}) async-start(), calls=%async_computation.5 | async-start | bytes 1966080 | tf_op jit(solution)/shard_map/all_gather | solution.py:15
  57.3 99.8 %all-gather.13.cloned.1.call-start = ((), (), s32[]{:S(2)}) async-start(), calls=%async_computation.7 | async-start | bytes 1966080 | tf_op jit(solution)/shard_map/all_gather | solution.py:35
  84.9 87.1 %all-gather.15.cloned.1.call-start = ((), (), s32[]{:S(2)}) async-start(), calls=%async_computation.8 | async-start | bytes 1966080 | tf_op jit(solution)/shard_map/all_gather | solution.py:36
  106.2 47.1 %collective-permute-start = (bf16[3072,256]{1,0:T(8,128)(2,1)}, bf16[3072,256]{1,0:T(8,128)(2,1)}, u32[]{:S(2)}, u32[]{:S(2)}) collective-permute-start(bf16[3072,256]{1,0:T(8,128)(2,1)} %all-gather.11.cloned.1.call-done), channel_id=1, source_target_pairs={{0,4},{4,0},{8,12},{12,8},{16,20},{20,16},{24,28},{28,24},{1,5},{5... | collective-permute-start | bytes 4718600 | tf_op jit(solution)/shard_map/ppermute | solution.py:11
  107.7 43.7 %collective-permute-start.1 = (f32[384,256]{0,1:T(8,128)}, f32[384,256]{0,1:T(8,128)S(1)}, u32[]{:S(2)}, u32[]{:S(2)}) collective-permute-start(f32[384,256]{0,1:T(8,128)} %reduce-scatter.5.cloned.1.call-done), channel_id=1, source_target_pairs={{0,4},{4,0},{8,12},{12,8},{16,20},{20,16},{24,28},{28,24},{1,5},{5... | collective-permute-start | bytes 1179656 | tf_op jit(solution)/shard_map/ppermute | solution.py:11
  152.2 67.2 %reduce-scatter.7.cloned.1.call-start = ((), (), s32[]{:S(2)}) async-start(), calls=%async_computation.9 | async-start | bytes 1966080 | tf_op jit(solution)/shard_map/reduce_scatter | solution.py:27
  191.0 37.9 %copy-start.20 = (bf16[384,256]{1,0:T(8,128)(2,1)S(1)}, bf16[384,256]{1,0:T(8,128)(2,1)}, u32[]{:S(2)}) copy-start(bf16[384,256]{1,0:T(8,128)(2,1)} %param.17) | copy-start | bytes 589828
  191.0 116.0 %all-gather.17.cloned.1.call-start = ((), (), s32[]{:S(2)}) async-start(), calls=%async_computation.10 | async-start | bytes 1966080 | tf_op jit(solution)/shard_map/all_gather | solution.py:35
  220.4 6.7 %collective-permute-start.4 = (bf16[384,256]{0,1:T(8,128)(2,1)S(1)}, bf16[384,256]{0,1:T(8,128)(2,1)S(1)}, u32[]{:S(2)}, u32[]{:S(2)}) collective-permute-start(bf16[384,256]{0,1:T(8,128)(2,1)S(1)} %convert_element_type.93), channel_id=1, source_target_pairs={{0,4},{4,0},{8,12},{12,8},{16,20},{20,16},{24,28},{28,24},{1,5},{5... | collective-permute-start | bytes 589832 | tf_op jit(solution)/shard_map/ppermute | solution.py:11
  228.9 95.0 %all-gather.19.cloned.1.call-start = ((), (), s32[]{:S(2)}) async-start(), calls=%async_computation.11 | async-start | bytes 1966080 | tf_op jit(solution)/shard_map/all_gather | solution.py:36
  236.5 19.8 %collective-permute-start.2 = (bf16[1536,256]{1,0:T(8,128)(2,1)S(1)}, bf16[1536,256]{1,0:T(8,128)(2,1)S(1)}, u32[]{:S(2)}, u32[]{:S(2)}) collective-permute-start(bf16[1536,256]{1,0:T(8,128)(2,1)S(1)} %all_gather.37), channel_id=1, source_target_pairs={{0,4},{4,0},{8,12},{12,8},{16,20},{20,16},{24,28},{28,24},{1,5},{5... | collective-permute-start | bytes 2359304 | tf_op jit(solution)/shard_map/ppermute | solution.py:11
  256.5 46.8 %copy-start.23 = (s32[4,12]{1,0:T(4,128)S(1)}, s32[4,12]{1,0:T(4,128)}, u32[]{:S(2)}) copy-start(s32[4,12]{1,0:T(4,128)} %param.28) | copy-start | bytes 580
  257.8 45.5 %collective-permute-start.3 = (bf16[3072,256]{1,0:T(8,128)(2,1)}, bf16[3072,256]{1,0:T(8,128)(2,1)}, u32[]{:S(2)}, u32[]{:S(2)}) collective-permute-start(bf16[3072,256]{1,0:T(8,128)(2,1)} %pad_maximum_fusion), channel_id=1, source_target_pairs={{0,8},{4,12},{8,0},{12,4},{16,24},{20,28},{24,16},{28,20},{1,9},{5... | collective-permute-start | bytes 4718600 | tf_op jit(solution)/shard_map/ppermute | solution.py:11
  259.4 42.9 %collective-permute-start.5 = (f32[384,256]{0,1:T(8,128)S(1)}, f32[384,256]{0,1:T(8,128)S(1)}, u32[]{:S(2)}, u32[]{:S(2)}) collective-permute-start(f32[384,256]{0,1:T(8,128)S(1)} %copy-done.12), channel_id=1, source_target_pairs={{0,8},{4,12},{8,0},{12,4},{16,24},{20,28},{24,16},{28,20},{1,9},{5... | collective-permute-start | bytes 1179656 | tf_op jit(solution)/shard_map/ppermute | solution.py:11
  303.1 64.0 %reduce-scatter.9.cloned.1.call-start = ((), (), s32[]{:S(2)}) async-start(), calls=%async_computation.12 | async-start | bytes 1966080 | tf_op jit(solution)/shard_map/reduce_scatter | solution.py:27
  337.0 32.7 %copy-start.21 = (bf16[192,256]{1,0:T(8,128)(2,1)S(1)}, bf16[192,256]{1,0:T(8,128)(2,1)}, u32[]{:S(2)}) copy-start(bf16[192,256]{1,0:T(8,128)(2,1)} %param.18) | copy-start | bytes 294916
  338.8 161.8 %all-gather.21.cloned.1.call-start = ((), (), s32[]{:S(2)}) async-start(), calls=%async_computation.13 | async-start | bytes 1966080 | tf_op jit(solution)/shard_map/all_gather | solution.py:35
  368.2 8.2 %collective-permute-start.9 = (bf16[384,256]{0,1:T(8,128)(2,1)S(1)}, bf16[384,256]{0,1:T(8,128)(2,1)S(1)}, u32[]{:S(2)}, u32[]{:S(2)}) collective-permute-start(bf16[384,256]{0,1:T(8,128)(2,1)S(1)} %convert_element_type.99), channel_id=1, source_target_pairs={{0,4},{4,0},{8,12},{12,8},{16,20},{20,16},{24,28},{28,24},{1,5},{5... | collective-permute-start | bytes 589832 | tf_op jit(solution)/shard_map/ppermute | solution.py:11
  375.9 11.4 %collective-permute-start.6 = (bf16[768,256]{1,0:T(8,128)(2,1)S(1)}, bf16[768,256]{1,0:T(8,128)(2,1)S(1)}, u32[]{:S(2)}, u32[]{:S(2)}) collective-permute-start(bf16[768,256]{1,0:T(8,128)(2,1)S(1)} %all_gather.40), channel_id=1, source_target_pairs={{0,4},{4,0},{8,12},{12,8},{16,20},{20,16},{24,28},{28,24},{1,5},{5... | collective-permute-start | bytes 1179656 | tf_op jit(solution)/shard_map/ppermute | solution.py:11
  377.5 9.8 %collective-permute-start.10 = (bf16[384,256]{0,1:T(8,128)(2,1)S(1)}, bf16[384,256]{0,1:T(8,128)(2,1)S(1)}, u32[]{:S(2)}, u32[]{:S(2)}) collective-permute-start(bf16[384,256]{0,1:T(8,128)(2,1)S(1)} %fusion.15), channel_id=1, source_target_pairs={{0,8},{4,12},{8,0},{12,4},{16,24},{20,28},{24,16},{28,20},{1,9},{5... | collective-permute-start | bytes 589832 | tf_op jit(solution)/shard_map/ppermute | solution.py:11
  388.2 127.4 %all-gather.23.cloned.1.call-start = ((), (), s32[]{:S(2)}) async-start(), calls=%async_computation.14 | async-start | bytes 1966080 | tf_op jit(solution)/shard_map/all_gather | solution.py:36
  388.3 19.1 %collective-permute-start.7 = (bf16[1536,256]{1,0:T(8,128)(2,1)S(1)}, bf16[1536,256]{1,0:T(8,128)(2,1)S(1)}, u32[]{:S(2)}, u32[]{:S(2)}) collective-permute-start(bf16[1536,256]{1,0:T(8,128)(2,1)S(1)} %pad_maximum_fusion.2), channel_id=1, source_target_pairs={{0,8},{4,12},{8,0},{12,4},{16,24},{20,28},{24,16},{28,20},{1,9},{5... | collective-permute-start | bytes 2359304 | tf_op jit(solution)/shard_map/ppermute | solution.py:11
  407.7 89.3 %copy-start.22 = (s32[2,12]{1,0:T(2,128)S(1)}, s32[2,12]{1,0:T(2,128)}, u32[]{:S(2)}) copy-start(s32[2,12]{1,0:T(2,128)} %param.29) | copy-start | bytes 292
  408.9 88.0 %collective-permute-start.8 = (bf16[3072,256]{1,0:T(8,128)(2,1)}, bf16[3072,256]{1,0:T(8,128)(2,1)}, u32[]{:S(2)}, u32[]{:S(2)}) collective-permute-start(bf16[3072,256]{1,0:T(8,128)(2,1)} %pad_maximum_fusion.1), channel_id=1, source_target_pairs={{0,16},{4,20},{8,24},{12,28},{16,0},{20,4},{24,8},{28,12},{1,17},{... | collective-permute-start | bytes 4718600 | tf_op jit(solution)/shard_map/ppermute | solution.py:11
  411.4 84.3 %collective-permute-start.11 = (f32[384,256]{0,1:T(8,128)S(1)}, f32[384,256]{0,1:T(8,128)S(1)}, u32[]{:S(2)}, u32[]{:S(2)}) collective-permute-start(f32[384,256]{0,1:T(8,128)S(1)} %copy-done.11), channel_id=1, source_target_pairs={{0,16},{4,20},{8,24},{12,28},{16,0},{20,4},{24,8},{28,12},{1,17},{... | collective-permute-start | bytes 1179656 | tf_op jit(solution)/shard_map/ppermute | solution.py:11
  496.5 61.1 %reduce-scatter.11.cloned.1.call-start = ((), (), s32[]{:S(2)}) async-start(), calls=%async_computation.15 | async-start | bytes 1966080 | tf_op jit(solution)/shard_map/reduce_scatter | solution.py:27
  558.6 6.7 %collective-permute-start.12 = (bf16[384,256]{0,1:T(8,128)(2,1)S(1)}, bf16[384,256]{0,1:T(8,128)(2,1)S(1)}, u32[]{:S(2)}, u32[]{:S(2)}) collective-permute-start(bf16[384,256]{0,1:T(8,128)(2,1)S(1)} %convert_element_type.106), channel_id=1, source_target_pairs={{0,4},{4,0},{8,12},{12,8},{16,20},{20,16},{24,28},{28,24},{1,5},{5... | collective-permute-start | bytes 589832 | tf_op jit(solution)/shard_map/ppermute | solution.py:11
  566.5 5.8 collective-permute-start.13
  574.8 10.3 %collective-permute-start.14 = (bf16[384,256]{0,1:T(8,128)(2,1)}, bf16[384,256]{0,1:T(8,128)(2,1)}, u32[]{:S(2)}, u32[]{:S(2)}) collective-permute-start(bf16[384,256]{0,1:T(8,128)(2,1)} %fusion.17), channel_id=1, source_target_pairs={{0,16},{4,20},{8,24},{12,28},{16,0},{20,4},{24,8},{28,12},{1,17},{... | collective-permute-start | bytes 589832 | tf_op jit(solution)/shard_map/ppermute | solution.py:11
  (31 other events, 205.7 us)
Sparse Core Ops, SparseCore 0:
  9.6 31.2 all-gather.8
  56.7 28.1 reduce-scatter.4
  86.5 19.6 all-gather.10
  107.7 19.6 all-gather.12
  152.3 19.6 all-gather.14
  191.1 28.1 reduce-scatter.6
  229.0 19.6 all-gather.16
  303.2 20.6 all-gather.18
  338.9 28.1 reduce-scatter.8
  388.3 19.0 all-gather.20
  496.6 18.9 all-gather.22
  529.3 28.1 reduce-scatter.10
where the time goes:
time: 606 us; the launch traced here: 602 us
  waiting for transfers between devices  412 us (68%)
  local copies, waits for them, and re-layouts  52.2 us (9%)
  matrix products  47.7 us (8%)
  other arithmetic  31 us (5%)
  starting transfers between devices  22.1 us (4%)
  blocking collectives  21.7 us (4%)
  between operations  15.1 us (2%)
    ppermute x15, waiting for transfers between devices, partner_2(): lax.ppermute(value, axis, [(i, i ^ 1 << apart) for i in range(lax.axis_si...  234 us
    reduce_scatter x4, waiting for transfers between devices, reduce_sliced(): lax.psum_scatter(partial_value, 'rows', scatter_dimension=0, tiled=True)  112 us
    all_gather x2, waiting for transfers between devices, stack_group(): gathered = lax.all_gather(local_rows, 'rows', axis=0, tiled=True)  54.2 us
    dot_general x6, local copies, waits for them, and re-layouts, place_rows(): jnp.einsum('us,ubn->sbn', selector, blocks, precision=lax.Precision.HIGHEST)  30.6 us
    dot_general x6, matrix products, place_rows(): jnp.einsum('us,ubn->sbn', selector, blocks, precision=lax.Precision.HIGHEST)  22.4 us
    ppermute x15, starting transfers between devices, partner_2(): lax.ppermute(value, axis, [(i, i ^ 1 << apart) for i in range(lax.axis_si...  20.7 us
    dot_general x4, matrix products, per_device(): jnp.dot(inverse_list[level_index], prepared, preferred_element_type=jnp.f...  15.2 us
    all_gather x2, blocking collectives, stack_group(): gathered = lax.all_gather(local_rows, 'rows', axis=0, tiled=True)  13.7 us
  transfers between devices with their start and end apart: 27, of which 19 were waited for; matrix products, arithmetic and copies ran while one was open for 9% of the time, Pallas kernels for 0%

commit v1 on v0

v1 whole, which is shorter than its diff:
```python
import functools

import jax
import jax.numpy as jnp
from jax import lax
from jax.experimental import pallas as pl
from jax.experimental.pallas import tpu as pltpu
from jax.sharding import Mesh
from jax.sharding import PartitionSpec as P

BF16 = jnp.bfloat16
F32 = jnp.float32
AXES = ("hi", "z2", "z1", "x", "rows")
VMEM = pl.BlockSpec(memory_space=pltpu.VMEM)
SMEM = pl.BlockSpec(memory_space=pltpu.SMEM)
MIB = 1 << 20


def permute(value, mask, upward=0):
    total = lax.axis_size(AXES)
    pairs = [(i, i ^ mask) for i in range(total) if not upward or (i ^ mask) > i]
    return lax.ppermute(value, AXES, pairs)


def in_vmem(value):
    return pltpu.with_memory_space_constraint(value, pltpu.VMEM)


def row_tile(rows):
    return next(t for t in (512, 384, 256, 192, 128, 96, 64, 48, 32, 16) if rows % t == 0)


def call(kernel, outs, scalars, operands, scratch=(), limit=24, flops=0):
    return pl.pallas_call(
        kernel,
        out_shape=[pltpu.VMEM(o.shape, o.dtype) for o in outs],
        in_specs=[SMEM] + [VMEM] * len(operands),
        out_specs=[VMEM] * len(outs),
        scratch_shapes=list(scratch),
        compiler_params=pltpu.CompilerParams(vmem_limit_bytes=limit * MIB),
        cost_estimate=pl.CostEstimate(
            flops=flops,
            bytes_accessed=sum(o.size * o.dtype.itemsize for o in operands),
            transcendentals=0,
        ),
    )(scalars, *[in_vmem(o) for o in operands])


def piece_kernel(has_acc, scalars, a0, a1, b0, b1, *rest):
    out = rest[-1]
    total = jnp.dot(a0[...], b0[...], preferred_element_type=F32)
    total += jnp.dot(a1[...], b1[...], preferred_element_type=F32)
    if has_acc:
        total += rest[0][...]
    out[...] = total.astype(out.dtype)


def add_pieces(inverse, columns, b0, b1, acc, out_dtype):
    rows, depth = inverse.shape[0], b0.shape[0]
    cols = b0.shape[1]
    tile = row_tile(rows)
    whole = pl.BlockSpec((depth, cols), lambda i, s: (0, 0))
    block = pl.BlockSpec((tile, cols), lambda i, s: (i, 0))
    specs = [
        pl.BlockSpec((tile, depth), lambda i, s: (i, s[0])),
        pl.BlockSpec((tile, depth), lambda i, s: (i, s[1])),
        whole,
        whole,
    ]
    operands = [inverse, inverse, b0, b1]
    if acc is not None:
        specs.append(block)
        operands.append(acc)
    return pl.pallas_call(
        functools.partial(piece_kernel, acc is not None),
        out_shape=jax.ShapeDtypeStruct((rows, cols), out_dtype),
        grid_spec=pltpu.PrefetchScalarGridSpec(
            num_scalar_prefetch=1, grid=(rows // tile,), in_specs=specs, out_specs=block
        ),
        compiler_params=pltpu.CompilerParams(vmem_limit_bytes=24 * MIB),
        cost_estimate=pl.CostEstimate(
            flops=4 * rows * depth * cols, bytes_accessed=4 * rows * depth, transcendentals=0
        ),
    )(columns, *operands)


def split_panel(core, panel, x_ref, keep, send):
    rows, half = keep.shape
    tile = row_tile(rows)

    def step(i, carry):
        at = pl.ds(pl.multiple_of(i * tile, tile), tile)
        part = jnp.dot(panel[at, :], x_ref[...], preferred_element_type=F32)
        low, high = part[:, :half], part[:, half:]
        keep[at, :] = jnp.where(core == 0, low, high)
        send[at, :] = jnp.where(core == 0, high, low).astype(BF16)
        return carry

    lax.fori_loop(0, rows // tile, step, 0)


def panel_kernel(scalars, panel, x_ref, keep, send):
    split_panel(scalars[0], panel, x_ref, keep, send)


def first_sum_kernel(chunk, scalars, keep, received, own, *sends):
    for mask in range(len(sends) + 1):
        at = pl.ds(pl.multiple_of((scalars[1] ^ mask) * chunk, chunk), chunk)
        total = keep[at, :] + received[at, :].astype(F32)
        if mask == 0:
            own[...] = total
        else:
            sends[mask - 1][...] = total.astype(BF16)


def second_sum_kernel(scalars, own, *rest):
    total = own[...]
    for other in rest[:-1]:
        total += other[...].astype(F32)
    rest[-1][...] = total.astype(rest[-1].dtype)


def reduce_plane(keep, send, scalars, masks):
    received = permute(send, 1)
    chunk, half = keep.shape[0] // len(masks), keep.shape[1]
    shapes = [jax.ShapeDtypeStruct((chunk, half), F32)]
    shapes += [jax.ShapeDtypeStruct((chunk, half), BF16)] * (len(masks) - 1)
    own, *sends = call(
        functools.partial(first_sum_kernel, chunk), shapes, scalars, [keep, received]
    )
    arrived = [permute(value, mask) for value, mask in zip(sends, masks[1:])]
    return call(
        second_sum_kernel,
        [jax.ShapeDtypeStruct((chunk, half), BF16)],
        scalars,
        [own, *arrived],
    )[0]


def select_kernel(rows_blocks, width, table, source, target, sems):
    copies = []
    for i in range(rows_blocks):
        at = pl.multiple_of(table[i] * width, width)
        copies.append(
            pltpu.make_async_copy(
                source.at[:, pl.ds(at, width)],
                target.at[:, pl.ds(i * width, width)],
                sems.at[i],
            )
        )
    for copy in copies:
        copy.start()
    for copy in copies:
        copy.wait()


def select_columns(inverse, table, width):
    count = table.shape[0]
    return pl.pallas_call(
        functools.partial(select_kernel, count, width),
        out_shape=jax.ShapeDtypeStruct((inverse.shape[0], count * width), BF16),
        in_specs=[SMEM, pl.BlockSpec(memory_space=pl.ANY)],
        out_specs=pl.BlockSpec(memory_space=pl.ANY),
        scratch_shapes=[pltpu.SemaphoreType.DMA((count,))],
    )(table, inverse)


def level_kernel(slots, split, scalars, *refs):
    count = len(slots)
    pieces, (picked, base, panel) = refs[: 2 * count], refs[2 * count : 2 * count + 3]
    outs = refs[2 * count + 3 : -2]
    update, x_ref = refs[-2:]
    core, place = scalars[0], scalars[1]
    chunk, half = pieces[0].shape
    child = update.shape[0] // 2
    for j, (slot, mask) in enumerate(slots):
        at = pl.multiple_of(slot * child + (place ^ mask) * chunk, 16)
        update[pl.ds(at, chunk), :half] = pieces[2 * j][...]
        update[pl.ds(at, chunk), half:] = pieces[2 * j + 1][...]
    rows = picked.shape[0]
    tile = row_tile(rows)

    def step(i, carry):
        at = pl.ds(pl.multiple_of(i * tile, tile), tile)
        part = jnp.dot(picked[at, :], update[...], preferred_element_type=F32)
        low, high = part[:, :half], part[:, half:]
        x_low = base[at, :half] - jnp.where(core == 0, low, high)
        x_high = base[at, half:] - jnp.where(core == 0, high, low)
        outs[0][at, :half] = x_low.astype(BF16)
        outs[0][at, half:] = x_high.astype(BF16)
        return carry

    lax.fori_loop(0, rows // tile, step, 0)
    if split:
        split_panel(core, panel, outs[0], outs[1], outs[2])
    else:
        tile = row_tile(panel.shape[0])

        def panel_step(i, carry):
            at = pl.ds(pl.multiple_of(i * tile, tile), tile)
            outs[1][at, :] = jnp.dot(panel[at, :], outs[0][...], preferred_element_type=F32)
            return carry

        lax.fori_loop(0, panel.shape[0] // tile, panel_step, 0)


def solve_level(pieces, slots, scalars, picked, base, panel, split):
    rows, cols = base.shape
    total = panel.shape[0]
    outs = [jax.ShapeDtypeStruct((rows, cols), BF16)]
    if split:
        outs += [
            jax.ShapeDtypeStruct((total, cols // 2), F32),
            jax.ShapeDtypeStruct((total, cols // 2), BF16),
        ]
    else:
        outs.append(jax.ShapeDtypeStruct((total, cols), F32))
    return call(
        functools.partial(level_kernel, slots, split),
        outs,
        scalars,
        [*pieces, picked, base, panel],
        scratch=[pltpu.VMEM((picked.shape[1], cols), BF16), pltpu.VMEM((8, 128), F32)],
        flops=2 * cols * (picked.size + panel.size),
    )


def in_order(bit, own, other):
    return jnp.where(
        bit == 0, jnp.concatenate([own, other], 0), jnp.concatenate([other, own], 0)
    )


def per_device(
    loads_first,
    loads_second,
    loads_third,
    loads_fourth,
    inverse_first,
    inverse_second,
    inverse_third,
    inverse_fourth,
    panel_first,
    panel_second,
    panel_third,
    panel_fourth,
    blocks_first,
    blocks_second,
    blocks_third,
):
    n_rows = lax.axis_size("rows")
    n_y = n_rows // 2
    row_index = lax.axis_index("rows")
    core, y_index = row_index & 1, row_index >> 1
    x_index, z1, z2 = (lax.axis_index(a) for a in ("x", "z1", "z2"))
    leaf = ((lax.axis_index("hi") * 2 + z2) * 2 + z1) * 2 + x_index
    mask_x, mask_z1, mask_z2 = n_rows, 2 * n_rows, 4 * n_rows
    plane = [x * mask_x + y * 2 for x in range(2) for y in range(n_y)]
    plane_index = x_index * n_y + y_index
    column = [y * 2 for y in range(n_y)]
    by_column = jnp.stack([core, y_index]).astype(jnp.int32)
    by_plane = jnp.stack([core, plane_index]).astype(jnp.int32)
    update_rows = panel_first.shape[0]
    width = update_rows // blocks_first.shape[1]

    def gather_plane(value):
        return lax.all_gather(value, ("x", "rows"), axis=0, tiled=True)

    all_second = gather_plane(loads_second)
    pair_third = in_order(z1, loads_third, permute(loads_third, mask_z1))
    low = in_order(z1, loads_fourth, permute(loads_fourth, mask_z1))
    high = in_order(z1, permute(loads_fourth, mask_z2), permute(loads_fourth, mask_z2 | mask_z1))
    quad_fourth = in_order(z2, low, high)

    def by_z(value, count):
        rows, cols = value.shape
        each = rows // (2 * n_rows * count)
        split = value.reshape(2 * n_rows, count, each, cols)
        return split.transpose(1, 0, 2, 3).reshape(rows, cols)

    all_third = by_z(gather_plane(pair_third), 2)
    all_fourth = by_z(gather_plane(quad_fourth), 4)
    bases = [
        jnp.dot(inverse, loads, preferred_element_type=F32)
        for inverse, loads in (
            (inverse_second, all_second),
            (inverse_third, all_third),
            (inverse_fourth, all_fourth),
        )
    ]
    picked = []
    for level, (inverse, table) in enumerate(
        (
            (inverse_second, blocks_first),
            (inverse_third, blocks_second),
            (inverse_fourth, blocks_third),
        )
    ):
        child = leaf >> level
        rows = [lax.dynamic_index_in_dim(table, c, 0, keepdims=False) for c in (child, child ^ 1)]
        picked.append(select_columns(inverse, jnp.concatenate(rows), width))

    sibling = permute(loads_first, 1)
    acc = None
    for mask in column:
        if mask == 0:
            b0, b1 = loads_first, sibling
        else:
            b0 = permute(loads_first, mask, upward=1)
            b1 = permute(b0, 1)
        places = jnp.stack([row_index ^ mask, row_index ^ mask ^ 1]).astype(jnp.int32)
        last = mask == column[-1]
        acc = add_pieces(inverse_first, places, b0, b1, acc, BF16 if last else F32)
    solved_first = acc
    half = solved_first.shape[1] // 2
    keep, send = call(
        panel_kernel,
        [
            jax.ShapeDtypeStruct((update_rows, half), F32),
            jax.ShapeDtypeStruct((update_rows, half), BF16),
        ],
        by_column,
        [panel_first, solved_first],
        flops=2 * panel_first.size * 2 * half,
    )
    part = reduce_plane(keep, send, by_column, column)
    pieces, slots = [], []
    for mask in plane:
        piece = part if mask == 0 else permute(part, mask)
        pieces += [piece, permute(piece, 1)]
        slots.append((mask // mask_x, (mask % mask_x) // 2))

    solved_second, keep, send = solve_level(
        pieces, slots, by_column, picked[0], bases[0], panel_second, True
    )
    part = reduce_plane(keep, send, by_plane, plane)

    def spread(own, sib):
        pieces, slots = [], []
        for slot, value in ((0, own), (1, sib)):
            for place, mask in enumerate(plane):
                piece = value if mask == 0 else permute(value, mask)
                pieces += [piece, permute(piece, 1)]
                slots.append((slot, place))
        return pieces, slots

    pieces, slots = spread(part, permute(part, mask_z1))

    solved_third, keep, send = solve_level(
        pieces, slots, by_plane, picked[1], bases[1], panel_third, True
    )
    part = reduce_plane(keep, send, by_plane, plane)
    part = (part.astype(F32) + permute(part, mask_z1).astype(F32)).astype(BF16)
    pieces, slots = spread(part, permute(part, mask_z2))

    solved_fourth, total = solve_level(
        pieces, slots, by_plane, picked[2], bases[2], panel_fourth, False
    )
    each = update_rows // (8 * n_rows)
    cols = total.shape[1]

    def pick(value, index):
        return lax.dynamic_index_in_dim(value, index, 0, keepdims=False)

    total = total.reshape(4, 2 * n_y, 2, each, cols)
    keep = lax.dynamic_index_in_dim(total, core, 2, keepdims=False)
    send = lax.dynamic_index_in_dim(total, core ^ 1, 2, keepdims=False)
    total = keep + permute(send.astype(BF16), 1).astype(F32)
    own = lax.dynamic_index_in_dim(total, plane_index, 1, keepdims=False)
    for place, mask in enumerate(plane[1:], 1):
        value = lax.dynamic_index_in_dim(total, plane_index ^ place, 1, keepdims=False)
        own = own + permute(value.astype(BF16), mask).astype(F32)
    z_index = z2 * 2 + z1
    ancestor = pick(own, z_index)
    for m in range(1, 4):
        value = pick(own, z_index ^ m).astype(BF16)
        ancestor = ancestor + permute(value, m * mask_z1).astype(F32)
    return solved_first, solved_second, solved_third, solved_fourth, ancestor


def solution(mesh):
    n_leaf, n_rows = mesh.shape["leaf"], mesh.shape["rows"]
    fine = Mesh(mesh.devices.reshape(n_leaf // 8, 2, 2, 2, n_rows), AXES)
    rows, cols = P(AXES, None), P(None, AXES)
    return jax.shard_map(
        per_device,
        mesh=fine,
        in_specs=(rows,) * 8 + (cols,) * 4 + (P(),) * 3,
        out_specs=(rows,) * 5,
        check_vma=False,
    )
```

time: 606 us -> 474 us (0.78)
  waiting for transfers between devices: 412 us -> 66.4 us
  Pallas kernels: 0 us -> 282 us
  matrix products: 47.7 us -> 10.9 us
  starting transfers between devices: 22.1 us -> 58.8 us
  other arithmetic: 31 us -> 6.68 us
  blocking collectives: 21.7 us -> 0 us
  local copies, waits for them, and re-layouts: 52.2 us -> 34.6 us
    pallas_call x0 -> x15, Pallas kernels: none -> 282 us  [the longest x3 256 us: select_columns(): pl.pallas_call(functools.partial(select_kernel, count, width), out_shape=...]
    ppermute x15 -> x62, waiting for transfers between devices: 234 us -> 65.7 us  [permute(): return lax.ppermute(value, AXES, pairs)]
    reduce_scatter x4 -> x0, waiting for transfers between devices: 112 us -> none  [reduce_sliced(): lax.psum_scatter(partial_value, 'rows', scatter_dimension=0, tiled=True)]
    all_gather x8 -> x3, waiting for transfers between devices: 64.1 us -> 0.04 us  [gather_plane(): return lax.all_gather(value, ('x', 'rows'), axis=0, tiled=True)]
    ppermute x15 -> x62, starting transfers between devices: 20.7 us -> 58.7 us  [permute(): return lax.ppermute(value, AXES, pairs)]
    dot_general x14 -> x3, matrix products: 47.7 us -> 10.9 us  [per_device(): jnp.dot(inverse, loads, preferred_element_type=F32)]
    dot_general x6 -> x0, local copies, waits for them, and re-layouts: 30.6 us -> none  [place_rows(): jnp.einsum('us,ubn->sbn', selector, blocks, precision=lax.Precision.HIGHEST)]
    unnamed x75 -> x88, local copies, waits for them, and re-layouts: 7.12 us -> 29.2 us
  transfers between devices with their start and end apart: 27 -> 65, of which waited for: 19 -> 22; matrix products, arithmetic and copies ran while one was open for 9% -> 5% of each run, Pallas kernels for 0% -> 59%
where the time goes in v1:
time: 474 us; the launch traced here: 473 us
  Pallas kernels  282 us (59%)
  waiting for transfers between devices  66.4 us (14%)
  starting transfers between devices  58.8 us (12%)
  local copies, waits for them, and re-layouts  34.6 us (7%)
  between operations  14.4 us (3%)
  matrix products  10.9 us (2%)
  other arithmetic  6.68 us (1%)
    pallas_call x3, Pallas kernels, select_columns(): pl.pallas_call(functools.partial(select_kernel, count, width), out_shape=...  256 us
    ppermute x62, waiting for transfers between devices, permute(): return lax.ppermute(value, AXES, pairs)  65.7 us
    ppermute x62, starting transfers between devices, permute(): return lax.ppermute(value, AXES, pairs)  58.7 us
    unnamed x88, local copies, waits for them, and re-layouts  29.2 us
    pallas_call x10, Pallas kernels, call(): pl.pallas_call(kernel, out_shape=[pltpu.VMEM(o.shape, o.dtype) for o in o...  15.2 us
    dot_general x3, matrix products, per_device(): jnp.dot(inverse, loads, preferred_element_type=F32)  10.9 us
    pallas_call x2, Pallas kernels, add_pieces(): pl.pallas_call(functools.partial(piece_kernel, acc is not None), out_shap...  10.3 us
  transfers between devices with their start and end apart: 65, of which 22 were waited for; matrix products, arithmetic and copies ran while one was open for 5% of the time, Pallas kernels for 59%

profile of v1, /device:TPU:0, one launch (start us, length us, event | category | flops | bytes accessed | tf_op | source)
XLA Modules:
  0.0 473.4 jit_solution(16148210572301503328)
XLA Ops:
  8.0 3.1 collective-permute-start.31
  11.0 5.1 %collective-permute-done.31 = bf16[384,256]{1,0:T(8,128)(2,1)S(1)} collective-permute-done((bf16[384,256]{1,0:T(8,128)(2,1)}, bf16[384,256]{1,0:T(8,128)(2,1)S(1)}, u32[]{:S(2)}, u32[]{:S(2)}) %collective-permute-start.31) | collective-permute-done | bytes 196640 | tf_op jit(solution)/shard_map/ppermute | solution.py:22
  16.2 1.9 maximum_select_fusion
  18.1 4.5 collective-permute-start
  24.2 2.5 collective-permute-start.54
  28.5 19.8 %collective-permute-done.b0 = bf16[1536,256]{1,0:T(8,128)(2,1)} collective-permute-done((bf16[1536,256]{1,0:T(8,128)(2,1)}, bf16[1536,256]{1,0:T(8,128)(2,1)}, u32[]{:S(2)}, u32[]{:S(2)}) %collective-permute-start) | collective-permute-done | bytes 786464 | tf_op jit(solution)/shard_map/ppermute | solution.py:22
  50.3 6.4 %copy-done = bf16[1536,6144]{1,0:T(8,128)(2,1)S(1)} copy-done((bf16[1536,6144]{1,0:T(8,128)(2,1)S(1)}, bf16[1536,6144]{1,0:T(8,128)(2,1)}, u32[]{:S(2)}) %copy-start) | copy-done | bytes 18874392
  57.8 4.2 shard_map.182.rest_0_
  63.2 1.9 copy-done.1
  66.5 6.1 %shard_map.183.x_ref = bf16[1536,256]{1,0:T(8,128)(2,1)} custom-call(s32[2]{0:T(128)S(1)} %get-tuple-element.57.scalars, bf16[1536,6144]{1,0:T(8,128)(2,1)S(1)} %copy-done.1, bf16[1536,6144]{1,0:T(8,128)(2,1)S(1)} %copy-done.1, bf16[1536,256]{1,0:T(8,128)(2,1)} %collective-permute-done.b0, bf16[1536,256]{1,0:T(8,128)(2,1)} %collective-permute-done.1.b1, ...), custom_call_target="tpu_custom_call" | custom-call | flops 2415919104 | bytes 9437184 | tf_op jit(solution)/shard_map/pallas_call | solution.py:74
  72.6 2.3 copy-done.6
  76.0 2.3 shard_map.184
  80.8 2.7 collective-permute-start.4
  83.6 7.3 %collective-permute-done.4.rest_0_ = bf16[768,128]{1,0:T(8,128)(2,1)S(1)} collective-permute-done((bf16[768,128]{1,0:T(8,128)(2,1)S(1)}, bf16[768,128]{1,0:T(8,128)(2,1)S(1)}, u32[]{:S(2)}, u32[]{:S(2)}) %collective-permute-start.4) | collective-permute-done | bytes 196640 | tf_op jit(solution)/shard_map/ppermute | solution.py:22
  96.4 144.9 %shard_map.187.refs_8_ = bf16[768,3072]{1,0:T(8,128)(2,1)} custom-call(s32[24]{0:T(128)} %pad_add_fusion.3.table, bf16[768,6144]{1,0:T(8,128)(2,1)} %source.3), custom_call_target="tpu_custom_call" | custom-call | tf_op jit(solution)/shard_map/pallas_call | solution.py:159
  242.5 6.3 %fusion.17.refs_9_ = f32[768,256]{1,0:T(8,128)S(1)} fusion(bf16[768,6144]{1,0:T(8,128)(2,1)} %source.3, bf16[6144,256]{1,0:T(8,128)(2,1)} %all-gather.4.cloned.1.call-done), kind=kOutput, calls=%fused_computation.49 | convolution fusion | flops 2415919104 | bytes 13369344 | tf_op jit(solution)/shard_map/dot_general | solution.py:284
  254.9 4.7 %shard_map.188 = (bf16[768,256]{1,0:T(8,128)(2,1)S(1)}, f32[1536,128]{1,0:T(8,128)S(1)}, bf16[1536,128]{1,0:T(8,128)(2,1)}) custom-call(s32[2]{0:T(128)S(1)} %get-tuple-element.58.scalars, bf16[768,128]{1,0:T(8,128)(2,1)S(1)} %copy-done.12, bf16[768,128]{1,0:T(8,128)(2,1)S(1)} %copy-done.23, bf16[768,128]{1,0:T(8,128)(2,1)S(1)} %copy-done.17, ...), custom_call_target="tpu_custom_call" | custom-call | flops 1811939328 | bytes 9437184 | tf_op jit(solution)/shard_map/pallas_call | solution.py:34
  267.3 3.1 collective-permute-done.15.rest_2_
  276.1 3.1 collective-permute-done.23.refs_8_
  283.8 73.5 %shard_map.191.refs_16_ = bf16[384,3072]{1,0:T(8,128)(2,1)} custom-call(s32[24]{0:T(128)} %pad_add_fusion.5.table, bf16[384,6144]{1,0:T(8,128)(2,1)} %source.4), custom_call_target="tpu_custom_call" | custom-call | tf_op jit(solution)/shard_map/pallas_call | solution.py:159
  357.3 2.2 copy.28
  360.7 3.9 convolution_bitcast_fusion.refs_17_
  364.7 2.7 shard_map.192
  375.9 2.4 collective-permute-done.35.rest_2_
  380.7 2.8 collective-permute-done.36
  387.2 2.4 collective-permute-start.44
  389.6 4.9 %collective-permute-done.44.refs_8_ = bf16[384,128]{1,0:T(8,128)(2,1)S(1)} collective-permute-done((bf16[384,128]{1,0:T(8,128)(2,1)S(1)}, bf16[384,128]{1,0:T(8,128)(2,1)S(1)}, u32[]{:S(2)}, u32[]{:S(2)}) %collective-permute-start.44) | collective-permute-done | bytes 98336 | tf_op jit(solution)/shard_map/ppermute | solution.py:22
  399.1 37.7 %shard_map.195.refs_16_ = bf16[192,3072]{1,0:T(8,128)(2,1)} custom-call(s32[24]{0:T(128)} %pad_add_fusion.6.table, bf16[192,6144]{1,0:T(8,128)(2,1)} %source.5), custom_call_target="tpu_custom_call" | custom-call | tf_op jit(solution)/shard_map/pallas_call | solution.py:159
  436.9 2.4 copy.30
  446.2 2.0 shard_map.196
  453.7 3.0 collective-permute-done.58
  458.2 3.4 collective-permute-start.61
  (229 shorter events, 83.7 us)
Async XLA Ops:
  7.2 235.3 %all-gather.4.cloned.1.call-start = ((), (), s32[]{:S(2)}) async-start(), calls=%async_computation | async-start | bytes 3538944 | tf_op jit(solution)/shard_map/all_gather | solution.py:267
  7.9 349.4 %all-gather.6.cloned.1.call-start = ((), (), s32[]{:S(2)}) async-start(), calls=%async_computation.1 | async-start | bytes 3538944 | tf_op jit(solution)/shard_map/all_gather | solution.py:267
  8.0 8.2 %collective-permute-start.31 = (bf16[384,256]{1,0:T(8,128)(2,1)}, bf16[384,256]{1,0:T(8,128)(2,1)S(1)}, u32[]{:S(2)}, u32[]{:S(2)}) collective-permute-start(bf16[384,256]{1,0:T(8,128)(2,1)} %param.17), channel_id=1, source_target_pairs={{0,8},{1,9},{2,10},{3,11},{4,12},{5,13},{6,14},{7,15},{8,0},{9,1},... | collective-permute-start | bytes 589832 | tf_op jit(solution)/shard_map/ppermute | solution.py:22
  18.1 418.8 %all-gather.8.cloned.1.call-start = ((), (), s32[]{:S(2)}) async-start(), calls=%async_computation.2 | async-start | bytes 3538944 | tf_op jit(solution)/shard_map/all_gather | solution.py:267
  18.1 30.2 %collective-permute-start = (bf16[1536,256]{1,0:T(8,128)(2,1)}, bf16[1536,256]{1,0:T(8,128)(2,1)}, u32[]{:S(2)}, u32[]{:S(2)}) collective-permute-start(bf16[1536,256]{1,0:T(8,128)(2,1)} %b0.1), channel_id=1, source_target_pairs={{0,2},{1,3},{4,6},{5,7},{8,10},{9,11},{12,14},{13,15},{16,18},{17,... | collective-permute-start | bytes 2359304 | tf_op jit(solution)/shard_map/ppermute | solution.py:22
  24.2 25.3 %collective-permute-start.2 = (bf16[1536,256]{1,0:T(8,128)(2,1)}, bf16[1536,256]{1,0:T(8,128)(2,1)S(1)}, u32[]{:S(2)}, u32[]{:S(2)}) collective-permute-start(bf16[1536,256]{1,0:T(8,128)(2,1)} %b0.1), channel_id=1, source_target_pairs={{0,1},{1,0},{2,3},{3,2},{4,5},{5,4},{6,7},{7,6},{8,9},{9,8},{10,11... | collective-permute-start | bytes 2359304 | tf_op jit(solution)/shard_map/ppermute | solution.py:22
  24.2 24.1 %collective-permute-start.54 = (bf16[192,256]{1,0:T(8,128)(2,1)}, bf16[192,256]{1,0:T(8,128)(2,1)S(1)}, u32[]{:S(2)}, u32[]{:S(2)}) collective-permute-start(bf16[192,256]{1,0:T(8,128)(2,1)} %param.18), channel_id=1, source_target_pairs={{0,24},{1,25},{2,26},{3,27},{4,28},{5,29},{6,30},{7,31},{8,16},{9,... | collective-permute-start | bytes 294920 | tf_op jit(solution)/shard_map/ppermute | solution.py:22
  26.6 21.6 %collective-permute-start.53 = (bf16[192,256]{1,0:T(8,128)(2,1)}, bf16[192,256]{1,0:T(8,128)(2,1)S(1)}, u32[]{:S(2)}, u32[]{:S(2)}) collective-permute-start(bf16[192,256]{1,0:T(8,128)(2,1)} %param.18), channel_id=1, source_target_pairs={{0,16},{1,17},{2,18},{3,19},{4,20},{5,21},{6,22},{7,23},{8,24},{9,... | collective-permute-start | bytes 294920 | tf_op jit(solution)/shard_map/ppermute | solution.py:22
  48.3 14.9 %collective-permute-start.1 = (bf16[1536,256]{1,0:T(8,128)(2,1)}, bf16[1536,256]{1,0:T(8,128)(2,1)}, u32[]{:S(2)}, u32[]{:S(2)}) collective-permute-start(bf16[1536,256]{1,0:T(8,128)(2,1)} %collective-permute-done.b0), channel_id=1, source_target_pairs={{0,1},{1,0},{2,3},{3,2},{4,5},{5,4},{6,7},{7,6},{8,9},{9,8},{10,11... | collective-permute-start | bytes 2359304 | tf_op jit(solution)/shard_map/ppermute | solution.py:22
  80.8 10.1 %collective-permute-start.4 = (bf16[768,128]{1,0:T(8,128)(2,1)S(1)}, bf16[768,128]{1,0:T(8,128)(2,1)S(1)}, u32[]{:S(2)}, u32[]{:S(2)}) collective-permute-start(bf16[768,128]{1,0:T(8,128)(2,1)S(1)} %get-tuple-element.28), channel_id=1, source_target_pairs={{0,2},{1,3},{2,0},{3,1},{4,6},{5,7},{6,4},{7,5},{8,10},{9,11},{10,... | collective-permute-start | bytes 589832 | tf_op jit(solution)/shard_map/ppermute | solution.py:22
  91.5 149.9 %collective-permute-start.6 = (bf16[768,128]{1,0:T(8,128)(2,1)S(1)}, bf16[768,128]{1,0:T(8,128)(2,1)S(1)}, u32[]{:S(2)}, u32[]{:S(2)}) collective-permute-start(bf16[768,128]{1,0:T(8,128)(2,1)S(1)} %shard_map.186.refs_0_), channel_id=1, source_target_pairs={{0,2},{1,3},{2,0},{3,1},{4,6},{5,7},{6,4},{7,5},{8,10},{9,11},{10,... | collective-permute-start | bytes 589832 | tf_op jit(solution)/shard_map/ppermute | solution.py:22
  91.9 150.1 %collective-permute-start.8 = (bf16[768,128]{1,0:T(8,128)(2,1)S(1)}, bf16[768,128]{1,0:T(8,128)(2,1)S(1)}, u32[]{:S(2)}, u32[]{:S(2)}) collective-permute-start(bf16[768,128]{1,0:T(8,128)(2,1)S(1)} %shard_map.186.refs_0_), channel_id=1, source_target_pairs={{0,4},{1,5},{2,6},{3,7},{4,0},{5,1},{6,2},{7,3},{8,12},{9,13},{10,... | collective-permute-start | bytes 589832 | tf_op jit(solution)/shard_map/ppermute | solution.py:22
  93.6 148.5 %collective-permute-start.10 = (bf16[768,128]{1,0:T(8,128)(2,1)S(1)}, bf16[768,128]{1,0:T(8,128)(2,1)S(1)}, u32[]{:S(2)}, u32[]{:S(2)}) collective-permute-start(bf16[768,128]{1,0:T(8,128)(2,1)S(1)} %shard_map.186.refs_0_), channel_id=1, source_target_pairs={{0,6},{1,7},{2,4},{3,5},{4,2},{5,3},{6,0},{7,1},{8,14},{9,15},{10,... | collective-permute-start | bytes 589832 | tf_op jit(solution)/shard_map/ppermute | solution.py:22
  242.0 8.2 %collective-permute-start.9 = (bf16[768,128]{1,0:T(8,128)(2,1)S(1)}, bf16[768,128]{1,0:T(8,128)(2,1)}, u32[]{:S(2)}, u32[]{:S(2)}) collective-permute-start(bf16[768,128]{1,0:T(8,128)(2,1)S(1)} %collective-permute-done.8.refs_4_), channel_id=1, source_target_pairs={{0,1},{1,0},{2,3},{3,2},{4,5},{5,4},{6,7},{7,6},{8,9},{9,8},{10,11... | collective-permute-start | bytes 589832 | tf_op jit(solution)/shard_map/ppermute | solution.py:22
  271.0 9.1 %collective-permute-start.16 = (bf16[384,128]{1,0:T(8,128)(2,1)S(1)}, bf16[384,128]{1,0:T(8,128)(2,1)S(1)}, u32[]{:S(2)}, u32[]{:S(2)}) collective-permute-start(bf16[384,128]{1,0:T(8,128)(2,1)S(1)} %shard_map.190.refs_0_), channel_id=1, source_target_pairs={{0,1},{1,0},{2,3},{3,2},{4,5},{5,4},{6,7},{7,6},{8,9},{9,8},{10,11... | collective-permute-start | bytes 294920 | tf_op jit(solution)/shard_map/ppermute | solution.py:22
  271.1 10.2 %collective-permute-start.17 = (bf16[384,128]{1,0:T(8,128)(2,1)S(1)}, bf16[384,128]{1,0:T(8,128)(2,1)S(1)}, u32[]{:S(2)}, u32[]{:S(2)}) collective-permute-start(bf16[384,128]{1,0:T(8,128)(2,1)S(1)} %shard_map.190.refs_0_), channel_id=1, source_target_pairs={{0,2},{1,3},{2,0},{3,1},{4,6},{5,7},{6,4},{7,5},{8,10},{9,11},{10,... | collective-permute-start | bytes 294920 | tf_op jit(solution)/shard_map/ppermute | solution.py:22
  272.0 10.8 %collective-permute-start.19 = (bf16[384,128]{1,0:T(8,128)(2,1)S(1)}, bf16[384,128]{1,0:T(8,128)(2,1)S(1)}, u32[]{:S(2)}, u32[]{:S(2)}) collective-permute-start(bf16[384,128]{1,0:T(8,128)(2,1)S(1)} %shard_map.190.refs_0_), channel_id=1, source_target_pairs={{0,4},{1,5},{2,6},{3,7},{4,0},{5,1},{6,2},{7,3},{8,12},{9,13},{10,... | collective-permute-start | bytes 294920 | tf_op jit(solution)/shard_map/ppermute | solution.py:22
  273.2 9.6 %collective-permute-start.21 = (bf16[384,128]{1,0:T(8,128)(2,1)S(1)}, bf16[384,128]{1,0:T(8,128)(2,1)S(1)}, u32[]{:S(2)}, u32[]{:S(2)}) collective-permute-start(bf16[384,128]{1,0:T(8,128)(2,1)S(1)} %shard_map.190.refs_0_), channel_id=1, source_target_pairs={{0,6},{1,7},{2,4},{3,5},{4,2},{5,3},{6,0},{7,1},{8,14},{9,15},{10,... | collective-permute-start | bytes 294920 | tf_op jit(solution)/shard_map/ppermute | solution.py:22
  279.2 80.9 %collective-permute-start.25 = (bf16[384,128]{1,0:T(8,128)(2,1)S(1)}, bf16[384,128]{1,0:T(8,128)(2,1)S(1)}, u32[]{:S(2)}, u32[]{:S(2)}) collective-permute-start(bf16[384,128]{1,0:T(8,128)(2,1)S(1)} %collective-permute-done.23.refs_8_), channel_id=1, source_target_pairs={{0,2},{1,3},{2,0},{3,1},{4,6},{5,7},{6,4},{7,5},{8,10},{9,11},{10,... | collective-permute-start | bytes 294920 | tf_op jit(solution)/shard_map/ppermute | solution.py:22
  280.1 80.1 %collective-permute-start.27 = (bf16[384,128]{1,0:T(8,128)(2,1)S(1)}, bf16[384,128]{1,0:T(8,128)(2,1)S(1)}, u32[]{:S(2)}, u32[]{:S(2)}) collective-permute-start(bf16[384,128]{1,0:T(8,128)(2,1)S(1)} %collective-permute-done.23.refs_8_), channel_id=1, source_target_pairs={{0,4},{1,5},{2,6},{3,7},{4,0},{5,1},{6,2},{7,3},{8,12},{9,13},{10,... | collective-permute-start | bytes 294920 | tf_op jit(solution)/shard_map/ppermute | solution.py:22
  281.3 79.3 %collective-permute-start.29 = (bf16[384,128]{1,0:T(8,128)(2,1)S(1)}, bf16[384,128]{1,0:T(8,128)(2,1)S(1)}, u32[]{:S(2)}, u32[]{:S(2)}) collective-permute-start(bf16[384,128]{1,0:T(8,128)(2,1)S(1)} %collective-permute-done.23.refs_8_), channel_id=1, source_target_pairs={{0,6},{1,7},{2,4},{3,5},{4,2},{5,3},{6,0},{7,1},{8,14},{9,15},{10,... | collective-permute-start | bytes 294920 | tf_op jit(solution)/shard_map/ppermute | solution.py:22
  282.7 76.8 %collective-permute-start.18 = (bf16[384,128]{1,0:T(8,128)(2,1)S(1)}, bf16[384,128]{1,0:T(8,128)(2,1)S(1)}, u32[]{:S(2)}, u32[]{:S(2)}) collective-permute-start(bf16[384,128]{1,0:T(8,128)(2,1)S(1)} %collective-permute-done.17.refs_2_), channel_id=1, source_target_pairs={{0,1},{1,0},{2,3},{3,2},{4,5},{5,4},{6,7},{7,6},{8,9},{9,8},{10,11... | collective-permute-start | bytes 294920 | tf_op jit(solution)/shard_map/ppermute | solution.py:22
  282.7 76.9 %collective-permute-start.20 = (bf16[384,128]{1,0:T(8,128)(2,1)S(1)}, bf16[384,128]{1,0:T(8,128)(2,1)S(1)}, u32[]{:S(2)}, u32[]{:S(2)}) collective-permute-start(bf16[384,128]{1,0:T(8,128)(2,1)S(1)} %collective-permute-done.19.refs_4_), channel_id=1, source_target_pairs={{0,1},{1,0},{2,3},{3,2},{4,5},{5,4},{6,7},{7,6},{8,9},{9,8},{10,11... | collective-permute-start | bytes 294920 | tf_op jit(solution)/shard_map/ppermute | solution.py:22
  383.6 11.8 %collective-permute-start.37 = (bf16[384,128]{1,0:T(8,128)(2,1)S(1)}, bf16[384,128]{1,0:T(8,128)(2,1)S(1)}, u32[]{:S(2)}, u32[]{:S(2)}) collective-permute-start(bf16[384,128]{1,0:T(8,128)(2,1)S(1)} %add_convert_fusion.refs_0_), channel_id=1, source_target_pairs={{0,1},{1,0},{2,3},{3,2},{4,5},{5,4},{6,7},{7,6},{8,9},{9,8},{10,11... | collective-permute-start | bytes 294920 | tf_op jit(solution)/shard_map/ppermute | solution.py:22
  383.7 12.9 %collective-permute-start.38 = (bf16[384,128]{1,0:T(8,128)(2,1)S(1)}, bf16[384,128]{1,0:T(8,128)(2,1)S(1)}, u32[]{:S(2)}, u32[]{:S(2)}) collective-permute-start(bf16[384,128]{1,0:T(8,128)(2,1)S(1)} %add_convert_fusion.refs_0_), channel_id=1, source_target_pairs={{0,2},{1,3},{2,0},{3,1},{4,6},{5,7},{6,4},{7,5},{8,10},{9,11},{10,... | collective-permute-start | bytes 294920 | tf_op jit(solution)/shard_map/ppermute | solution.py:22
  384.6 13.5 %collective-permute-start.40 = (bf16[384,128]{1,0:T(8,128)(2,1)S(1)}, bf16[384,128]{1,0:T(8,128)(2,1)S(1)}, u32[]{:S(2)}, u32[]{:S(2)}) collective-permute-start(bf16[384,128]{1,0:T(8,128)(2,1)S(1)} %add_convert_fusion.refs_0_), channel_id=1, source_target_pairs={{0,4},{1,5},{2,6},{3,7},{4,0},{5,1},{6,2},{7,3},{8,12},{9,13},{10,... | collective-permute-start | bytes 294920 | tf_op jit(solution)/shard_map/ppermute | solution.py:22
  385.7 12.3 %collective-permute-start.42 = (bf16[384,128]{1,0:T(8,128)(2,1)S(1)}, bf16[384,128]{1,0:T(8,128)(2,1)S(1)}, u32[]{:S(2)}, u32[]{:S(2)}) collective-permute-start(bf16[384,128]{1,0:T(8,128)(2,1)S(1)} %add_convert_fusion.refs_0_), channel_id=1, source_target_pairs={{0,6},{1,7},{2,4},{3,5},{4,2},{5,3},{6,0},{7,1},{8,14},{9,15},{10,... | collective-permute-start | bytes 294920 | tf_op jit(solution)/shard_map/ppermute | solution.py:22
  394.5 45.4 %collective-permute-start.46 = (bf16[384,128]{1,0:T(8,128)(2,1)S(1)}, bf16[384,128]{1,0:T(8,128)(2,1)S(1)}, u32[]{:S(2)}, u32[]{:S(2)}) collective-permute-start(bf16[384,128]{1,0:T(8,128)(2,1)S(1)} %collective-permute-done.44.refs_8_), channel_id=1, source_target_pairs={{0,2},{1,3},{2,0},{3,1},{4,6},{5,7},{6,4},{7,5},{8,10},{9,11},{10,... | collective-permute-start | bytes 294920 | tf_op jit(solution)/shard_map/ppermute | solution.py:22
  395.4 44.7 %collective-permute-start.48 = (bf16[384,128]{1,0:T(8,128)(2,1)S(1)}, bf16[384,128]{1,0:T(8,128)(2,1)S(1)}, u32[]{:S(2)}, u32[]{:S(2)}) collective-permute-start(bf16[384,128]{1,0:T(8,128)(2,1)S(1)} %collective-permute-done.44.refs_8_), channel_id=1, source_target_pairs={{0,4},{1,5},{2,6},{3,7},{4,0},{5,1},{6,2},{7,3},{8,12},{9,13},{10,... | collective-permute-start | bytes 294920 | tf_op jit(solution)/shard_map/ppermute | solution.py:22
  396.6 43.9 %collective-permute-start.50 = (bf16[384,128]{1,0:T(8,128)(2,1)S(1)}, bf16[384,128]{1,0:T(8,128)(2,1)S(1)}, u32[]{:S(2)}, u32[]{:S(2)}) collective-permute-start(bf16[384,128]{1,0:T(8,128)(2,1)S(1)} %collective-permute-done.44.refs_8_), channel_id=1, source_target_pairs={{0,6},{1,7},{2,4},{3,5},{4,2},{5,3},{6,0},{7,1},{8,14},{9,15},{10,... | collective-permute-start | bytes 294920 | tf_op jit(solution)/shard_map/ppermute | solution.py:22
  398.0 41.3 %collective-permute-start.39 = (bf16[384,128]{1,0:T(8,128)(2,1)S(1)}, bf16[384,128]{1,0:T(8,128)(2,1)S(1)}, u32[]{:S(2)}, u32[]{:S(2)}) collective-permute-start(bf16[384,128]{1,0:T(8,128)(2,1)S(1)} %collective-permute-done.38.refs_2_), channel_id=1, source_target_pairs={{0,1},{1,0},{2,3},{3,2},{4,5},{5,4},{6,7},{7,6},{8,9},{9,8},{10,11... | collective-permute-start | bytes 294920 | tf_op jit(solution)/shard_map/ppermute | solution.py:22
  398.0 41.4 %collective-permute-start.41 = (bf16[384,128]{1,0:T(8,128)(2,1)S(1)}, bf16[384,128]{1,0:T(8,128)(2,1)S(1)}, u32[]{:S(2)}, u32[]{:S(2)}) collective-permute-start(bf16[384,128]{1,0:T(8,128)(2,1)S(1)} %collective-permute-done.40.refs_4_), channel_id=1, source_target_pairs={{0,1},{1,0},{2,3},{3,2},{4,5},{5,4},{6,7},{7,6},{8,9},{9,8},{10,11... | collective-permute-start | bytes 294920 | tf_op jit(solution)/shard_map/ppermute | solution.py:22
  (75 other events, 563.8 us)
Sparse Core Ops, SparseCore 0:
  9.9 40.4 all-gather.3
  52.3 38.0 all-gather.5
  92.3 33.4 all-gather.7

commit v2 on v0

v2 whole, which is shorter than its diff:
```python
import functools
import math

import jax
import jax.numpy as jnp
from jax import lax
from jax.experimental import pallas as pl
from jax.experimental.pallas import tpu as pltpu
from jax.sharding import Mesh
from jax.sharding import PartitionSpec as P

BF16 = jnp.bfloat16
F32 = jnp.float32
AXES = ("hi", "z2", "z1", "x", "y", "core")
PLANE = ("x", "y")
VMEM = pl.BlockSpec(memory_space=pltpu.VMEM)
SMEM = pl.BlockSpec(memory_space=pltpu.SMEM)
MIB = 1 << 20


def permute(value, mask, upward=False):
    total = lax.axis_size(AXES)
    pairs = [(i, i ^ mask) for i in range(total) if not upward or (i ^ mask) > i]
    return lax.ppermute(value, AXES, pairs)


def row_tile(rows):
    return next(t for t in (512, 384, 256, 192, 128, 96, 64, 48, 32, 16) if rows % t == 0)


def aval(rows, cols, dtype):
    return jax.ShapeDtypeStruct((rows, cols), dtype)


def call(kernel, outs, scalars, operands, scratch=(), limit=12, flops=0):
    operands = [pltpu.with_memory_space_constraint(o, pltpu.VMEM) for o in operands]
    return pl.pallas_call(
        kernel,
        out_shape=[pltpu.VMEM(o.shape, o.dtype) for o in outs],
        in_specs=[SMEM] + [VMEM] * len(operands),
        out_specs=[VMEM] * len(outs),
        scratch_shapes=list(scratch),
        compiler_params=pltpu.CompilerParams(vmem_limit_bytes=limit * MIB),
        cost_estimate=pl.CostEstimate(
            flops=flops,
            bytes_accessed=sum(o.size * o.dtype.itemsize for o in operands),
            transcendentals=0,
        ),
    )(scalars, *operands)


def tiles(rows, step):
    tile = row_tile(rows)

    def body(i, carry):
        step(pl.ds(pl.multiple_of(i * tile, tile), tile))
        return carry

    lax.fori_loop(0, rows // tile, body, 0)


def dot(a, b):
    return jnp.dot(a, b, preferred_element_type=F32)


def piece_kernel(scalars, inverse, b0, b1, *rest):
    out, depth = rest[-1], b0.shape[0]
    at0 = pl.ds(pl.multiple_of(scalars[1] * depth, depth), depth)
    at1 = pl.ds(pl.multiple_of(scalars[2] * depth, depth), depth)

    def step(at):
        total = dot(inverse[at, at0], b0[...]) + dot(inverse[at, at1], b1[...])
        if len(rest) > 1:
            total += rest[0][at, :]
        out[at, :] = total

    tiles(inverse.shape[0], step)


def last_piece_kernel(scalars, inverse, b0, b1, acc, panel, out, keep, send):
    depth = b0.shape[0]
    at0 = pl.ds(pl.multiple_of(scalars[1] * depth, depth), depth)
    at1 = pl.ds(pl.multiple_of(scalars[2] * depth, depth), depth)

    def step(at):
        total = acc[at, :] + dot(inverse[at, at0], b0[...])
        out[at, :] = (total + dot(inverse[at, at1], b1[...])).astype(BF16)

    tiles(inverse.shape[0], step)
    split_panel(scalars[0], panel, out, keep, send)


def split_panel(core, panel, x_ref, keep, send):
    half = keep.shape[1]

    def step(at):
        part = dot(panel[at, :], x_ref[...])
        low, high = part[:, :half], part[:, half:]
        keep[at, :] = jnp.where(core == 0, low, high)
        send[at, :] = jnp.where(core == 0, high, low).astype(BF16)

    tiles(panel.shape[0], step)


def pair_sum_kernel(scalars, keep, received, out):
    out[...] = (keep[...] + received[...].astype(F32)).astype(out.dtype)


def chunk_sum_kernel(count, scalars, chunks, out):
    rows = out.shape[0]
    total = chunks[:rows, :].astype(F32)
    for i in range(1, count):
        total += chunks[i * rows : (i + 1) * rows, :].astype(F32)
    out[...] = total.astype(out.dtype)


def reduce_over(value, axes, scalars, dtype):
    count = lax.axis_size(axes)
    arrived = lax.all_to_all(value, axes, 0, 0, tiled=True)
    rows, cols = value.shape
    return call(
        functools.partial(chunk_sum_kernel, count),
        [aval(rows // count, cols, dtype)],
        scalars,
        [arrived],
    )[0]


def pair_sum(keep, send, scalars):
    received = permute(send, 1)
    return call(pair_sum_kernel, [aval(*keep.shape, BF16)], scalars, [keep, received])[0]


def level_kernel(places, unit, last, scalars, table, mine, other, loads, inverse, panel, *rest):
    solved, keep, send, ready = rest[:4]
    core, half, width = scalars[0], mine.shape[1], table.shape[1]
    block = panel.shape[0] // width
    ready[...] = loads[...]
    for i, (child, index, row) in enumerate(places):
        at = pl.multiple_of(table[child, index] * block + row, unit)
        a = mine[i * unit : (i + 1) * unit, :].astype(F32)
        b = other[i * unit : (i + 1) * unit, :].astype(F32)
        low = ready[pl.ds(at, unit), :half].astype(F32) - jnp.where(core == 0, a, b)
        high = ready[pl.ds(at, unit), half:].astype(F32) - jnp.where(core == 0, b, a)
        ready[pl.ds(at, unit), :half] = low.astype(BF16)
        ready[pl.ds(at, unit), half:] = high.astype(BF16)

    def step(at):
        solved[at, :] = dot(inverse[at, :], ready[...]).astype(BF16)

    tiles(inverse.shape[0], step)
    if not last:
        split_panel(core, panel, solved, keep, send)
        return
    total, outgoing = rest[4:]

    def panel_step(at):
        total[at, :] = dot(panel[at, :], solved[...])

    tiles(panel.shape[0], panel_step)
    each = keep.shape[0] // (4 * last)
    for z in range(4):
        for place in range(last):
            source = (z * last + place) * 2
            at = pl.ds((place * 4 + z) * each, each)
            keep[at, :] = total[pl.ds(pl.multiple_of((source + core) * each, 8), each), :]
            outgoing[at, :] = total[pl.ds(pl.multiple_of((source + 1 - core) * each, 8), each), :]
    send[...] = outgoing[...].astype(BF16)


def solve_level(table, places, unit, scalars, mine, other, loads, inverse, panel, last=0):
    rows, cols = inverse.shape[0], loads.shape[1]
    total = panel.shape[0]
    shape = (total // 2, cols) if last else (total, cols // 2)
    scratch = [pltpu.VMEM(loads.shape, BF16)]
    if last:
        scratch += [pltpu.VMEM((total, cols), F32), pltpu.VMEM(shape, F32)]

    def kernel(scalars, *refs):
        level_kernel(places, unit, last, scalars, *refs)

    operands = [mine, other, loads, inverse, panel]
    operands = [pltpu.with_memory_space_constraint(o, pltpu.VMEM) for o in operands]
    outs = [aval(rows, cols, BF16), aval(*shape, F32), aval(*shape, BF16)]
    return pl.pallas_call(
        kernel,
        out_shape=[pltpu.VMEM(o.shape, o.dtype) for o in outs],
        in_specs=[SMEM, SMEM] + [VMEM] * len(operands),
        out_specs=[VMEM] * len(outs),
        scratch_shapes=scratch,
        compiler_params=pltpu.CompilerParams(vmem_limit_bytes=16 * MIB),
        cost_estimate=pl.CostEstimate(
            flops=2 * cols * (inverse.size + panel.size),
            bytes_accessed=2 * (inverse.size + panel.size),
            transcendentals=0,
        ),
    )(scalars, table, *operands)


def in_order(bit, own, other):
    return jnp.where(
        bit == 0, jnp.concatenate([own, other], 0), jnp.concatenate([other, own], 0)
    )


def per_device(
    loads_first,
    loads_second,
    loads_third,
    loads_fourth,
    inverse_first,
    inverse_second,
    inverse_third,
    inverse_fourth,
    panel_first,
    panel_second,
    panel_third,
    panel_fourth,
    blocks_first,
    blocks_second,
    blocks_third,
):
    n_y, n_rows = lax.axis_size("y"), 2 * lax.axis_size("y")
    core, x_index, z1, z2 = (lax.axis_index(a) for a in ("core", "x", "z1", "z2"))
    row_index = lax.axis_index("y") * 2 + core
    leaf = ((lax.axis_index("hi") * 2 + z2) * 2 + z1) * 2 + x_index
    mask_z1, mask_z2 = 2 * n_rows, 4 * n_rows
    cores = core[None].astype(jnp.int32)
    update_rows = panel_first.shape[0]
    block = update_rows // blocks_first.shape[1]
    cols = loads_first.shape[1]
    half = cols // 2

    sibling = permute(loads_first, 1)
    acc = None
    arrived = [(0, loads_first, sibling)]
    for y in range(1, n_y):
        piece = permute(loads_first, 2 * y, upward=True)
        arrived.append((2 * y, piece, permute(piece, 1)))
    for mask, b0, b1 in arrived[:-1]:
        scalars = jnp.stack([core, row_index ^ mask, row_index ^ mask ^ 1]).astype(jnp.int32)
        operands = [inverse_first, b0, b1] + ([acc] if mask else [])
        acc = call(
            piece_kernel,
            [aval(inverse_first.shape[0], cols, F32)],
            scalars,
            operands,
            flops=4 * inverse_first.shape[0] * b0.size,
        )[0]

    loads_third, loads_fourth, acc = lax.optimization_barrier((loads_third, loads_fourth, acc))

    def gather_plane(value):
        return lax.all_gather(value, ("x", "y", "core"), axis=0, tiled=True)

    def by_z(value, count):
        rows = value.shape[0]
        split = value.reshape(2 * n_rows, count, rows // (2 * n_rows * count), cols)
        return split.transpose(1, 0, 2, 3).reshape(rows, cols)

    all_second = gather_plane(loads_second)
    pair_third = in_order(z1, loads_third, permute(loads_third, mask_z1))
    low = in_order(z1, loads_fourth, permute(loads_fourth, mask_z1))
    high = in_order(z1, permute(loads_fourth, mask_z2), permute(loads_fourth, mask_z2 | mask_z1))
    quad_fourth = in_order(z2, low, high)
    all_third = by_z(gather_plane(pair_third), 2)
    all_fourth = by_z(gather_plane(quad_fourth), 4)

    mask, b0, b1 = arrived[-1]
    scalars = jnp.stack([core, row_index ^ mask, row_index ^ mask ^ 1]).astype(jnp.int32)
    solved_first, keep, send = call(
        last_piece_kernel,
        [
            aval(inverse_first.shape[0], cols, BF16),
            aval(update_rows, half, F32),
            aval(update_rows, half, BF16),
        ],
        scalars,
        [inverse_first, b0, b1, acc, panel_first],
        flops=4 * inverse_first.shape[0] * b0.size + 2 * panel_first.size * cols,
    )
    part = reduce_over(pair_sum(keep, send, cores), "y", cores, BF16)

    def spread(value):
        mine = lax.all_gather(value, PLANE, axis=0, tiled=True)
        return mine, permute(mine, 1)

    def both_tables(table, level):
        child = leaf >> level
        return jnp.stack(
            [lax.dynamic_index_in_dim(table, c, 0, keepdims=False) for c in (child, child ^ 1)]
        )

    mine, other = spread(part)
    chunk = part.shape[0]
    unit = math.gcd(chunk, block)
    places = []
    for row in range(0, 2 * update_rows, unit):
        child, row = divmod(row, update_rows)
        places.append((child, row // block, row % block))
    first_two = blocks_first.reshape(-1, 2, blocks_first.shape[1])
    table = lax.dynamic_index_in_dim(first_two, leaf >> 1, 0, keepdims=False)
    solved_second, keep, send = solve_level(
        table, places, unit, cores, mine, other, all_second, inverse_second, panel_second
    )
    part = reduce_over(pair_sum(keep, send, cores), PLANE, cores, BF16)

    chunk = part.shape[0]
    unit = math.gcd(chunk, block)
    places = []
    for place in range(2 * n_y):
        for child in range(2):
            for row in range(place * chunk, (place + 1) * chunk, unit):
                places.append((child, row // block, row % block))

    mine, other = spread(jnp.concatenate([part, permute(part, mask_z1)], 0))
    solved_third, keep, send = solve_level(
        both_tables(blocks_second, 1),
        places,
        unit,
        cores,
        mine,
        other,
        all_third,
        inverse_third,
        panel_third,
    )
    part = reduce_over(pair_sum(keep, send, cores), PLANE, cores, BF16)
    part = (part.astype(F32) + permute(part, mask_z1).astype(F32)).astype(BF16)
    mine, other = spread(jnp.concatenate([part, permute(part, mask_z2)], 0))
    solved_fourth, keep, send = solve_level(
        both_tables(blocks_third, 2),
        places,
        unit,
        cores,
        mine,
        other,
        all_fourth,
        inverse_fourth,
        panel_fourth,
        last=2 * n_y,
    )
    part = reduce_over(pair_sum(keep, send, cores), PLANE, cores, F32)
    parts = part.reshape(4, -1, cols)
    z_index = z2 * 2 + z1
    ancestor = lax.dynamic_index_in_dim(parts, z_index, 0, keepdims=False)
    for m in range(1, 4):
        value = lax.dynamic_index_in_dim(parts, z_index ^ m, 0, keepdims=False)
        ancestor = ancestor + permute(value.astype(BF16), m * mask_z1).astype(F32)
    return solved_first, solved_second, solved_third, solved_fourth, ancestor


def solution(mesh):
    n_leaf, n_rows = mesh.shape["leaf"], mesh.shape["rows"]
    fine = Mesh(mesh.devices.reshape(n_leaf // 8, 2, 2, 2, n_rows // 2, 2), AXES)
    rows, cols = P(AXES, None), P(None, AXES)
    return jax.shard_map(
        per_device,
        mesh=fine,
        in_specs=(rows,) * 8 + (cols,) * 4 + (P(),) * 3,
        out_specs=(rows,) * 5,
        check_vma=False,
    )
```

time: 606 us -> 242 us (0.40)
  waiting for transfers between devices: 412 us -> 77.3 us
  matrix products: 47.7 us -> 0 us
  blocking collectives: 21.7 us -> 58.5 us
  other arithmetic: 31 us -> 3.78 us
  Pallas kernels: 0 us -> 23.4 us
  local copies, waits for them, and re-layouts: 52.2 us -> 38.7 us
    ppermute x15 -> x20, waiting for transfers between devices: 234 us -> 62.6 us  [permute(): return lax.ppermute(value, AXES, pairs)]
    reduce_scatter x4 -> x0, waiting for transfers between devices: 112 us -> none  [reduce_sliced(): lax.psum_scatter(partial_value, 'rows', scatter_dimension=0, tiled=True)]
    all_gather x8 -> x3, waiting for transfers between devices: 64.1 us -> 0.04 us  [gather_plane(): return lax.all_gather(value, ('x', 'y', 'core'), axis=0, tiled=True)]
    dot_general x14 -> x0, matrix products: 47.7 us -> none  [the longest x6 22.4 us: place_rows(): jnp.einsum('us,ubn->sbn', selector, blocks, precision=lax.Precision.HIGHEST)]
    dot_general x6 -> x0, local copies, waits for them, and re-layouts: 30.6 us -> none  [place_rows(): jnp.einsum('us,ubn->sbn', selector, blocks, precision=lax.Precision.HIGHEST)]
    unnamed x75 -> x45, local copies, waits for them, and re-layouts: 7.12 us -> 34 us
    pallas_call x0 -> x13, Pallas kernels: none -> 23.4 us  [the longest x3 12.7 us: solve_level(): pl.pallas_call(kernel, out_shape=[pltpu.VMEM(o.shape, o.dtype) for o in o...]
    all_to_all x0 -> x2, blocking collectives: none -> 20.4 us  [reduce_over(): arrived = lax.all_to_all(value, axes, 0, 0, tiled=True)]
  transfers between devices with their start and end apart: 27 -> 25, of which waited for: 19 -> 16; matrix products, arithmetic and copies ran while one was open for 9% -> 5% of each run, Pallas kernels for 0% -> 8%
where the time goes in v2:
time: 242 us; the launch traced here: 241 us
  waiting for transfers between devices  77.3 us (32%)
  blocking collectives  58.5 us (24%)
  local copies, waits for them, and re-layouts  38.7 us (16%)
  starting transfers between devices  25.3 us (10%)
  Pallas kernels  23.4 us (10%)
  between operations  14.1 us (6%)
  other arithmetic  3.78 us (2%)
    ppermute x20, waiting for transfers between devices, permute(): return lax.ppermute(value, AXES, pairs)  62.6 us
    all_gather x3, blocking collectives, spread(): mine = lax.all_gather(value, PLANE, axis=0, tiled=True)  38.1 us
    unnamed x45, local copies, waits for them, and re-layouts  34 us
    all_to_all x2, blocking collectives, reduce_over(): arrived = lax.all_to_all(value, axes, 0, 0, tiled=True)  20.4 us
    ppermute x20, starting transfers between devices, permute(): return lax.ppermute(value, AXES, pairs)  18.2 us
    all_to_all x2, waiting for transfers between devices, reduce_over(): arrived = lax.all_to_all(value, axes, 0, 0, tiled=True)  13.9 us
    pallas_call x3, Pallas kernels, solve_level(): pl.pallas_call(kernel, out_shape=[pltpu.VMEM(o.shape, o.dtype) for o in o...  12.7 us
    pallas_call x10, Pallas kernels, call(): pl.pallas_call(kernel, out_shape=[pltpu.VMEM(o.shape, o.dtype) for o in o...  10.8 us
  transfers between devices with their start and end apart: 25, of which 16 were waited for; matrix products, arithmetic and copies ran while one was open for 5% of the time, Pallas kernels for 8%

profile of v2, /device:TPU:0, one launch (start us, length us, event | category | flops | bytes accessed | tf_op | source)
XLA Modules:
  0.0 241.1 jit_solution(9383991738256391585)
XLA Ops:
  10.6 6.4 %copy-done.2 = bf16[1536,6144]{1,0:T(8,128)(2,1)S(1)} copy-done((bf16[1536,6144]{1,0:T(8,128)(2,1)S(1)}, bf16[1536,6144]{1,0:T(8,128)(2,1)}, u32[]{:S(2)}) %copy-start.2) | copy-done | bytes 18874392
  18.1 3.6 %shard_map.182.acc = f32[1536,256]{1,0:T(8,128)S(1)} custom-call(s32[3]{0:T(128)S(1)} %pad_add_fusion.3.scalars, bf16[1536,6144]{1,0:T(8,128)(2,1)S(1)} %copy-done.2, bf16[1536,256]{1,0:T(8,128)(2,1)S(1)} %copy-done.11, bf16[1536,256]{1,0:T(8,128)(2,1)S(1)} %collective-permute-done.2.b1), custom_call_target="tpu_custom_call" | custom-call | flops 2415919104 | bytes 20447232 | tf_op jit(solution)/shard_map/pallas_call | solution.py:37
  21.7 3.0 %collective-permute-start.8 = (bf16[384,256]{1,0:T(8,128)(2,1)S(1)}, bf16[384,256]{1,0:T(8,128)(2,1)S(1)}, u32[]{:S(2)}, u32[]{:S(2)}) collective-permute-start(bf16[384,256]{1,0:T(8,128)(2,1)S(1)} %copy-done.17), channel_id=1, source_target_pairs={{0,8},{1,9},{2,10},{3,11},{4,12},{5,13},{6,14},{7,15},{8,0},{9,1},... | collective-permute-start | bytes 589832 | tf_op jit(solution)/shard_map/ppermute | solution.py:24
  24.7 5.2 %collective-permute-done.8 = bf16[384,256]{1,0:T(8,128)(2,1)S(1)} collective-permute-done((bf16[384,256]{1,0:T(8,128)(2,1)S(1)}, bf16[384,256]{1,0:T(8,128)(2,1)S(1)}, u32[]{:S(2)}, u32[]{:S(2)}) %collective-permute-start.8) | collective-permute-done | bytes 196640 | tf_op jit(solution)/shard_map/ppermute | solution.py:24
  30.9 3.6 %collective-permute-start = (bf16[1536,256]{1,0:T(8,128)(2,1)S(1)}, bf16[1536,256]{1,0:T(8,128)(2,1)S(1)}, u32[]{:S(2)}, u32[]{:S(2)}) collective-permute-start(bf16[1536,256]{1,0:T(8,128)(2,1)S(1)} %copy-done.12), channel_id=1, source_target_pairs={{0,2},{1,3},{4,6},{5,7},{8,10},{9,11},{12,14},{13,15},{16,18},{17,... | collective-permute-start | bytes 2359304 | tf_op jit(solution)/shard_map/ppermute | solution.py:24
  34.5 23.5 %collective-permute-done.b0 = bf16[1536,256]{1,0:T(8,128)(2,1)S(1)} collective-permute-done((bf16[1536,256]{1,0:T(8,128)(2,1)S(1)}, bf16[1536,256]{1,0:T(8,128)(2,1)S(1)}, u32[]{:S(2)}, u32[]{:S(2)}) %collective-permute-start) | collective-permute-done | bytes 786464 | tf_op jit(solution)/shard_map/ppermute | solution.py:24
  61.1 6.5 %copy-done.3 = bf16[1536,6144]{1,0:T(8,128)(2,1)S(1)} copy-done((bf16[1536,6144]{1,0:T(8,128)(2,1)S(1)}, bf16[1536,6144]{1,0:T(8,128)(2,1)}, u32[]{:S(2)}) %copy-start.3) | copy-done | bytes 18874392
  67.6 2.3 copy-done.6
  71.1 5.3 %shard_map.183 = (bf16[1536,256]{1,0:T(8,128)(2,1)S(1)}, f32[1536,128]{1,0:T(8,128)S(1)}, bf16[1536,128]{1,0:T(8,128)(2,1)S(1)}) custom-call(s32[3]{0:T(128)S(1)} %pad_add_fusion.2.scalars, bf16[1536,6144]{1,0:T(8,128)(2,1)S(1)} %copy-done.3, bf16[1536,256]{1,0:T(8,128)(2,1)S(1)} %collective-permute-done.b0, bf16[1536,256]{1,0:T(8,128)(2,1)S(1)} %copy-done.14, ...), custom_call_target="tpu_custom_call" | custom-call | flops 3623878656 | bytes 26738688 | tf_op jit(solution)/shard_map/pallas_call | solution.py:37
  79.2 2.4 collective-permute-start.15
  83.7 3.8 %collective-permute-done.15 = bf16[192,256]{1,0:T(8,128)(2,1)S(1)} collective-permute-done((bf16[192,256]{1,0:T(8,128)(2,1)}, bf16[192,256]{1,0:T(8,128)(2,1)S(1)}, u32[]{:S(2)}, u32[]{:S(2)}) %collective-permute-start.15) | collective-permute-done | bytes 98336 | tf_op jit(solution)/shard_map/ppermute | solution.py:24
  87.6 3.6 %collective-permute-done.14 = bf16[192,256]{1,0:T(8,128)(2,1)S(1)} collective-permute-done((bf16[192,256]{1,0:T(8,128)(2,1)}, bf16[192,256]{1,0:T(8,128)(2,1)S(1)}, u32[]{:S(2)}, u32[]{:S(2)}) %collective-permute-start.14) | collective-permute-done | bytes 98336 | tf_op jit(solution)/shard_map/ppermute | solution.py:24
  93.2 3.6 %all-to-all-start = ((bf16[2,768,128]{2,1,0:T(8,128)(2,1)}), bf16[2,768,128]{2,1,0:T(8,128)(2,1)S(1)}, u32[]{:S(2)}, u32[]{:S(2)}) async-start(bf16[2,768,128]{2,1,0:T(8,128)(2,1)} %bitcast.7), calls=%async_computation | async-start | bytes 786432 | tf_op jit(solution)/shard_map/all_to_all | solution.py:119
  97.7 6.5 %all-to-all-done = bf16[2,768,128]{2,1,0:T(8,128)(2,1)S(1)} async-done(((bf16[2,768,128]{2,1,0:T(8,128)(2,1)}), bf16[2,768,128]{2,1,0:T(8,128)(2,1)S(1)}, u32[]{:S(2)}, u32[]{:S(2)}) %all-to-all-start) | async-done | bytes 393248 | tf_op jit(solution)/shard_map/all_to_all | solution.py:119
  104.3 15.0 %all_gather.18.refs_1_ = bf16[3072,128]{1,0:T(8,128)(2,1)S(1)} all-gather(bf16[768,128]{1,0:T(8,128)(2,1)S(1)} %shard_map.185), channel_id=1, replica_groups=mesh['hi'=1,'z2'=2,'z1'=2,'x'=2,'y'=2,'core'=2] {'x','y'}, dimensions={0}, use_global_device_ids=true | all-gather | bytes 983040 | tf_op jit(solution)/shard_map/all_gather | solution.py:285
  119.3 2.2 collective-permute-done.4.refs_2_
  121.5 4.2 %copy-done.4 = bf16[768,6144]{1,0:T(8,128)(2,1)S(1)} copy-done((bf16[768,6144]{1,0:T(8,128)(2,1)S(1)}, bf16[768,6144]{1,0:T(8,128)(2,1)}, u32[]{:S(2)}) %copy-start.4) | copy-done | bytes 9437208
  129.3 5.4 %shard_map.186 = (bf16[768,256]{1,0:T(8,128)(2,1)S(1)}, f32[1536,128]{1,0:T(8,128)S(1)}, bf16[1536,128]{1,0:T(8,128)(2,1)S(1)}) custom-call(s32[1]{0:T(128)} %bitcast.scalars, s32[2,12]{1,0:T(2,128)S(1)} %fusion.5.refs_0_, bf16[3072,128]{1,0:T(8,128)(2,1)S(1)} %all_gather.18.refs_1_, bf16[3072,128]{1,0:T(8,128)(2,1)S(1)} %collective-permute-done.4.refs_2_, ...), custom_call_target="tpu_custom_call" | custom-call | flops 3019898880 | bytes 11796480 | tf_op jit(solution)/shard_map/pallas_call | solution.py:185
  136.6 10.1 %all_to_all.44 = bf16[4,384,128]{2,1,0:T(8,128)(2,1)S(1)} all-to-all(bf16[4,384,128]{2,1,0:T(8,128)(2,1)S(1)} %bitcast.44), channel_id=1, replica_groups=mesh['hi'=1,'z2'=2,'z1'=2,'x'=2,'y'=2,'core'=2] {'x','y'}, dimensions={0} | all-to-all | bytes 786432 | tf_op jit(solution)/shard_map/all_to_all | solution.py:119
  146.8 4.6 %collective-permute-done.6 = bf16[384,128]{1,0:T(8,128)(2,1)S(1)} collective-permute-done((bf16[384,128]{1,0:T(8,128)(2,1)S(1)}, bf16[384,128]{1,0:T(8,128)(2,1)S(1)}, u32[]{:S(2)}, u32[]{:S(2)}) %collective-permute-start.6) | collective-permute-done | bytes 98336 | tf_op jit(solution)/shard_map/ppermute | solution.py:24
  151.4 11.5 %all_gather.20.refs_1_ = bf16[3072,128]{1,0:T(8,128)(2,1)S(1)} all-gather(bf16[768,128]{1,0:T(8,128)(2,1)S(1)} %pad_maximum_fusion), channel_id=1, replica_groups=mesh['hi'=1,'z2'=2,'z1'=2,'x'=2,'y'=2,'core'=2] {'x','y'}, dimensions={0}, use_global_device_ids=true | all-gather | bytes 983040 | tf_op jit(solution)/shard_map/all_gather | solution.py:285
  163.0 2.3 copy.20
  166.6 3.7 %shard_map.189 = (bf16[384,256]{1,0:T(8,128)(2,1)S(1)}, f32[1536,128]{1,0:T(8,128)S(1)}, bf16[1536,128]{1,0:T(8,128)(2,1)S(1)}) custom-call(s32[1]{0:T(128)} %bitcast.scalars, s32[2,12]{1,0:T(2,128)S(1)} %pad_add_fusion.refs_0_, bf16[3072,128]{1,0:T(8,128)(2,1)S(1)} %all_gather.20.refs_1_, bf16[3072,128]{1,0:T(8,128)(2,1)S(1)} %collective-permute-done.7.refs_2_, ...), custom_call_target="tpu_custom_call" | custom-call | flops 1509949440 | bytes 5898240 | tf_op jit(solution)/shard_map/pallas_call | solution.py:185
  172.3 10.3 %all_to_all.45 = bf16[4,384,128]{2,1,0:T(8,128)(2,1)S(1)} all-to-all(bf16[4,384,128]{2,1,0:T(8,128)(2,1)S(1)} %bitcast.45), channel_id=1, replica_groups=mesh['hi'=1,'z2'=2,'z1'=2,'x'=2,'y'=2,'core'=2] {'x','y'}, dimensions={0} | all-to-all | bytes 786432 | tf_op jit(solution)/shard_map/all_to_all | solution.py:119
  182.9 4.5 %collective-permute-done.10 = bf16[384,128]{1,0:T(8,128)(2,1)S(1)} collective-permute-done((bf16[384,128]{1,0:T(8,128)(2,1)S(1)}, bf16[384,128]{1,0:T(8,128)(2,1)S(1)}, u32[]{:S(2)}, u32[]{:S(2)}) %collective-permute-start.10) | collective-permute-done | bytes 98336 | tf_op jit(solution)/shard_map/ppermute | solution.py:24
  188.1 5.5 %collective-permute-done.11 = bf16[384,128]{1,0:T(8,128)(2,1)S(1)} collective-permute-done((bf16[384,128]{1,0:T(8,128)(2,1)S(1)}, bf16[384,128]{1,0:T(8,128)(2,1)S(1)}, u32[]{:S(2)}, u32[]{:S(2)}) %collective-permute-start.11) | collective-permute-done | bytes 98336 | tf_op jit(solution)/shard_map/ppermute | solution.py:24
  193.6 11.6 %all_gather.22.refs_1_ = bf16[3072,128]{1,0:T(8,128)(2,1)S(1)} all-gather(bf16[768,128]{1,0:T(8,128)(2,1)S(1)} %pad_maximum_fusion.1), channel_id=1, replica_groups=mesh['hi'=1,'z2'=2,'z1'=2,'x'=2,'y'=2,'core'=2] {'x','y'}, dimensions={0}, use_global_device_ids=true | all-gather | bytes 983040 | tf_op jit(solution)/shard_map/all_gather | solution.py:285
  206.6 2.4 copy.21
  209.2 3.6 %shard_map.192 = (bf16[192,256]{1,0:T(8,128)(2,1)S(1)}, f32[768,256]{1,0:T(8,128)S(1)}, bf16[768,256]{1,0:T(8,128)(2,1)S(1)}) custom-call(s32[1]{0:T(128)} %bitcast.scalars, s32[2,12]{1,0:T(2,128)S(1)} %pad_add_fusion.1.refs_0_, bf16[3072,128]{1,0:T(8,128)(2,1)S(1)} %all_gather.22.refs_1_, bf16[3072,128]{1,0:T(8,128)(2,1)} %collective-permute-done.12.refs_2_, ...), custom_call_target="tpu_custom_call" | custom-call | flops 754974720 | bytes 2949120 | tf_op jit(solution)/shard_map/pallas_call | solution.py:185
  215.6 3.5 %all-to-all-start.3 = ((bf16[4,192,256]{2,1,0:T(8,128)(2,1)}), bf16[4,192,256]{2,1,0:T(8,128)(2,1)S(1)}, u32[]{:S(2)}, u32[]{:S(2)}) async-start(bf16[4,192,256]{2,1,0:T(8,128)(2,1)} %bitcast.19), calls=%async_computation.3 | async-start | bytes 786432 | tf_op jit(solution)/shard_map/all_to_all | solution.py:119
  219.1 7.4 %all-to-all-done.3 = bf16[4,192,256]{2,1,0:T(8,128)(2,1)S(1)} async-done(((bf16[4,192,256]{2,1,0:T(8,128)(2,1)}), bf16[4,192,256]{2,1,0:T(8,128)(2,1)S(1)}, u32[]{:S(2)}, u32[]{:S(2)}) %all-to-all-start.3) | async-done | bytes 393248 | tf_op jit(solution)/shard_map/all_to_all | solution.py:119
  228.4 2.6 %collective-permute-start.17 = (bf16[48,256]{1,0:T(8,128)(2,1)S(1)}, bf16[48,256]{1,0:T(8,128)(2,1)S(1)}, u32[]{:S(2)}, u32[]{:S(2)}) collective-permute-start(bf16[48,256]{1,0:T(8,128)(2,1)S(1)} %get-tuple-element.35), channel_id=1, source_target_pairs={{0,8},{1,9},{2,10},{3,11},{4,12},{5,13},{6,14},{7,15},{8,0},{9,1},... | collective-permute-start | bytes 73736 | tf_op jit(solution)/shard_map/ppermute | solution.py:24
  (102 shorter events, 37.4 us)
Async XLA Ops:
  7.2 112.1 %copy-start = (s32[8,12]{1,0:T(8,128)S(1)}, s32[8,12]{1,0:T(8,128)}, u32[]{:S(2)}) copy-start(s32[8,12]{1,0:T(8,128)} %param.27) | copy-start | bytes 1156
  7.2 114.4 %all-gather.4.cloned.1.call-start = ((), (), s32[]{:S(2)}) async-start(), calls=%async_computation.4 | async-start | bytes 3538944 | tf_op jit(solution)/shard_map/all_gather | solution.py:254
  7.9 155.1 %all-gather.6.cloned.1.call-start = ((), (), s32[]{:S(2)}) async-start(), calls=%async_computation.5 | async-start | bytes 3538944 | tf_op jit(solution)/shard_map/all_gather | solution.py:254
  8.0 2.6 %collective-permute-start.2 = (bf16[1536,256]{1,0:T(8,128)(2,1)}, bf16[1536,256]{1,0:T(8,128)(2,1)S(1)}, u32[]{:S(2)}, u32[]{:S(2)}) collective-permute-start(bf16[1536,256]{1,0:T(8,128)(2,1)} %b0.1), channel_id=1, source_target_pairs={{0,1},{1,0},{2,3},{3,2},{4,5},{5,4},{6,7},{7,6},{8,9},{9,8},{10,11... | collective-permute-start | bytes 2359304 | tf_op jit(solution)/shard_map/ppermute | solution.py:24
  10.6 6.4 %copy-start.2 = (bf16[1536,6144]{1,0:T(8,128)(2,1)S(1)}, bf16[1536,6144]{1,0:T(8,128)(2,1)}, u32[]{:S(2)}) copy-start(bf16[1536,6144]{1,0:T(8,128)(2,1)} %inverse.3) | copy-start | bytes 56623108
  18.1 12.7 %copy-start.12 = (bf16[1536,256]{1,0:T(8,128)(2,1)S(1)}, bf16[1536,256]{1,0:T(8,128)(2,1)}, u32[]{:S(2)}) copy-start(bf16[1536,256]{1,0:T(8,128)(2,1)} %b0.1) | copy-start | bytes 2359300
  21.7 8.2 %collective-permute-start.8 = (bf16[384,256]{1,0:T(8,128)(2,1)S(1)}, bf16[384,256]{1,0:T(8,128)(2,1)S(1)}, u32[]{:S(2)}, u32[]{:S(2)}) collective-permute-start(bf16[384,256]{1,0:T(8,128)(2,1)S(1)} %copy-done.17), channel_id=1, source_target_pairs={{0,8},{1,9},{2,10},{3,11},{4,12},{5,13},{6,14},{7,15},{8,0},{9,1},... | collective-permute-start | bytes 589832 | tf_op jit(solution)/shard_map/ppermute | solution.py:24
  30.9 27.1 %collective-permute-start = (bf16[1536,256]{1,0:T(8,128)(2,1)S(1)}, bf16[1536,256]{1,0:T(8,128)(2,1)S(1)}, u32[]{:S(2)}, u32[]{:S(2)}) collective-permute-start(bf16[1536,256]{1,0:T(8,128)(2,1)S(1)} %copy-done.12), channel_id=1, source_target_pairs={{0,2},{1,3},{4,6},{5,7},{8,10},{9,11},{12,14},{13,15},{16,18},{17,... | collective-permute-start | bytes 2359304 | tf_op jit(solution)/shard_map/ppermute | solution.py:24
  58.0 2.3 collective-permute-start.1
  61.1 6.5 %copy-start.3 = (bf16[1536,6144]{1,0:T(8,128)(2,1)S(1)}, bf16[1536,6144]{1,0:T(8,128)(2,1)}, u32[]{:S(2)}) copy-start(bf16[1536,6144]{1,0:T(8,128)(2,1)} %inverse.3) | copy-start | bytes 56623108
  77.3 14.0 %collective-permute-start.3 = (bf16[1536,128]{1,0:T(8,128)(2,1)S(1)}, bf16[1536,128]{1,0:T(8,128)(2,1)S(1)}, u32[]{:S(2)}, u32[]{:S(2)}) collective-permute-start(bf16[1536,128]{1,0:T(8,128)(2,1)S(1)} %get-tuple-element.23), channel_id=1, source_target_pairs={{0,1},{1,0},{2,3},{3,2},{4,5},{5,4},{6,7},{7,6},{8,9},{9,8},{10,11... | collective-permute-start | bytes 1179656 | tf_op jit(solution)/shard_map/ppermute | solution.py:24
  77.5 5.2 %collective-permute-start.13 = (bf16[192,256]{1,0:T(8,128)(2,1)}, bf16[192,256]{1,0:T(8,128)(2,1)S(1)}, u32[]{:S(2)}, u32[]{:S(2)}) collective-permute-start(bf16[192,256]{1,0:T(8,128)(2,1)} %param.18), channel_id=1, source_target_pairs={{0,8},{1,9},{2,10},{3,11},{4,12},{5,13},{6,14},{7,15},{8,0},{9,1},... | collective-permute-start | bytes 294920 | tf_op jit(solution)/shard_map/ppermute | solution.py:24
  79.2 8.4 %collective-permute-start.15 = (bf16[192,256]{1,0:T(8,128)(2,1)}, bf16[192,256]{1,0:T(8,128)(2,1)S(1)}, u32[]{:S(2)}, u32[]{:S(2)}) collective-permute-start(bf16[192,256]{1,0:T(8,128)(2,1)} %param.18), channel_id=1, source_target_pairs={{0,24},{1,25},{2,26},{3,27},{4,28},{5,29},{6,30},{7,31},{8,16},{9,... | collective-permute-start | bytes 294920 | tf_op jit(solution)/shard_map/ppermute | solution.py:24
  81.6 9.6 %collective-permute-start.14 = (bf16[192,256]{1,0:T(8,128)(2,1)}, bf16[192,256]{1,0:T(8,128)(2,1)S(1)}, u32[]{:S(2)}, u32[]{:S(2)}) collective-permute-start(bf16[192,256]{1,0:T(8,128)(2,1)} %param.18), channel_id=1, source_target_pairs={{0,16},{1,17},{2,18},{3,19},{4,20},{5,21},{6,22},{7,23},{8,24},{9,... | collective-permute-start | bytes 294920 | tf_op jit(solution)/shard_map/ppermute | solution.py:24
  93.2 11.0 %all-to-all-start = ((bf16[2,768,128]{2,1,0:T(8,128)(2,1)}), bf16[2,768,128]{2,1,0:T(8,128)(2,1)S(1)}, u32[]{:S(2)}, u32[]{:S(2)}) async-start(bf16[2,768,128]{2,1,0:T(8,128)(2,1)} %bitcast.7), calls=%async_computation | async-start | bytes 786432 | tf_op jit(solution)/shard_map/all_to_all | solution.py:119
  96.8 109.8 %all-gather.8.cloned.1.call-start = ((), (), s32[]{:S(2)}) async-start(), calls=%async_computation.6 | async-start | bytes 3538944 | tf_op jit(solution)/shard_map/all_gather | solution.py:254
  119.3 2.3 collective-permute-start.4
  134.7 28.2 %copy-start.19 = (s32[4,12]{1,0:T(4,128)S(1)}, s32[4,12]{1,0:T(4,128)}, u32[]{:S(2)}) copy-start(s32[4,12]{1,0:T(4,128)} %param.28) | copy-start | bytes 580
  134.7 1.8 collective-permute-start.5
  146.7 4.7 %collective-permute-start.6 = (bf16[384,128]{1,0:T(8,128)(2,1)S(1)}, bf16[384,128]{1,0:T(8,128)(2,1)S(1)}, u32[]{:S(2)}, u32[]{:S(2)}) collective-permute-start(bf16[384,128]{1,0:T(8,128)(2,1)S(1)} %shard_map.188), channel_id=1, source_target_pairs={{0,8},{1,9},{2,10},{3,11},{4,12},{5,13},{6,14},{7,15},{8,0},{9,1},... | collective-permute-start | bytes 294920 | tf_op jit(solution)/shard_map/ppermute | solution.py:24
  162.9 2.4 %collective-permute-start.7 = (bf16[3072,128]{1,0:T(8,128)(2,1)S(1)}, bf16[3072,128]{1,0:T(8,128)(2,1)S(1)}, u32[]{:S(2)}, u32[]{:S(2)}) collective-permute-start(bf16[3072,128]{1,0:T(8,128)(2,1)S(1)} %all_gather.20.refs_1_), channel_id=1, source_target_pairs={{0,1},{1,0},{2,3},{3,2},{4,5},{5,4},{6,7},{7,6},{8,9},{9,8},{10,11... | collective-permute-start | bytes 2359304 | tf_op jit(solution)/shard_map/ppermute | solution.py:24
  170.3 36.2 %copy-start.18 = (s32[2,12]{1,0:T(2,128)S(1)}, s32[2,12]{1,0:T(2,128)}, u32[]{:S(2)}) copy-start(s32[2,12]{1,0:T(2,128)} %param.29) | copy-start | bytes 292
  170.3 1.9 collective-permute-start.9
  182.7 4.7 %collective-permute-start.10 = (bf16[384,128]{1,0:T(8,128)(2,1)S(1)}, bf16[384,128]{1,0:T(8,128)(2,1)S(1)}, u32[]{:S(2)}, u32[]{:S(2)}) collective-permute-start(bf16[384,128]{1,0:T(8,128)(2,1)S(1)} %shard_map.191), channel_id=1, source_target_pairs={{0,8},{1,9},{2,10},{3,11},{4,12},{5,13},{6,14},{7,15},{8,0},{9,1},... | collective-permute-start | bytes 294920 | tf_op jit(solution)/shard_map/ppermute | solution.py:24
  187.4 6.2 %collective-permute-start.11 = (bf16[384,128]{1,0:T(8,128)(2,1)S(1)}, bf16[384,128]{1,0:T(8,128)(2,1)S(1)}, u32[]{:S(2)}, u32[]{:S(2)}) collective-permute-start(bf16[384,128]{1,0:T(8,128)(2,1)S(1)} %add_convert_fusion), channel_id=1, source_target_pairs={{0,16},{1,17},{2,18},{3,19},{4,20},{5,21},{6,22},{7,23},{8,24},{9,... | collective-permute-start | bytes 294920 | tf_op jit(solution)/shard_map/ppermute | solution.py:24
  205.2 3.8 %collective-permute-start.12 = (bf16[3072,128]{1,0:T(8,128)(2,1)S(1)}, bf16[3072,128]{1,0:T(8,128)(2,1)}, u32[]{:S(2)}, u32[]{:S(2)}) collective-permute-start(bf16[3072,128]{1,0:T(8,128)(2,1)S(1)} %all_gather.22.refs_1_), channel_id=1, source_target_pairs={{0,1},{1,0},{2,3},{3,2},{4,5},{5,4},{6,7},{7,6},{8,9},{9,8},{10,11... | collective-permute-start | bytes 2359304 | tf_op jit(solution)/shard_map/ppermute | solution.py:24
  209.2 25.3 %copy-start.1 = (s32[8,12]{1,0:T(8,128)S(1)}, s32[8,12]{1,0:T(8,128)}, u32[]{:S(2)}) copy-start(s32[8,12]{1,0:T(8,128)} %param.27) | copy-start | bytes 1156
  212.9 1.9 collective-permute-start.16
  215.6 10.9 %all-to-all-start.3 = ((bf16[4,192,256]{2,1,0:T(8,128)(2,1)}), bf16[4,192,256]{2,1,0:T(8,128)(2,1)S(1)}, u32[]{:S(2)}, u32[]{:S(2)}) async-start(bf16[4,192,256]{2,1,0:T(8,128)(2,1)} %bitcast.19), calls=%async_computation.3 | async-start | bytes 786432 | tf_op jit(solution)/shard_map/all_to_all | solution.py:119
  226.5 7.4 %collective-permute-start.19 = (bf16[48,256]{1,0:T(8,128)(2,1)S(1)}, bf16[48,256]{1,0:T(8,128)(2,1)S(1)}, u32[]{:S(2)}, u32[]{:S(2)}) collective-permute-start(bf16[48,256]{1,0:T(8,128)(2,1)S(1)} %get-tuple-element.36), channel_id=1, source_target_pairs={{0,24},{1,25},{2,26},{3,27},{4,28},{5,29},{6,30},{7,31},{8,16},{9,... | collective-permute-start | bytes 73736 | tf_op jit(solution)/shard_map/ppermute | solution.py:24
  228.4 5.5 %collective-permute-start.18 = (bf16[48,256]{1,0:T(8,128)(2,1)S(1)}, bf16[48,256]{1,0:T(8,128)(2,1)S(1)}, u32[]{:S(2)}, u32[]{:S(2)}) collective-permute-start(bf16[48,256]{1,0:T(8,128)(2,1)S(1)} %get-tuple-element.37), channel_id=1, source_target_pairs={{0,16},{1,17},{2,18},{3,19},{4,20},{5,21},{6,22},{7,23},{8,24},{9,... | collective-permute-start | bytes 73736 | tf_op jit(solution)/shard_map/ppermute | solution.py:24
  228.4 5.5 %collective-permute-start.17 = (bf16[48,256]{1,0:T(8,128)(2,1)S(1)}, bf16[48,256]{1,0:T(8,128)(2,1)S(1)}, u32[]{:S(2)}, u32[]{:S(2)}) collective-permute-start(bf16[48,256]{1,0:T(8,128)(2,1)S(1)} %get-tuple-element.35), channel_id=1, source_target_pairs={{0,8},{1,9},{2,10},{3,11},{4,12},{5,13},{6,14},{7,15},{8,0},{9,1},... | collective-permute-start | bytes 73736 | tf_op jit(solution)/shard_map/ppermute | solution.py:24
  (13 other events, 28.4 us)
Sparse Core Ops, SparseCore 0:
  9.9 38.2 all-gather.3
  50.1 36.1 all-gather.5
  100.1 35.0 all-gather.7

commit v3 on v0

v3 whole, which is shorter than its diff:
```python
import functools
import math

import jax
import jax.numpy as jnp
from jax import lax
from jax.experimental import pallas as pl
from jax.experimental.pallas import tpu as pltpu
from jax.sharding import Mesh
from jax.sharding import PartitionSpec as P

BF16 = jnp.bfloat16
F32 = jnp.float32
AXES = ("hi", "z2", "z1", "x", "y", "core")
PLANE = ("x", "y")
VMEM = pl.BlockSpec(memory_space=pltpu.VMEM)
SMEM = pl.BlockSpec(memory_space=pltpu.SMEM)
ANY = pl.BlockSpec(memory_space=pl.ANY)
MIB = 1 << 20


def permute(value, mask, upward=False):
    total = lax.axis_size(AXES)
    pairs = [(i, i ^ mask) for i in range(total) if not upward or (i ^ mask) > i]
    return lax.ppermute(value, AXES, pairs)


def row_tile(rows):
    return next(t for t in (512, 384, 256, 192, 128, 96, 64, 48, 32, 16) if rows % t == 0)


def aval(rows, cols, dtype):
    return jax.ShapeDtypeStruct((rows, cols), dtype)


def kernel_call(kernel, outs, scalars, vmem, hbm=(), scratch=(), limit=8, pin=True):
    operands = [pltpu.with_memory_space_constraint(o, pltpu.VMEM) if pin else o for o in vmem]
    return pl.pallas_call(
        kernel,
        out_shape=[pltpu.VMEM(o.shape, o.dtype) if inside else o for o, inside in outs],
        in_specs=[SMEM] + [VMEM] * len(vmem) + [ANY] * len(hbm),
        out_specs=[VMEM if inside else ANY for _, inside in outs],
        scratch_shapes=list(scratch),
        compiler_params=pltpu.CompilerParams(vmem_limit_bytes=limit * MIB),
        cost_estimate=pl.CostEstimate(flops=0, bytes_accessed=0, transcendentals=0),
    )(scalars, *operands, *[pltpu.with_memory_space_constraint(o, pltpu.HBM) for o in hbm])


def tiles(rows, step):
    tile = row_tile(rows)

    def body(i, carry):
        step(pl.ds(pl.multiple_of(i * tile, tile), tile))
        return carry

    lax.fori_loop(0, rows // tile, body, 0)


def dot(a, b):
    return jnp.dot(a, b, preferred_element_type=F32)


def start_all(sources, targets, sems):
    copies = [
        pltpu.make_async_copy(source, target, sems.at[i])
        for i, (source, target) in enumerate(zip(sources, targets))
    ]
    for copy in copies:
        copy.start()
    return copies


def near_kernel(scalars, b0, b1, inverse, panel, acc, far, panel_out, near, sems):
    rows, depth = inverse.shape[0], b0.shape[0]
    tile = row_tile(rows)
    n_far = far.shape[1] // depth
    columns = [
        pl.ds(pl.multiple_of(scalars[1 + i] * depth, depth), depth) for i in range(2 + n_far)
    ]
    sources, targets = [], []
    for i in range(rows // tile):
        at = pl.ds(i * tile, tile)
        for j in range(2):
            sources.append(inverse.at[at, columns[j]])
            targets.append(near.at[at, pl.ds(j * depth, depth)])
    for j in range(n_far):
        sources.append(inverse.at[:, columns[2 + j]])
        targets.append(far.at[:, pl.ds(j * depth, depth)])
    sources.append(panel)
    targets.append(panel_out)
    copies = start_all(sources, targets, sems)
    for i in range(rows // tile):
        at = pl.ds(i * tile, tile)
        copies[2 * i].wait()
        copies[2 * i + 1].wait()
        acc[at, :] = dot(near[at, :depth], b0[...]) + dot(near[at, depth:], b1[...])
    for copy in copies[2 * (rows // tile) :]:
        copy.wait()


def far_kernel(n_far, scalars, acc, panel, far, *refs):
    pieces, (solved, keep, send, x_ref, sem) = refs[:n_far], refs[n_far:]
    depth = pieces[0].shape[0]
    core, half = scalars[0], keep.shape[1]

    def step(at):
        total = acc[at, :]
        for j, piece in enumerate(pieces):
            total += dot(far[at, j * depth : (j + 1) * depth], piece[...])
        x_ref[at, :] = total.astype(BF16)

    tiles(far.shape[0], step)
    result = pltpu.make_async_copy(x_ref, solved, sem)
    result.start()

    def panel_step(at):
        part = dot(panel[at, :], x_ref[...])
        low, high = part[:, :half], part[:, half:]
        keep[at, :] = jnp.where(core == 0, low, high)
        send[at, :] = jnp.where(core == 0, high, low).astype(BF16)

    tiles(panel.shape[0], panel_step)
    result.wait()


def split_kernel(scalars, *refs):
    *arrays, keep, send = refs
    core, half, first = scalars[0], keep.shape[1], 0
    for array in arrays:
        at = pl.ds(first, array.shape[0])
        first += array.shape[0]
        low, high = array[:, :half], array[:, half:]
        keep[at, :] = jnp.where(core == 0, low, high)
        send[at, :] = jnp.where(core == 0, high, low)


def pack_kernel(scalars, keep, received, *outs):
    first = 0
    for out in outs:
        rows = out.shape[0] // 2
        out[:rows, :] = keep[pl.ds(first, rows), :]
        out[rows:, :] = received[pl.ds(first, rows), :]
        first += rows


def join_columns(core, own, other):
    return jnp.where(
        core == 0, jnp.concatenate([own, other], 1), jnp.concatenate([other, own], 1)
    )


def pair_sum_kernel(scalars, keep, received, out):
    out[...] = (keep[...] + received[...].astype(F32)).astype(out.dtype)


def chunk_sum_kernel(count, scalars, chunks, out):
    rows = out.shape[0]
    total = chunks[:rows, :].astype(F32)
    for i in range(1, count):
        total += chunks[i * rows : (i + 1) * rows, :].astype(F32)
    out[...] = total.astype(out.dtype)


def reduce_over(value, axes, scalars, dtype):
    count = lax.axis_size(axes)
    arrived = lax.all_to_all(value, axes, 0, 0, tiled=True)
    rows, cols = value.shape
    return kernel_call(
        functools.partial(chunk_sum_kernel, count),
        [(aval(rows // count, cols, dtype), True)],
        scalars,
        [arrived],
    )[0]


def z_split_kernel(at_z, scalars, value, own, *sends):
    rows = own.shape[0]
    for mask in range(4):
        at = pl.ds(pl.multiple_of((scalars[at_z] ^ mask) * rows, rows), rows)
        if mask == 0:
            own[...] = value[at, :]
        else:
            sends[mask - 1][...] = value[at, :].astype(BF16)


def z_sum_kernel(scalars, own, a, b, c, keep, send, total):
    total[...] = own[...] + a[...].astype(F32) + b[...].astype(F32) + c[...].astype(F32)
    rows = keep.shape[0]
    keep[...] = total[pl.ds(pl.multiple_of(scalars[0] * rows, 8), rows), :]
    send[...] = total[pl.ds(pl.multiple_of((1 - scalars[0]) * rows, 8), rows), :]


def level_kernel(plan, scalars, mine, *refs):
    unit, places, block, at_table, at_order, size, n_pieces, plane = plan
    sources, refs = refs[:4], refs[4:]
    pieces, refs = refs[:n_pieces], refs[n_pieces:]
    update, x_keep, x_send, ready, *held = refs[:8]
    sems, part_sems, *spare = refs[8:]
    rows = x_keep.shape[0]
    tile = min(192, row_tile(rows))
    count = rows // tile

    def fetch(which, i):
        at = pl.ds(pl.multiple_of(i * tile, tile), tile)
        return pltpu.make_async_copy(
            sources[which].at[at, :], held[which].at[at, :], part_sems.at[which * count + i]
        )

    def fetch_panel(which):
        return pltpu.make_async_copy(
            sources[2 + which], held[2 + which], part_sems.at[2 * count + which]
        )

    runs, targets = [], []
    for piece in pieces:
        for row in range(0, piece.shape[0], size):
            at = pl.multiple_of(scalars[at_order + len(runs)] * size, size)
            runs.append(piece.at[pl.ds(row, size), :])
            targets.append(ready.at[pl.ds(at, size), :])
    copies = start_all(runs, targets, sems)
    for which in range(2):
        fetch(which, 0).start()
    for copy in copies:
        copy.wait()
    for i, (index, row) in enumerate(places):
        at = pl.ds(pl.multiple_of(scalars[at_table + index] * block + row, unit), unit)
        value = mine[i * unit : (i + 1) * unit, :].astype(F32)
        ready[at, :] = (ready[at, :].astype(F32) - value).astype(BF16)

    def step(i, carry):
        at = pl.ds(pl.multiple_of(i * tile, tile), tile)
        for which, out in ((0, x_keep), (1, x_send)):
            fetch(which, i).wait()

            @pl.when(i + 1 < count)
            def _():
                fetch(which, i + 1).start()

            @pl.when(i + 1 == count)
            def _():
                fetch_panel(which).start()

            out[at, :] = dot(held[which][at, :], ready[...]).astype(BF16)
        return carry

    lax.fori_loop(0, count, step, 0)
    panel_a, panel_b = held[2:]
    for which in range(2):
        fetch_panel(which).wait()
    if not plane:

        def panel_step(at):
            part = dot(panel_a[at, :], x_keep[...]) + dot(panel_b[at, :], x_send[...])
            update[at, :] = part.astype(BF16)

        tiles(update.shape[0], panel_step)
        return
    total = spare[0]

    def last_step(at):
        dims = (((0,), (0,)), ((), ()))
        part = lax.dot_general(panel_a[:, at], x_keep[...], dims, preferred_element_type=F32)
        part += lax.dot_general(panel_b[:, at], x_send[...], dims, preferred_element_type=F32)
        total[at, :] = part.astype(BF16)

    tiles(update.shape[0], last_step)
    each = update.shape[0] // (4 * plane)
    for z in range(4):
        for place in range(plane):
            source = (z * plane + place) * each
            target = (place * 4 + z) * each
            update[target : target + each, :] = total[source : source + each, :]


def solve_level(scalars, plan, mine, inverses, panels, pieces, update_rows):
    rows, depth = inverses[0].shape
    half, size, plane = mine.shape[1], plan[5], plan[7]
    count = rows // min(192, row_tile(rows))
    scratch = [pltpu.VMEM((depth, half), BF16)]
    scratch += [pltpu.VMEM(v.shape, BF16) for v in (*inverses, *panels)]
    scratch += [pltpu.SemaphoreType.DMA((depth // size,)), pltpu.SemaphoreType.DMA((2 * count + 2,))]
    if plane:
        scratch.append(pltpu.VMEM((update_rows, half), BF16))
    outs = [(aval(r, half, BF16), True) for r in (update_rows, rows, rows)]
    return kernel_call(
        functools.partial(level_kernel, plan),
        outs,
        scalars,
        [mine],
        [*inverses, *panels, *pieces],
        scratch,
        limit=34,
    )


def per_device(
    loads_first,
    loads_second,
    loads_third,
    loads_fourth,
    inverse_first,
    inverse_second,
    inverse_third,
    inverse_fourth,
    panel_first,
    panel_second,
    panel_third,
    panel_fourth,
    blocks_first,
    blocks_second,
    blocks_third,
):
    n_y, n_rows = lax.axis_size("y"), 2 * lax.axis_size("y")
    core, x_index, y_index = (lax.axis_index(a) for a in ("core", "x", "y"))
    z1, z2 = lax.axis_index("z1"), lax.axis_index("z2")
    row_index = y_index * 2 + core
    z_index = z2 * 2 + z1
    leaf = (lax.axis_index("hi") * 4 + z_index) * 2 + x_index
    mask_x, mask_z1, mask_z2 = n_rows, 2 * n_rows, 4 * n_rows
    y_masks = [2 * y for y in range(1, n_y)]
    plane_masks = [(x, y) for y in range(n_y) for x in range(2)]
    update_rows, width = panel_first.shape[0], blocks_first.shape[1]
    block = update_rows // width
    rows, depth = inverse_first.shape[0], loads_first.shape[0]
    cols = loads_first.shape[1]
    half = cols // 2

    values = [core, row_index, row_index ^ 1]
    for mask in y_masks:
        values += [row_index ^ mask, row_index ^ mask ^ 1]
    at_z = len(values)
    values.append(z_index)
    at_order = []
    for planes in ([0], [z1, z1 ^ 1], [z_index, z_index ^ 2, z_index ^ 1, z_index ^ 3]):
        at_order.append(len(values))
        for x, y in plane_masks:
            place = ((x_index ^ x) * n_y + (y_index ^ y)) * 2
            for z in planes:
                values += [z * 2 * n_rows + place + (core ^ other) for other in range(2)]
    at_table = [len(values) + 2 * width * i for i in range(3)]
    children = [(leaf >> 1) * 2, (leaf >> 1) * 2 + 1]
    parts = [jnp.stack([jnp.asarray(v, jnp.int32) for v in values])]
    for table, pair in (
        (blocks_first, children),
        (blocks_second, [leaf >> 1, (leaf >> 1) ^ 1]),
        (blocks_third, [leaf >> 2, (leaf >> 2) ^ 1]),
    ):
        parts += [lax.dynamic_index_in_dim(table, c, 0, keepdims=False) for c in pair]
    scalars = jnp.concatenate(parts)
    scalars, loads_second, loads_third, loads_fourth = lax.optimization_barrier(
        (scalars, loads_second, loads_third, loads_fourth)
    )

    tie = lax.optimization_barrier

    n_far = 2 * len(y_masks)
    sibling = permute(loads_first, 1)
    shards = [permute(loads_first, mask, upward=True) for mask in y_masks]
    loads = [loads_second, loads_third, loads_fourth]
    sizes = [v.shape[0] for v in loads]
    keep, send = kernel_call(
        split_kernel, [(aval(sum(sizes), half, BF16), True)] * 2, scalars, loads, pin=False
    )
    received = permute(send, 1)
    keep, received, inverse_third, panel_third = tie((keep, received, inverse_third, panel_third))
    across_third = permute(inverse_third, 1), permute(panel_third, 1)
    acc, far, panel = kernel_call(
        near_kernel,
        [
            (aval(rows, cols, F32), True),
            (aval(rows, n_far * depth, BF16), True),
            (aval(*panel_first.shape, BF16), True),
        ],
        scalars,
        [loads_first, sibling],
        [inverse_first, panel_first],
        [
            pltpu.VMEM((rows, 2 * depth), BF16),
            pltpu.SemaphoreType.DMA((2 * (rows // row_tile(rows)) + n_far + 1,)),
        ],
        limit=16,
    )
    own_second, half_third, half_fourth = kernel_call(
        pack_kernel, [(aval(2 * s, half, BF16), True) for s in sizes], scalars, [keep, received]
    )
    x_second = permute(own_second, mask_x)
    z1_third = permute(half_third, mask_z1)
    z2_fourth = permute(half_fourth, mask_z2)
    shards, acc, own_second, x_second, z1_third, z2_fourth, across_third, panel_second = tie(
        (shards, acc, own_second, x_second, z1_third, z2_fourth, across_third, panel_second)
    )

    pieces = [v for shard in shards for v in (shard, permute(shard, 1))]
    pieces, panel_second = tie((pieces, panel_second))
    across_panel = permute(panel_second, 1)
    own_third = jnp.concatenate([half_third, z1_third], 0)
    half_fourth = jnp.concatenate([half_fourth, z2_fourth], 0)
    z1_fourth = permute(half_fourth, mask_z1)
    y_second = [permute(own_second, mask) for mask in y_masks]
    x_third = permute(own_third, mask_x)
    solved_first, keep, send = kernel_call(
        functools.partial(far_kernel, n_far),
        [
            (aval(rows, cols, BF16), False),
            (aval(update_rows, half, F32), True),
            (aval(update_rows, half, BF16), True),
        ],
        scalars,
        [acc, panel, far, *pieces],
        [],
        [pltpu.VMEM((rows, cols), BF16), pltpu.SemaphoreType.DMA],
    )
    keep, send, x_third, across_panel = tie((keep, send, x_third, across_panel))
    received = permute(send, 1)
    update = kernel_call(
        pair_sum_kernel, [(aval(*keep.shape, BF16), True)], scalars, [keep, received]
    )[0]
    update, y_second, z1_fourth, inverse_second = tie(
        (update, y_second, z1_fourth, inverse_second)
    )

    def with_x(x_piece, own, y_pieces):
        pieces = [own, x_piece]
        for piece in y_pieces:
            pieces += [piece, permute(piece, mask_x)]
        return pieces

    inverses = [(inverse_second, permute(inverse_second, 1))]
    panels = [(panel_second, across_panel), (panel_third, across_third[1])]
    inverses.append((inverse_third, across_third[0]))
    pieces_second = with_x(x_second, own_second, y_second)
    own_fourth = jnp.concatenate([half_fourth, z1_fourth], 0)
    part = reduce_over(update, "y", scalars, BF16)
    part, pieces_second, own_fourth = tie((part, pieces_second, own_fourth))

    def spread(value):
        return lax.all_gather(value, PLANE, axis=0, tiled=True)

    def plan_of(level, chunk, both):
        unit = math.gcd(chunk, block)
        places = []
        for place in range(2 * n_y):
            for child in range(2) if both else [place // n_y]:
                start = (place if both else place % n_y) * chunk
                for row in range(start, start + chunk, unit):
                    places.append((child * width + row // block, row % block))
        last = 2 * n_y if level == 2 else 0
        pieces = len(plane_masks)
        return (
            unit, places, block, at_table[level], at_order[level], sizes[level], pieces, last,
        )

    mine = spread(part)
    mine, own_third, own_fourth = tie((mine, own_third, own_fourth))
    y_third = [permute(own_third, mask) for mask in y_masks]
    x_fourth = permute(own_fourth, mask_x)
    update, keep, send = solve_level(
        scalars,
        plan_of(0, part.shape[0], False),
        mine,
        inverses[0],
        panels[0],
        pieces_second,
        update_rows,
    )
    update, y_third, x_fourth, keep, send, inverse_fourth, panel_fourth = tie(
        (update, y_third, x_fourth, keep, send, inverse_fourth, panel_fourth)
    )
    panel_fourth = panel_fourth.T
    inverses.append((inverse_fourth, permute(inverse_fourth, 1)))
    panels.append((panel_fourth, permute(panel_fourth, 1)))

    part = reduce_over(update, PLANE, scalars, BF16)
    part, y_third, own_fourth, keep, send = tie((part, y_third, own_fourth, keep, send))
    sibling = permute(part, mask_z1)
    pieces_third = with_x(x_third, own_third, y_third)
    y_fourth = [permute(own_fourth, mask) for mask in y_masks]
    solved_second = join_columns(core, keep, permute(send, 1))
    part, sibling, pieces_third, y_fourth, solved_second, inverses, panels = tie(
        (part, sibling, pieces_third, y_fourth, solved_second, inverses, panels)
    )
    mine = spread(jnp.concatenate([part, sibling], 0))
    update, keep, send = solve_level(
        scalars,
        plan_of(1, part.shape[0], True),
        mine,
        inverses[1],
        panels[1],
        pieces_third,
        update_rows,
    )

    part = reduce_over(update, PLANE, scalars, BF16)
    part, y_fourth, keep, send = tie((part, y_fourth, keep, send))
    pieces_fourth = with_x(x_fourth, own_fourth, y_fourth)
    solved_third = join_columns(core, keep, permute(send, 1))
    part = (part.astype(F32) + permute(part, mask_z1).astype(F32)).astype(BF16)
    sibling = permute(part, mask_z2)
    part, sibling, pieces_fourth, solved_third = tie((part, sibling, pieces_fourth, solved_third))
    mine = spread(jnp.concatenate([part, sibling], 0))
    update, keep_fourth, send_fourth = solve_level(
        scalars,
        plan_of(2, part.shape[0], True),
        mine,
        inverses[2],
        panels[2],
        pieces_fourth,
        update_rows,
    )
    solved_fourth = join_columns(core, keep_fourth, permute(send_fourth, 1))
    part = reduce_over(update, PLANE, scalars, F32)
    chunk = part.shape[0] // 4
    own, *sends = kernel_call(
        functools.partial(z_split_kernel, at_z),
        [(aval(chunk, half, F32), True)] + [(aval(chunk, half, BF16), True)] * 3,
        scalars,
        [part],
    )
    arrived = [permute(value, (i + 1) * mask_z1) for i, value in enumerate(sends)]
    keep, send = kernel_call(
        z_sum_kernel,
        [(aval(chunk // 2, half, F32), True)] * 2,
        scalars,
        [own, *arrived],
        scratch=[pltpu.VMEM((chunk, half), F32)],
    )
    ancestor = join_columns(core, keep, permute(send, 1))
    return solved_first, solved_second, solved_third, solved_fourth, ancestor


def solution(mesh):
    n_leaf, n_rows = mesh.shape["leaf"], mesh.shape["rows"]
    fine = Mesh(mesh.devices.reshape(n_leaf // 8, 2, 2, 2, n_rows // 2, 2), AXES)
    rows, cols = P(AXES, None), P(None, AXES)
    return jax.shard_map(
        per_device,
        mesh=fine,
        in_specs=(rows,) * 8 + (cols,) * 4 + (P(),) * 3,
        out_specs=(rows,) * 5,
        check_vma=False,
    )
```

time: 606 us -> 206 us (0.34)
  waiting for transfers between devices: 412 us -> 61 us
  Pallas kernels: 0 us -> 49.5 us
  matrix products: 47.7 us -> 0 us
  local copies, waits for them, and re-layouts: 52.2 us -> 7.13 us
  other arithmetic: 31 us -> 3.01 us
  blocking collectives: 21.7 us -> 42.5 us
  starting transfers between devices: 22.1 us -> 40.5 us
  between operations: 15.1 us -> 1.24 us
    ppermute x15 -> x33, waiting for transfers between devices: 234 us -> 41.3 us  [permute(): return lax.ppermute(value, AXES, pairs)]
    reduce_scatter x4 -> x0, waiting for transfers between devices: 112 us -> none  [reduce_sliced(): lax.psum_scatter(partial_value, 'rows', scatter_dimension=0, tiled=True)]
    all_gather x8 -> x0, waiting for transfers between devices: 64.1 us -> none  [the longest x2 54.2 us: stack_group(): gathered = lax.all_gather(local_rows, 'rows', axis=0, tiled=True)]
    pallas_call x0 -> x14, Pallas kernels: none -> 49.5 us  [kernel_call(): pl.pallas_call(kernel, out_shape=[pltpu.VMEM(o.shape, o.dtype) if inside...]
    dot_general x14 -> x0, matrix products: 47.7 us -> none  [the longest x6 22.4 us: place_rows(): jnp.einsum('us,ubn->sbn', selector, blocks, precision=lax.Precision.HIGHEST)]
    dot_general x6 -> x0, local copies, waits for them, and re-layouts: 30.6 us -> none  [place_rows(): jnp.einsum('us,ubn->sbn', selector, blocks, precision=lax.Precision.HIGHEST)]
    all_to_all x0 -> x3, waiting for transfers between devices: none -> 19.7 us  [reduce_over(): arrived = lax.all_to_all(value, axes, 0, 0, tiled=True)]
    convert_element_type x11 -> x1, other arithmetic: 14.1 us -> 0.03 us  [per_device(): part = (part.astype(F32) + permute(part, mask_z1).astype(F32)).astype(BF16)]
  transfers between devices with their start and end apart: 27 -> 36, of which waited for: 19 -> 19; matrix products, arithmetic and copies ran while one was open for 9% -> 1% of each run, Pallas kernels for 0% -> 16%
where the time goes in v3:
time: 206 us; the launch traced here: 205 us
  waiting for transfers between devices  61 us (30%)
  Pallas kernels  49.5 us (24%)
  blocking collectives  42.5 us (21%)
  starting transfers between devices  40.5 us (20%)
  local copies, waits for them, and re-layouts  7.13 us (3%)
  other arithmetic  3.01 us (1%)
    pallas_call x14, Pallas kernels, kernel_call(): pl.pallas_call(kernel, out_shape=[pltpu.VMEM(o.shape, o.dtype) if inside...  49.5 us
    ppermute x33, waiting for transfers between devices, permute(): return lax.ppermute(value, AXES, pairs)  41.3 us
    all_gather x3, blocking collectives, spread(): return lax.all_gather(value, PLANE, axis=0, tiled=True)  32.7 us
    ppermute x33, starting transfers between devices, permute(): return lax.ppermute(value, AXES, pairs)  30.1 us
    all_to_all x3, waiting for transfers between devices, reduce_over(): arrived = lax.all_to_all(value, axes, 0, 0, tiled=True)  19.7 us
    all_to_all x3, starting transfers between devices, reduce_over(): arrived = lax.all_to_all(value, axes, 0, 0, tiled=True)  10.4 us
    all_to_all x1, blocking collectives, reduce_over(): arrived = lax.all_to_all(value, axes, 0, 0, tiled=True)  9.79 us
    unnamed x39, local copies, waits for them, and re-layouts  5.4 us
  transfers between devices with their start and end apart: 36, of which 19 were waited for; matrix products, arithmetic and copies ran while one was open for 1% of the time, Pallas kernels for 16%

profile of v3, /device:TPU:0, one launch (start us, length us, event | category | flops | bytes accessed | tf_op | source)
XLA Modules:
  0.0 204.8 jit_solution(7830262088400932213)
XLA Ops:
  8.6 4.6 %collective-permute-start = (bf16[1536,256]{1,0:T(8,128)(2,1)}, bf16[1536,256]{1,0:T(8,128)(2,1)S(1)}, u32[]{:S(2)}, u32[]{:S(2)}) collective-permute-start(bf16[1536,256]{1,0:T(8,128)(2,1)} %b0.1), channel_id=1, source_target_pairs={{0,2},{1,3},{4,6},{5,7},{8,10},{9,11},{12,14},{13,15},{16,18},{17,... | collective-permute-start | bytes 2359304 | tf_op jit(solution)/shard_map/ppermute | solution.py:25
  13.9 2.7 %collective-permute-start.5 = (bf16[384,128]{1,0:T(8,128)(2,1)S(1)}, bf16[384,128]{1,0:T(8,128)(2,1)S(1)}, u32[]{:S(2)}, u32[]{:S(2)}) collective-permute-start(bf16[384,128]{1,0:T(8,128)(2,1)S(1)} %get-tuple-element.118), channel_id=1, source_target_pairs={{0,16},{1,17},{2,18},{3,19},{4,20},{5,21},{6,22},{7,23},{8,24},{9,... | collective-permute-start | bytes 294920 | tf_op jit(solution)/shard_map/ppermute | solution.py:25
  16.5 5.2 %collective-permute-done.5 = bf16[384,128]{1,0:T(8,128)(2,1)S(1)} collective-permute-done((bf16[384,128]{1,0:T(8,128)(2,1)S(1)}, bf16[384,128]{1,0:T(8,128)(2,1)S(1)}, u32[]{:S(2)}, u32[]{:S(2)}) %collective-permute-start.5) | collective-permute-done | bytes 98336 | tf_op jit(solution)/shard_map/ppermute | solution.py:25
  21.7 1.5 collective-permute-start.3
  25.0 8.6 %shard_map.182 = (f32[1536,256]{1,0:T(8,128)S(1)}, bf16[1536,3072]{1,0:T(8,128)(2,1)S(1)}, bf16[1536,1536]{1,0:T(8,128)(2,1)S(1)}) custom-call(s32[134]{0:T(256)S(1)} %concatenate.43.scalars, bf16[1536,256]{1,0:T(8,128)(2,1)S(1)} %copy-done, bf16[1536,256]{1,0:T(8,128)(2,1)S(1)} %collective-permute-done.1.b1, bf16[1536,6144]{1,0:T(8,128)(2,1)} %inverse.1, ...), custom_call_target="tpu_custom_call" | custom-call | tf_op jit(solution)/shard_map/pallas_call | solution.py:38
  33.8 2.3 %collective-permute-done.8.refs_1_ = bf16[1536,256]{1,0:T(8,128)(2,1)S(1)} collective-permute-done((bf16[1536,256]{1,0:T(8,128)(2,1)S(1)}, bf16[1536,256]{1,0:T(8,128)(2,1)S(1)}, u32[]{:S(2)}, u32[]{:S(2)}) %collective-permute-start.8) | collective-permute-done | bytes 786464 | tf_op jit(solution)/shard_map/ppermute | solution.py:25
  36.9 5.3 %shard_map.185 = (bf16[1536,256]{1,0:T(8,128)(2,1)}, f32[1536,128]{1,0:T(8,128)S(1)}, bf16[1536,128]{1,0:T(8,128)(2,1)S(1)}) custom-call(s32[134]{0:T(256)S(1)} %concatenate.43.scalars, f32[1536,256]{1,0:T(8,128)S(1)} %get-tuple-element.121.acc, bf16[1536,1536]{1,0:T(8,128)(2,1)S(1)} %get-tuple-element.122.panel, ...), custom_call_target="tpu_custom_call" | custom-call | tf_op jit(solution)/shard_map/pallas_call | solution.py:38
  42.2 5.5 %collective-permute-done.9.refs_5_ = bf16[1536,128]{1,0:T(8,128)(2,1)S(1)} collective-permute-done((bf16[1536,128]{1,0:T(8,128)(2,1)S(1)}, bf16[1536,128]{1,0:T(8,128)(2,1)S(1)}, u32[]{:S(2)}, u32[]{:S(2)}) %collective-permute-start.9) | collective-permute-done | bytes 393248 | tf_op jit(solution)/shard_map/ppermute | solution.py:25
  50.9 4.3 %collective-permute-done.13 = bf16[768,128]{1,0:T(8,128)(2,1)S(1)} collective-permute-done((bf16[768,128]{1,0:T(8,128)(2,1)S(1)}, bf16[768,128]{1,0:T(8,128)(2,1)S(1)}, u32[]{:S(2)}, u32[]{:S(2)}) %collective-permute-start.13) | collective-permute-done | bytes 196640 | tf_op jit(solution)/shard_map/ppermute | solution.py:25
  55.2 4.1 %collective-permute-done.12.refs_6_ = bf16[1536,128]{1,0:T(8,128)(2,1)S(1)} collective-permute-done((bf16[1536,128]{1,0:T(8,128)(2,1)S(1)}, bf16[1536,128]{1,0:T(8,128)(2,1)S(1)}, u32[]{:S(2)}, u32[]{:S(2)}) %collective-permute-start.12) | collective-permute-done | bytes 393248 | tf_op jit(solution)/shard_map/ppermute | solution.py:25
  60.0 3.5 %all-to-all-start = ((bf16[2,768,128]{2,1,0:T(8,128)(2,1)}), bf16[2,768,128]{2,1,0:T(8,128)(2,1)S(1)}, u32[]{:S(2)}, u32[]{:S(2)}) async-start(bf16[2,768,128]{2,1,0:T(8,128)(2,1)} %bitcast.68), calls=%async_computation | async-start | bytes 786432 | tf_op jit(solution)/shard_map/all_to_all | solution.py:166
  63.5 7.1 %all-to-all-done = bf16[2,768,128]{2,1,0:T(8,128)(2,1)S(1)} async-done(((bf16[2,768,128]{2,1,0:T(8,128)(2,1)}), bf16[2,768,128]{2,1,0:T(8,128)(2,1)S(1)}, u32[]{:S(2)}, u32[]{:S(2)}) %all-to-all-start) | async-done | bytes 393248 | tf_op jit(solution)/shard_map/all_to_all | solution.py:166
  72.0 11.8 %all_gather.9.mine = bf16[3072,128]{1,0:T(8,128)(2,1)S(1)} all-gather(bf16[768,128]{1,0:T(8,128)(2,1)S(1)} %shard_map.187), channel_id=1, replica_groups=mesh['hi'=1,'z2'=2,'z1'=2,'x'=2,'y'=2,'core'=2] {'x','y'}, dimensions={0}, use_global_device_ids=true | all-gather | bytes 983040 | tf_op jit(solution)/shard_map/all_gather | solution.py:437
  83.9 2.0 collective-permute-start.17
  85.9 13.7 %shard_map.188 = (bf16[1536,128]{1,0:T(8,128)(2,1)}, bf16[768,128]{1,0:T(8,128)(2,1)S(1)}, bf16[768,128]{1,0:T(8,128)(2,1)S(1)}) custom-call(s32[134]{0:T(256)S(1)} %concatenate.43.scalars, bf16[3072,128]{1,0:T(8,128)(2,1)S(1)} %all_gather.9.mine, bf16[768,6144]{1,0:T(8,128)(2,1)} %refs_0_.1, bf16[768,6144]{1,0:T(8,128)(2,1)} %collective-permute-done.15.refs_1_, ...), custom_call_target="tpu_custom_call" | custom-call | tf_op jit(solution)/shard_map/pallas_call | solution.py:38
  100.3 3.5 %all-to-all-start.1 = ((bf16[4,384,128]{2,1,0:T(8,128)(2,1)}), bf16[4,384,128]{2,1,0:T(8,128)(2,1)S(1)}, u32[]{:S(2)}, u32[]{:S(2)}) async-start(bf16[4,384,128]{2,1,0:T(8,128)(2,1)} %bitcast.70), calls=%async_computation.1 | async-start | bytes 786432 | tf_op jit(solution)/shard_map/all_to_all | solution.py:166
  103.9 6.8 %all-to-all-done.1 = bf16[4,384,128]{2,1,0:T(8,128)(2,1)S(1)} async-done(((bf16[4,384,128]{2,1,0:T(8,128)(2,1)}), bf16[4,384,128]{2,1,0:T(8,128)(2,1)S(1)}, u32[]{:S(2)}, u32[]{:S(2)}) %all-to-all-start.1) | async-done | bytes 393248 | tf_op jit(solution)/shard_map/all_to_all | solution.py:166
  117.0 2.6 %collective-permute-done.18 = bf16[384,128]{1,0:T(8,128)(2,1)S(1)} collective-permute-done((bf16[384,128]{1,0:T(8,128)(2,1)S(1)}, bf16[384,128]{1,0:T(8,128)(2,1)S(1)}, u32[]{:S(2)}, u32[]{:S(2)}) %collective-permute-start.18) | collective-permute-done | bytes 98336 | tf_op jit(solution)/shard_map/ppermute | solution.py:25
  119.6 2.7 %collective-permute-done.19.refs_7_ = bf16[1536,128]{1,0:T(8,128)(2,1)S(1)} collective-permute-done((bf16[1536,128]{1,0:T(8,128)(2,1)}, bf16[1536,128]{1,0:T(8,128)(2,1)S(1)}, u32[]{:S(2)}, u32[]{:S(2)}) %collective-permute-start.19) | collective-permute-done | bytes 393248 | tf_op jit(solution)/shard_map/ppermute | solution.py:25
  122.3 1.6 collective-permute-done.20.refs_6_
  123.9 10.2 %all_gather.10.mine = bf16[3072,128]{1,0:T(8,128)(2,1)S(1)} all-gather(bf16[768,128]{1,0:T(8,128)(2,1)S(1)} %pad_maximum_fusion.2), channel_id=1, replica_groups=mesh['hi'=1,'z2'=2,'z1'=2,'x'=2,'y'=2,'core'=2] {'x','y'}, dimensions={0}, use_global_device_ids=true | all-gather | bytes 983040 | tf_op jit(solution)/shard_map/all_gather | solution.py:437
  134.0 8.9 %shard_map.190 = (bf16[1536,128]{1,0:T(8,128)(2,1)S(1)}, bf16[384,128]{1,0:T(8,128)(2,1)S(1)}, bf16[384,128]{1,0:T(8,128)(2,1)S(1)}) custom-call(s32[134]{0:T(256)S(1)} %concatenate.43.scalars, bf16[3072,128]{1,0:T(8,128)(2,1)S(1)} %all_gather.10.mine, bf16[384,6144]{1,0:T(8,128)(2,1)} %refs_0_.2, bf16[384,6144]{1,0:T(8,128)(2,1)} %copy-done.5, ...), custom_call_target="tpu_custom_call" | custom-call | tf_op jit(solution)/shard_map/pallas_call | solution.py:38
  142.9 9.8 %all_to_all.44 = bf16[4,384,128]{2,1,0:T(8,128)(2,1)S(1)} all-to-all(bf16[4,384,128]{2,1,0:T(8,128)(2,1)S(1)} %bitcast.87), channel_id=1, replica_groups=mesh['hi'=1,'z2'=2,'z1'=2,'x'=2,'y'=2,'core'=2] {'x','y'}, dimensions={0} | all-to-all | bytes 786432 | tf_op jit(solution)/shard_map/all_to_all | solution.py:166
  155.6 2.3 %collective-permute-done.24 = bf16[384,128]{1,0:T(8,128)(2,1)S(1)} collective-permute-done((bf16[384,128]{1,0:T(8,128)(2,1)S(1)}, bf16[384,128]{1,0:T(8,128)(2,1)S(1)}, u32[]{:S(2)}, u32[]{:S(2)}) %collective-permute-start.24) | collective-permute-done | bytes 98336 | tf_op jit(solution)/shard_map/ppermute | solution.py:25
  158.0 3.7 %collective-permute-start.25 = (bf16[384,128]{1,0:T(8,128)(2,1)S(1)}, bf16[384,128]{1,0:T(8,128)(2,1)S(1)}, u32[]{:S(2)}, u32[]{:S(2)}) collective-permute-start(bf16[384,128]{1,0:T(8,128)(2,1)S(1)} %add_convert_fusion), channel_id=1, source_target_pairs={{0,16},{1,17},{2,18},{3,19},{4,20},{5,21},{6,22},{7,23},{8,24},{9,... | collective-permute-start | bytes 294920 | tf_op jit(solution)/shard_map/ppermute | solution.py:25
  162.4 2.9 %collective-permute-done.25 = bf16[384,128]{1,0:T(8,128)(2,1)S(1)} collective-permute-done((bf16[384,128]{1,0:T(8,128)(2,1)S(1)}, bf16[384,128]{1,0:T(8,128)(2,1)S(1)}, u32[]{:S(2)}, u32[]{:S(2)}) %collective-permute-start.25) | collective-permute-done | bytes 98336 | tf_op jit(solution)/shard_map/ppermute | solution.py:25
  165.4 10.8 %all_gather.11.mine = bf16[3072,128]{1,0:T(8,128)(2,1)S(1)} all-gather(bf16[768,128]{1,0:T(8,128)(2,1)S(1)} %pad_maximum_fusion.3), channel_id=1, replica_groups=mesh['hi'=1,'z2'=2,'z1'=2,'x'=2,'y'=2,'core'=2] {'x','y'}, dimensions={0}, use_global_device_ids=true | all-gather | bytes 983040 | tf_op jit(solution)/shard_map/all_gather | solution.py:437
  176.2 6.9 %shard_map.192 = (bf16[1536,128]{1,0:T(8,128)(2,1)}, bf16[192,128]{1,0:T(8,128)(2,1)S(1)}, bf16[192,128]{1,0:T(8,128)(2,1)S(1)}) custom-call(s32[134]{0:T(256)S(1)} %concatenate.43.scalars, bf16[3072,128]{1,0:T(8,128)(2,1)S(1)} %all_gather.11.mine, bf16[192,6144]{1,0:T(8,128)(2,1)} %refs_0_.3, bf16[192,6144]{1,0:T(8,128)(2,1)} %collective-permute-done.22.refs_1_, ...), custom_call_target="tpu_custom_call" | custom-call | tf_op jit(solution)/shard_map/pallas_call | solution.py:38
  183.1 3.5 %all-to-all-start.3 = ((bf16[4,384,128]{2,1,0:T(8,128)(2,1)}), bf16[4,384,128]{2,1,0:T(8,128)(2,1)S(1)}, u32[]{:S(2)}, u32[]{:S(2)}) async-start(bf16[4,384,128]{2,1,0:T(8,128)(2,1)} %bitcast.75), calls=%async_computation.3 | async-start | bytes 786432 | tf_op jit(solution)/shard_map/all_to_all | solution.py:166
  186.6 5.8 %all-to-all-done.3 = bf16[4,384,128]{2,1,0:T(8,128)(2,1)S(1)} async-done(((bf16[4,384,128]{2,1,0:T(8,128)(2,1)}), bf16[4,384,128]{2,1,0:T(8,128)(2,1)S(1)}, u32[]{:S(2)}, u32[]{:S(2)}) %all-to-all-start.3) | async-done | bytes 393248 | tf_op jit(solution)/shard_map/all_to_all | solution.py:166
  194.2 2.5 %collective-permute-start.30 = (bf16[96,128]{1,0:T(8,128)(2,1)S(1)}, bf16[96,128]{1,0:T(8,128)(2,1)S(1)}, u32[]{:S(2)}, u32[]{:S(2)}) collective-permute-start(bf16[96,128]{1,0:T(8,128)(2,1)S(1)} %get-tuple-element.205), channel_id=1, source_target_pairs={{0,16},{1,17},{2,18},{3,19},{4,20},{5,21},{6,22},{7,23},{8,24},{9,... | collective-permute-start | bytes 73736 | tf_op jit(solution)/shard_map/ppermute | solution.py:25
  198.9 3.4 %collective-permute-done.31.c = bf16[96,128]{1,0:T(8,128)(2,1)S(1)} collective-permute-done((bf16[96,128]{1,0:T(8,128)(2,1)S(1)}, bf16[96,128]{1,0:T(8,128)(2,1)S(1)}, u32[]{:S(2)}, u32[]{:S(2)}) %collective-permute-start.31) | collective-permute-done | bytes 24608 | tf_op jit(solution)/shard_map/ppermute | solution.py:25
  (110 shorter events, 33.8 us)
Async XLA Ops:
  7.7 26.0 %collective-permute-start.6 = (bf16[384,6144]{1,0:T(8,128)(2,1)}, bf16[384,6144]{1,0:T(8,128)(2,1)S(1)}, u32[]{:S(2)}, u32[]{:S(2)}) collective-permute-start(bf16[384,6144]{1,0:T(8,128)(2,1)} %refs_0_.2), channel_id=1, source_target_pairs={{0,1},{1,0},{2,3},{3,2},{4,5},{5,4},{6,7},{7,6},{8,9},{9,8},{10,11... | collective-permute-start | bytes 14155784 | tf_op jit(solution)/shard_map/ppermute | solution.py:25
  8.1 25.6 %collective-permute-start.7 = (bf16[1536,384]{1,0:T(8,128)(2,1)}, bf16[1536,384]{1,0:T(8,128)(2,1)S(1)}, u32[]{:S(2)}, u32[]{:S(2)}) collective-permute-start(bf16[1536,384]{1,0:T(8,128)(2,1)} %refs_2_.2), channel_id=1, source_target_pairs={{0,1},{1,0},{2,3},{3,2},{4,5},{5,4},{6,7},{7,6},{8,9},{9,8},{10,11... | collective-permute-start | bytes 3538952 | tf_op jit(solution)/shard_map/ppermute | solution.py:25
  8.2 14.9 %collective-permute-start.1 = (bf16[1536,256]{1,0:T(8,128)(2,1)}, bf16[1536,256]{1,0:T(8,128)(2,1)S(1)}, u32[]{:S(2)}, u32[]{:S(2)}) collective-permute-start(bf16[1536,256]{1,0:T(8,128)(2,1)} %b0.1), channel_id=1, source_target_pairs={{0,1},{1,0},{2,3},{3,2},{4,5},{5,4},{6,7},{7,6},{8,9},{9,8},{10,11... | collective-permute-start | bytes 2359304 | tf_op jit(solution)/shard_map/ppermute | solution.py:25
  8.6 25.1 %collective-permute-start = (bf16[1536,256]{1,0:T(8,128)(2,1)}, bf16[1536,256]{1,0:T(8,128)(2,1)S(1)}, u32[]{:S(2)}, u32[]{:S(2)}) collective-permute-start(bf16[1536,256]{1,0:T(8,128)(2,1)} %b0.1), channel_id=1, source_target_pairs={{0,2},{1,3},{4,6},{5,7},{8,10},{9,11},{12,14},{13,15},{16,18},{17,... | collective-permute-start | bytes 2359304 | tf_op jit(solution)/shard_map/ppermute | solution.py:25
  13.9 7.8 %collective-permute-start.5 = (bf16[384,128]{1,0:T(8,128)(2,1)S(1)}, bf16[384,128]{1,0:T(8,128)(2,1)S(1)}, u32[]{:S(2)}, u32[]{:S(2)}) collective-permute-start(bf16[384,128]{1,0:T(8,128)(2,1)S(1)} %get-tuple-element.118), channel_id=1, source_target_pairs={{0,16},{1,17},{2,18},{3,19},{4,20},{5,21},{6,22},{7,23},{8,24},{9,... | collective-permute-start | bytes 294920 | tf_op jit(solution)/shard_map/ppermute | solution.py:25
  21.7 11.9 %collective-permute-start.3 = (bf16[1536,128]{1,0:T(8,128)(2,1)S(1)}, bf16[1536,128]{1,0:T(8,128)(2,1)S(1)}, u32[]{:S(2)}, u32[]{:S(2)}) collective-permute-start(bf16[1536,128]{1,0:T(8,128)(2,1)S(1)} %get-tuple-element.146.refs_4_), channel_id=1, source_target_pairs={{0,4},{1,5},{2,6},{3,7},{4,0},{5,1},{6,2},{7,3},{8,12},{9,13},{10,... | collective-permute-start | bytes 1179656 | tf_op jit(solution)/shard_map/ppermute | solution.py:25
  23.2 10.4 %collective-permute-start.4 = (bf16[768,128]{1,0:T(8,128)(2,1)S(1)}, bf16[768,128]{1,0:T(8,128)(2,1)S(1)}, u32[]{:S(2)}, u32[]{:S(2)}) collective-permute-start(bf16[768,128]{1,0:T(8,128)(2,1)S(1)} %get-tuple-element.117), channel_id=1, source_target_pairs={{0,8},{1,9},{2,10},{3,11},{4,12},{5,13},{6,14},{7,15},{8,0},{9,1},... | collective-permute-start | bytes 589832 | tf_op jit(solution)/shard_map/ppermute | solution.py:25
  33.7 2.4 %collective-permute-start.8 = (bf16[1536,256]{1,0:T(8,128)(2,1)S(1)}, bf16[1536,256]{1,0:T(8,128)(2,1)S(1)}, u32[]{:S(2)}, u32[]{:S(2)}) collective-permute-start(bf16[1536,256]{1,0:T(8,128)(2,1)S(1)} %collective-permute-done.refs_0_), channel_id=1, source_target_pairs={{0,1},{1,0},{2,3},{3,2},{4,5},{5,4},{6,7},{7,6},{8,9},{9,8},{10,11... | collective-permute-start | bytes 2359304 | tf_op jit(solution)/shard_map/ppermute | solution.py:25
  36.1 11.7 %collective-permute-start.10 = (bf16[1536,768]{1,0:T(8,128)(2,1)S(1)}, bf16[1536,768]{1,0:T(8,128)(2,1)S(1)}, u32[]{:S(2)}, u32[]{:S(2)}) collective-permute-start(bf16[1536,768]{1,0:T(8,128)(2,1)S(1)} %copy-done.6), channel_id=1, source_target_pairs={{0,1},{1,0},{2,3},{3,2},{4,5},{5,4},{6,7},{7,6},{8,9},{9,8},{10,11... | collective-permute-start | bytes 7077896 | tf_op jit(solution)/shard_map/ppermute | solution.py:25
  36.3 11.5 %collective-permute-start.9 = (bf16[1536,128]{1,0:T(8,128)(2,1)S(1)}, bf16[1536,128]{1,0:T(8,128)(2,1)S(1)}, u32[]{:S(2)}, u32[]{:S(2)}) collective-permute-start(bf16[1536,128]{1,0:T(8,128)(2,1)S(1)} %constant_dynamic-update-slice_fusion.refs_4_), channel_id=1, source_target_pairs={{0,4},{1,5},{2,6},{3,7},{4,0},{5,1},{6,2},{7,3},{8,12},{9,13},{10,... | collective-permute-start | bytes 1179656 | tf_op jit(solution)/shard_map/ppermute | solution.py:25
  47.8 11.5 %collective-permute-start.12 = (bf16[1536,128]{1,0:T(8,128)(2,1)S(1)}, bf16[1536,128]{1,0:T(8,128)(2,1)S(1)}, u32[]{:S(2)}, u32[]{:S(2)}) collective-permute-start(bf16[1536,128]{1,0:T(8,128)(2,1)S(1)} %get-tuple-element.146.refs_4_), channel_id=1, source_target_pairs={{0,2},{1,3},{2,0},{3,1},{4,6},{5,7},{6,4},{7,5},{8,10},{9,11},{10,... | collective-permute-start | bytes 1179656 | tf_op jit(solution)/shard_map/ppermute | solution.py:25
  47.9 7.3 %collective-permute-start.13 = (bf16[768,128]{1,0:T(8,128)(2,1)S(1)}, bf16[768,128]{1,0:T(8,128)(2,1)S(1)}, u32[]{:S(2)}, u32[]{:S(2)}) collective-permute-start(bf16[768,128]{1,0:T(8,128)(2,1)S(1)} %pad_maximum_fusion.1), channel_id=1, source_target_pairs={{0,8},{1,9},{2,10},{3,11},{4,12},{5,13},{6,14},{7,15},{8,0},{9,1},... | collective-permute-start | bytes 589832 | tf_op jit(solution)/shard_map/ppermute | solution.py:25
  59.4 26.5 %collective-permute-start.15 = (bf16[768,6144]{1,0:T(8,128)(2,1)}, bf16[768,6144]{1,0:T(8,128)(2,1)}, u32[]{:S(2)}, u32[]{:S(2)}) collective-permute-start(bf16[768,6144]{1,0:T(8,128)(2,1)} %refs_0_.1), channel_id=1, source_target_pairs={{0,1},{1,0},{2,3},{3,2},{4,5},{5,4},{6,7},{7,6},{8,9},{9,8},{10,11... | collective-permute-start | bytes 28311560 | tf_op jit(solution)/shard_map/ppermute | solution.py:25
  59.4 11.8 %collective-permute-start.14 = (bf16[1536,128]{1,0:T(8,128)(2,1)S(1)}, bf16[1536,128]{1,0:T(8,128)(2,1)S(1)}, u32[]{:S(2)}, u32[]{:S(2)}) collective-permute-start(bf16[1536,128]{1,0:T(8,128)(2,1)S(1)} %collective-permute-done.12.refs_6_), channel_id=1, source_target_pairs={{0,4},{1,5},{2,6},{3,7},{4,0},{5,1},{6,2},{7,3},{8,12},{9,13},{10,... | collective-permute-start | bytes 1179656 | tf_op jit(solution)/shard_map/ppermute | solution.py:25
  60.0 10.6 %all-to-all-start = ((bf16[2,768,128]{2,1,0:T(8,128)(2,1)}), bf16[2,768,128]{2,1,0:T(8,128)(2,1)S(1)}, u32[]{:S(2)}, u32[]{:S(2)}) async-start(bf16[2,768,128]{2,1,0:T(8,128)(2,1)} %bitcast.68), calls=%async_computation | async-start | bytes 786432 | tf_op jit(solution)/shard_map/all_to_all | solution.py:166
  83.8 15.8 %collective-permute-start.16 = (bf16[1536,128]{1,0:T(8,128)(2,1)S(1)}, bf16[1536,128]{1,0:T(8,128)(2,1)}, u32[]{:S(2)}, u32[]{:S(2)}) collective-permute-start(bf16[1536,128]{1,0:T(8,128)(2,1)S(1)} %constant_dynamic-update-slice_fusion.refs_4_), channel_id=1, source_target_pairs={{0,2},{1,3},{2,0},{3,1},{4,6},{5,7},{6,4},{7,5},{8,10},{9,11},{10,... | collective-permute-start | bytes 1179656 | tf_op jit(solution)/shard_map/ppermute | solution.py:25
  83.9 15.7 %collective-permute-start.17 = (bf16[1536,128]{1,0:T(8,128)(2,1)S(1)}, bf16[1536,128]{1,0:T(8,128)(2,1)S(1)}, u32[]{:S(2)}, u32[]{:S(2)}) collective-permute-start(bf16[1536,128]{1,0:T(8,128)(2,1)S(1)} %pad_maximum_fusion.refs_4_), channel_id=1, source_target_pairs={{0,4},{1,5},{2,6},{3,7},{4,0},{5,1},{6,2},{7,3},{8,12},{9,13},{10,... | collective-permute-start | bytes 1179656 | tf_op jit(solution)/shard_map/ppermute | solution.py:25
  99.6 24.2 %collective-permute-start.22 = (bf16[192,6144]{1,0:T(8,128)(2,1)S(1)}, bf16[192,6144]{1,0:T(8,128)(2,1)}, u32[]{:S(2)}, u32[]{:S(2)}) collective-permute-start(bf16[192,6144]{1,0:T(8,128)(2,1)S(1)} %copy-done.8), channel_id=1, source_target_pairs={{0,1},{1,0},{2,3},{3,2},{4,5},{5,4},{6,7},{7,6},{8,9},{9,8},{10,11... | collective-permute-start | bytes 7077896 | tf_op jit(solution)/shard_map/ppermute | solution.py:25
  100.3 10.3 %all-to-all-start.1 = ((bf16[4,384,128]{2,1,0:T(8,128)(2,1)}), bf16[4,384,128]{2,1,0:T(8,128)(2,1)S(1)}, u32[]{:S(2)}, u32[]{:S(2)}) async-start(bf16[4,384,128]{2,1,0:T(8,128)(2,1)} %bitcast.70), calls=%async_computation.1 | async-start | bytes 786432 | tf_op jit(solution)/shard_map/all_to_all | solution.py:166
  103.8 15.8 %collective-permute-start.23 = (bf16[192,1536]{1,0:T(8,128)(2,1)}, bf16[192,1536]{1,0:T(8,128)(2,1)}, u32[]{:S(2)}, u32[]{:S(2)}) collective-permute-start(bf16[192,1536]{1,0:T(8,128)(2,1)} %bitcast.88), channel_id=1, source_target_pairs={{0,1},{1,0},{2,3},{3,2},{4,5},{5,4},{6,7},{7,6},{8,9},{9,8},{10,11... | collective-permute-start | bytes 1769480 | tf_op jit(solution)/shard_map/ppermute | solution.py:25
  111.3 11.0 %collective-permute-start.19 = (bf16[1536,128]{1,0:T(8,128)(2,1)}, bf16[1536,128]{1,0:T(8,128)(2,1)S(1)}, u32[]{:S(2)}, u32[]{:S(2)}) collective-permute-start(bf16[1536,128]{1,0:T(8,128)(2,1)} %collective-permute-done.16.refs_6_), channel_id=1, source_target_pairs={{0,4},{1,5},{2,6},{3,7},{4,0},{5,1},{6,2},{7,3},{8,12},{9,13},{10,... | collective-permute-start | bytes 1179656 | tf_op jit(solution)/shard_map/ppermute | solution.py:25
  112.8 11.1 %collective-permute-start.20 = (bf16[1536,128]{1,0:T(8,128)(2,1)}, bf16[1536,128]{1,0:T(8,128)(2,1)}, u32[]{:S(2)}, u32[]{:S(2)}) collective-permute-start(bf16[1536,128]{1,0:T(8,128)(2,1)} %copy-done.9), channel_id=1, source_target_pairs={{0,2},{1,3},{2,0},{3,1},{4,6},{5,7},{6,4},{7,5},{8,10},{9,11},{10,... | collective-permute-start | bytes 1179656 | tf_op jit(solution)/shard_map/ppermute | solution.py:25
  114.8 4.8 %collective-permute-start.18 = (bf16[384,128]{1,0:T(8,128)(2,1)S(1)}, bf16[384,128]{1,0:T(8,128)(2,1)S(1)}, u32[]{:S(2)}, u32[]{:S(2)}) collective-permute-start(bf16[384,128]{1,0:T(8,128)(2,1)S(1)} %shard_map.189), channel_id=1, source_target_pairs={{0,8},{1,9},{2,10},{3,11},{4,12},{5,13},{6,14},{7,15},{8,0},{9,1},... | collective-permute-start | bytes 294920 | tf_op jit(solution)/shard_map/ppermute | solution.py:25
  153.3 4.7 %collective-permute-start.24 = (bf16[384,128]{1,0:T(8,128)(2,1)S(1)}, bf16[384,128]{1,0:T(8,128)(2,1)S(1)}, u32[]{:S(2)}, u32[]{:S(2)}) collective-permute-start(bf16[384,128]{1,0:T(8,128)(2,1)S(1)} %shard_map.191), channel_id=1, source_target_pairs={{0,8},{1,9},{2,10},{3,11},{4,12},{5,13},{6,14},{7,15},{8,0},{9,1},... | collective-permute-start | bytes 294920 | tf_op jit(solution)/shard_map/ppermute | solution.py:25
  154.7 10.6 %collective-permute-start.26 = (bf16[1536,128]{1,0:T(8,128)(2,1)}, bf16[1536,128]{1,0:T(8,128)(2,1)S(1)}, u32[]{:S(2)}, u32[]{:S(2)}) collective-permute-start(bf16[1536,128]{1,0:T(8,128)(2,1)} %collective-permute-done.20.refs_6_), channel_id=1, source_target_pairs={{0,4},{1,5},{2,6},{3,7},{4,0},{5,1},{6,2},{7,3},{8,12},{9,13},{10,... | collective-permute-start | bytes 1179656 | tf_op jit(solution)/shard_map/ppermute | solution.py:25
  155.6 6.1 %collective-permute-start.27 = (bf16[384,128]{1,0:T(8,128)(2,1)S(1)}, bf16[384,128]{1,0:T(8,128)(2,1)S(1)}, u32[]{:S(2)}, u32[]{:S(2)}) collective-permute-start(bf16[384,128]{1,0:T(8,128)(2,1)S(1)} %get-tuple-element.188), channel_id=1, source_target_pairs={{0,1},{1,0},{2,3},{3,2},{4,5},{5,4},{6,7},{7,6},{8,9},{9,8},{10,11... | collective-permute-start | bytes 294920 | tf_op jit(solution)/shard_map/ppermute | solution.py:25
  158.0 7.3 %collective-permute-start.25 = (bf16[384,128]{1,0:T(8,128)(2,1)S(1)}, bf16[384,128]{1,0:T(8,128)(2,1)S(1)}, u32[]{:S(2)}, u32[]{:S(2)}) collective-permute-start(bf16[384,128]{1,0:T(8,128)(2,1)S(1)} %add_convert_fusion), channel_id=1, source_target_pairs={{0,16},{1,17},{2,18},{3,19},{4,20},{5,21},{6,22},{7,23},{8,24},{9,... | collective-permute-start | bytes 294920 | tf_op jit(solution)/shard_map/ppermute | solution.py:25
  183.1 9.3 %all-to-all-start.3 = ((bf16[4,384,128]{2,1,0:T(8,128)(2,1)}), bf16[4,384,128]{2,1,0:T(8,128)(2,1)S(1)}, u32[]{:S(2)}, u32[]{:S(2)}) async-start(bf16[4,384,128]{2,1,0:T(8,128)(2,1)} %bitcast.75), calls=%async_computation.3 | async-start | bytes 786432 | tf_op jit(solution)/shard_map/all_to_all | solution.py:166
  186.6 16.4 %collective-permute-start.28 = (bf16[192,128]{1,0:T(8,128)(2,1)S(1)}, bf16[192,128]{1,0:T(8,128)(2,1)S(1)}, u32[]{:S(2)}, u32[]{:S(2)}) collective-permute-start(bf16[192,128]{1,0:T(8,128)(2,1)S(1)} %get-tuple-element.201), channel_id=1, source_target_pairs={{0,1},{1,0},{2,3},{3,2},{4,5},{5,4},{6,7},{7,6},{8,9},{9,8},{10,11... | collective-permute-start | bytes 147464 | tf_op jit(solution)/shard_map/ppermute | solution.py:25
  193.6 4.5 %collective-permute-start.29 = (bf16[96,128]{1,0:T(8,128)(2,1)S(1)}, bf16[96,128]{1,0:T(8,128)(2,1)S(1)}, u32[]{:S(2)}, u32[]{:S(2)}) collective-permute-start(bf16[96,128]{1,0:T(8,128)(2,1)S(1)} %get-tuple-element.204), channel_id=1, source_target_pairs={{0,8},{1,9},{2,10},{3,11},{4,12},{5,13},{6,14},{7,15},{8,0},{9,1},... | collective-permute-start | bytes 73736 | tf_op jit(solution)/shard_map/ppermute | solution.py:25
  194.2 4.7 %collective-permute-start.30 = (bf16[96,128]{1,0:T(8,128)(2,1)S(1)}, bf16[96,128]{1,0:T(8,128)(2,1)S(1)}, u32[]{:S(2)}, u32[]{:S(2)}) collective-permute-start(bf16[96,128]{1,0:T(8,128)(2,1)S(1)} %get-tuple-element.205), channel_id=1, source_target_pairs={{0,16},{1,17},{2,18},{3,19},{4,20},{5,21},{6,22},{7,23},{8,24},{9,... | collective-permute-start | bytes 73736 | tf_op jit(solution)/shard_map/ppermute | solution.py:25
  196.7 5.6 %collective-permute-start.31 = (bf16[96,128]{1,0:T(8,128)(2,1)S(1)}, bf16[96,128]{1,0:T(8,128)(2,1)S(1)}, u32[]{:S(2)}, u32[]{:S(2)}) collective-permute-start(bf16[96,128]{1,0:T(8,128)(2,1)S(1)} %get-tuple-element.206), channel_id=1, source_target_pairs={{0,24},{1,25},{2,26},{3,27},{4,28},{5,29},{6,30},{7,31},{8,16},{9,... | collective-permute-start | bytes 73736 | tf_op jit(solution)/shard_map/ppermute | solution.py:25
  (23 other events, 239.3 us)

commit v4 on v3

v4 whole, which is shorter than its diff:
```python
import functools
import math

import jax
import jax.numpy as jnp
from jax import lax
from jax.experimental import pallas as pl
from jax.experimental.pallas import tpu as pltpu
from jax.sharding import Mesh
from jax.sharding import PartitionSpec as P

BF16 = jnp.bfloat16
F32 = jnp.float32
AXES = ("hi", "z2", "z1", "x", "y", "core")
PLANE = ("x", "y")
VMEM = pl.BlockSpec(memory_space=pltpu.VMEM)
SMEM = pl.BlockSpec(memory_space=pltpu.SMEM)
ANY = pl.BlockSpec(memory_space=pl.ANY)
MIB = 1 << 20


def permute(value, mask, upward=False):
    total = lax.axis_size(AXES)
    pairs = [(i, i ^ mask) for i in range(total) if not upward or (i ^ mask) > i]
    return lax.ppermute(value, AXES, pairs)


def row_tile(rows):
    return next(t for t in (512, 384, 256, 192, 128, 96, 64, 48, 32, 16) if rows % t == 0)


def aval(rows, cols, dtype):
    return jax.ShapeDtypeStruct((rows, cols), dtype)


def kernel_call(kernel, outs, scalars, vmem, hbm=(), scratch=(), limit=8):
    operands = [pltpu.with_memory_space_constraint(o, pltpu.VMEM) for o in vmem]
    return pl.pallas_call(
        kernel,
        out_shape=[pltpu.VMEM(o.shape, o.dtype) if inside else o for o, inside in outs],
        in_specs=[SMEM] + [VMEM] * len(vmem) + [ANY] * len(hbm),
        out_specs=[ANY if inside is False else VMEM for _, inside in outs],
        scratch_shapes=list(scratch),
        compiler_params=pltpu.CompilerParams(vmem_limit_bytes=limit * MIB),
        cost_estimate=pl.CostEstimate(flops=1, bytes_accessed=1, transcendentals=0),
    )(scalars, *operands, *[pltpu.with_memory_space_constraint(o, pltpu.HBM) for o in hbm])


def tiles(rows, step):
    tile = row_tile(rows)

    def body(i, carry):
        step(pl.ds(pl.multiple_of(i * tile, tile), tile))
        return carry

    lax.fori_loop(0, rows // tile, body, 0)


def dot(a, b):
    return jnp.dot(a, b, preferred_element_type=F32)


def start_all(sources, targets, sems):
    copies = [
        pltpu.make_async_copy(source, target, sems.at[i])
        for i, (source, target) in enumerate(zip(sources, targets))
    ]
    for copy in copies:
        copy.start()
    return copies


def near_kernel(scalars, b0, b1, inverse, panel, acc, far, panel_out, near, sems):
    rows, depth = inverse.shape[0], b0.shape[0]
    tile = row_tile(rows)
    n_far = far.shape[1] // depth
    columns = [
        pl.ds(pl.multiple_of(scalars[1 + i] * depth, depth), depth) for i in range(2 + n_far)
    ]
    sources, targets = [], []
    for i in range(rows // tile):
        at = pl.ds(i * tile, tile)
        for j in range(2):
            sources.append(inverse.at[at, columns[j]])
            targets.append(near.at[at, pl.ds(j * depth, depth)])
    for j in range(n_far):
        sources.append(inverse.at[:, columns[2 + j]])
        targets.append(far.at[:, pl.ds(j * depth, depth)])
    sources.append(panel)
    targets.append(panel_out)
    copies = start_all(sources, targets, sems)
    for i in range(rows // tile):
        at = pl.ds(i * tile, tile)
        copies[2 * i].wait()
        copies[2 * i + 1].wait()
        acc[at, :] = dot(near[at, :depth], b0[...]) + dot(near[at, depth:], b1[...])
    for copy in copies[2 * (rows // tile) :]:
        copy.wait()


def split_panel(core, panel, x_ref, keep, send):
    half = keep.shape[1]

    def step(at):
        part = dot(panel[at, :], x_ref[...])
        low, high = part[:, :half], part[:, half:]
        keep[at, :] = jnp.where(core == 0, low, high)
        send[at, :] = jnp.where(core == 0, high, low).astype(BF16)

    tiles(panel.shape[0], step)


def far_kernel(n_far, n_next, scalars, acc, panel, far, *refs):
    pieces, refs = refs[:n_far], refs[n_far:]
    solved, keep, send = refs[n_next : n_next + 3]
    x_ref, sem, sems = refs[-3:]
    copies = start_all(refs[:n_next], refs[n_next + 3 : -3], sems)
    depth = pieces[0].shape[0]

    def step(at):
        total = acc[at, :]
        for j, piece in enumerate(pieces):
            total += dot(far[at, j * depth : (j + 1) * depth], piece[...])
        x_ref[at, :] = total.astype(BF16)

    tiles(far.shape[0], step)
    result = pltpu.make_async_copy(x_ref, solved, sem)
    result.start()
    split_panel(scalars[0], panel, x_ref, keep, send)
    for copy in [*copies, result]:
        copy.wait()


def split_kernel(scalars, *refs):
    *arrays, keep, send, held, sems = refs
    core, half, first, targets = scalars[0], keep.shape[1], 0, []
    for array in arrays:
        targets.append(held.at[pl.ds(first, array.shape[0]), :])
        first += array.shape[0]
    for copy in start_all(arrays, targets, sems):
        copy.wait()
    low, high = held[:, :half], held[:, half:]
    keep[...] = jnp.where(core == 0, low, high)
    send[...] = jnp.where(core == 0, high, low)


def pack_kernel(groups, scalars, keep, received, *outs):
    for group, out in zip(groups, outs):
        at = 0
        for first, rows in group:
            out[at : at + rows, :] = keep[first : first + rows, :]
            out[at + rows : at + 2 * rows, :] = received[first : first + rows, :]
            at += 2 * rows


def join_kernel(scalars, own, other, out):
    half = own.shape[1]
    out[:, :half] = jnp.where(scalars[0] == 0, own[...], other[...])
    out[:, half:] = jnp.where(scalars[0] == 0, other[...], own[...])


def join_columns(scalars, own, other):
    rows, half = own.shape
    return kernel_call(join_kernel, [(aval(rows, 2 * half, own.dtype), None)], scalars, [own, other])[0]


def hand_out(place, value, own, sends):
    rows = own.shape[0]
    for mask, out in enumerate([own, *sends]):
        at = pl.ds(pl.multiple_of((place ^ mask) * rows, rows), rows)
        out[...] = value[at, :].astype(out.dtype)


def pair_sum_kernel(at_place, scalars, keep, received, own, *rest):
    *sends, total = rest
    total[...] = keep[...] + received[...].astype(F32)
    hand_out(scalars[at_place], total, own, sends)


def sum_kernel(scalars, own, *rest):
    total = own[...]
    for other in rest[:-1]:
        total += other[...].astype(F32)
    rest[-1][...] = total.astype(rest[-1].dtype)


def chunks_of(rows, cols, masks):
    rows //= len(masks)
    return [(aval(rows, cols, F32), True)] + [(aval(rows, cols, BF16), True)] * (len(masks) - 1)


def pair_sum(keep, send, scalars, at_place, masks):
    received = permute(send, 1)
    return kernel_call(
        functools.partial(pair_sum_kernel, at_place),
        chunks_of(*keep.shape, masks),
        scalars,
        [keep, received],
        scratch=[pltpu.VMEM(keep.shape, F32)],
    )


def reduce_chunks(chunks, masks, scalars):
    own, *sends = chunks
    arrived = [permute(value, mask) for value, mask in zip(sends, masks[1:])]
    return kernel_call(
        sum_kernel, [(aval(*own.shape, BF16), True)], scalars, [own, *arrived]
    )[0]


def core_split_kernel(count, scalars, chunks, keep, send, total):
    rows = total.shape[0]
    value = chunks[:rows, :].astype(F32)
    for i in range(1, count):
        value += chunks[i * rows : (i + 1) * rows, :].astype(F32)
    total[...] = value
    rows = keep.shape[0]
    keep[...] = total[pl.ds(pl.multiple_of(scalars[0] * rows, 8), rows), :]
    send[...] = total[pl.ds(pl.multiple_of((1 - scalars[0]) * rows, 8), rows), :]


def start_loads(scalars, at_order, size, pieces, ready, lanes, sems, first):
    copies = []
    for piece in pieces:
        for row in range(0, piece.shape[0], size):
            i = len(copies)
            at = pl.multiple_of(scalars[at_order + i] * size, size)
            target = ready.at[pl.ds(at, size), lanes]
            copies.append(
                pltpu.make_async_copy(piece.at[pl.ds(row, size), :], target, sems.at[first + i])
            )
    for copy in copies:
        copy.start()
    return copies


def subtract_updates(scalars, plan, update, ready, lanes):
    unit, places, block, at_table = plan[:4]
    for i, (index, row) in enumerate(places):
        at = pl.ds(pl.multiple_of(scalars[at_table + index] * block + row, unit), unit)
        value = update[i * unit : (i + 1) * unit, :].astype(F32)
        ready[at, lanes] = (ready[at, lanes].astype(F32) - value).astype(BF16)


def whole_kernel(plan, scalars, mine, other, inverse, panel, *refs):
    at_order, size, n_pieces, n_next = plan[4:]
    pieces, refs = refs[: 2 * n_pieces], refs[2 * n_pieces :]
    nexts, (solved, keep, send) = refs[:n_next], refs[n_next : n_next + 3]
    ready, x_ref, load_sems, sem, sems = refs[-5:]
    core, half = scalars[0], keep.shape[1]
    lanes = [pl.ds(pl.multiple_of(c * half, half), half) for c in (core, 1 - core)]
    runs = load_sems.shape[0] // 2
    arriving = []
    for i in range(2):
        part = pieces[i * n_pieces : (i + 1) * n_pieces]
        arriving += start_loads(
            scalars, at_order + i * runs, size, part, ready, lanes[i], load_sems, i * runs
        )
    for copy in arriving:
        copy.wait()
    copies = start_all(nexts, refs[n_next + 3 : -5], sems)
    subtract_updates(scalars, plan, mine, ready, lanes[0])
    subtract_updates(scalars, plan, other, ready, lanes[1])

    def step(at):
        x_ref[at, :] = dot(inverse[at, :], ready[...]).astype(BF16)

    tiles(inverse.shape[0], step)
    result = pltpu.make_async_copy(x_ref, solved, sem)
    result.start()
    split_panel(core, panel, x_ref, keep, send)
    for copy in [*copies, result]:
        copy.wait()


def half_kernel(plan, turned, at_place, n_chunks, scalars, mine, inverse_a, inverse_b, panel_a, panel_b, *refs):
    at_order, size, n_pieces, n_next = plan[4:]
    pieces, refs = refs[:n_pieces], refs[n_pieces:]
    nexts, refs = refs[:n_next], refs[n_next:]
    chunks, (x_keep, x_send) = refs[:n_chunks], refs[n_chunks : n_chunks + 2]
    ready, update, load_sems, sems = refs[-4:]
    lanes = pl.ds(0, mine.shape[1])
    arriving = start_loads(scalars, at_order, size, pieces, ready, lanes, load_sems, 0)
    for copy in arriving:
        copy.wait()
    copies = start_all(nexts, refs[n_chunks + 2 : -4], sems)
    subtract_updates(scalars, plan, mine, ready, lanes)

    def step(at):
        x_keep[at, :] = dot(inverse_a[at, :], ready[...]).astype(BF16)
        x_send[at, :] = dot(inverse_b[at, :], ready[...]).astype(BF16)

    tiles(inverse_a.shape[0], step)

    def panel_step(at):
        if turned:
            dims = (((0,), (0,)), ((), ()))
            part = lax.dot_general(panel_a[:, at], x_keep[...], dims, preferred_element_type=F32)
            part += lax.dot_general(panel_b[:, at], x_send[...], dims, preferred_element_type=F32)
        else:
            part = dot(panel_a[at, :], x_keep[...]) + dot(panel_b[at, :], x_send[...])
        update[at, :] = part.astype(update.dtype)

    tiles(update.shape[0], panel_step)
    if n_chunks > 1:
        hand_out(scalars[at_place], update, chunks[0], chunks[1:])
    else:
        chunks[0][...] = update[...].astype(BF16)
    for copy in copies:
        copy.wait()


def in_vmem(arrays):
    return [(aval(*v.shape, BF16), True) for v in arrays]


def solve_whole(scalars, plan, mine, other, inverse, panel, pieces, nexts):
    (rows, depth), half = inverse.shape, mine.shape[1]
    outs = [(aval(rows, 2 * half, BF16), False)]
    outs += [(aval(panel.shape[0], half, t), True) for t in (F32, BF16)]
    return kernel_call(
        functools.partial(whole_kernel, plan),
        outs + in_vmem(nexts),
        scalars,
        [mine, other, inverse, panel],
        [*pieces, *nexts],
        [
            pltpu.VMEM((depth, 2 * half), BF16),
            pltpu.VMEM((rows, 2 * half), BF16),
            pltpu.SemaphoreType.DMA((2 * depth // plan[5],)),
            pltpu.SemaphoreType.DMA,
            pltpu.SemaphoreType.DMA((max(1, len(nexts)),)),
        ],
        limit=14,
    )


def solve_half(scalars, plan, mine, inverses, panels, pieces, nexts, update_rows, at_place, masks):
    (rows, depth), half = inverses[0].shape, mine.shape[1]
    chunks = chunks_of(update_rows, half, masks) if masks else [(aval(update_rows, half, BF16), True)]
    outs = chunks + [(aval(rows, half, BF16), True)] * 2
    turned = panels[0].shape[0] != update_rows
    return kernel_call(
        functools.partial(half_kernel, plan, turned, at_place, len(chunks)),
        outs + in_vmem(nexts),
        scalars,
        [mine, *inverses, *panels],
        [*pieces, *nexts],
        [
            pltpu.VMEM((depth, half), BF16),
            pltpu.VMEM((update_rows, half), F32),
            pltpu.SemaphoreType.DMA((depth // plan[5],)),
            pltpu.SemaphoreType.DMA((max(1, len(nexts)),)),
        ],
        limit=12,
    )


def per_device(
    loads_first,
    loads_second,
    loads_third,
    loads_fourth,
    inverse_first,
    inverse_second,
    inverse_third,
    inverse_fourth,
    panel_first,
    panel_second,
    panel_third,
    panel_fourth,
    blocks_first,
    blocks_second,
    blocks_third,
):
    n_y, n_rows = lax.axis_size("y"), 2 * lax.axis_size("y")
    core, x_index, y_index = (lax.axis_index(a) for a in ("core", "x", "y"))
    z1, z2 = lax.axis_index("z1"), lax.axis_index("z2")
    row_index = y_index * 2 + core
    z_index = z2 * 2 + z1
    leaf = (lax.axis_index("hi") * 4 + z_index) * 2 + x_index
    mask_x, mask_z1, mask_z2 = n_rows, 2 * n_rows, 4 * n_rows
    y_masks = [2 * y for y in range(1, n_y)]
    plane_masks = [(x, y) for y in range(n_y) for x in range(2)]
    update_rows, width = panel_first.shape[0], blocks_first.shape[1]
    block = update_rows // width
    rows, depth = inverse_first.shape[0], loads_first.shape[0]
    cols = loads_first.shape[1]
    half = cols // 2

    values = [core, row_index, row_index ^ 1]
    for mask in y_masks:
        values += [row_index ^ mask, row_index ^ mask ^ 1]
    at_place = len(values)
    values += [y_index, x_index * n_y + y_index]
    column = [0, *y_masks]
    plane = [x * mask_x + y * 2 for x in range(2) for y in range(n_y)]
    at_order = []
    for planes in ([0], [z1, z1 ^ 1], [z_index, z_index ^ 2, z_index ^ 1, z_index ^ 3]):
        at_order.append(len(values))
        for x, y in plane_masks:
            place = ((x_index ^ x) * n_y + (y_index ^ y)) * 2
            for z in planes:
                values += [z * 2 * n_rows + place + (core ^ other) for other in range(2)]
        if len(planes) == 1:
            for x, y in plane_masks:
                place = ((x_index ^ x) * n_y + (y_index ^ y)) * 2
                values += [place + (core ^ other) for other in (1, 0)]
    at_table = [len(values) + 2 * width * i for i in range(3)]
    children = [(leaf >> 1) * 2, (leaf >> 1) * 2 + 1]
    parts = [jnp.stack([jnp.asarray(v, jnp.int32) for v in values])]
    for table, pair in (
        (blocks_first, children),
        (blocks_second, [leaf >> 1, (leaf >> 1) ^ 1]),
        (blocks_third, [leaf >> 2, (leaf >> 2) ^ 1]),
    ):
        parts += [lax.dynamic_index_in_dim(table, c, 0, keepdims=False) for c in pair]
    scalars = jnp.concatenate(parts)
    scalars, loads_second, loads_third, loads_fourth = lax.optimization_barrier(
        (scalars, loads_second, loads_third, loads_fourth)
    )

    tie = lax.optimization_barrier

    n_far = 2 * len(y_masks)
    sibling = permute(loads_first, 1)
    shards = [permute(loads_first, mask, upward=True) for mask in y_masks]
    loads = [loads_second, loads_third, loads_fourth]
    sizes = [v.shape[0] for v in loads]
    keep, send = kernel_call(
        split_kernel,
        [(aval(sum(sizes), half, BF16), True)] * 2,
        scalars,
        [],
        loads,
        [pltpu.VMEM((sum(sizes), cols), BF16), pltpu.SemaphoreType.DMA((len(loads),))],
    )
    received = permute(send, 1)
    keep, received, sibling, inverse_third, panel_third = tie(
        (keep, received, sibling, inverse_third, panel_third)
    )
    inverses = inverse_third, permute(inverse_third, 1)
    panels = panel_third, permute(panel_third, 1)
    acc, far, panel = kernel_call(
        near_kernel,
        [
            (aval(rows, cols, F32), True),
            (aval(rows, n_far * depth, BF16), True),
            (aval(*panel_first.shape, BF16), True),
        ],
        scalars,
        [loads_first, sibling],
        [inverse_first, panel_first],
        [
            pltpu.VMEM((rows, 2 * depth), BF16),
            pltpu.SemaphoreType.DMA((2 * (rows // row_tile(rows)) + n_far + 1,)),
        ],
        limit=16,
    )
    runs = [(sum(sizes[:i]), n) for i, n in enumerate(sizes)]
    groups = [[run] for run in runs]
    own_second, half_third, half_fourth = kernel_call(
        functools.partial(pack_kernel, groups),
        [(aval(2 * sum(n for _, n in group), half, BF16), True) for group in groups],
        scalars,
        [keep, received],
    )
    x_second = permute(own_second, mask_x)
    by_z2 = permute(half_fourth, mask_z2)
    acc, by_z2 = tie((acc, by_z2))
    half_later = jnp.concatenate([half_third, half_fourth, by_z2], 0)
    by_z1 = permute(half_later, mask_z1)
    shards, acc, far, panel, own_second, x_second, inverses, panels = tie(
        (shards, acc, far, panel, own_second, x_second, inverses, panels)
    )

    pieces = [v for shard in shards for v in (shard, permute(shard, 1))]
    y_second = [permute(own_second, mask) for mask in y_masks]
    nexts = [inverse_second, panel_second]
    solved_first, keep, send, inverse_second, panel_second = kernel_call(
        functools.partial(far_kernel, n_far, len(nexts)),
        [
            (aval(rows, cols, BF16), False),
            (aval(update_rows, half, F32), True),
            (aval(update_rows, half, BF16), True),
        ]
        + in_vmem(nexts),
        scalars,
        [acc, panel, far, *pieces],
        nexts,
        [
            pltpu.VMEM((rows, cols), BF16),
            pltpu.SemaphoreType.DMA,
            pltpu.SemaphoreType.DMA((len(nexts),)),
        ],
    )
    keep, send, y_second, by_z1 = tie((keep, send, y_second, by_z1))
    chunks = pair_sum(keep, send, scalars, at_place, column)

    def with_x(x_piece, own, y_pieces):
        pieces = [own, x_piece]
        for piece in y_pieces:
            pieces += [piece, permute(piece, mask_x)]
        return pieces

    pieces_second = with_x(x_second, own_second, y_second)
    early = [own_second, x_second, *y_second]
    across_early = [permute(piece, 1) for piece in early]
    cut = 2 * sizes[1]
    own_third = jnp.concatenate([half_later[:cut], by_z1[:cut]], 0)
    own_fourth = jnp.concatenate([half_later[cut:], by_z1[cut:]], 0)
    part = reduce_chunks(chunks, column, scalars)
    part, pieces_second, across_early, own_third, own_fourth = tie(
        (part, pieces_second, across_early, own_third, own_fourth)
    )

    def spread(value):
        return lax.all_gather(value, PLANE, axis=0, tiled=True)

    def plan_of(level, chunk, both):
        unit = math.gcd(chunk, block)
        places = []
        for place in range(2 * n_y):
            for child in range(2) if both else [place // n_y]:
                start = (place if both else place % n_y) * chunk
                for row in range(start, start + chunk, unit):
                    places.append((child * width + row // block, row % block))
        n_next = 4 if level < 2 else 0
        return unit, places, block, at_table[level], at_order[level], sizes[level], n_pieces, n_next

    n_pieces = len(plane_masks)

    across = across_early[:2]
    for i in range(len(y_masks)):
        across += [across_early[2 + i], permute(pieces_second[3 + 2 * i], 1)]
    pieces_second += across
    mine = spread(part)
    other = permute(mine, 1)
    mine, other, pieces_second, own_third, own_fourth = tie(
        (mine, other, pieces_second, own_third, own_fourth)
    )
    x_third = permute(own_third, mask_x)
    y_third = [permute(own_third, mask) for mask in y_masks]
    solved_second, keep, send, *nexts = solve_whole(
        scalars,
        plan_of(0, part.shape[0], False),
        mine,
        other,
        inverse_second,
        panel_second,
        pieces_second,
        [*inverses, *panels],
    )
    keep, send, x_third, y_third = tie((keep, send, x_third, y_third))

    chunks = pair_sum(keep, send, scalars, at_place + 1, plane)
    chunks, y_third, inverse_fourth, panel_fourth = tie(
        (chunks, y_third, inverse_fourth, panel_fourth)
    )
    part = reduce_chunks(chunks, plane, scalars)
    part, y_third = tie((part, y_third))
    sibling = permute(part, mask_z1)
    pieces_third = with_x(x_third, own_third, y_third)
    panel_fourth = panel_fourth.T
    fourth = [
        inverse_fourth, permute(inverse_fourth, 1), panel_fourth, permute(panel_fourth, 1),
    ]
    part, sibling, pieces_third, fourth = tie((part, sibling, pieces_third, fourth))
    mine = spread(jnp.concatenate([part, sibling], 0))
    mine, own_fourth = tie((mine, own_fourth))
    x_fourth = permute(own_fourth, mask_x)
    y_fourth = [permute(own_fourth, mask) for mask in y_masks]
    *chunks, keep, send, a, b, c, d = solve_half(
        scalars,
        plan_of(1, part.shape[0], True),
        mine,
        nexts[:2],
        nexts[2:],
        pieces_third,
        fourth,
        update_rows,
        at_place + 1,
        plane,
    )
    fourth = [a, b, c, d]
    chunks, keep, send, x_fourth, y_fourth = tie((chunks, keep, send, x_fourth, y_fourth))

    part = reduce_chunks(chunks, plane, scalars)
    part, keep, send, x_fourth, y_fourth = tie((part, keep, send, x_fourth, y_fourth))
    pieces_fourth = with_x(x_fourth, own_fourth, y_fourth)
    solved_third = join_columns(scalars, keep, permute(send, 1))
    part = (part.astype(F32) + permute(part, mask_z1).astype(F32)).astype(BF16)
    sibling = permute(part, mask_z2)
    part, sibling, pieces_fourth, solved_third = tie((part, sibling, pieces_fourth, solved_third))
    mine = spread(jnp.concatenate([part, sibling], 0))
    update, keep_fourth, send_fourth = solve_half(
        scalars,
        plan_of(2, part.shape[0], True),
        mine,
        fourth[:2],
        fourth[2:],
        pieces_fourth,
        [],
        update_rows,
        0,
        [],
    )
    solved_fourth = join_columns(scalars, keep_fourth, permute(send_fourth, 1))
    everywhere = ("z2", "z1", "x", "y")
    count = lax.axis_size(everywhere)
    arrived = lax.all_to_all(update, everywhere, 0, 0, tiled=True)
    chunk = update_rows // count
    keep, send = kernel_call(
        functools.partial(core_split_kernel, count),
        [(aval(chunk // 2, half, F32), True)] * 2,
        scalars,
        [arrived],
        scratch=[pltpu.VMEM((chunk, half), F32)],
    )
    ancestor = join_columns(scalars, keep, permute(send, 1))
    return solved_first, solved_second, solved_third, solved_fourth, ancestor


def solution(mesh):
    n_leaf, n_rows = mesh.shape["leaf"], mesh.shape["rows"]
    fine = Mesh(mesh.devices.reshape(n_leaf // 8, 2, 2, 2, n_rows // 2, 2), AXES)
    rows, cols = P(AXES, None), P(None, AXES)
    return jax.shard_map(
        per_device,
        mesh=fine,
        in_specs=(rows,) * 8 + (cols,) * 4 + (P(),) * 3,
        out_specs=(rows,) * 5,
        check_vma=False,
    )
```

time: 206 us -> 183 us (0.89)
  Pallas kernels: 49.5 us -> 42.8 us
  local copies, waits for them, and re-layouts: 7.13 us -> 1.83 us
  blocking collectives: 42.5 us -> 37.5 us
  waiting for transfers between devices: 61 us -> 57.1 us
  other arithmetic: 3.01 us -> 0.14 us
    all_to_all x3 -> x1, waiting for transfers between devices: 19.7 us -> 9.55 us  [per_device(): arrived = lax.all_to_all(update, everywhere, 0, 0, tiled=True)]
    all_to_all x1 -> x0, blocking collectives: 9.79 us -> none  [reduce_over(): arrived = lax.all_to_all(value, axes, 0, 0, tiled=True)]
    ppermute x33 -> x39, starting transfers between devices: 30.1 us -> 37.6 us  [permute(): return lax.ppermute(value, AXES, pairs)]
    pallas_call x14 -> x16, Pallas kernels: 49.5 us -> 42.8 us  [kernel_call(): pl.pallas_call(kernel, out_shape=[pltpu.VMEM(o.shape, o.dtype) if inside...]
    ppermute x33 -> x39, waiting for transfers between devices: 41.3 us -> 47.5 us  [permute(): return lax.ppermute(value, AXES, pairs)]
    all_to_all x3 -> x1, starting transfers between devices: 10.4 us -> 4.7 us  [per_device(): arrived = lax.all_to_all(update, everywhere, 0, 0, tiled=True)]
    unnamed x39 -> x46, local copies, waits for them, and re-layouts: 5.4 us -> 0.1 us
    all_gather x3, blocking collectives: 32.7 us -> 37.5 us  [spread(): return lax.all_gather(value, PLANE, axis=0, tiled=True)]
  transfers between devices with their start and end apart: 36 -> 40, of which waited for: 19 -> 23; matrix products, arithmetic and copies ran while one was open for 1% -> 1% of each run, Pallas kernels for 16% -> 19%
where the time goes in v4:
time: 183 us
  waiting for transfers between devices  57.1 us (31%)
  Pallas kernels  42.8 us (23%)
  starting transfers between devices  42.3 us (23%)
  blocking collectives  37.5 us (20%)
  local copies, waits for them, and re-layouts  1.83 us (1%)
    ppermute x39, waiting for transfers between devices, permute(): return lax.ppermute(value, AXES, pairs)  47.5 us
    pallas_call x16, Pallas kernels, kernel_call(): pl.pallas_call(kernel, out_shape=[pltpu.VMEM(o.shape, o.dtype) if inside...  42.8 us
    ppermute x39, starting transfers between devices, permute(): return lax.ppermute(value, AXES, pairs)  37.6 us
    all_gather x3, blocking collectives, spread(): return lax.all_gather(value, PLANE, axis=0, tiled=True)  37.5 us
    all_to_all x1, waiting for transfers between devices, per_device(): arrived = lax.all_to_all(update, everywhere, 0, 0, tiled=True)  9.55 us
    all_to_all x1, starting transfers between devices, per_device(): arrived = lax.all_to_all(update, everywhere, 0, 0, tiled=True)  4.7 us
  transfers between devices with their start and end apart: 40, of which 23 were waited for; matrix products, arithmetic and copies ran while one was open for 1% of the time, Pallas kernels for 19%

profile of v4, /device:TPU:0, one launch (start us, length us, event | category | flops | bytes accessed | tf_op | source)
XLA Modules:
  0.0 182.8 jit_solution(16186199637650460470)
XLA Ops:
  2.9 1.8 shard_map.182
  6.9 4.6 %collective-permute-start = (bf16[1536,256]{1,0:T(8,128)(2,1)}, bf16[1536,256]{1,0:T(8,128)(2,1)S(1)}, u32[]{:S(2)}, u32[]{:S(2)}) collective-permute-start(bf16[1536,256]{1,0:T(8,128)(2,1)} %b0.1), channel_id=1, source_target_pairs={{0,2},{1,3},{4,6},{5,7},{8,10},{9,11},{12,14},{13,15},{16,18},{17,... | collective-permute-start | bytes 2359304 | tf_op jit(solution)/shard_map/ppermute | solution.py:25
  13.7 2.6 %collective-permute-start.3 = (bf16[384,128]{1,0:T(8,128)(2,1)S(1)}, bf16[384,128]{1,0:T(8,128)(2,1)S(1)}, u32[]{:S(2)}, u32[]{:S(2)}) collective-permute-start(bf16[384,128]{1,0:T(8,128)(2,1)S(1)} %get-tuple-element.148), channel_id=1, source_target_pairs={{0,16},{1,17},{2,18},{3,19},{4,20},{5,21},{6,22},{7,23},{8,24},{9,... | collective-permute-start | bytes 294920 | tf_op jit(solution)/shard_map/ppermute | solution.py:25
  16.3 8.5 %shard_map.183 = (f32[1536,256]{1,0:T(8,128)S(1)}, bf16[1536,3072]{1,0:T(8,128)(2,1)S(1)}, bf16[1536,1536]{1,0:T(8,128)(2,1)S(1)}) custom-call(s32[143]{0:T(256)S(1)} %concatenate.20.scalars, bf16[1536,256]{1,0:T(8,128)(2,1)S(1)} %copy-done, bf16[1536,256]{1,0:T(8,128)(2,1)S(1)} %collective-permute-done.2.b1, bf16[1536,6144]{1,0:T(8,128)(2,1)} %inverse.1, ...), custom_call_target="tpu_custom_call" | custom-call | flops 1 | bytes 1 | tf_op jit(solution)/shard_map/pallas_call | solution.py:38
  24.8 4.3 %collective-permute-done.refs_0_ = bf16[1536,256]{1,0:T(8,128)(2,1)S(1)} collective-permute-done((bf16[1536,256]{1,0:T(8,128)(2,1)}, bf16[1536,256]{1,0:T(8,128)(2,1)S(1)}, u32[]{:S(2)}, u32[]{:S(2)}) %collective-permute-start) | collective-permute-done | bytes 786464 | tf_op jit(solution)/shard_map/ppermute | solution.py:25
  30.9 2.4 %collective-permute-start.8 = (bf16[1536,128]{1,0:T(8,128)(2,1)S(1)}, bf16[1536,128]{1,0:T(8,128)(2,1)S(1)}, u32[]{:S(2)}, u32[]{:S(2)}) collective-permute-start(bf16[1536,128]{1,0:T(8,128)(2,1)S(1)} %get-tuple-element.186.refs_0_), channel_id=1, source_target_pairs={{0,2},{1,3},{2,0},{3,1},{4,6},{5,7},{6,4},{7,5},{8,10},{9,11},{10,... | collective-permute-start | bytes 1179656 | tf_op jit(solution)/shard_map/ppermute | solution.py:25
  33.8 5.2 %shard_map.185 = (bf16[1536,256]{1,0:T(8,128)(2,1)}, f32[1536,128]{1,0:T(8,128)S(1)}, bf16[1536,128]{1,0:T(8,128)(2,1)S(1)}, bf16[768,6144]{1,0:T(8,128)(2,1)S(1)}, bf16[1536,768]{1,0:T(8,128)(2,1)S(1)}) custom-call(s32[143]{0:T(256)S(1)} %concatenate.20.scalars, f32[1536,256]{1,0:T(8,128)S(1)} %get-tuple-element.155.acc, ...), custom_call_target="tpu_custom_call" | custom-call | flops 1 | bytes 1 | tf_op jit(solution)/shard_map/pallas_call | solution.py:38
  39.1 1.8 collective-permute-done.9
  40.8 1.9 %collective-permute-done.8.refs_2_ = bf16[1536,128]{1,0:T(8,128)(2,1)S(1)} collective-permute-done((bf16[1536,128]{1,0:T(8,128)(2,1)S(1)}, bf16[1536,128]{1,0:T(8,128)(2,1)S(1)}, u32[]{:S(2)}, u32[]{:S(2)}) %collective-permute-start.8) | collective-permute-done | bytes 393248 | tf_op jit(solution)/shard_map/ppermute | solution.py:25
  47.2 1.8 collective-permute-start.11
  49.1 5.2 %collective-permute-done.11.rest_0_ = bf16[768,128]{1,0:T(8,128)(2,1)S(1)} collective-permute-done((bf16[768,128]{1,0:T(8,128)(2,1)S(1)}, bf16[768,128]{1,0:T(8,128)(2,1)S(1)}, u32[]{:S(2)}, u32[]{:S(2)}) %collective-permute-start.11) | collective-permute-done | bytes 196640 | tf_op jit(solution)/shard_map/ppermute | solution.py:25
  54.9 11.8 %all_gather.9.mine = bf16[3072,128]{1,0:T(8,128)(2,1)S(1)} all-gather(bf16[768,128]{1,0:T(8,128)(2,1)S(1)} %shard_map.187), channel_id=1, replica_groups=mesh['hi'=1,'z2'=2,'z1'=2,'x'=2,'y'=2,'core'=2] {'x','y'}, dimensions={0}, use_global_device_ids=true | all-gather | bytes 983040 | tf_op jit(solution)/shard_map/all_gather | solution.py:518
  67.3 2.3 %collective-permute-done.17.refs_7_ = bf16[1536,128]{1,0:T(8,128)(2,1)S(1)} collective-permute-done((bf16[1536,128]{1,0:T(8,128)(2,1)S(1)}, bf16[1536,128]{1,0:T(8,128)(2,1)S(1)}, u32[]{:S(2)}, u32[]{:S(2)}) %collective-permute-start.17) | collective-permute-done | bytes 393248 | tf_op jit(solution)/shard_map/ppermute | solution.py:25
  69.7 2.0 %collective-permute-start.19 = (bf16[1536,128]{1,0:T(8,128)(2,1)S(1)}, bf16[1536,128]{1,0:T(8,128)(2,1)S(1)}, u32[]{:S(2)}, u32[]{:S(2)}) collective-permute-start(bf16[1536,128]{1,0:T(8,128)(2,1)S(1)} %pad_maximum_fusion.refs_0_), channel_id=1, source_target_pairs={{0,2},{1,3},{2,0},{3,1},{4,6},{5,7},{6,4},{7,5},{8,10},{9,11},{10,... | collective-permute-start | bytes 1179656 | tf_op jit(solution)/shard_map/ppermute | solution.py:25
  71.8 7.5 %shard_map.188 = (bf16[768,256]{1,0:T(8,128)(2,1)}, f32[1536,128]{1,0:T(8,128)S(1)}, bf16[1536,128]{1,0:T(8,128)(2,1)S(1)}, bf16[384,6144]{1,0:T(8,128)(2,1)S(1)...) custom-call(s32[143]{0:T(256)S(1)} %concatenate.20.scalars, ...), custom_call_target="tpu_custom_call" | custom-call | flops 1 | bytes 1 | tf_op jit(solution)/shard_map/pallas_call | solution.py:38
  80.9 1.7 collective-permute-done.20.received
  88.7 2.4 %collective-permute-done.22.rest_1_ = bf16[384,128]{1,0:T(8,128)(2,1)S(1)} collective-permute-done((bf16[384,128]{1,0:T(8,128)(2,1)S(1)}, bf16[384,128]{1,0:T(8,128)(2,1)S(1)}, u32[]{:S(2)}, u32[]{:S(2)}) %collective-permute-start.22) | collective-permute-done | bytes 98336 | tf_op jit(solution)/shard_map/ppermute | solution.py:25
  92.7 1.7 collective-permute-start.25
  94.9 4.2 %collective-permute-done.24 = bf16[384,128]{1,0:T(8,128)(2,1)S(1)} collective-permute-done((bf16[384,128]{1,0:T(8,128)(2,1)S(1)}, bf16[384,128]{1,0:T(8,128)(2,1)S(1)}, u32[]{:S(2)}, u32[]{:S(2)}) %collective-permute-start.24) | collective-permute-done | bytes 98336 | tf_op jit(solution)/shard_map/ppermute | solution.py:25
  99.1 3.8 %collective-permute-done.25.refs_3_ = bf16[1536,128]{1,0:T(8,128)(2,1)S(1)} collective-permute-done((bf16[1536,128]{1,0:T(8,128)(2,1)S(1)}, bf16[1536,128]{1,0:T(8,128)(2,1)S(1)}, u32[]{:S(2)}, u32[]{:S(2)}) %collective-permute-start.25) | collective-permute-done | bytes 393248 | tf_op jit(solution)/shard_map/ppermute | solution.py:25
  103.0 14.3 %all_gather.10.mine = bf16[3072,128]{1,0:T(8,128)(2,1)S(1)} all-gather(bf16[768,128]{1,0:T(8,128)(2,1)S(1)} %pad_maximum_fusion.3), channel_id=1, replica_groups=mesh['hi'=1,'z2'=2,'z1'=2,'x'=2,'y'=2,'core'=2] {'x','y'}, dimensions={0}, use_global_device_ids=true | all-gather | bytes 983040 | tf_op jit(solution)/shard_map/all_gather | solution.py:518
  117.2 2.0 %collective-permute-start.29 = (bf16[1536,128]{1,0:T(8,128)(2,1)S(1)}, bf16[1536,128]{1,0:T(8,128)(2,1)S(1)}, u32[]{:S(2)}, u32[]{:S(2)}) collective-permute-start(bf16[1536,128]{1,0:T(8,128)(2,1)S(1)} %pad_maximum_fusion.2.refs_0_), channel_id=1, source_target_pairs={{0,2},{1,3},{2,0},{3,1},{4,6},{5,7},{6,4},{7,5},{8,10},{9,11},{10,... | collective-permute-start | bytes 1179656 | tf_op jit(solution)/shard_map/ppermute | solution.py:25
  119.3 6.1 %shard_map.191 = (f32[384,128]{1,0:T(8,128)S(1)}, bf16[384,128]{1,0:T(8,128)(2,1)S(1)}, bf16[384,128]{1,0:T(8,128)(2,1)S(1)}, bf16[384,128]{1,0:T(8,128)(2,1)S(1...) custom-call(s32[143]{0:T(256)S(1)} %concatenate.20.scalars, ...), custom_call_target="tpu_custom_call" | custom-call | flops 1 | bytes 1 | tf_op jit(solution)/shard_map/pallas_call | solution.py:38
  131.8 2.7 %collective-permute-done.31.rest_1_ = bf16[384,128]{1,0:T(8,128)(2,1)S(1)} collective-permute-done((bf16[384,128]{1,0:T(8,128)(2,1)S(1)}, bf16[384,128]{1,0:T(8,128)(2,1)S(1)}, u32[]{:S(2)}, u32[]{:S(2)}) %collective-permute-start.31) | collective-permute-done | bytes 98336 | tf_op jit(solution)/shard_map/ppermute | solution.py:25
  134.4 2.0 %collective-permute-done.32.rest_2_ = bf16[384,128]{1,0:T(8,128)(2,1)S(1)} collective-permute-done((bf16[384,128]{1,0:T(8,128)(2,1)S(1)}, bf16[384,128]{1,0:T(8,128)(2,1)S(1)}, u32[]{:S(2)}, u32[]{:S(2)}) %collective-permute-start.32) | collective-permute-done | bytes 98336 | tf_op jit(solution)/shard_map/ppermute | solution.py:25
  139.1 2.7 %collective-permute-done.33 = bf16[384,128]{1,0:T(8,128)(2,1)S(1)} collective-permute-done((bf16[384,128]{1,0:T(8,128)(2,1)S(1)}, bf16[384,128]{1,0:T(8,128)(2,1)S(1)}, u32[]{:S(2)}, u32[]{:S(2)}) %collective-permute-start.33) | collective-permute-done | bytes 98336 | tf_op jit(solution)/shard_map/ppermute | solution.py:25
  141.8 2.7 %collective-permute-start.34 = (bf16[384,128]{1,0:T(8,128)(2,1)S(1)}, bf16[384,128]{1,0:T(8,128)(2,1)S(1)}, u32[]{:S(2)}, u32[]{:S(2)}) collective-permute-start(bf16[384,128]{1,0:T(8,128)(2,1)S(1)} %add_convert_fusion), channel_id=1, source_target_pairs={{0,16},{1,17},{2,18},{3,19},{4,20},{5,21},{6,22},{7,23},{8,24},{9,... | collective-permute-start | bytes 294920 | tf_op jit(solution)/shard_map/ppermute | solution.py:25
  145.7 2.5 %collective-permute-done.34 = bf16[384,128]{1,0:T(8,128)(2,1)S(1)} collective-permute-done((bf16[384,128]{1,0:T(8,128)(2,1)S(1)}, bf16[384,128]{1,0:T(8,128)(2,1)S(1)}, u32[]{:S(2)}, u32[]{:S(2)}) %collective-permute-start.34) | collective-permute-done | bytes 98336 | tf_op jit(solution)/shard_map/ppermute | solution.py:25
  148.2 11.4 %all_gather.11.mine = bf16[3072,128]{1,0:T(8,128)(2,1)S(1)} all-gather(bf16[768,128]{1,0:T(8,128)(2,1)S(1)} %pad_maximum_fusion.4), channel_id=1, replica_groups=mesh['hi'=1,'z2'=2,'z1'=2,'x'=2,'y'=2,'core'=2] {'x','y'}, dimensions={0}, use_global_device_ids=true | all-gather | bytes 983040 | tf_op jit(solution)/shard_map/all_gather | solution.py:518
  159.7 5.7 %shard_map.194 = (bf16[1536,128]{1,0:T(8,128)(2,1)}, bf16[192,128]{1,0:T(8,128)(2,1)S(1)}, bf16[192,128]{1,0:T(8,128)(2,1)S(1)}) custom-call(s32[143]{0:T(256)S(1)} %concatenate.20.scalars, bf16[3072,128]{1,0:T(8,128)(2,1)S(1)} %all_gather.11.mine, bf16[192,6144]{1,0:T(8,128)(2,1)S(1)} %get-tuple-element.258.inverse_a, ...), custom_call_target="tpu_custom_call" | custom-call | flops 1 | bytes 1 | tf_op jit(solution)/shard_map/pallas_call | solution.py:38
  165.3 4.7 %all-to-all-start = ((bf16[16,96,128]{2,1,0:T(8,128)(2,1)}), bf16[16,96,128]{2,1,0:T(8,128)(2,1)S(1)}, u32[]{:S(2)}, u32[]{:S(2)}) async-start(bf16[16,96,128]{2,1,0:T(8,128)(2,1)} %bitcast.70), calls=%async_computation | async-start | bytes 786432 | tf_op jit(solution)/shard_map/all_to_all | solution.py:611
  170.1 9.6 %all-to-all-done = bf16[16,96,128]{2,1,0:T(8,128)(2,1)S(1)} async-done(((bf16[16,96,128]{2,1,0:T(8,128)(2,1)}), bf16[16,96,128]{2,1,0:T(8,128)(2,1)S(1)}, u32[]{:S(2)}, u32[]{:S(2)}) %all-to-all-start) | async-done | bytes 393248 | tf_op jit(solution)/shard_map/all_to_all | solution.py:611
  (123 shorter events, 37.8 us)
Async XLA Ops:
  0.6 5.8 %collective-permute-start.2 = (bf16[1536,256]{1,0:T(8,128)(2,1)}, bf16[1536,256]{1,0:T(8,128)(2,1)S(1)}, u32[]{:S(2)}, u32[]{:S(2)}) collective-permute-start(bf16[1536,256]{1,0:T(8,128)(2,1)} %b0.1), channel_id=1, source_target_pairs={{0,1},{1,0},{2,3},{3,2},{4,5},{5,4},{6,7},{7,6},{8,9},{9,8},{10,11... | collective-permute-start | bytes 2359304 | tf_op jit(solution)/shard_map/ppermute | solution.py:25
  6.4 22.7 %collective-permute-start.5 = (bf16[384,6144]{1,0:T(8,128)(2,1)}, bf16[384,6144]{1,0:T(8,128)(2,1)S(1)}, u32[]{:S(2)}, u32[]{:S(2)}) collective-permute-start(bf16[384,6144]{1,0:T(8,128)(2,1)} %refs_8_), channel_id=1, source_target_pairs={{0,1},{1,0},{2,3},{3,2},{4,5},{5,4},{6,7},{7,6},{8,9},{9,8},{10,11... | collective-permute-start | bytes 14155784 | tf_op jit(solution)/shard_map/ppermute | solution.py:25
  6.5 22.6 %collective-permute-start.6 = (bf16[1536,384]{1,0:T(8,128)(2,1)}, bf16[1536,384]{1,0:T(8,128)(2,1)S(1)}, u32[]{:S(2)}, u32[]{:S(2)}) collective-permute-start(bf16[1536,384]{1,0:T(8,128)(2,1)} %refs_10_), channel_id=1, source_target_pairs={{0,1},{1,0},{2,3},{3,2},{4,5},{5,4},{6,7},{7,6},{8,9},{9,8},{10,11... | collective-permute-start | bytes 3538952 | tf_op jit(solution)/shard_map/ppermute | solution.py:25
  6.9 22.2 %collective-permute-start = (bf16[1536,256]{1,0:T(8,128)(2,1)}, bf16[1536,256]{1,0:T(8,128)(2,1)S(1)}, u32[]{:S(2)}, u32[]{:S(2)}) collective-permute-start(bf16[1536,256]{1,0:T(8,128)(2,1)} %b0.1), channel_id=1, source_target_pairs={{0,2},{1,3},{4,6},{5,7},{8,10},{9,11},{12,14},{13,15},{16,18},{17,... | collective-permute-start | bytes 2359304 | tf_op jit(solution)/shard_map/ppermute | solution.py:25
  12.1 17.0 %collective-permute-start.4 = (bf16[1536,128]{1,0:T(8,128)(2,1)S(1)}, bf16[1536,128]{1,0:T(8,128)(2,1)S(1)}, u32[]{:S(2)}, u32[]{:S(2)}) collective-permute-start(bf16[1536,128]{1,0:T(8,128)(2,1)S(1)} %get-tuple-element.186.refs_0_), channel_id=1, source_target_pairs={{0,4},{1,5},{2,6},{3,7},{4,0},{5,1},{6,2},{7,3},{8,12},{9,13},{10,... | collective-permute-start | bytes 1179656 | tf_op jit(solution)/shard_map/ppermute | solution.py:25
  13.7 11.1 %collective-permute-start.3 = (bf16[384,128]{1,0:T(8,128)(2,1)S(1)}, bf16[384,128]{1,0:T(8,128)(2,1)S(1)}, u32[]{:S(2)}, u32[]{:S(2)}) collective-permute-start(bf16[384,128]{1,0:T(8,128)(2,1)S(1)} %get-tuple-element.148), channel_id=1, source_target_pairs={{0,16},{1,17},{2,18},{3,19},{4,20},{5,21},{6,22},{7,23},{8,24},{9,... | collective-permute-start | bytes 294920 | tf_op jit(solution)/shard_map/ppermute | solution.py:25
  29.1 4.7 %collective-permute-start.7 = (bf16[1536,256]{1,0:T(8,128)(2,1)S(1)}, bf16[1536,256]{1,0:T(8,128)(2,1)S(1)}, u32[]{:S(2)}, u32[]{:S(2)}) collective-permute-start(bf16[1536,256]{1,0:T(8,128)(2,1)S(1)} %collective-permute-done.refs_0_), channel_id=1, source_target_pairs={{0,1},{1,0},{2,3},{3,2},{4,5},{5,4},{6,7},{7,6},{8,9},{9,8},{10,11... | collective-permute-start | bytes 2359304 | tf_op jit(solution)/shard_map/ppermute | solution.py:25
  29.2 11.6 %collective-permute-start.9 = (bf16[1536,128]{1,0:T(8,128)(2,1)S(1)}, bf16[1536,128]{1,0:T(8,128)(2,1)S(1)}, u32[]{:S(2)}, u32[]{:S(2)}) collective-permute-start(bf16[1536,128]{1,0:T(8,128)(2,1)S(1)} %fusion), channel_id=1, source_target_pairs={{0,8},{1,9},{2,10},{3,11},{4,12},{5,13},{6,14},{7,15},{8,0},{9,1},... | collective-permute-start | bytes 1179656 | tf_op jit(solution)/shard_map/ppermute | solution.py:25
  30.9 11.9 %collective-permute-start.8 = (bf16[1536,128]{1,0:T(8,128)(2,1)S(1)}, bf16[1536,128]{1,0:T(8,128)(2,1)S(1)}, u32[]{:S(2)}, u32[]{:S(2)}) collective-permute-start(bf16[1536,128]{1,0:T(8,128)(2,1)S(1)} %get-tuple-element.186.refs_0_), channel_id=1, source_target_pairs={{0,2},{1,3},{2,0},{3,1},{4,6},{5,7},{6,4},{7,5},{8,10},{9,11},{10,... | collective-permute-start | bytes 1179656 | tf_op jit(solution)/shard_map/ppermute | solution.py:25
  33.3 21.6 %collective-permute-start.13 = (bf16[1536,128]{1,0:T(8,128)(2,1)S(1)}, bf16[1536,128]{1,0:T(8,128)(2,1)S(1)}, u32[]{:S(2)}, u32[]{:S(2)}) collective-permute-start(bf16[1536,128]{1,0:T(8,128)(2,1)S(1)} %get-tuple-element.186.refs_0_), channel_id=1, source_target_pairs={{0,1},{1,0},{2,3},{3,2},{4,5},{5,4},{6,7},{7,6},{8,9},{9,8},{10,11... | collective-permute-start | bytes 1179656 | tf_op jit(solution)/shard_map/ppermute | solution.py:25
  33.3 21.6 %collective-permute-start.14 = (bf16[1536,128]{1,0:T(8,128)(2,1)S(1)}, bf16[1536,128]{1,0:T(8,128)(2,1)S(1)}, u32[]{:S(2)}, u32[]{:S(2)}) collective-permute-start(bf16[1536,128]{1,0:T(8,128)(2,1)S(1)} %collective-permute-done.4.refs_1_), channel_id=1, source_target_pairs={{0,1},{1,0},{2,3},{3,2},{4,5},{5,4},{6,7},{7,6},{8,9},{9,8},{10,11... | collective-permute-start | bytes 1179656 | tf_op jit(solution)/shard_map/ppermute | solution.py:25
  42.8 12.1 %collective-permute-start.12 = (bf16[1536,128]{1,0:T(8,128)(2,1)S(1)}, bf16[1536,128]{1,0:T(8,128)(2,1)S(1)}, u32[]{:S(2)}, u32[]{:S(2)}) collective-permute-start(bf16[1536,128]{1,0:T(8,128)(2,1)S(1)} %collective-permute-done.8.refs_2_), channel_id=1, source_target_pairs={{0,4},{1,5},{2,6},{3,7},{4,0},{5,1},{6,2},{7,3},{8,12},{9,13},{10,... | collective-permute-start | bytes 1179656 | tf_op jit(solution)/shard_map/ppermute | solution.py:25
  44.3 10.6 %collective-permute-start.15 = (bf16[1536,128]{1,0:T(8,128)(2,1)S(1)}, bf16[1536,128]{1,0:T(8,128)(2,1)S(1)}, u32[]{:S(2)}, u32[]{:S(2)}) collective-permute-start(bf16[1536,128]{1,0:T(8,128)(2,1)S(1)} %collective-permute-done.8.refs_2_), channel_id=1, source_target_pairs={{0,1},{1,0},{2,3},{3,2},{4,5},{5,4},{6,7},{7,6},{8,9},{9,8},{10,11... | collective-permute-start | bytes 1179656 | tf_op jit(solution)/shard_map/ppermute | solution.py:25
  47.2 7.0 %collective-permute-start.11 = (bf16[768,128]{1,0:T(8,128)(2,1)S(1)}, bf16[768,128]{1,0:T(8,128)(2,1)S(1)}, u32[]{:S(2)}, u32[]{:S(2)}) collective-permute-start(bf16[768,128]{1,0:T(8,128)(2,1)S(1)} %get-tuple-element.168), channel_id=1, source_target_pairs={{0,2},{1,3},{2,0},{3,1},{4,6},{5,7},{6,4},{7,5},{8,10},{9,11},{10,... | collective-permute-start | bytes 589832 | tf_op jit(solution)/shard_map/ppermute | solution.py:25
  69.7 11.2 %collective-permute-start.18 = (bf16[1536,128]{1,0:T(8,128)(2,1)S(1)}, bf16[1536,128]{1,0:T(8,128)(2,1)S(1)}, u32[]{:S(2)}, u32[]{:S(2)}) collective-permute-start(bf16[1536,128]{1,0:T(8,128)(2,1)S(1)} %pad_maximum_fusion.refs_0_), channel_id=1, source_target_pairs={{0,4},{1,5},{2,6},{3,7},{4,0},{5,1},{6,2},{7,3},{8,12},{9,13},{10,... | collective-permute-start | bytes 1179656 | tf_op jit(solution)/shard_map/ppermute | solution.py:25
  69.7 11.2 %collective-permute-start.19 = (bf16[1536,128]{1,0:T(8,128)(2,1)S(1)}, bf16[1536,128]{1,0:T(8,128)(2,1)S(1)}, u32[]{:S(2)}, u32[]{:S(2)}) collective-permute-start(bf16[1536,128]{1,0:T(8,128)(2,1)S(1)} %pad_maximum_fusion.refs_0_), channel_id=1, source_target_pairs={{0,2},{1,3},{2,0},{3,1},{4,6},{5,7},{6,4},{7,5},{8,10},{9,11},{10,... | collective-permute-start | bytes 1179656 | tf_op jit(solution)/shard_map/ppermute | solution.py:25
  83.3 19.6 %collective-permute-start.26 = (bf16[192,6144]{1,0:T(8,128)(2,1)S(1)}, bf16[192,6144]{1,0:T(8,128)(2,1)S(1)}, u32[]{:S(2)}, u32[]{:S(2)}) collective-permute-start(bf16[192,6144]{1,0:T(8,128)(2,1)S(1)} %copy-done.3), channel_id=1, source_target_pairs={{0,1},{1,0},{2,3},{3,2},{4,5},{5,4},{6,7},{7,6},{8,9},{9,8},{10,11... | collective-permute-start | bytes 7077896 | tf_op jit(solution)/shard_map/ppermute | solution.py:25
  83.5 19.4 %collective-permute-start.27 = (bf16[192,1536]{1,0:T(8,128)(2,1)S(1)}, bf16[192,1536]{1,0:T(8,128)(2,1)S(1)}, u32[]{:S(2)}, u32[]{:S(2)}) collective-permute-start(bf16[192,1536]{1,0:T(8,128)(2,1)S(1)} %bitcast.80), channel_id=1, source_target_pairs={{0,1},{1,0},{2,3},{3,2},{4,5},{5,4},{6,7},{7,6},{8,9},{9,8},{10,11... | collective-permute-start | bytes 1769480 | tf_op jit(solution)/shard_map/ppermute | solution.py:25
  83.9 4.8 %collective-permute-start.21 = (bf16[384,128]{1,0:T(8,128)(2,1)S(1)}, bf16[384,128]{1,0:T(8,128)(2,1)S(1)}, u32[]{:S(2)}, u32[]{:S(2)}) collective-permute-start(bf16[384,128]{1,0:T(8,128)(2,1)S(1)} %get-tuple-element.210), channel_id=1, source_target_pairs={{0,2},{1,3},{2,0},{3,1},{4,6},{5,7},{6,4},{7,5},{8,10},{9,11},{10,... | collective-permute-start | bytes 294920 | tf_op jit(solution)/shard_map/ppermute | solution.py:25
  85.6 5.6 %collective-permute-start.22 = (bf16[384,128]{1,0:T(8,128)(2,1)S(1)}, bf16[384,128]{1,0:T(8,128)(2,1)S(1)}, u32[]{:S(2)}, u32[]{:S(2)}) collective-permute-start(bf16[384,128]{1,0:T(8,128)(2,1)S(1)} %get-tuple-element.211), channel_id=1, source_target_pairs={{0,4},{1,5},{2,6},{3,7},{4,0},{5,1},{6,2},{7,3},{8,12},{9,13},{10,... | collective-permute-start | bytes 294920 | tf_op jit(solution)/shard_map/ppermute | solution.py:25
  85.9 6.2 %collective-permute-start.23 = (bf16[384,128]{1,0:T(8,128)(2,1)S(1)}, bf16[384,128]{1,0:T(8,128)(2,1)S(1)}, u32[]{:S(2)}, u32[]{:S(2)}) collective-permute-start(bf16[384,128]{1,0:T(8,128)(2,1)S(1)} %get-tuple-element.212), channel_id=1, source_target_pairs={{0,6},{1,7},{2,4},{3,5},{4,2},{5,3},{6,0},{7,1},{8,14},{9,15},{10,... | collective-permute-start | bytes 294920 | tf_op jit(solution)/shard_map/ppermute | solution.py:25
  92.7 10.2 %collective-permute-start.25 = (bf16[1536,128]{1,0:T(8,128)(2,1)S(1)}, bf16[1536,128]{1,0:T(8,128)(2,1)S(1)}, u32[]{:S(2)}, u32[]{:S(2)}) collective-permute-start(bf16[1536,128]{1,0:T(8,128)(2,1)S(1)} %collective-permute-done.19.refs_2_), channel_id=1, source_target_pairs={{0,4},{1,5},{2,6},{3,7},{4,0},{5,1},{6,2},{7,3},{8,12},{9,13},{10,... | collective-permute-start | bytes 1179656 | tf_op jit(solution)/shard_map/ppermute | solution.py:25
  117.2 9.9 %collective-permute-start.28 = (bf16[1536,128]{1,0:T(8,128)(2,1)S(1)}, bf16[1536,128]{1,0:T(8,128)(2,1)S(1)}, u32[]{:S(2)}, u32[]{:S(2)}) collective-permute-start(bf16[1536,128]{1,0:T(8,128)(2,1)S(1)} %pad_maximum_fusion.2.refs_0_), channel_id=1, source_target_pairs={{0,4},{1,5},{2,6},{3,7},{4,0},{5,1},{6,2},{7,3},{8,12},{9,13},{10,... | collective-permute-start | bytes 1179656 | tf_op jit(solution)/shard_map/ppermute | solution.py:25
  117.2 9.9 %collective-permute-start.29 = (bf16[1536,128]{1,0:T(8,128)(2,1)S(1)}, bf16[1536,128]{1,0:T(8,128)(2,1)S(1)}, u32[]{:S(2)}, u32[]{:S(2)}) collective-permute-start(bf16[1536,128]{1,0:T(8,128)(2,1)S(1)} %pad_maximum_fusion.2.refs_0_), channel_id=1, source_target_pairs={{0,2},{1,3},{2,0},{3,1},{4,6},{5,7},{6,4},{7,5},{8,10},{9,11},{10,... | collective-permute-start | bytes 1179656 | tf_op jit(solution)/shard_map/ppermute | solution.py:25
  128.7 5.7 %collective-permute-start.31 = (bf16[384,128]{1,0:T(8,128)(2,1)S(1)}, bf16[384,128]{1,0:T(8,128)(2,1)S(1)}, u32[]{:S(2)}, u32[]{:S(2)}) collective-permute-start(bf16[384,128]{1,0:T(8,128)(2,1)S(1)} %get-tuple-element.244), channel_id=1, source_target_pairs={{0,4},{1,5},{2,6},{3,7},{4,0},{5,1},{6,2},{7,3},{8,12},{9,13},{10,... | collective-permute-start | bytes 294920 | tf_op jit(solution)/shard_map/ppermute | solution.py:25
  129.2 7.3 %collective-permute-start.32 = (bf16[384,128]{1,0:T(8,128)(2,1)S(1)}, bf16[384,128]{1,0:T(8,128)(2,1)S(1)}, u32[]{:S(2)}, u32[]{:S(2)}) collective-permute-start(bf16[384,128]{1,0:T(8,128)(2,1)S(1)} %get-tuple-element.245), channel_id=1, source_target_pairs={{0,6},{1,7},{2,4},{3,5},{4,2},{5,3},{6,0},{7,1},{8,14},{9,15},{10,... | collective-permute-start | bytes 294920 | tf_op jit(solution)/shard_map/ppermute | solution.py:25
  137.1 4.7 %collective-permute-start.33 = (bf16[384,128]{1,0:T(8,128)(2,1)S(1)}, bf16[384,128]{1,0:T(8,128)(2,1)S(1)}, u32[]{:S(2)}, u32[]{:S(2)}) collective-permute-start(bf16[384,128]{1,0:T(8,128)(2,1)S(1)} %shard_map.192), channel_id=1, source_target_pairs={{0,8},{1,9},{2,10},{3,11},{4,12},{5,13},{6,14},{7,15},{8,0},{9,1},... | collective-permute-start | bytes 294920 | tf_op jit(solution)/shard_map/ppermute | solution.py:25
  137.4 10.7 %collective-permute-start.35 = (bf16[1536,128]{1,0:T(8,128)(2,1)S(1)}, bf16[1536,128]{1,0:T(8,128)(2,1)S(1)}, u32[]{:S(2)}, u32[]{:S(2)}) collective-permute-start(bf16[1536,128]{1,0:T(8,128)(2,1)S(1)} %collective-permute-done.29.refs_2_), channel_id=1, source_target_pairs={{0,4},{1,5},{2,6},{3,7},{4,0},{5,1},{6,2},{7,3},{8,12},{9,13},{10,... | collective-permute-start | bytes 1179656 | tf_op jit(solution)/shard_map/ppermute | solution.py:25
  139.1 5.3 %collective-permute-start.36 = (bf16[384,128]{1,0:T(8,128)(2,1)S(1)}, bf16[384,128]{1,0:T(8,128)(2,1)S(1)}, u32[]{:S(2)}, u32[]{:S(2)}) collective-permute-start(bf16[384,128]{1,0:T(8,128)(2,1)S(1)} %get-tuple-element.254), channel_id=1, source_target_pairs={{0,1},{1,0},{2,3},{3,2},{4,5},{5,4},{6,7},{7,6},{8,9},{9,8},{10,11... | collective-permute-start | bytes 294920 | tf_op jit(solution)/shard_map/ppermute | solution.py:25
  141.8 6.4 %collective-permute-start.34 = (bf16[384,128]{1,0:T(8,128)(2,1)S(1)}, bf16[384,128]{1,0:T(8,128)(2,1)S(1)}, u32[]{:S(2)}, u32[]{:S(2)}) collective-permute-start(bf16[384,128]{1,0:T(8,128)(2,1)S(1)} %add_convert_fusion), channel_id=1, source_target_pairs={{0,16},{1,17},{2,18},{3,19},{4,20},{5,21},{6,22},{7,23},{8,24},{9,... | collective-permute-start | bytes 294920 | tf_op jit(solution)/shard_map/ppermute | solution.py:25
  165.3 14.3 %all-to-all-start = ((bf16[16,96,128]{2,1,0:T(8,128)(2,1)}), bf16[16,96,128]{2,1,0:T(8,128)(2,1)S(1)}, u32[]{:S(2)}, u32[]{:S(2)}) async-start(bf16[16,96,128]{2,1,0:T(8,128)(2,1)} %bitcast.70), calls=%async_computation | async-start | bytes 786432 | tf_op jit(solution)/shard_map/all_to_all | solution.py:611
  170.0 10.3 %collective-permute-start.37 = (bf16[192,128]{1,0:T(8,128)(2,1)S(1)}, bf16[192,128]{1,0:T(8,128)(2,1)S(1)}, u32[]{:S(2)}, u32[]{:S(2)}) collective-permute-start(bf16[192,128]{1,0:T(8,128)(2,1)S(1)} %get-tuple-element.267), channel_id=1, source_target_pairs={{0,1},{1,0},{2,3},{3,2},{4,5},{5,4},{6,7},{7,6},{8,9},{9,8},{10,11... | collective-permute-start | bytes 147464 | tf_op jit(solution)/shard_map/ppermute | solution.py:25
  (31 other events, 510.3 us)

commit v5 on v4

--- a/solution.py
+++ b/solution.py
@@ -145,11 +145,13 @@
 
 
 def pack_kernel(groups, scalars, keep, received, *outs):
+    core = scalars[0]
     for group, out in zip(groups, outs):
         at = 0
         for first, rows in group:
-            out[at : at + rows, :] = keep[first : first + rows, :]
-            out[at + rows : at + 2 * rows, :] = received[first : first + rows, :]
+            for lane, part in ((core, keep), (1 - core, received)):
+                target = pl.ds(pl.multiple_of(at + lane * rows, math.gcd(rows, 16)), rows)
+                out[target, :] = part[first : first + rows, :]
             at += 2 * rows
 
 
@@ -159,9 +161,19 @@
     out[:, half:] = jnp.where(scalars[0] == 0, other[...], own[...])
 
 
-def join_columns(scalars, own, other):
-    rows, half = own.shape
-    return kernel_call(join_kernel, [(aval(rows, 2 * half, own.dtype), None)], scalars, [own, other])[0]
+def join_all_kernel(scalars, *refs):
+    count = len(refs) // 3
+    for i in range(count):
+        join_kernel(scalars, refs[2 * i], refs[2 * i + 1], refs[2 * count + i])
+
+
+def join_columns(scalars, pairs):
+    return kernel_call(
+        join_all_kernel,
+        [(aval(own.shape[0], 2 * own.shape[1], own.dtype), None) for own, _ in pairs],
+        scalars,
+        [v for pair in pairs for v in pair],
+    )
 
 
 def hand_out(place, value, own, sends):
@@ -398,14 +410,10 @@
     at_order = []
     for planes in ([0], [z1, z1 ^ 1], [z_index, z_index ^ 2, z_index ^ 1, z_index ^ 3]):
         at_order.append(len(values))
-        for x, y in plane_masks:
-            place = ((x_index ^ x) * n_y + (y_index ^ y)) * 2
-            for z in planes:
-                values += [z * 2 * n_rows + place + (core ^ other) for other in range(2)]
-        if len(planes) == 1:
+        for _ in range(2 if len(planes) == 1 else 1):
             for x, y in plane_masks:
-                place = ((x_index ^ x) * n_y + (y_index ^ y)) * 2
-                values += [place + (core ^ other) for other in (1, 0)]
+                place = (x_index ^ x) * n_y + (y_index ^ y)
+                values += [z * n_rows + place for z in planes]
     at_table = [len(values) + 2 * width * i for i in range(3)]
     children = [(leaf >> 1) * 2, (leaf >> 1) * 2 + 1]
     parts = [jnp.stack([jnp.asarray(v, jnp.int32) for v in values])]
@@ -416,9 +424,6 @@
     ):
         parts += [lax.dynamic_index_in_dim(table, c, 0, keepdims=False) for c in pair]
     scalars = jnp.concatenate(parts)
-    scalars, loads_second, loads_third, loads_fourth = lax.optimization_barrier(
-        (scalars, loads_second, loads_third, loads_fourth)
-    )
 
     tie = lax.optimization_barrier
 
@@ -430,14 +435,14 @@
     keep, send = kernel_call(
         split_kernel,
         [(aval(sum(sizes), half, BF16), True)] * 2,
-        scalars,
+        core[None].astype(jnp.int32),
         [],
         loads,
         [pltpu.VMEM((sum(sizes), cols), BF16), pltpu.SemaphoreType.DMA((len(loads),))],
     )
     received = permute(send, 1)
-    keep, received, sibling, inverse_third, panel_third = tie(
-        (keep, received, sibling, inverse_third, panel_third)
+    scalars, keep, received, sibling, inverse_third, panel_third = tie(
+        (scalars, keep, received, sibling, inverse_third, panel_third)
     )
     inverses = inverse_third, permute(inverse_third, 1)
     panels = panel_third, permute(panel_third, 1)
@@ -467,9 +472,12 @@
     )
     x_second = permute(own_second, mask_x)
     by_z2 = permute(half_fourth, mask_z2)
-    acc, by_z2 = tie((acc, by_z2))
-    half_later = jnp.concatenate([half_third, half_fourth, by_z2], 0)
-    by_z1 = permute(half_later, mask_z1)
+    by_z1 = permute(half_third, mask_z1)
+    acc, by_z1, by_z2 = tie((acc, by_z1, by_z2))
+    own_third = jnp.concatenate([half_third, by_z1], 0)
+    half_fourth = jnp.concatenate([half_fourth, by_z2], 0)
+    x_third = permute(own_third, mask_x)
+    by_z1 = permute(half_fourth, mask_z1)
     shards, acc, far, panel, own_second, x_second, inverses, panels = tie(
         (shards, acc, far, panel, own_second, x_second, inverses, panels)
     )
@@ -494,7 +502,7 @@
             pltpu.SemaphoreType.DMA((len(nexts),)),
         ],
     )
-    keep, send, y_second, by_z1 = tie((keep, send, y_second, by_z1))
+    keep, send, y_second, by_z1, x_third = tie((keep, send, y_second, by_z1, x_third))
     chunks = pair_sum(keep, send, scalars, at_place, column)
 
     def with_x(x_piece, own, y_pieces):
@@ -506,9 +514,7 @@
     pieces_second = with_x(x_second, own_second, y_second)
     early = [own_second, x_second, *y_second]
     across_early = [permute(piece, 1) for piece in early]
-    cut = 2 * sizes[1]
-    own_third = jnp.concatenate([half_later[:cut], by_z1[:cut]], 0)
-    own_fourth = jnp.concatenate([half_later[cut:], by_z1[cut:]], 0)
+    own_fourth = jnp.concatenate([half_fourth, by_z1], 0)
     part = reduce_chunks(chunks, column, scalars)
     part, pieces_second, across_early, own_third, own_fourth = tie(
         (part, pieces_second, across_early, own_third, own_fourth)
@@ -526,7 +532,7 @@
                 for row in range(start, start + chunk, unit):
                     places.append((child * width + row // block, row % block))
         n_next = 4 if level < 2 else 0
-        return unit, places, block, at_table[level], at_order[level], sizes[level], n_pieces, n_next
+        return unit, places, block, at_table[level], at_order[level], 2 * sizes[level], n_pieces, n_next
 
     n_pieces = len(plane_masks)
 
@@ -535,11 +541,11 @@
         across += [across_early[2 + i], permute(pieces_second[3 + 2 * i], 1)]
     pieces_second += across
     mine = spread(part)
+    mine, pieces_second, own_third, own_fourth = tie(
+        (mine, pieces_second, own_third, own_fourth)
+    )
     other = permute(mine, 1)
-    mine, other, pieces_second, own_third, own_fourth = tie(
-        (mine, other, pieces_second, own_third, own_fourth)
-    )
-    x_third = permute(own_third, mask_x)
+    x_fourth = permute(own_fourth, mask_x)
     y_third = [permute(own_third, mask) for mask in y_masks]
     solved_second, keep, send, *nexts = solve_whole(
         scalars,
@@ -551,25 +557,26 @@
         pieces_second,
         [*inverses, *panels],
     )
-    keep, send, x_third, y_third = tie((keep, send, x_third, y_third))
+    keep, send, x_fourth, y_third = tie((keep, send, x_fourth, y_third))
 
     chunks = pair_sum(keep, send, scalars, at_place + 1, plane)
     chunks, y_third, inverse_fourth, panel_fourth = tie(
         (chunks, y_third, inverse_fourth, panel_fourth)
     )
     part = reduce_chunks(chunks, plane, scalars)
-    part, y_third = tie((part, y_third))
+    part, y_third, own_fourth = tie((part, y_third, own_fourth))
     sibling = permute(part, mask_z1)
     pieces_third = with_x(x_third, own_third, y_third)
+    y_fourth = [permute(own_fourth, mask) for mask in y_masks]
     panel_fourth = panel_fourth.T
     fourth = [
         inverse_fourth, permute(inverse_fourth, 1), panel_fourth, permute(panel_fourth, 1),
     ]
-    part, sibling, pieces_third, fourth = tie((part, sibling, pieces_third, fourth))
+    part, sibling, pieces_third, fourth, y_fourth = tie(
+        (part, sibling, pieces_third, fourth, y_fourth)
+    )
     mine = spread(jnp.concatenate([part, sibling], 0))
     mine, own_fourth = tie((mine, own_fourth))
-    x_fourth = permute(own_fourth, mask_x)
-    y_fourth = [permute(own_fourth, mask) for mask in y_masks]
     *chunks, keep, send, a, b, c, d = solve_half(
         scalars,
         plan_of(1, part.shape[0], True),
@@ -583,15 +590,15 @@
         plane,
     )
     fourth = [a, b, c, d]
-    chunks, keep, send, x_fourth, y_fourth = tie((chunks, keep, send, x_fourth, y_fourth))
+    chunks, keep, send = tie((chunks, keep, send))
 
     part = reduce_chunks(chunks, plane, scalars)
-    part, keep, send, x_fourth, y_fourth = tie((part, keep, send, x_fourth, y_fourth))
+    part, keep, send, y_fourth = tie((part, keep, send, y_fourth))
     pieces_fourth = with_x(x_fourth, own_fourth, y_fourth)
-    solved_third = join_columns(scalars, keep, permute(send, 1))
+    halves_third = keep, permute(send, 1)
     part = (part.astype(F32) + permute(part, mask_z1).astype(F32)).astype(BF16)
     sibling = permute(part, mask_z2)
-    part, sibling, pieces_fourth, solved_third = tie((part, sibling, pieces_fourth, solved_third))
+    part, sibling, pieces_fourth, halves_third = tie((part, sibling, pieces_fourth, halves_third))
     mine = spread(jnp.concatenate([part, sibling], 0))
     update, keep_fourth, send_fourth = solve_half(
         scalars,
@@ -605,7 +612,7 @@
         0,
         [],
     )
-    solved_fourth = join_columns(scalars, keep_fourth, permute(send_fourth, 1))
+    halves_fourth = keep_fourth, permute(send_fourth, 1)
     everywhere = ("z2", "z1", "x", "y")
     count = lax.axis_size(everywhere)
     arrived = lax.all_to_all(update, everywhere, 0, 0, tiled=True)
@@ -617,7 +624,8 @@
         [arrived],
         scratch=[pltpu.VMEM((chunk, half), F32)],
     )
-    ancestor = join_columns(scalars, keep, permute(send, 1))
+    solved_third, solved_fourth = join_columns(scalars, [halves_third, halves_fourth])
+    ancestor = join_columns(scalars, [(keep, permute(send, 1))])[0]
     return solved_first, solved_second, solved_third, solved_fourth, ancestor
 
 

time: 183 us -> 176 us (0.962)
  waiting for transfers between devices: 57.1 us -> 51.5 us
  Pallas kernels: 42.8 us -> 40.7 us
    ppermute x39 -> x40, waiting for transfers between devices: 47.5 us -> 41.9 us  [permute(): return lax.ppermute(value, AXES, pairs)]
    pallas_call x16 -> x15, Pallas kernels: 42.8 us -> 40.7 us  [kernel_call(): pl.pallas_call(kernel, out_shape=[pltpu.VMEM(o.shape, o.dtype) if inside...]
    ppermute x39 -> x40, starting transfers between devices: 37.6 us -> 37.8 us  [permute(): return lax.ppermute(value, AXES, pairs)]
  transfers between devices with their start and end apart: 40 -> 41, of which waited for: 23 -> 21; matrix products, arithmetic and copies ran while one was open for 1% -> 1% of each run, Pallas kernels for 19% -> 15%
where the time goes in v5:
time: 176 us; the launch traced here: 175 us
  waiting for transfers between devices  51.5 us (29%)
  starting transfers between devices  42.9 us (24%)
  Pallas kernels  40.7 us (23%)
  blocking collectives  35.9 us (20%)
  local copies, waits for them, and re-layouts  2.93 us (2%)
    ppermute x40, waiting for transfers between devices, permute(): return lax.ppermute(value, AXES, pairs)  41.9 us
    pallas_call x15, Pallas kernels, kernel_call(): pl.pallas_call(kernel, out_shape=[pltpu.VMEM(o.shape, o.dtype) if inside...  40.7 us
    ppermute x40, starting transfers between devices, permute(): return lax.ppermute(value, AXES, pairs)  37.8 us
    all_gather x3, blocking collectives, spread(): return lax.all_gather(value, PLANE, axis=0, tiled=True)  35.9 us
    all_to_all x1, waiting for transfers between devices, per_device(): arrived = lax.all_to_all(update, everywhere, 0, 0, tiled=True)  9.55 us
    all_to_all x1, starting transfers between devices, per_device(): arrived = lax.all_to_all(update, everywhere, 0, 0, tiled=True)  5.04 us
  transfers between devices with their start and end apart: 41, of which 21 were waited for; matrix products, arithmetic and copies ran while one was open for 1% of the time, Pallas kernels for 15%

profile of v5, /device:TPU:0, one launch (start us, length us, event | category | flops | bytes accessed | tf_op | source)
XLA Modules:
  0.0 175.2 jit_solution(13356853626272256394)
XLA Ops:
  4.8 4.9 %collective-permute-start.2 = (bf16[1536,256]{1,0:T(8,128)(2,1)}, bf16[1536,256]{1,0:T(8,128)(2,1)S(1)}, u32[]{:S(2)}, u32[]{:S(2)}) collective-permute-start(bf16[1536,256]{1,0:T(8,128)(2,1)} %b0.1), channel_id=1, source_target_pairs={{0,2},{1,3},{4,6},{5,7},{8,10},{9,11},{12,14},{13,15},{16,18},{17,... | collective-permute-start | bytes 2359304 | tf_op jit(solution)/shard_map/ppermute | solution.py:25
  10.3 1.6 collective-permute-start.5
  11.9 2.6 %collective-permute-start.4 = (bf16[384,128]{1,0:T(8,128)(2,1)S(1)}, bf16[384,128]{1,0:T(8,128)(2,1)S(1)}, u32[]{:S(2)}, u32[]{:S(2)}) collective-permute-start(bf16[384,128]{1,0:T(8,128)(2,1)S(1)} %get-tuple-element.146), channel_id=1, source_target_pairs={{0,16},{1,17},{2,18},{3,19},{4,20},{5,21},{6,22},{7,23},{8,24},{9,... | collective-permute-start | bytes 294920 | tf_op jit(solution)/shard_map/ppermute | solution.py:25
  14.5 4.6 %collective-permute-done.4 = bf16[384,128]{1,0:T(8,128)(2,1)S(1)} collective-permute-done((bf16[384,128]{1,0:T(8,128)(2,1)S(1)}, bf16[384,128]{1,0:T(8,128)(2,1)S(1)}, u32[]{:S(2)}, u32[]{:S(2)}) %collective-permute-start.4) | collective-permute-done | bytes 98336 | tf_op jit(solution)/shard_map/ppermute | solution.py:25
  20.9 8.5 %shard_map.183 = (f32[1536,256]{1,0:T(8,128)S(1)}, bf16[1536,3072]{1,0:T(8,128)(2,1)S(1)}, bf16[1536,1536]{1,0:T(8,128)(2,1)S(1)}) custom-call(s32[111]{0:T(128)S(1)} %concatenate.19.scalars, bf16[1536,256]{1,0:T(8,128)(2,1)S(1)} %copy-done, bf16[1536,256]{1,0:T(8,128)(2,1)S(1)} %collective-permute-done.1.b1, bf16[1536,6144]{1,0:T(8,128)(2,1)} %inverse.1, ...), custom_call_target="tpu_custom_call" | custom-call | flops 1 | bytes 1 | tf_op jit(solution)/shard_map/pallas_call | solution.py:38
  31.1 1.6 collective-permute-start.10
  32.8 5.3 %shard_map.185 = (bf16[1536,256]{1,0:T(8,128)(2,1)}, f32[1536,128]{1,0:T(8,128)S(1)}, bf16[1536,128]{1,0:T(8,128)(2,1)S(1)}, bf16[768,6144]{1,0:T(8,128)(2,1)S(1)}, bf16[1536,768]{1,0:T(8,128)(2,1)S(1)}) custom-call(s32[111]{0:T(128)S(1)} %concatenate.19.scalars, f32[1536,256]{1,0:T(8,128)S(1)} %get-tuple-element.153.acc, ...), custom_call_target="tpu_custom_call" | custom-call | flops 1 | bytes 1 | tf_op jit(solution)/shard_map/pallas_call | solution.py:38
  38.1 3.1 %collective-permute-done.11.refs_1_ = bf16[1536,128]{1,0:T(8,128)(2,1)S(1)} collective-permute-done((bf16[1536,128]{1,0:T(8,128)(2,1)S(1)}, bf16[1536,128]{1,0:T(8,128)(2,1)S(1)}, u32[]{:S(2)}, u32[]{:S(2)}) %collective-permute-start.11) | collective-permute-done | bytes 393248 | tf_op jit(solution)/shard_map/ppermute | solution.py:25
  42.0 1.5 collective-permute-start.14
  44.9 6.7 %collective-permute-done.13.rest_0_ = bf16[768,128]{1,0:T(8,128)(2,1)S(1)} collective-permute-done((bf16[768,128]{1,0:T(8,128)(2,1)S(1)}, bf16[768,128]{1,0:T(8,128)(2,1)S(1)}, u32[]{:S(2)}, u32[]{:S(2)}) %collective-permute-start.13) | collective-permute-done | bytes 196640 | tf_op jit(solution)/shard_map/ppermute | solution.py:25
  53.6 12.8 %all_gather.9.mine = bf16[3072,128]{1,0:T(8,128)(2,1)S(1)} all-gather(bf16[768,128]{1,0:T(8,128)(2,1)S(1)} %shard_map.187), channel_id=1, replica_groups=mesh['hi'=1,'z2'=2,'z1'=2,'x'=2,'y'=2,'core'=2] {'x','y'}, dimensions={0}, use_global_device_ids=true | all-gather | bytes 983040 | tf_op jit(solution)/shard_map/all_gather | solution.py:524
  68.8 7.3 %shard_map.188 = (bf16[768,256]{1,0:T(8,128)(2,1)}, f32[1536,128]{1,0:T(8,128)S(1)}, bf16[1536,128]{1,0:T(8,128)(2,1)S(1)}, bf16[384,6144]{1,0:T(8,128)(2,1)S(1)...) custom-call(s32[111]{0:T(128)S(1)} %concatenate.19.scalars, ...), custom_call_target="tpu_custom_call" | custom-call | flops 1 | bytes 1 | tf_op jit(solution)/shard_map/pallas_call | solution.py:38
  76.1 1.9 %collective-permute-done.20.refs_1_ = bf16[1536,128]{1,0:T(8,128)(2,1)S(1)} collective-permute-done((bf16[1536,128]{1,0:T(8,128)(2,1)S(1)}, bf16[1536,128]{1,0:T(8,128)(2,1)S(1)}, u32[]{:S(2)}, u32[]{:S(2)}) %collective-permute-start.20) | collective-permute-done | bytes 393248 | tf_op jit(solution)/shard_map/ppermute | solution.py:25
  78.2 1.7 collective-permute-done.22.received
  81.2 1.5 collective-permute-start.23
  86.1 2.3 %collective-permute-done.24.rest_1_ = bf16[384,128]{1,0:T(8,128)(2,1)S(1)} collective-permute-done((bf16[384,128]{1,0:T(8,128)(2,1)S(1)}, bf16[384,128]{1,0:T(8,128)(2,1)S(1)}, u32[]{:S(2)}, u32[]{:S(2)}) %collective-permute-start.24) | collective-permute-done | bytes 98336 | tf_op jit(solution)/shard_map/ppermute | solution.py:25
  90.0 1.6 collective-permute-start.27
  93.5 3.3 %collective-permute-done.26 = bf16[384,128]{1,0:T(8,128)(2,1)S(1)} collective-permute-done((bf16[384,128]{1,0:T(8,128)(2,1)S(1)}, bf16[384,128]{1,0:T(8,128)(2,1)S(1)}, u32[]{:S(2)}, u32[]{:S(2)}) %collective-permute-start.26) | collective-permute-done | bytes 98336 | tf_op jit(solution)/shard_map/ppermute | solution.py:25
  96.7 3.5 %collective-permute-done.27.refs_3_ = bf16[1536,128]{1,0:T(8,128)(2,1)S(1)} collective-permute-done((bf16[1536,128]{1,0:T(8,128)(2,1)S(1)}, bf16[1536,128]{1,0:T(8,128)(2,1)S(1)}, u32[]{:S(2)}, u32[]{:S(2)}) %collective-permute-start.27) | collective-permute-done | bytes 393248 | tf_op jit(solution)/shard_map/ppermute | solution.py:25
  101.5 11.2 %all_gather.10.mine = bf16[3072,128]{1,0:T(8,128)(2,1)S(1)} all-gather(bf16[768,128]{1,0:T(8,128)(2,1)S(1)} %pad_maximum_fusion.2), channel_id=1, replica_groups=mesh['hi'=1,'z2'=2,'z1'=2,'x'=2,'y'=2,'core'=2] {'x','y'}, dimensions={0}, use_global_device_ids=true | all-gather | bytes 983040 | tf_op jit(solution)/shard_map/all_gather | solution.py:524
  112.7 6.0 %shard_map.191 = (f32[384,128]{1,0:T(8,128)S(1)}, bf16[384,128]{1,0:T(8,128)(2,1)S(1)}, bf16[384,128]{1,0:T(8,128)(2,1)S(1)}, bf16[384,128]{1,0:T(8,128)(2,1)S(1...) custom-call(s32[111]{0:T(128)S(1)} %concatenate.19.scalars, ...), custom_call_target="tpu_custom_call" | custom-call | flops 1 | bytes 1 | tf_op jit(solution)/shard_map/pallas_call | solution.py:38
  118.8 1.7 collective-permute-start.31
  123.4 1.6 collective-permute-done.32.rest_1_
  125.1 1.9 %collective-permute-done.33.rest_2_ = bf16[384,128]{1,0:T(8,128)(2,1)S(1)} collective-permute-done((bf16[384,128]{1,0:T(8,128)(2,1)S(1)}, bf16[384,128]{1,0:T(8,128)(2,1)S(1)}, u32[]{:S(2)}, u32[]{:S(2)}) %collective-permute-start.33) | collective-permute-done | bytes 98336 | tf_op jit(solution)/shard_map/ppermute | solution.py:25
  127.6 1.9 %collective-permute-start.34 = (bf16[384,128]{1,0:T(8,128)(2,1)S(1)}, bf16[384,128]{1,0:T(8,128)(2,1)S(1)}, u32[]{:S(2)}, u32[]{:S(2)}) collective-permute-start(bf16[384,128]{1,0:T(8,128)(2,1)S(1)} %shard_map.192), channel_id=1, source_target_pairs={{0,8},{1,9},{2,10},{3,11},{4,12},{5,13},{6,14},{7,15},{8,0},{9,1},... | collective-permute-start | bytes 294920 | tf_op jit(solution)/shard_map/ppermute | solution.py:25
  129.4 1.9 %collective-permute-start.36 = (bf16[1536,128]{1,0:T(8,128)(2,1)S(1)}, bf16[1536,128]{1,0:T(8,128)(2,1)S(1)}, u32[]{:S(2)}, u32[]{:S(2)}) collective-permute-start(bf16[1536,128]{1,0:T(8,128)(2,1)S(1)} %collective-permute-done.30.refs_2_), channel_id=1, source_target_pairs={{0,4},{1,5},{2,6},{3,7},{4,0},{5,1},{6,2},{7,3},{8,12},{9,13},{10,... | collective-permute-start | bytes 1179656 | tf_op jit(solution)/shard_map/ppermute | solution.py:25
  132.3 3.8 %collective-permute-start.35 = (bf16[384,128]{1,0:T(8,128)(2,1)S(1)}, bf16[384,128]{1,0:T(8,128)(2,1)S(1)}, u32[]{:S(2)}, u32[]{:S(2)}) collective-permute-start(bf16[384,128]{1,0:T(8,128)(2,1)S(1)} %add_convert_fusion), channel_id=1, source_target_pairs={{0,16},{1,17},{2,18},{3,19},{4,20},{5,21},{6,22},{7,23},{8,24},{9,... | collective-permute-start | bytes 294920 | tf_op jit(solution)/shard_map/ppermute | solution.py:25
  136.1 3.6 %collective-permute-done.35 = bf16[384,128]{1,0:T(8,128)(2,1)S(1)} collective-permute-done((bf16[384,128]{1,0:T(8,128)(2,1)S(1)}, bf16[384,128]{1,0:T(8,128)(2,1)S(1)}, u32[]{:S(2)}, u32[]{:S(2)}) %collective-permute-start.35) | collective-permute-done | bytes 98336 | tf_op jit(solution)/shard_map/ppermute | solution.py:25
  139.8 11.9 %all_gather.11.mine = bf16[3072,128]{1,0:T(8,128)(2,1)S(1)} all-gather(bf16[768,128]{1,0:T(8,128)(2,1)S(1)} %pad_maximum_fusion.3), channel_id=1, replica_groups=mesh['hi'=1,'z2'=2,'z1'=2,'x'=2,'y'=2,'core'=2] {'x','y'}, dimensions={0}, use_global_device_ids=true | all-gather | bytes 983040 | tf_op jit(solution)/shard_map/all_gather | solution.py:524
  151.7 5.6 %shard_map.193 = (bf16[1536,128]{1,0:T(8,128)(2,1)}, bf16[192,128]{1,0:T(8,128)(2,1)S(1)}, bf16[192,128]{1,0:T(8,128)(2,1)S(1)}) custom-call(s32[111]{0:T(128)S(1)} %concatenate.19.scalars, bf16[3072,128]{1,0:T(8,128)(2,1)S(1)} %all_gather.11.mine, bf16[192,6144]{1,0:T(8,128)(2,1)S(1)} %get-tuple-element.256.inverse_a, ...), custom_call_target="tpu_custom_call" | custom-call | flops 1 | bytes 1 | tf_op jit(solution)/shard_map/pallas_call | solution.py:38
  157.3 5.0 %all-to-all-start = ((bf16[16,96,128]{2,1,0:T(8,128)(2,1)}), bf16[16,96,128]{2,1,0:T(8,128)(2,1)S(1)}, u32[]{:S(2)}, u32[]{:S(2)}) async-start(bf16[16,96,128]{2,1,0:T(8,128)(2,1)} %bitcast.41), calls=%async_computation | async-start | bytes 786432 | tf_op jit(solution)/shard_map/all_to_all | solution.py:618
  162.5 9.6 %all-to-all-done = bf16[16,96,128]{2,1,0:T(8,128)(2,1)S(1)} async-done(((bf16[16,96,128]{2,1,0:T(8,128)(2,1)}), bf16[16,96,128]{2,1,0:T(8,128)(2,1)S(1)}, u32[]{:S(2)}, u32[]{:S(2)}) %all-to-all-start) | async-done | bytes 393248 | tf_op jit(solution)/shard_map/all_to_all | solution.py:618
  (124 shorter events, 32.1 us)
Async XLA Ops:
  4.2 25.2 %collective-permute-start.6 = (bf16[384,6144]{1,0:T(8,128)(2,1)}, bf16[384,6144]{1,0:T(8,128)(2,1)S(1)}, u32[]{:S(2)}, u32[]{:S(2)}) collective-permute-start(bf16[384,6144]{1,0:T(8,128)(2,1)} %refs_8_), channel_id=1, source_target_pairs={{0,1},{1,0},{2,3},{3,2},{4,5},{5,4},{6,7},{7,6},{8,9},{9,8},{10,11... | collective-permute-start | bytes 14155784 | tf_op jit(solution)/shard_map/ppermute | solution.py:25
  4.7 24.7 %collective-permute-start.7 = (bf16[1536,384]{1,0:T(8,128)(2,1)}, bf16[1536,384]{1,0:T(8,128)(2,1)S(1)}, u32[]{:S(2)}, u32[]{:S(2)}) collective-permute-start(bf16[1536,384]{1,0:T(8,128)(2,1)} %refs_10_), channel_id=1, source_target_pairs={{0,1},{1,0},{2,3},{3,2},{4,5},{5,4},{6,7},{7,6},{8,9},{9,8},{10,11... | collective-permute-start | bytes 3538952 | tf_op jit(solution)/shard_map/ppermute | solution.py:25
  4.8 24.6 %collective-permute-start.2 = (bf16[1536,256]{1,0:T(8,128)(2,1)}, bf16[1536,256]{1,0:T(8,128)(2,1)S(1)}, u32[]{:S(2)}, u32[]{:S(2)}) collective-permute-start(bf16[1536,256]{1,0:T(8,128)(2,1)} %b0.1), channel_id=1, source_target_pairs={{0,2},{1,3},{4,6},{5,7},{8,10},{9,11},{12,14},{13,15},{16,18},{17,... | collective-permute-start | bytes 2359304 | tf_op jit(solution)/shard_map/ppermute | solution.py:25
  10.3 19.1 %collective-permute-start.5 = (bf16[1536,128]{1,0:T(8,128)(2,1)S(1)}, bf16[1536,128]{1,0:T(8,128)(2,1)S(1)}, u32[]{:S(2)}, u32[]{:S(2)}) collective-permute-start(bf16[1536,128]{1,0:T(8,128)(2,1)S(1)} %get-tuple-element.183.refs_0_), channel_id=1, source_target_pairs={{0,4},{1,5},{2,6},{3,7},{4,0},{5,1},{6,2},{7,3},{8,12},{9,13},{10,... | collective-permute-start | bytes 1179656 | tf_op jit(solution)/shard_map/ppermute | solution.py:25
  11.9 7.2 %collective-permute-start.4 = (bf16[384,128]{1,0:T(8,128)(2,1)S(1)}, bf16[384,128]{1,0:T(8,128)(2,1)S(1)}, u32[]{:S(2)}, u32[]{:S(2)}) collective-permute-start(bf16[384,128]{1,0:T(8,128)(2,1)S(1)} %get-tuple-element.146), channel_id=1, source_target_pairs={{0,16},{1,17},{2,18},{3,19},{4,20},{5,21},{6,22},{7,23},{8,24},{9,... | collective-permute-start | bytes 294920 | tf_op jit(solution)/shard_map/ppermute | solution.py:25
  19.1 10.3 %collective-permute-start.3 = (bf16[768,128]{1,0:T(8,128)(2,1)S(1)}, bf16[768,128]{1,0:T(8,128)(2,1)S(1)}, u32[]{:S(2)}, u32[]{:S(2)}) collective-permute-start(bf16[768,128]{1,0:T(8,128)(2,1)S(1)} %get-tuple-element.145), channel_id=1, source_target_pairs={{0,8},{1,9},{2,10},{3,11},{4,12},{5,13},{6,14},{7,15},{8,0},{9,1},... | collective-permute-start | bytes 589832 | tf_op jit(solution)/shard_map/ppermute | solution.py:25
  29.6 11.6 %collective-permute-start.11 = (bf16[1536,128]{1,0:T(8,128)(2,1)S(1)}, bf16[1536,128]{1,0:T(8,128)(2,1)S(1)}, u32[]{:S(2)}, u32[]{:S(2)}) collective-permute-start(bf16[1536,128]{1,0:T(8,128)(2,1)S(1)} %constant_dynamic-update-slice_fusion.refs_0_), channel_id=1, source_target_pairs={{0,4},{1,5},{2,6},{3,7},{4,0},{5,1},{6,2},{7,3},{8,12},{9,13},{10,... | collective-permute-start | bytes 1179656 | tf_op jit(solution)/shard_map/ppermute | solution.py:25
  30.2 11.2 %collective-permute-start.9 = (bf16[1536,128]{1,0:T(8,128)(2,1)S(1)}, bf16[1536,128]{1,0:T(8,128)(2,1)S(1)}, u32[]{:S(2)}, u32[]{:S(2)}) collective-permute-start(bf16[1536,128]{1,0:T(8,128)(2,1)S(1)} %get-tuple-element.183.refs_0_), channel_id=1, source_target_pairs={{0,2},{1,3},{2,0},{3,1},{4,6},{5,7},{6,4},{7,5},{8,10},{9,11},{10,... | collective-permute-start | bytes 1179656 | tf_op jit(solution)/shard_map/ppermute | solution.py:25
  31.1 6.9 %collective-permute-start.10 = (bf16[768,128]{1,0:T(8,128)(2,1)S(1)}, bf16[768,128]{1,0:T(8,128)(2,1)S(1)}, u32[]{:S(2)}, u32[]{:S(2)}) collective-permute-start(bf16[768,128]{1,0:T(8,128)(2,1)S(1)} %pad_maximum_fusion.1), channel_id=1, source_target_pairs={{0,8},{1,9},{2,10},{3,11},{4,12},{5,13},{6,14},{7,15},{8,0},{9,1},... | collective-permute-start | bytes 589832 | tf_op jit(solution)/shard_map/ppermute | solution.py:25
  41.5 10.7 %collective-permute-start.15 = (bf16[1536,128]{1,0:T(8,128)(2,1)S(1)}, bf16[1536,128]{1,0:T(8,128)(2,1)S(1)}, u32[]{:S(2)}, u32[]{:S(2)}) collective-permute-start(bf16[1536,128]{1,0:T(8,128)(2,1)S(1)} %get-tuple-element.183.refs_0_), channel_id=1, source_target_pairs={{0,1},{1,0},{2,3},{3,2},{4,5},{5,4},{6,7},{7,6},{8,9},{9,8},{10,11... | collective-permute-start | bytes 1179656 | tf_op jit(solution)/shard_map/ppermute | solution.py:25
  42.0 10.2 %collective-permute-start.16 = (bf16[1536,128]{1,0:T(8,128)(2,1)S(1)}, bf16[1536,128]{1,0:T(8,128)(2,1)S(1)}, u32[]{:S(2)}, u32[]{:S(2)}) collective-permute-start(bf16[1536,128]{1,0:T(8,128)(2,1)S(1)} %collective-permute-done.5.refs_1_), channel_id=1, source_target_pairs={{0,1},{1,0},{2,3},{3,2},{4,5},{5,4},{6,7},{7,6},{8,9},{9,8},{10,11... | collective-permute-start | bytes 1179656 | tf_op jit(solution)/shard_map/ppermute | solution.py:25
  42.0 11.5 %collective-permute-start.14 = (bf16[1536,128]{1,0:T(8,128)(2,1)S(1)}, bf16[1536,128]{1,0:T(8,128)(2,1)S(1)}, u32[]{:S(2)}, u32[]{:S(2)}) collective-permute-start(bf16[1536,128]{1,0:T(8,128)(2,1)S(1)} %collective-permute-done.9.refs_2_), channel_id=1, source_target_pairs={{0,4},{1,5},{2,6},{3,7},{4,0},{5,1},{6,2},{7,3},{8,12},{9,13},{10,... | collective-permute-start | bytes 1179656 | tf_op jit(solution)/shard_map/ppermute | solution.py:25
  43.5 10.0 %collective-permute-start.17 = (bf16[1536,128]{1,0:T(8,128)(2,1)S(1)}, bf16[1536,128]{1,0:T(8,128)(2,1)S(1)}, u32[]{:S(2)}, u32[]{:S(2)}) collective-permute-start(bf16[1536,128]{1,0:T(8,128)(2,1)S(1)} %collective-permute-done.9.refs_2_), channel_id=1, source_target_pairs={{0,1},{1,0},{2,3},{3,2},{4,5},{5,4},{6,7},{7,6},{8,9},{9,8},{10,11... | collective-permute-start | bytes 1179656 | tf_op jit(solution)/shard_map/ppermute | solution.py:25
  44.4 7.2 %collective-permute-start.13 = (bf16[768,128]{1,0:T(8,128)(2,1)S(1)}, bf16[768,128]{1,0:T(8,128)(2,1)S(1)}, u32[]{:S(2)}, u32[]{:S(2)}) collective-permute-start(bf16[768,128]{1,0:T(8,128)(2,1)S(1)} %get-tuple-element.166), channel_id=1, source_target_pairs={{0,2},{1,3},{2,0},{3,1},{4,6},{5,7},{6,4},{7,5},{8,10},{9,11},{10,... | collective-permute-start | bytes 589832 | tf_op jit(solution)/shard_map/ppermute | solution.py:25
  53.5 12.8 %collective-permute-start.18 = (bf16[1536,128]{1,0:T(8,128)(2,1)S(1)}, bf16[1536,128]{1,0:T(8,128)(2,1)S(1)}, u32[]{:S(2)}, u32[]{:S(2)}) collective-permute-start(bf16[1536,128]{1,0:T(8,128)(2,1)S(1)} %collective-permute-done.14.refs_3_), channel_id=1, source_target_pairs={{0,1},{1,0},{2,3},{3,2},{4,5},{5,4},{6,7},{7,6},{8,9},{9,8},{10,11... | collective-permute-start | bytes 1179656 | tf_op jit(solution)/shard_map/ppermute | solution.py:25
  66.4 11.5 %collective-permute-start.20 = (bf16[1536,128]{1,0:T(8,128)(2,1)S(1)}, bf16[1536,128]{1,0:T(8,128)(2,1)S(1)}, u32[]{:S(2)}, u32[]{:S(2)}) collective-permute-start(bf16[1536,128]{1,0:T(8,128)(2,1)S(1)} %pad_maximum_fusion.refs_0_), channel_id=1, source_target_pairs={{0,4},{1,5},{2,6},{3,7},{4,0},{5,1},{6,2},{7,3},{8,12},{9,13},{10,... | collective-permute-start | bytes 1179656 | tf_op jit(solution)/shard_map/ppermute | solution.py:25
  67.0 11.2 %collective-permute-start.21 = (bf16[1536,128]{1,0:T(8,128)(2,1)S(1)}, bf16[1536,128]{1,0:T(8,128)(2,1)S(1)}, u32[]{:S(2)}, u32[]{:S(2)}) collective-permute-start(bf16[1536,128]{1,0:T(8,128)(2,1)S(1)} %constant_dynamic-update-slice_fusion.refs_0_), channel_id=1, source_target_pairs={{0,2},{1,3},{2,0},{3,1},{4,6},{5,7},{6,4},{7,5},{8,10},{9,11},{10,... | collective-permute-start | bytes 1179656 | tf_op jit(solution)/shard_map/ppermute | solution.py:25
  80.6 20.8 %collective-permute-start.28 = (bf16[192,6144]{1,0:T(8,128)(2,1)S(1)}, bf16[192,6144]{1,0:T(8,128)(2,1)S(1)}, u32[]{:S(2)}, u32[]{:S(2)}) collective-permute-start(bf16[192,6144]{1,0:T(8,128)(2,1)S(1)} %copy-done.3), channel_id=1, source_target_pairs={{0,1},{1,0},{2,3},{3,2},{4,5},{5,4},{6,7},{7,6},{8,9},{9,8},{10,11... | collective-permute-start | bytes 7077896 | tf_op jit(solution)/shard_map/ppermute | solution.py:25
  80.9 20.6 %collective-permute-start.29 = (bf16[192,1536]{1,0:T(8,128)(2,1)S(1)}, bf16[192,1536]{1,0:T(8,128)(2,1)S(1)}, u32[]{:S(2)}, u32[]{:S(2)}) collective-permute-start(bf16[192,1536]{1,0:T(8,128)(2,1)S(1)} %bitcast.51), channel_id=1, source_target_pairs={{0,1},{1,0},{2,3},{3,2},{4,5},{5,4},{6,7},{7,6},{8,9},{9,8},{10,11... | collective-permute-start | bytes 1769480 | tf_op jit(solution)/shard_map/ppermute | solution.py:25
  81.2 4.8 %collective-permute-start.23 = (bf16[384,128]{1,0:T(8,128)(2,1)S(1)}, bf16[384,128]{1,0:T(8,128)(2,1)S(1)}, u32[]{:S(2)}, u32[]{:S(2)}) collective-permute-start(bf16[384,128]{1,0:T(8,128)(2,1)S(1)} %get-tuple-element.208), channel_id=1, source_target_pairs={{0,2},{1,3},{2,0},{3,1},{4,6},{5,7},{6,4},{7,5},{8,10},{9,11},{10,... | collective-permute-start | bytes 294920 | tf_op jit(solution)/shard_map/ppermute | solution.py:25
  82.7 5.6 %collective-permute-start.24 = (bf16[384,128]{1,0:T(8,128)(2,1)S(1)}, bf16[384,128]{1,0:T(8,128)(2,1)S(1)}, u32[]{:S(2)}, u32[]{:S(2)}) collective-permute-start(bf16[384,128]{1,0:T(8,128)(2,1)S(1)} %get-tuple-element.209), channel_id=1, source_target_pairs={{0,4},{1,5},{2,6},{3,7},{4,0},{5,1},{6,2},{7,3},{8,12},{9,13},{10,... | collective-permute-start | bytes 294920 | tf_op jit(solution)/shard_map/ppermute | solution.py:25
  83.3 6.2 %collective-permute-start.25 = (bf16[384,128]{1,0:T(8,128)(2,1)S(1)}, bf16[384,128]{1,0:T(8,128)(2,1)S(1)}, u32[]{:S(2)}, u32[]{:S(2)}) collective-permute-start(bf16[384,128]{1,0:T(8,128)(2,1)S(1)} %get-tuple-element.210), channel_id=1, source_target_pairs={{0,6},{1,7},{2,4},{3,5},{4,2},{5,3},{6,0},{7,1},{8,14},{9,15},{10,... | collective-permute-start | bytes 294920 | tf_op jit(solution)/shard_map/ppermute | solution.py:25
  90.0 10.2 %collective-permute-start.27 = (bf16[1536,128]{1,0:T(8,128)(2,1)S(1)}, bf16[1536,128]{1,0:T(8,128)(2,1)S(1)}, u32[]{:S(2)}, u32[]{:S(2)}) collective-permute-start(bf16[1536,128]{1,0:T(8,128)(2,1)S(1)} %collective-permute-done.21.refs_2_), channel_id=1, source_target_pairs={{0,4},{1,5},{2,6},{3,7},{4,0},{5,1},{6,2},{7,3},{8,12},{9,13},{10,... | collective-permute-start | bytes 1179656 | tf_op jit(solution)/shard_map/ppermute | solution.py:25
  91.6 9.9 %collective-permute-start.30 = (bf16[1536,128]{1,0:T(8,128)(2,1)S(1)}, bf16[1536,128]{1,0:T(8,128)(2,1)S(1)}, u32[]{:S(2)}, u32[]{:S(2)}) collective-permute-start(bf16[1536,128]{1,0:T(8,128)(2,1)S(1)} %pad_maximum_fusion.refs_0_), channel_id=1, source_target_pairs={{0,2},{1,3},{2,0},{3,1},{4,6},{5,7},{6,4},{7,5},{8,10},{9,11},{10,... | collective-permute-start | bytes 1179656 | tf_op jit(solution)/shard_map/ppermute | solution.py:25
  118.8 4.7 %collective-permute-start.31 = (bf16[384,128]{1,0:T(8,128)(2,1)S(1)}, bf16[384,128]{1,0:T(8,128)(2,1)S(1)}, u32[]{:S(2)}, u32[]{:S(2)}) collective-permute-start(bf16[384,128]{1,0:T(8,128)(2,1)S(1)} %get-tuple-element.240), channel_id=1, source_target_pairs={{0,2},{1,3},{2,0},{3,1},{4,6},{5,7},{6,4},{7,5},{8,10},{9,11},{10,... | collective-permute-start | bytes 294920 | tf_op jit(solution)/shard_map/ppermute | solution.py:25
  120.9 6.1 %collective-permute-start.33 = (bf16[384,128]{1,0:T(8,128)(2,1)S(1)}, bf16[384,128]{1,0:T(8,128)(2,1)S(1)}, u32[]{:S(2)}, u32[]{:S(2)}) collective-permute-start(bf16[384,128]{1,0:T(8,128)(2,1)S(1)} %get-tuple-element.242), channel_id=1, source_target_pairs={{0,6},{1,7},{2,4},{3,5},{4,2},{5,3},{6,0},{7,1},{8,14},{9,15},{10,... | collective-permute-start | bytes 294920 | tf_op jit(solution)/shard_map/ppermute | solution.py:25
  127.6 4.7 %collective-permute-start.34 = (bf16[384,128]{1,0:T(8,128)(2,1)S(1)}, bf16[384,128]{1,0:T(8,128)(2,1)S(1)}, u32[]{:S(2)}, u32[]{:S(2)}) collective-permute-start(bf16[384,128]{1,0:T(8,128)(2,1)S(1)} %shard_map.192), channel_id=1, source_target_pairs={{0,8},{1,9},{2,10},{3,11},{4,12},{5,13},{6,14},{7,15},{8,0},{9,1},... | collective-permute-start | bytes 294920 | tf_op jit(solution)/shard_map/ppermute | solution.py:25
  129.4 10.3 %collective-permute-start.36 = (bf16[1536,128]{1,0:T(8,128)(2,1)S(1)}, bf16[1536,128]{1,0:T(8,128)(2,1)S(1)}, u32[]{:S(2)}, u32[]{:S(2)}) collective-permute-start(bf16[1536,128]{1,0:T(8,128)(2,1)S(1)} %collective-permute-done.30.refs_2_), channel_id=1, source_target_pairs={{0,4},{1,5},{2,6},{3,7},{4,0},{5,1},{6,2},{7,3},{8,12},{9,13},{10,... | collective-permute-start | bytes 1179656 | tf_op jit(solution)/shard_map/ppermute | solution.py:25
  131.4 4.7 %collective-permute-start.37 = (bf16[384,128]{1,0:T(8,128)(2,1)S(1)}, bf16[384,128]{1,0:T(8,128)(2,1)S(1)}, u32[]{:S(2)}, u32[]{:S(2)}) collective-permute-start(bf16[384,128]{1,0:T(8,128)(2,1)S(1)} %get-tuple-element.251), channel_id=1, source_target_pairs={{0,1},{1,0},{2,3},{3,2},{4,5},{5,4},{6,7},{7,6},{8,9},{9,8},{10,11... | collective-permute-start | bytes 294920 | tf_op jit(solution)/shard_map/ppermute | solution.py:25
  132.3 7.5 %collective-permute-start.35 = (bf16[384,128]{1,0:T(8,128)(2,1)S(1)}, bf16[384,128]{1,0:T(8,128)(2,1)S(1)}, u32[]{:S(2)}, u32[]{:S(2)}) collective-permute-start(bf16[384,128]{1,0:T(8,128)(2,1)S(1)} %add_convert_fusion), channel_id=1, source_target_pairs={{0,16},{1,17},{2,18},{3,19},{4,20},{5,21},{6,22},{7,23},{8,24},{9,... | collective-permute-start | bytes 294920 | tf_op jit(solution)/shard_map/ppermute | solution.py:25
  157.3 14.7 %all-to-all-start = ((bf16[16,96,128]{2,1,0:T(8,128)(2,1)}), bf16[16,96,128]{2,1,0:T(8,128)(2,1)S(1)}, u32[]{:S(2)}, u32[]{:S(2)}) async-start(bf16[16,96,128]{2,1,0:T(8,128)(2,1)} %bitcast.41), calls=%async_computation | async-start | bytes 786432 | tf_op jit(solution)/shard_map/all_to_all | solution.py:618
  162.4 10.3 %collective-permute-start.38 = (bf16[192,128]{1,0:T(8,128)(2,1)S(1)}, bf16[192,128]{1,0:T(8,128)(2,1)S(1)}, u32[]{:S(2)}, u32[]{:S(2)}) collective-permute-start(bf16[192,128]{1,0:T(8,128)(2,1)S(1)} %get-tuple-element.265), channel_id=1, source_target_pairs={{0,1},{1,0},{2,3},{3,2},{4,5},{5,4},{6,7},{7,6},{8,9},{9,8},{10,11... | collective-permute-start | bytes 147464 | tf_op jit(solution)/shard_map/ppermute | solution.py:25
  (32 other events, 474.0 us)

commit v6 on v5

--- a/solution.py
+++ b/solution.py
@@ -254,6 +254,20 @@
         ready[at, lanes] = (ready[at, lanes].astype(F32) - value).astype(BF16)
 
 
+def subtract_parts(scalars, plan, parts, ready, lanes):
+    unit, (width, at_place), block, at_table = plan[:4]
+    chunk = parts[0].shape[0] // 2
+    for mask, part in enumerate(parts):
+        first = (scalars[at_place] ^ mask) * chunk
+        for child in range(2):
+            for start in range(0, chunk, unit):
+                row = first + start
+                index = scalars[at_table + child * width + lax.div(row, block)]
+                at = pl.ds(pl.multiple_of(index * block + lax.rem(row, block), unit), unit)
+                value = part[pl.ds(child * chunk + start, unit), :].astype(F32)
+                ready[at, lanes] = (ready[at, lanes].astype(F32) - value).astype(BF16)
+
+
 def whole_kernel(plan, scalars, mine, other, inverse, panel, *refs):
     at_order, size, n_pieces, n_next = plan[4:]
     pieces, refs = refs[: 2 * n_pieces], refs[2 * n_pieces :]
@@ -285,18 +299,20 @@
         copy.wait()
 
 
-def half_kernel(plan, turned, at_place, n_chunks, scalars, mine, inverse_a, inverse_b, panel_a, panel_b, *refs):
+def half_kernel(plan, turned, at_place, n_chunks, n_parts, scalars, *refs):
+    parts, refs = refs[:n_parts], refs[n_parts:]
+    (inverse_a, inverse_b, panel_a, panel_b), refs = refs[:4], refs[4:]
     at_order, size, n_pieces, n_next = plan[4:]
     pieces, refs = refs[:n_pieces], refs[n_pieces:]
     nexts, refs = refs[:n_next], refs[n_next:]
     chunks, (x_keep, x_send) = refs[:n_chunks], refs[n_chunks : n_chunks + 2]
     ready, update, load_sems, sems = refs[-4:]
-    lanes = pl.ds(0, mine.shape[1])
+    lanes = pl.ds(0, parts[0].shape[1])
     arriving = start_loads(scalars, at_order, size, pieces, ready, lanes, load_sems, 0)
     for copy in arriving:
         copy.wait()
     copies = start_all(nexts, refs[n_chunks + 2 : -4], sems)
-    subtract_updates(scalars, plan, mine, ready, lanes)
+    subtract_parts(scalars, plan, parts, ready, lanes)
 
     def step(at):
         x_keep[at, :] = dot(inverse_a[at, :], ready[...]).astype(BF16)
@@ -347,16 +363,16 @@
     )
 
 
-def solve_half(scalars, plan, mine, inverses, panels, pieces, nexts, update_rows, at_place, masks):
-    (rows, depth), half = inverses[0].shape, mine.shape[1]
+def solve_half(scalars, plan, parts, inverses, panels, pieces, nexts, update_rows, at_place, masks):
+    (rows, depth), half = inverses[0].shape, parts[0].shape[1]
     chunks = chunks_of(update_rows, half, masks) if masks else [(aval(update_rows, half, BF16), True)]
     outs = chunks + [(aval(rows, half, BF16), True)] * 2
     turned = panels[0].shape[0] != update_rows
     return kernel_call(
-        functools.partial(half_kernel, plan, turned, at_place, len(chunks)),
+        functools.partial(half_kernel, plan, turned, at_place, len(chunks), len(parts)),
         outs + in_vmem(nexts),
         scalars,
-        [mine, *inverses, *panels],
+        [*parts, *inverses, *panels],
         [*pieces, *nexts],
         [
             pltpu.VMEM((depth, half), BF16),
@@ -441,11 +457,10 @@
         [pltpu.VMEM((sum(sizes), cols), BF16), pltpu.SemaphoreType.DMA((len(loads),))],
     )
     received = permute(send, 1)
-    scalars, keep, received, sibling, inverse_third, panel_third = tie(
-        (scalars, keep, received, sibling, inverse_third, panel_third)
+    scalars, keep, received, sibling, inverse_third = tie(
+        (scalars, keep, received, sibling, inverse_third)
     )
     inverses = inverse_third, permute(inverse_third, 1)
-    panels = panel_third, permute(panel_third, 1)
     acc, far, panel = kernel_call(
         near_kernel,
         [
@@ -478,8 +493,8 @@
     half_fourth = jnp.concatenate([half_fourth, by_z2], 0)
     x_third = permute(own_third, mask_x)
     by_z1 = permute(half_fourth, mask_z1)
-    shards, acc, far, panel, own_second, x_second, inverses, panels = tie(
-        (shards, acc, far, panel, own_second, x_second, inverses, panels)
+    shards, acc, far, panel, own_second, x_second, inverses = tie(
+        (shards, acc, far, panel, own_second, x_second, inverses)
     )
 
     pieces = [v for shard in shards for v in (shard, permute(shard, 1))]
@@ -504,6 +519,8 @@
     )
     keep, send, y_second, by_z1, x_third = tie((keep, send, y_second, by_z1, x_third))
     chunks = pair_sum(keep, send, scalars, at_place, column)
+    chunks, panel_third = tie((chunks, panel_third))
+    panels = panel_third, permute(panel_third, 1)
 
     def with_x(x_piece, own, y_pieces):
         pieces = [own, x_piece]
@@ -523,14 +540,16 @@
     def spread(value):
         return lax.all_gather(value, PLANE, axis=0, tiled=True)
 
-    def plan_of(level, chunk, both):
+    def spread_both(own, sib):
+        both = jnp.concatenate([own, sib], 0)
+        return [both] + [permute(both, mask) for mask in plane[1:]]
+
+    def plan_of(level, chunk):
         unit = math.gcd(chunk, block)
-        places = []
-        for place in range(2 * n_y):
-            for child in range(2) if both else [place // n_y]:
-                start = (place if both else place % n_y) * chunk
-                for row in range(start, start + chunk, unit):
-                    places.append((child * width + row // block, row % block))
+        places = width, at_place + 1
+        if level == 0:
+            rows = [divmod(row, block) for row in range(0, update_rows, unit)]
+            places = [(child * width + i, row) for child in range(2) for i, row in rows]
         n_next = 4 if level < 2 else 0
         return unit, places, block, at_table[level], at_order[level], 2 * sizes[level], n_pieces, n_next
 
@@ -549,7 +568,7 @@
     y_third = [permute(own_third, mask) for mask in y_masks]
     solved_second, keep, send, *nexts = solve_whole(
         scalars,
-        plan_of(0, part.shape[0], False),
+        plan_of(0, part.shape[0]),
         mine,
         other,
         inverse_second,
@@ -575,12 +594,11 @@
     part, sibling, pieces_third, fourth, y_fourth = tie(
         (part, sibling, pieces_third, fourth, y_fourth)
     )
-    mine = spread(jnp.concatenate([part, sibling], 0))
-    mine, own_fourth = tie((mine, own_fourth))
+    parts = spread_both(part, sibling)
     *chunks, keep, send, a, b, c, d = solve_half(
         scalars,
-        plan_of(1, part.shape[0], True),
-        mine,
+        plan_of(1, part.shape[0]),
+        parts,
         nexts[:2],
         nexts[2:],
         pieces_third,
@@ -599,11 +617,11 @@
     part = (part.astype(F32) + permute(part, mask_z1).astype(F32)).astype(BF16)
     sibling = permute(part, mask_z2)
     part, sibling, pieces_fourth, halves_third = tie((part, sibling, pieces_fourth, halves_third))
-    mine = spread(jnp.concatenate([part, sibling], 0))
+    parts = spread_both(part, sibling)
     update, keep_fourth, send_fourth = solve_half(
         scalars,
-        plan_of(2, part.shape[0], True),
-        mine,
+        plan_of(2, part.shape[0]),
+        parts,
         fourth[:2],
         fourth[2:],
         pieces_fourth,
@@ -616,6 +634,8 @@
     everywhere = ("z2", "z1", "x", "y")
     count = lax.axis_size(everywhere)
     arrived = lax.all_to_all(update, everywhere, 0, 0, tiled=True)
+    solved_third, solved_fourth = join_columns(scalars, [halves_third, halves_fourth])
+    arrived, solved_third, solved_fourth = tie((arrived, solved_third, solved_fourth))
     chunk = update_rows // count
     keep, send = kernel_call(
         functools.partial(core_split_kernel, count),
@@ -624,7 +644,6 @@
         [arrived],
         scratch=[pltpu.VMEM((chunk, half), F32)],
     )
-    solved_third, solved_fourth = join_columns(scalars, [halves_third, halves_fourth])
     ancestor = join_columns(scalars, [(keep, permute(send, 1))])[0]
     return solved_first, solved_second, solved_third, solved_fourth, ancestor
 

time: 176 us -> 172 us (0.977)
  blocking collectives: 35.9 us -> 12.3 us
  starting transfers between devices: 42.9 us -> 53 us
  waiting for transfers between devices: 51.5 us -> 60 us
    all_gather x3 -> x1, blocking collectives: 35.9 us -> 12.3 us  [spread(): return lax.all_gather(value, PLANE, axis=0, tiled=True)]
    ppermute x40 -> x46, waiting for transfers between devices: 41.9 us -> 53 us  [permute(): return lax.ppermute(value, AXES, pairs)]
    ppermute x40 -> x46, starting transfers between devices: 37.8 us -> 47.2 us  [permute(): return lax.ppermute(value, AXES, pairs)]
    all_to_all x1, waiting for transfers between devices: 9.55 us -> 7.04 us  [per_device(): arrived = lax.all_to_all(update, everywhere, 0, 0, tiled=True)]
  transfers between devices with their start and end apart: 41 -> 47, of which waited for: 21 -> 29; matrix products, arithmetic and copies ran while one was open for 1% -> 1% of each run, Pallas kernels for 15% -> 15%
where the time goes in v6:
time: 172 us; the launch traced here: 171 us
  waiting for transfers between devices  60 us (35%)
  starting transfers between devices  53 us (31%)
  Pallas kernels  40.8 us (24%)
  blocking collectives  12.3 us (7%)
  local copies, waits for them, and re-layouts  3.84 us (2%)
    ppermute x46, waiting for transfers between devices, permute(): return lax.ppermute(value, AXES, pairs)  53 us
    ppermute x46, starting transfers between devices, permute(): return lax.ppermute(value, AXES, pairs)  47.2 us
    pallas_call x15, Pallas kernels, kernel_call(): pl.pallas_call(kernel, out_shape=[pltpu.VMEM(o.shape, o.dtype) if inside...  40.8 us
    all_gather x1, blocking collectives, spread(): return lax.all_gather(value, PLANE, axis=0, tiled=True)  12.3 us
    all_to_all x1, waiting for transfers between devices, per_device(): arrived = lax.all_to_all(update, everywhere, 0, 0, tiled=True)  7.04 us
    all_to_all x1, starting transfers between devices, per_device(): arrived = lax.all_to_all(update, everywhere, 0, 0, tiled=True)  5.8 us
  transfers between devices with their start and end apart: 47, of which 29 were waited for; matrix products, arithmetic and copies ran while one was open for 1% of the time, Pallas kernels for 15%

profile of v6, /device:TPU:0, one launch (start us, length us, event | category | flops | bytes accessed | tf_op | source)
XLA Modules:
  0.0 171.1 jit_solution(14434765260516737183)
XLA Ops:
  4.7 4.5 %collective-permute-start.2 = (bf16[1536,256]{1,0:T(8,128)(2,1)}, bf16[1536,256]{1,0:T(8,128)(2,1)S(1)}, u32[]{:S(2)}, u32[]{:S(2)}) collective-permute-start(bf16[1536,256]{1,0:T(8,128)(2,1)} %b0.1), channel_id=1, source_target_pairs={{0,2},{1,3},{4,6},{5,7},{8,10},{9,11},{12,14},{13,15},{16,18},{17,... | collective-permute-start | bytes 2359304 | tf_op jit(solution)/shard_map/ppermute | solution.py:25
  11.4 1.6 collective-permute-start.3
  13.0 2.6 %collective-permute-start.4 = (bf16[384,128]{1,0:T(8,128)(2,1)S(1)}, bf16[384,128]{1,0:T(8,128)(2,1)S(1)}, u32[]{:S(2)}, u32[]{:S(2)}) collective-permute-start(bf16[384,128]{1,0:T(8,128)(2,1)S(1)} %get-tuple-element.147), channel_id=1, source_target_pairs={{0,16},{1,17},{2,18},{3,19},{4,20},{5,21},{6,22},{7,23},{8,24},{9,... | collective-permute-start | bytes 294920 | tf_op jit(solution)/shard_map/ppermute | solution.py:25
  16.7 8.5 %shard_map.183 = (f32[1536,256]{1,0:T(8,128)S(1)}, bf16[1536,3072]{1,0:T(8,128)(2,1)S(1)}, bf16[1536,1536]{1,0:T(8,128)(2,1)S(1)}) custom-call(s32[111]{0:T(128)S(1)} %concatenate.19.scalars, bf16[1536,256]{1,0:T(8,128)(2,1)S(1)} %copy-done, bf16[1536,256]{1,0:T(8,128)(2,1)S(1)} %collective-permute-done.1.b1, bf16[1536,6144]{1,0:T(8,128)(2,1)} %inverse.1, ...), custom_call_target="tpu_custom_call" | custom-call | flops 1 | bytes 1 | tf_op jit(solution)/shard_map/pallas_call | solution.py:38
  25.2 1.7 collective-permute-done.2.refs_0_
  28.6 2.4 %collective-permute-start.8 = (bf16[1536,128]{1,0:T(8,128)(2,1)S(1)}, bf16[1536,128]{1,0:T(8,128)(2,1)S(1)}, u32[]{:S(2)}, u32[]{:S(2)}) collective-permute-start(bf16[1536,128]{1,0:T(8,128)(2,1)S(1)} %get-tuple-element.185.refs_0_), channel_id=1, source_target_pairs={{0,2},{1,3},{2,0},{3,1},{4,6},{5,7},{6,4},{7,5},{8,10},{9,11},{10,... | collective-permute-start | bytes 1179656 | tf_op jit(solution)/shard_map/ppermute | solution.py:25
  31.0 1.6 collective-permute-start.9
  32.7 5.2 %shard_map.185 = (bf16[1536,256]{1,0:T(8,128)(2,1)}, f32[1536,128]{1,0:T(8,128)S(1)}, bf16[1536,128]{1,0:T(8,128)(2,1)S(1)}, bf16[768,6144]{1,0:T(8,128)(2,1)S(1)}, bf16[1536,768]{1,0:T(8,128)(2,1)S(1)}) custom-call(s32[111]{0:T(128)S(1)} %concatenate.19.scalars, f32[1536,256]{1,0:T(8,128)S(1)} %get-tuple-element.153.acc, ...), custom_call_target="tpu_custom_call" | custom-call | flops 1 | bytes 1 | tf_op jit(solution)/shard_map/pallas_call | solution.py:38
  38.7 1.8 %collective-permute-done.8.refs_2_ = bf16[1536,128]{1,0:T(8,128)(2,1)S(1)} collective-permute-done((bf16[1536,128]{1,0:T(8,128)(2,1)S(1)}, bf16[1536,128]{1,0:T(8,128)(2,1)S(1)}, u32[]{:S(2)}, u32[]{:S(2)}) %collective-permute-start.8) | collective-permute-done | bytes 393248 | tf_op jit(solution)/shard_map/ppermute | solution.py:25
  42.9 1.8 %collective-permute-start.12 = (bf16[768,128]{1,0:T(8,128)(2,1)S(1)}, bf16[768,128]{1,0:T(8,128)(2,1)S(1)}, u32[]{:S(2)}, u32[]{:S(2)}) collective-permute-start(bf16[768,128]{1,0:T(8,128)(2,1)S(1)} %get-tuple-element.168), channel_id=1, source_target_pairs={{0,2},{1,3},{2,0},{3,1},{4,6},{5,7},{6,4},{7,5},{8,10},{9,11},{10,... | collective-permute-start | bytes 589832 | tf_op jit(solution)/shard_map/ppermute | solution.py:25
  44.8 5.2 %collective-permute-done.12.rest_0_ = bf16[768,128]{1,0:T(8,128)(2,1)S(1)} collective-permute-done((bf16[768,128]{1,0:T(8,128)(2,1)S(1)}, bf16[768,128]{1,0:T(8,128)(2,1)S(1)}, u32[]{:S(2)}, u32[]{:S(2)}) %collective-permute-start.12) | collective-permute-done | bytes 196640 | tf_op jit(solution)/shard_map/ppermute | solution.py:25
  50.6 2.0 %collective-permute-done.13.refs_3_ = bf16[1536,128]{1,0:T(8,128)(2,1)S(1)} collective-permute-done((bf16[1536,128]{1,0:T(8,128)(2,1)S(1)}, bf16[1536,128]{1,0:T(8,128)(2,1)S(1)}, u32[]{:S(2)}, u32[]{:S(2)}) %collective-permute-start.13) | collective-permute-done | bytes 393248 | tf_op jit(solution)/shard_map/ppermute | solution.py:25
  53.1 12.3 %all_gather.3.mine = bf16[3072,128]{1,0:T(8,128)(2,1)S(1)} all-gather(bf16[768,128]{1,0:T(8,128)(2,1)S(1)} %shard_map.187), channel_id=1, replica_groups=mesh['hi'=1,'z2'=2,'z1'=2,'x'=2,'y'=2,'core'=2] {'x','y'}, dimensions={0}, use_global_device_ids=true | all-gather | bytes 983040 | tf_op jit(solution)/shard_map/all_gather | solution.py:541
  68.7 7.3 %shard_map.188 = (bf16[768,256]{1,0:T(8,128)(2,1)}, f32[1536,128]{1,0:T(8,128)S(1)}, bf16[1536,128]{1,0:T(8,128)(2,1)S(1)}, bf16[384,6144]{1,0:T(8,128)(2,1)S(1)...) custom-call(s32[111]{0:T(128)S(1)} %concatenate.19.scalars, ...), custom_call_target="tpu_custom_call" | custom-call | flops 1 | bytes 1 | tf_op jit(solution)/shard_map/pallas_call | solution.py:38
  77.4 1.7 %collective-permute-done.22.received = bf16[1536,128]{1,0:T(8,128)(2,1)S(1)} collective-permute-done((bf16[1536,128]{1,0:T(8,128)(2,1)S(1)}, bf16[1536,128]{1,0:T(8,128)(2,1)S(1)}, u32[]{:S(2)}, u32[]{:S(2)}) %collective-permute-start.22) | collective-permute-done | bytes 393248 | tf_op jit(solution)/shard_map/ppermute | solution.py:25
  85.2 2.3 %collective-permute-done.24.rest_1_ = bf16[384,128]{1,0:T(8,128)(2,1)S(1)} collective-permute-done((bf16[384,128]{1,0:T(8,128)(2,1)S(1)}, bf16[384,128]{1,0:T(8,128)(2,1)S(1)}, u32[]{:S(2)}, u32[]{:S(2)}) %collective-permute-start.24) | collective-permute-done | bytes 98336 | tf_op jit(solution)/shard_map/ppermute | solution.py:25
  92.8 3.0 %collective-permute-done.26 = bf16[384,128]{1,0:T(8,128)(2,1)S(1)} collective-permute-done((bf16[384,128]{1,0:T(8,128)(2,1)S(1)}, bf16[384,128]{1,0:T(8,128)(2,1)S(1)}, u32[]{:S(2)}, u32[]{:S(2)}) %collective-permute-start.26) | collective-permute-done | bytes 98336 | tf_op jit(solution)/shard_map/ppermute | solution.py:25
  95.8 3.5 %collective-permute-done.27.refs_11_ = bf16[1536,128]{1,0:T(8,128)(2,1)S(1)} collective-permute-done((bf16[1536,128]{1,0:T(8,128)(2,1)S(1)}, bf16[1536,128]{1,0:T(8,128)(2,1)S(1)}, u32[]{:S(2)}, u32[]{:S(2)}) %collective-permute-start.27) | collective-permute-done | bytes 393248 | tf_op jit(solution)/shard_map/ppermute | solution.py:25
  104.2 4.3 %collective-permute-done.31.refs_1_ = bf16[768,128]{1,0:T(8,128)(2,1)S(1)} collective-permute-done((bf16[768,128]{1,0:T(8,128)(2,1)S(1)}, bf16[768,128]{1,0:T(8,128)(2,1)S(1)}, u32[]{:S(2)}, u32[]{:S(2)}) %collective-permute-start.31) | collective-permute-done | bytes 196640 | tf_op jit(solution)/shard_map/ppermute | solution.py:25
  108.5 2.4 %collective-permute-done.33.refs_3_ = bf16[768,128]{1,0:T(8,128)(2,1)S(1)} collective-permute-done((bf16[768,128]{1,0:T(8,128)(2,1)S(1)}, bf16[768,128]{1,0:T(8,128)(2,1)S(1)}, u32[]{:S(2)}, u32[]{:S(2)}) %collective-permute-start.33) | collective-permute-done | bytes 196640 | tf_op jit(solution)/shard_map/ppermute | solution.py:25
  110.9 6.1 %shard_map.191 = (f32[384,128]{1,0:T(8,128)S(1)}, bf16[384,128]{1,0:T(8,128)(2,1)S(1)}, bf16[384,128]{1,0:T(8,128)(2,1)S(1)}, bf16[384,128]{1,0:T(8,128)(2,1)S(1...) custom-call(s32[111]{0:T(128)S(1)} %concatenate.19.scalars, ...), custom_call_target="tpu_custom_call" | custom-call | flops 1 | bytes 1 | tf_op jit(solution)/shard_map/pallas_call | solution.py:38
  122.2 3.0 %collective-permute-done.36.rest_2_ = bf16[384,128]{1,0:T(8,128)(2,1)S(1)} collective-permute-done((bf16[384,128]{1,0:T(8,128)(2,1)S(1)}, bf16[384,128]{1,0:T(8,128)(2,1)S(1)}, u32[]{:S(2)}, u32[]{:S(2)}) %collective-permute-start.36) | collective-permute-done | bytes 98336 | tf_op jit(solution)/shard_map/ppermute | solution.py:25
  125.9 1.9 %collective-permute-start.37 = (bf16[384,128]{1,0:T(8,128)(2,1)S(1)}, bf16[384,128]{1,0:T(8,128)(2,1)S(1)}, u32[]{:S(2)}, u32[]{:S(2)}) collective-permute-start(bf16[384,128]{1,0:T(8,128)(2,1)S(1)} %shard_map.192), channel_id=1, source_target_pairs={{0,8},{1,9},{2,10},{3,11},{4,12},{5,13},{6,14},{7,15},{8,0},{9,1},... | collective-permute-start | bytes 294920 | tf_op jit(solution)/shard_map/ppermute | solution.py:25
  128.3 2.2 %collective-permute-done.37 = bf16[384,128]{1,0:T(8,128)(2,1)S(1)} collective-permute-done((bf16[384,128]{1,0:T(8,128)(2,1)S(1)}, bf16[384,128]{1,0:T(8,128)(2,1)S(1)}, u32[]{:S(2)}, u32[]{:S(2)}) %collective-permute-start.37) | collective-permute-done | bytes 98336 | tf_op jit(solution)/shard_map/ppermute | solution.py:25
  130.6 3.4 %collective-permute-start.38 = (bf16[384,128]{1,0:T(8,128)(2,1)S(1)}, bf16[384,128]{1,0:T(8,128)(2,1)S(1)}, u32[]{:S(2)}, u32[]{:S(2)}) collective-permute-start(bf16[384,128]{1,0:T(8,128)(2,1)S(1)} %add_convert_fusion), channel_id=1, source_target_pairs={{0,16},{1,17},{2,18},{3,19},{4,20},{5,21},{6,22},{7,23},{8,24},{9,... | collective-permute-start | bytes 294920 | tf_op jit(solution)/shard_map/ppermute | solution.py:25
  134.0 3.6 %collective-permute-done.38 = bf16[384,128]{1,0:T(8,128)(2,1)S(1)} collective-permute-done((bf16[384,128]{1,0:T(8,128)(2,1)S(1)}, bf16[384,128]{1,0:T(8,128)(2,1)S(1)}, u32[]{:S(2)}, u32[]{:S(2)}) %collective-permute-start.38) | collective-permute-done | bytes 98336 | tf_op jit(solution)/shard_map/ppermute | solution.py:25
  137.7 2.0 %collective-permute-start.42 = (bf16[768,128]{1,0:T(8,128)(2,1)S(1)}, bf16[768,128]{1,0:T(8,128)(2,1)S(1)}, u32[]{:S(2)}, u32[]{:S(2)}) collective-permute-start(bf16[768,128]{1,0:T(8,128)(2,1)S(1)} %constant_dynamic-update-slice_fusion.4.refs_0_), channel_id=1, source_target_pairs={{0,4},{1,5},{2,6},{3,7},{4,0},{5,1},{6,2},{7,3},{8,12},{9,13},{10,... | collective-permute-start | bytes 589832 | tf_op jit(solution)/shard_map/ppermute | solution.py:25
  141.2 3.2 %collective-permute-done.41.refs_1_ = bf16[768,128]{1,0:T(8,128)(2,1)S(1)} collective-permute-done((bf16[768,128]{1,0:T(8,128)(2,1)S(1)}, bf16[768,128]{1,0:T(8,128)(2,1)S(1)}, u32[]{:S(2)}, u32[]{:S(2)}) %collective-permute-start.41) | collective-permute-done | bytes 196640 | tf_op jit(solution)/shard_map/ppermute | solution.py:25
  144.6 2.3 %collective-permute-done.43.refs_3_ = bf16[768,128]{1,0:T(8,128)(2,1)S(1)} collective-permute-done((bf16[768,128]{1,0:T(8,128)(2,1)S(1)}, bf16[768,128]{1,0:T(8,128)(2,1)S(1)}, u32[]{:S(2)}, u32[]{:S(2)}) %collective-permute-start.43) | collective-permute-done | bytes 196640 | tf_op jit(solution)/shard_map/ppermute | solution.py:25
  147.0 5.7 %shard_map.193 = (bf16[1536,128]{1,0:T(8,128)(2,1)}, bf16[192,128]{1,0:T(8,128)(2,1)S(1)}, bf16[192,128]{1,0:T(8,128)(2,1)S(1)}) custom-call(s32[111]{0:T(128)S(1)} %concatenate.19.scalars, bf16[768,128]{1,0:T(8,128)(2,1)S(1)} %constant_dynamic-update-slice_fusion.4.refs_0_, bf16[768,128]{1,0:T(8,128)(2,1)S(1)} %collective-permute-done.41.refs_1_, ...), custom_call_target="tpu_custom_call" | custom-call | flops 1 | bytes 1 | tf_op jit(solution)/shard_map/pallas_call | solution.py:38
  152.7 5.8 %all-to-all-start = ((bf16[16,96,128]{2,1,0:T(8,128)(2,1)}), bf16[16,96,128]{2,1,0:T(8,128)(2,1)S(1)}, u32[]{:S(2)}, u32[]{:S(2)}) async-start(bf16[16,96,128]{2,1,0:T(8,128)(2,1)} %bitcast.41), calls=%async_computation | async-start | bytes 786432 | tf_op jit(solution)/shard_map/all_to_all | solution.py:636
  161.1 7.0 %all-to-all-done = bf16[16,96,128]{2,1,0:T(8,128)(2,1)S(1)} async-done(((bf16[16,96,128]{2,1,0:T(8,128)(2,1)}), bf16[16,96,128]{2,1,0:T(8,128)(2,1)S(1)}, u32[]{:S(2)}, u32[]{:S(2)}) %all-to-all-start) | async-done | bytes 393248 | tf_op jit(solution)/shard_map/all_to_all | solution.py:636
  (138 shorter events, 47.9 us)
Async XLA Ops:
  4.2 22.7 %collective-permute-start.6 = (bf16[384,6144]{1,0:T(8,128)(2,1)}, bf16[384,6144]{1,0:T(8,128)(2,1)S(1)}, u32[]{:S(2)}, u32[]{:S(2)}) collective-permute-start(bf16[384,6144]{1,0:T(8,128)(2,1)} %refs_8_), channel_id=1, source_target_pairs={{0,1},{1,0},{2,3},{3,2},{4,5},{5,4},{6,7},{7,6},{8,9},{9,8},{10,11... | collective-permute-start | bytes 14155784 | tf_op jit(solution)/shard_map/ppermute | solution.py:25
  4.7 22.2 %collective-permute-start.2 = (bf16[1536,256]{1,0:T(8,128)(2,1)}, bf16[1536,256]{1,0:T(8,128)(2,1)S(1)}, u32[]{:S(2)}, u32[]{:S(2)}) collective-permute-start(bf16[1536,256]{1,0:T(8,128)(2,1)} %b0.1), channel_id=1, source_target_pairs={{0,2},{1,3},{4,6},{5,7},{8,10},{9,11},{12,14},{13,15},{16,18},{17,... | collective-permute-start | bytes 2359304 | tf_op jit(solution)/shard_map/ppermute | solution.py:25
  9.9 17.0 %collective-permute-start.5 = (bf16[1536,128]{1,0:T(8,128)(2,1)S(1)}, bf16[1536,128]{1,0:T(8,128)(2,1)S(1)}, u32[]{:S(2)}, u32[]{:S(2)}) collective-permute-start(bf16[1536,128]{1,0:T(8,128)(2,1)S(1)} %get-tuple-element.185.refs_0_), channel_id=1, source_target_pairs={{0,4},{1,5},{2,6},{3,7},{4,0},{5,1},{6,2},{7,3},{8,12},{9,13},{10,... | collective-permute-start | bytes 1179656 | tf_op jit(solution)/shard_map/ppermute | solution.py:25
  11.4 13.8 %collective-permute-start.3 = (bf16[768,128]{1,0:T(8,128)(2,1)S(1)}, bf16[768,128]{1,0:T(8,128)(2,1)S(1)}, u32[]{:S(2)}, u32[]{:S(2)}) collective-permute-start(bf16[768,128]{1,0:T(8,128)(2,1)S(1)} %get-tuple-element.146), channel_id=1, source_target_pairs={{0,8},{1,9},{2,10},{3,11},{4,12},{5,13},{6,14},{7,15},{8,0},{9,1},... | collective-permute-start | bytes 589832 | tf_op jit(solution)/shard_map/ppermute | solution.py:25
  13.0 12.2 %collective-permute-start.4 = (bf16[384,128]{1,0:T(8,128)(2,1)S(1)}, bf16[384,128]{1,0:T(8,128)(2,1)S(1)}, u32[]{:S(2)}, u32[]{:S(2)}) collective-permute-start(bf16[384,128]{1,0:T(8,128)(2,1)S(1)} %get-tuple-element.147), channel_id=1, source_target_pairs={{0,16},{1,17},{2,18},{3,19},{4,20},{5,21},{6,22},{7,23},{8,24},{9,... | collective-permute-start | bytes 294920 | tf_op jit(solution)/shard_map/ppermute | solution.py:25
  27.1 11.6 %collective-permute-start.10 = (bf16[1536,128]{1,0:T(8,128)(2,1)S(1)}, bf16[1536,128]{1,0:T(8,128)(2,1)S(1)}, u32[]{:S(2)}, u32[]{:S(2)}) collective-permute-start(bf16[1536,128]{1,0:T(8,128)(2,1)S(1)} %constant_dynamic-update-slice_fusion.refs_8_), channel_id=1, source_target_pairs={{0,4},{1,5},{2,6},{3,7},{4,0},{5,1},{6,2},{7,3},{8,12},{9,13},{10,... | collective-permute-start | bytes 1179656 | tf_op jit(solution)/shard_map/ppermute | solution.py:25
  28.6 11.9 %collective-permute-start.8 = (bf16[1536,128]{1,0:T(8,128)(2,1)S(1)}, bf16[1536,128]{1,0:T(8,128)(2,1)S(1)}, u32[]{:S(2)}, u32[]{:S(2)}) collective-permute-start(bf16[1536,128]{1,0:T(8,128)(2,1)S(1)} %get-tuple-element.185.refs_0_), channel_id=1, source_target_pairs={{0,2},{1,3},{2,0},{3,1},{4,6},{5,7},{6,4},{7,5},{8,10},{9,11},{10,... | collective-permute-start | bytes 1179656 | tf_op jit(solution)/shard_map/ppermute | solution.py:25
  31.0 6.9 %collective-permute-start.9 = (bf16[768,128]{1,0:T(8,128)(2,1)S(1)}, bf16[768,128]{1,0:T(8,128)(2,1)S(1)}, u32[]{:S(2)}, u32[]{:S(2)}) collective-permute-start(bf16[768,128]{1,0:T(8,128)(2,1)S(1)} %pad_maximum_fusion.1), channel_id=1, source_target_pairs={{0,8},{1,9},{2,10},{3,11},{4,12},{5,13},{6,14},{7,15},{8,0},{9,1},... | collective-permute-start | bytes 589832 | tf_op jit(solution)/shard_map/ppermute | solution.py:25
  40.5 10.0 %collective-permute-start.14 = (bf16[1536,128]{1,0:T(8,128)(2,1)S(1)}, bf16[1536,128]{1,0:T(8,128)(2,1)S(1)}, u32[]{:S(2)}, u32[]{:S(2)}) collective-permute-start(bf16[1536,128]{1,0:T(8,128)(2,1)S(1)} %get-tuple-element.185.refs_0_), channel_id=1, source_target_pairs={{0,1},{1,0},{2,3},{3,2},{4,5},{5,4},{6,7},{7,6},{8,9},{9,8},{10,11... | collective-permute-start | bytes 1179656 | tf_op jit(solution)/shard_map/ppermute | solution.py:25
  41.0 9.5 %collective-permute-start.15 = (bf16[1536,128]{1,0:T(8,128)(2,1)S(1)}, bf16[1536,128]{1,0:T(8,128)(2,1)S(1)}, u32[]{:S(2)}, u32[]{:S(2)}) collective-permute-start(bf16[1536,128]{1,0:T(8,128)(2,1)S(1)} %collective-permute-done.5.refs_1_), channel_id=1, source_target_pairs={{0,1},{1,0},{2,3},{3,2},{4,5},{5,4},{6,7},{7,6},{8,9},{9,8},{10,11... | collective-permute-start | bytes 1179656 | tf_op jit(solution)/shard_map/ppermute | solution.py:25
  41.1 11.5 %collective-permute-start.13 = (bf16[1536,128]{1,0:T(8,128)(2,1)S(1)}, bf16[1536,128]{1,0:T(8,128)(2,1)S(1)}, u32[]{:S(2)}, u32[]{:S(2)}) collective-permute-start(bf16[1536,128]{1,0:T(8,128)(2,1)S(1)} %collective-permute-done.8.refs_2_), channel_id=1, source_target_pairs={{0,4},{1,5},{2,6},{3,7},{4,0},{5,1},{6,2},{7,3},{8,12},{9,13},{10,... | collective-permute-start | bytes 1179656 | tf_op jit(solution)/shard_map/ppermute | solution.py:25
  41.6 10.9 %collective-permute-start.16 = (bf16[1536,128]{1,0:T(8,128)(2,1)S(1)}, bf16[1536,128]{1,0:T(8,128)(2,1)S(1)}, u32[]{:S(2)}, u32[]{:S(2)}) collective-permute-start(bf16[1536,128]{1,0:T(8,128)(2,1)S(1)} %collective-permute-done.8.refs_2_), channel_id=1, source_target_pairs={{0,1},{1,0},{2,3},{3,2},{4,5},{5,4},{6,7},{7,6},{8,9},{9,8},{10,11... | collective-permute-start | bytes 1179656 | tf_op jit(solution)/shard_map/ppermute | solution.py:25
  42.9 7.0 %collective-permute-start.12 = (bf16[768,128]{1,0:T(8,128)(2,1)S(1)}, bf16[768,128]{1,0:T(8,128)(2,1)S(1)}, u32[]{:S(2)}, u32[]{:S(2)}) collective-permute-start(bf16[768,128]{1,0:T(8,128)(2,1)S(1)} %get-tuple-element.168), channel_id=1, source_target_pairs={{0,2},{1,3},{2,0},{3,1},{4,6},{5,7},{6,4},{7,5},{8,10},{9,11},{10,... | collective-permute-start | bytes 589832 | tf_op jit(solution)/shard_map/ppermute | solution.py:25
  52.6 12.9 %collective-permute-start.17 = (bf16[1536,128]{1,0:T(8,128)(2,1)S(1)}, bf16[1536,128]{1,0:T(8,128)(2,1)S(1)}, u32[]{:S(2)}, u32[]{:S(2)}) collective-permute-start(bf16[1536,128]{1,0:T(8,128)(2,1)S(1)} %collective-permute-done.13.refs_3_), channel_id=1, source_target_pairs={{0,1},{1,0},{2,3},{3,2},{4,5},{5,4},{6,7},{7,6},{8,9},{9,8},{10,11... | collective-permute-start | bytes 1179656 | tf_op jit(solution)/shard_map/ppermute | solution.py:25
  52.6 15.0 %collective-permute-start.19 = (bf16[1536,384]{1,0:T(8,128)(2,1)S(1)}, bf16[1536,384]{1,0:T(8,128)(2,1)S(1)}, u32[]{:S(2)}, u32[]{:S(2)}) collective-permute-start(bf16[1536,384]{1,0:T(8,128)(2,1)S(1)} %copy-done.6), channel_id=1, source_target_pairs={{0,1},{1,0},{2,3},{3,2},{4,5},{5,4},{6,7},{7,6},{8,9},{9,8},{10,11... | collective-permute-start | bytes 3538952 | tf_op jit(solution)/shard_map/ppermute | solution.py:25
  65.6 11.5 %collective-permute-start.20 = (bf16[1536,128]{1,0:T(8,128)(2,1)S(1)}, bf16[1536,128]{1,0:T(8,128)(2,1)S(1)}, u32[]{:S(2)}, u32[]{:S(2)}) collective-permute-start(bf16[1536,128]{1,0:T(8,128)(2,1)S(1)} %pad_maximum_fusion.refs_8_), channel_id=1, source_target_pairs={{0,4},{1,5},{2,6},{3,7},{4,0},{5,1},{6,2},{7,3},{8,12},{9,13},{10,... | collective-permute-start | bytes 1179656 | tf_op jit(solution)/shard_map/ppermute | solution.py:25
  66.2 11.2 %collective-permute-start.21 = (bf16[1536,128]{1,0:T(8,128)(2,1)S(1)}, bf16[1536,128]{1,0:T(8,128)(2,1)S(1)}, u32[]{:S(2)}, u32[]{:S(2)}) collective-permute-start(bf16[1536,128]{1,0:T(8,128)(2,1)S(1)} %constant_dynamic-update-slice_fusion.refs_8_), channel_id=1, source_target_pairs={{0,2},{1,3},{2,0},{3,1},{4,6},{5,7},{6,4},{7,5},{8,10},{9,11},{10,... | collective-permute-start | bytes 1179656 | tf_op jit(solution)/shard_map/ppermute | solution.py:25
  79.8 20.8 %collective-permute-start.28 = (bf16[192,6144]{1,0:T(8,128)(2,1)S(1)}, bf16[192,6144]{1,0:T(8,128)(2,1)S(1)}, u32[]{:S(2)}, u32[]{:S(2)}) collective-permute-start(bf16[192,6144]{1,0:T(8,128)(2,1)S(1)} %copy-done.3), channel_id=1, source_target_pairs={{0,1},{1,0},{2,3},{3,2},{4,5},{5,4},{6,7},{7,6},{8,9},{9,8},{10,11... | collective-permute-start | bytes 7077896 | tf_op jit(solution)/shard_map/ppermute | solution.py:25
  80.0 20.6 %collective-permute-start.29 = (bf16[192,1536]{1,0:T(8,128)(2,1)S(1)}, bf16[192,1536]{1,0:T(8,128)(2,1)S(1)}, u32[]{:S(2)}, u32[]{:S(2)}) collective-permute-start(bf16[192,1536]{1,0:T(8,128)(2,1)S(1)} %bitcast.51), channel_id=1, source_target_pairs={{0,1},{1,0},{2,3},{3,2},{4,5},{5,4},{6,7},{7,6},{8,9},{9,8},{10,11... | collective-permute-start | bytes 1769480 | tf_op jit(solution)/shard_map/ppermute | solution.py:25
  82.4 6.2 %collective-permute-start.25 = (bf16[384,128]{1,0:T(8,128)(2,1)S(1)}, bf16[384,128]{1,0:T(8,128)(2,1)S(1)}, u32[]{:S(2)}, u32[]{:S(2)}) collective-permute-start(bf16[384,128]{1,0:T(8,128)(2,1)S(1)} %get-tuple-element.211), channel_id=1, source_target_pairs={{0,6},{1,7},{2,4},{3,5},{4,2},{5,3},{6,0},{7,1},{8,14},{9,15},{10,... | collective-permute-start | bytes 294920 | tf_op jit(solution)/shard_map/ppermute | solution.py:25
  89.1 10.2 %collective-permute-start.27 = (bf16[1536,128]{1,0:T(8,128)(2,1)S(1)}, bf16[1536,128]{1,0:T(8,128)(2,1)S(1)}, u32[]{:S(2)}, u32[]{:S(2)}) collective-permute-start(bf16[1536,128]{1,0:T(8,128)(2,1)S(1)} %collective-permute-done.21.refs_10_), channel_id=1, source_target_pairs={{0,4},{1,5},{2,6},{3,7},{4,0},{5,1},{6,2},{7,3},{8,12},{9,13},{10,... | collective-permute-start | bytes 1179656 | tf_op jit(solution)/shard_map/ppermute | solution.py:25
  90.7 9.9 %collective-permute-start.30 = (bf16[1536,128]{1,0:T(8,128)(2,1)S(1)}, bf16[1536,128]{1,0:T(8,128)(2,1)S(1)}, u32[]{:S(2)}, u32[]{:S(2)}) collective-permute-start(bf16[1536,128]{1,0:T(8,128)(2,1)S(1)} %pad_maximum_fusion.refs_8_), channel_id=1, source_target_pairs={{0,2},{1,3},{2,0},{3,1},{4,6},{5,7},{6,4},{7,5},{8,10},{9,11},{10,... | collective-permute-start | bytes 1179656 | tf_op jit(solution)/shard_map/ppermute | solution.py:25
  100.6 7.8 %collective-permute-start.31 = (bf16[768,128]{1,0:T(8,128)(2,1)S(1)}, bf16[768,128]{1,0:T(8,128)(2,1)S(1)}, u32[]{:S(2)}, u32[]{:S(2)}) collective-permute-start(bf16[768,128]{1,0:T(8,128)(2,1)S(1)} %constant_dynamic-update-slice_fusion.2.refs_0_), channel_id=1, source_target_pairs={{0,2},{1,3},{2,0},{3,1},{4,6},{5,7},{6,4},{7,5},{8,10},{9,11},{10,... | collective-permute-start | bytes 589832 | tf_op jit(solution)/shard_map/ppermute | solution.py:25
  101.2 7.2 %collective-permute-start.32 = (bf16[768,128]{1,0:T(8,128)(2,1)S(1)}, bf16[768,128]{1,0:T(8,128)(2,1)S(1)}, u32[]{:S(2)}, u32[]{:S(2)}) collective-permute-start(bf16[768,128]{1,0:T(8,128)(2,1)S(1)} %constant_dynamic-update-slice_fusion.2.refs_0_), channel_id=1, source_target_pairs={{0,4},{1,5},{2,6},{3,7},{4,0},{5,1},{6,2},{7,3},{8,12},{9,13},{10,... | collective-permute-start | bytes 589832 | tf_op jit(solution)/shard_map/ppermute | solution.py:25
  102.7 8.1 %collective-permute-start.33 = (bf16[768,128]{1,0:T(8,128)(2,1)S(1)}, bf16[768,128]{1,0:T(8,128)(2,1)S(1)}, u32[]{:S(2)}, u32[]{:S(2)}) collective-permute-start(bf16[768,128]{1,0:T(8,128)(2,1)S(1)} %constant_dynamic-update-slice_fusion.2.refs_0_), channel_id=1, source_target_pairs={{0,6},{1,7},{2,4},{3,5},{4,2},{5,3},{6,0},{7,1},{8,14},{9,15},{10,... | collective-permute-start | bytes 589832 | tf_op jit(solution)/shard_map/ppermute | solution.py:25
  119.1 6.2 %collective-permute-start.36 = (bf16[384,128]{1,0:T(8,128)(2,1)S(1)}, bf16[384,128]{1,0:T(8,128)(2,1)S(1)}, u32[]{:S(2)}, u32[]{:S(2)}) collective-permute-start(bf16[384,128]{1,0:T(8,128)(2,1)S(1)} %get-tuple-element.242), channel_id=1, source_target_pairs={{0,6},{1,7},{2,4},{3,5},{4,2},{5,3},{6,0},{7,1},{8,14},{9,15},{10,... | collective-permute-start | bytes 294920 | tf_op jit(solution)/shard_map/ppermute | solution.py:25
  127.8 9.8 %collective-permute-start.39 = (bf16[1536,128]{1,0:T(8,128)(2,1)S(1)}, bf16[1536,128]{1,0:T(8,128)(2,1)S(1)}, u32[]{:S(2)}, u32[]{:S(2)}) collective-permute-start(bf16[1536,128]{1,0:T(8,128)(2,1)S(1)} %collective-permute-done.30.refs_10_), channel_id=1, source_target_pairs={{0,4},{1,5},{2,6},{3,7},{4,0},{5,1},{6,2},{7,3},{8,12},{9,13},{10,... | collective-permute-start | bytes 1179656 | tf_op jit(solution)/shard_map/ppermute | solution.py:25
  130.6 7.0 %collective-permute-start.38 = (bf16[384,128]{1,0:T(8,128)(2,1)S(1)}, bf16[384,128]{1,0:T(8,128)(2,1)S(1)}, u32[]{:S(2)}, u32[]{:S(2)}) collective-permute-start(bf16[384,128]{1,0:T(8,128)(2,1)S(1)} %add_convert_fusion), channel_id=1, source_target_pairs={{0,16},{1,17},{2,18},{3,19},{4,20},{5,21},{6,22},{7,23},{8,24},{9,... | collective-permute-start | bytes 294920 | tf_op jit(solution)/shard_map/ppermute | solution.py:25
  137.7 6.7 %collective-permute-start.41 = (bf16[768,128]{1,0:T(8,128)(2,1)S(1)}, bf16[768,128]{1,0:T(8,128)(2,1)S(1)}, u32[]{:S(2)}, u32[]{:S(2)}) collective-permute-start(bf16[768,128]{1,0:T(8,128)(2,1)S(1)} %constant_dynamic-update-slice_fusion.4.refs_0_), channel_id=1, source_target_pairs={{0,2},{1,3},{2,0},{3,1},{4,6},{5,7},{6,4},{7,5},{8,10},{9,11},{10,... | collective-permute-start | bytes 589832 | tf_op jit(solution)/shard_map/ppermute | solution.py:25
  137.7 6.9 %collective-permute-start.42 = (bf16[768,128]{1,0:T(8,128)(2,1)S(1)}, bf16[768,128]{1,0:T(8,128)(2,1)S(1)}, u32[]{:S(2)}, u32[]{:S(2)}) collective-permute-start(bf16[768,128]{1,0:T(8,128)(2,1)S(1)} %constant_dynamic-update-slice_fusion.4.refs_0_), channel_id=1, source_target_pairs={{0,4},{1,5},{2,6},{3,7},{4,0},{5,1},{6,2},{7,3},{8,12},{9,13},{10,... | collective-permute-start | bytes 589832 | tf_op jit(solution)/shard_map/ppermute | solution.py:25
  139.7 7.2 %collective-permute-start.43 = (bf16[768,128]{1,0:T(8,128)(2,1)S(1)}, bf16[768,128]{1,0:T(8,128)(2,1)S(1)}, u32[]{:S(2)}, u32[]{:S(2)}) collective-permute-start(bf16[768,128]{1,0:T(8,128)(2,1)S(1)} %constant_dynamic-update-slice_fusion.4.refs_0_), channel_id=1, source_target_pairs={{0,6},{1,7},{2,4},{3,5},{4,2},{5,3},{6,0},{7,1},{8,14},{9,15},{10,... | collective-permute-start | bytes 589832 | tf_op jit(solution)/shard_map/ppermute | solution.py:25
  152.7 15.4 %all-to-all-start = ((bf16[16,96,128]{2,1,0:T(8,128)(2,1)}), bf16[16,96,128]{2,1,0:T(8,128)(2,1)S(1)}, u32[]{:S(2)}, u32[]{:S(2)}) async-start(bf16[16,96,128]{2,1,0:T(8,128)(2,1)} %bitcast.41), calls=%async_computation | async-start | bytes 786432 | tf_op jit(solution)/shard_map/all_to_all | solution.py:636
  (39 other events, 508.5 us)

commit v7 on v6

--- a/solution.py
+++ b/solution.py
@@ -579,11 +579,9 @@
     keep, send, x_fourth, y_third = tie((keep, send, x_fourth, y_third))
 
     chunks = pair_sum(keep, send, scalars, at_place + 1, plane)
-    chunks, y_third, inverse_fourth, panel_fourth = tie(
-        (chunks, y_third, inverse_fourth, panel_fourth)
-    )
+    chunks, inverse_fourth, panel_fourth = tie((chunks, inverse_fourth, panel_fourth))
     part = reduce_chunks(chunks, plane, scalars)
-    part, y_third, own_fourth = tie((part, y_third, own_fourth))
+    part, own_fourth = tie((part, own_fourth))
     sibling = permute(part, mask_z1)
     pieces_third = with_x(x_third, own_third, y_third)
     y_fourth = [permute(own_fourth, mask) for mask in y_masks]

time: 172 us -> 171 us (level)
  waiting for transfers between devices: 60 us -> 57 us
  starting transfers between devices: 53 us -> 55 us
    ppermute x46, waiting for transfers between devices: 53 us -> 50 us  [permute(): return lax.ppermute(value, AXES, pairs)]
  transfers between devices with their start and end apart: 47 -> 47, of which waited for: 29 -> 28; matrix products, arithmetic and copies ran while one was open for 1% -> 1% of each run, Pallas kernels for 15% -> 15%
where the time goes in v7:
time: 171 us; the launch traced here: 170 us
  waiting for transfers between devices  57 us (33%)
  starting transfers between devices  55 us (32%)
  Pallas kernels  40.8 us (24%)
  blocking collectives  12.3 us (7%)
  local copies, waits for them, and re-layouts  3.84 us (2%)
    ppermute x46, waiting for transfers between devices, permute(): return lax.ppermute(value, AXES, pairs)  50 us
    ppermute x46, starting transfers between devices, permute(): return lax.ppermute(value, AXES, pairs)  48.7 us
    pallas_call x15, Pallas kernels, kernel_call(): pl.pallas_call(kernel, out_shape=[pltpu.VMEM(o.shape, o.dtype) if inside...  40.8 us
    all_gather x1, blocking collectives, spread(): return lax.all_gather(value, PLANE, axis=0, tiled=True)  12.3 us
    all_to_all x1, waiting for transfers between devices, per_device(): arrived = lax.all_to_all(update, everywhere, 0, 0, tiled=True)  7.04 us
    all_to_all x1, starting transfers between devices, per_device(): arrived = lax.all_to_all(update, everywhere, 0, 0, tiled=True)  6.3 us
  transfers between devices with their start and end apart: 47, of which 28 were waited for; matrix products, arithmetic and copies ran while one was open for 1% of the time, Pallas kernels for 15%

profile of v7, /device:TPU:0, one launch (start us, length us, event | category | flops | bytes accessed | tf_op | source)
XLA Modules:
  0.0 170.1 jit_solution(710761021805015556)
XLA Ops:
  4.7 4.5 %collective-permute-start.2 = (bf16[1536,256]{1,0:T(8,128)(2,1)}, bf16[1536,256]{1,0:T(8,128)(2,1)S(1)}, u32[]{:S(2)}, u32[]{:S(2)}) collective-permute-start(bf16[1536,256]{1,0:T(8,128)(2,1)} %b0.1), channel_id=1, source_target_pairs={{0,2},{1,3},{4,6},{5,7},{8,10},{9,11},{12,14},{13,15},{16,18},{17,... | collective-permute-start | bytes 2359304 | tf_op jit(solution)/shard_map/ppermute | solution.py:25
  11.4 1.6 collective-permute-start.3
  13.0 2.6 %collective-permute-start.4 = (bf16[384,128]{1,0:T(8,128)(2,1)S(1)}, bf16[384,128]{1,0:T(8,128)(2,1)S(1)}, u32[]{:S(2)}, u32[]{:S(2)}) collective-permute-start(bf16[384,128]{1,0:T(8,128)(2,1)S(1)} %get-tuple-element.145), channel_id=1, source_target_pairs={{0,16},{1,17},{2,18},{3,19},{4,20},{5,21},{6,22},{7,23},{8,24},{9,... | collective-permute-start | bytes 294920 | tf_op jit(solution)/shard_map/ppermute | solution.py:25
  16.7 8.5 %shard_map.183 = (f32[1536,256]{1,0:T(8,128)S(1)}, bf16[1536,3072]{1,0:T(8,128)(2,1)S(1)}, bf16[1536,1536]{1,0:T(8,128)(2,1)S(1)}) custom-call(s32[111]{0:T(128)S(1)} %concatenate.19.scalars, bf16[1536,256]{1,0:T(8,128)(2,1)S(1)} %copy-done, bf16[1536,256]{1,0:T(8,128)(2,1)S(1)} %collective-permute-done.1.b1, bf16[1536,6144]{1,0:T(8,128)(2,1)} %inverse.1, ...), custom_call_target="tpu_custom_call" | custom-call | flops 1 | bytes 1 | tf_op jit(solution)/shard_map/pallas_call | solution.py:38
  25.2 1.7 collective-permute-done.2.refs_0_
  28.6 2.4 %collective-permute-start.8 = (bf16[1536,128]{1,0:T(8,128)(2,1)S(1)}, bf16[1536,128]{1,0:T(8,128)(2,1)S(1)}, u32[]{:S(2)}, u32[]{:S(2)}) collective-permute-start(bf16[1536,128]{1,0:T(8,128)(2,1)S(1)} %get-tuple-element.183.refs_0_), channel_id=1, source_target_pairs={{0,2},{1,3},{2,0},{3,1},{4,6},{5,7},{6,4},{7,5},{8,10},{9,11},{10,... | collective-permute-start | bytes 1179656 | tf_op jit(solution)/shard_map/ppermute | solution.py:25
  31.0 1.6 collective-permute-start.9
  32.7 5.2 %shard_map.185 = (bf16[1536,256]{1,0:T(8,128)(2,1)}, f32[1536,128]{1,0:T(8,128)S(1)}, bf16[1536,128]{1,0:T(8,128)(2,1)S(1)}, bf16[768,6144]{1,0:T(8,128)(2,1)S(1)}, bf16[1536,768]{1,0:T(8,128)(2,1)S(1)}) custom-call(s32[111]{0:T(128)S(1)} %concatenate.19.scalars, f32[1536,256]{1,0:T(8,128)S(1)} %get-tuple-element.151.acc, ...), custom_call_target="tpu_custom_call" | custom-call | flops 1 | bytes 1 | tf_op jit(solution)/shard_map/pallas_call | solution.py:38
  38.7 1.8 %collective-permute-done.8.refs_2_ = bf16[1536,128]{1,0:T(8,128)(2,1)S(1)} collective-permute-done((bf16[1536,128]{1,0:T(8,128)(2,1)S(1)}, bf16[1536,128]{1,0:T(8,128)(2,1)S(1)}, u32[]{:S(2)}, u32[]{:S(2)}) %collective-permute-start.8) | collective-permute-done | bytes 393248 | tf_op jit(solution)/shard_map/ppermute | solution.py:25
  42.9 1.8 %collective-permute-start.12 = (bf16[768,128]{1,0:T(8,128)(2,1)S(1)}, bf16[768,128]{1,0:T(8,128)(2,1)S(1)}, u32[]{:S(2)}, u32[]{:S(2)}) collective-permute-start(bf16[768,128]{1,0:T(8,128)(2,1)S(1)} %get-tuple-element.166), channel_id=1, source_target_pairs={{0,2},{1,3},{2,0},{3,1},{4,6},{5,7},{6,4},{7,5},{8,10},{9,11},{10,... | collective-permute-start | bytes 589832 | tf_op jit(solution)/shard_map/ppermute | solution.py:25
  44.8 5.2 %collective-permute-done.12.rest_0_ = bf16[768,128]{1,0:T(8,128)(2,1)S(1)} collective-permute-done((bf16[768,128]{1,0:T(8,128)(2,1)S(1)}, bf16[768,128]{1,0:T(8,128)(2,1)S(1)}, u32[]{:S(2)}, u32[]{:S(2)}) %collective-permute-start.12) | collective-permute-done | bytes 196640 | tf_op jit(solution)/shard_map/ppermute | solution.py:25
  50.6 2.0 %collective-permute-done.13.refs_3_ = bf16[1536,128]{1,0:T(8,128)(2,1)S(1)} collective-permute-done((bf16[1536,128]{1,0:T(8,128)(2,1)S(1)}, bf16[1536,128]{1,0:T(8,128)(2,1)S(1)}, u32[]{:S(2)}, u32[]{:S(2)}) %collective-permute-start.13) | collective-permute-done | bytes 393248 | tf_op jit(solution)/shard_map/ppermute | solution.py:25
  53.1 12.3 %all_gather.3.mine = bf16[3072,128]{1,0:T(8,128)(2,1)S(1)} all-gather(bf16[768,128]{1,0:T(8,128)(2,1)S(1)} %shard_map.187), channel_id=1, replica_groups=mesh['hi'=1,'z2'=2,'z1'=2,'x'=2,'y'=2,'core'=2] {'x','y'}, dimensions={0}, use_global_device_ids=true | all-gather | bytes 983040 | tf_op jit(solution)/shard_map/all_gather | solution.py:541
  68.7 7.3 %shard_map.188 = (bf16[768,256]{1,0:T(8,128)(2,1)}, f32[1536,128]{1,0:T(8,128)S(1)}, bf16[1536,128]{1,0:T(8,128)(2,1)S(1)}, bf16[384,6144]{1,0:T(8,128)(2,1)S(1)...) custom-call(s32[111]{0:T(128)S(1)} %concatenate.19.scalars, ...), custom_call_target="tpu_custom_call" | custom-call | flops 1 | bytes 1 | tf_op jit(solution)/shard_map/pallas_call | solution.py:38
  77.4 1.7 %collective-permute-done.22.received = bf16[1536,128]{1,0:T(8,128)(2,1)S(1)} collective-permute-done((bf16[1536,128]{1,0:T(8,128)(2,1)S(1)}, bf16[1536,128]{1,0:T(8,128)(2,1)S(1)}, u32[]{:S(2)}, u32[]{:S(2)}) %collective-permute-start.22) | collective-permute-done | bytes 393248 | tf_op jit(solution)/shard_map/ppermute | solution.py:25
  89.6 2.1 %collective-permute-start.30 = (bf16[1536,128]{1,0:T(8,128)(2,1)S(1)}, bf16[1536,128]{1,0:T(8,128)(2,1)S(1)}, u32[]{:S(2)}, u32[]{:S(2)}) collective-permute-start(bf16[1536,128]{1,0:T(8,128)(2,1)S(1)} %pad_maximum_fusion.refs_8_), channel_id=1, source_target_pairs={{0,2},{1,3},{2,0},{3,1},{4,6},{5,7},{6,4},{7,5},{8,10},{9,11},{10,... | collective-permute-start | bytes 1179656 | tf_op jit(solution)/shard_map/ppermute | solution.py:25
  93.2 3.7 %collective-permute-done.27.refs_11_ = bf16[1536,128]{1,0:T(8,128)(2,1)S(1)} collective-permute-done((bf16[1536,128]{1,0:T(8,128)(2,1)S(1)}, bf16[1536,128]{1,0:T(8,128)(2,1)S(1)}, u32[]{:S(2)}, u32[]{:S(2)}) %collective-permute-start.27) | collective-permute-done | bytes 393248 | tf_op jit(solution)/shard_map/ppermute | solution.py:25
  97.0 2.4 %collective-permute-done.30.refs_10_ = bf16[1536,128]{1,0:T(8,128)(2,1)S(1)} collective-permute-done((bf16[1536,128]{1,0:T(8,128)(2,1)S(1)}, bf16[1536,128]{1,0:T(8,128)(2,1)S(1)}, u32[]{:S(2)}, u32[]{:S(2)}) %collective-permute-start.30) | collective-permute-done | bytes 393248 | tf_op jit(solution)/shard_map/ppermute | solution.py:25
  103.0 4.3 %collective-permute-done.31.refs_1_ = bf16[768,128]{1,0:T(8,128)(2,1)S(1)} collective-permute-done((bf16[768,128]{1,0:T(8,128)(2,1)S(1)}, bf16[768,128]{1,0:T(8,128)(2,1)S(1)}, u32[]{:S(2)}, u32[]{:S(2)}) %collective-permute-start.31) | collective-permute-done | bytes 196640 | tf_op jit(solution)/shard_map/ppermute | solution.py:25
  107.3 2.2 %collective-permute-done.33.refs_3_ = bf16[768,128]{1,0:T(8,128)(2,1)S(1)} collective-permute-done((bf16[768,128]{1,0:T(8,128)(2,1)S(1)}, bf16[768,128]{1,0:T(8,128)(2,1)S(1)}, u32[]{:S(2)}, u32[]{:S(2)}) %collective-permute-start.33) | collective-permute-done | bytes 196640 | tf_op jit(solution)/shard_map/ppermute | solution.py:25
  109.5 6.1 %shard_map.191 = (f32[384,128]{1,0:T(8,128)S(1)}, bf16[384,128]{1,0:T(8,128)(2,1)S(1)}, bf16[384,128]{1,0:T(8,128)(2,1)S(1)}, bf16[384,128]{1,0:T(8,128)(2,1)S(1...) custom-call(s32[111]{0:T(128)S(1)} %concatenate.19.scalars, ...), custom_call_target="tpu_custom_call" | custom-call | flops 1 | bytes 1 | tf_op jit(solution)/shard_map/pallas_call | solution.py:38
  121.2 3.1 %collective-permute-done.36.rest_2_ = bf16[384,128]{1,0:T(8,128)(2,1)S(1)} collective-permute-done((bf16[384,128]{1,0:T(8,128)(2,1)S(1)}, bf16[384,128]{1,0:T(8,128)(2,1)S(1)}, u32[]{:S(2)}, u32[]{:S(2)}) %collective-permute-start.36) | collective-permute-done | bytes 98336 | tf_op jit(solution)/shard_map/ppermute | solution.py:25
  124.8 1.9 %collective-permute-start.37 = (bf16[384,128]{1,0:T(8,128)(2,1)S(1)}, bf16[384,128]{1,0:T(8,128)(2,1)S(1)}, u32[]{:S(2)}, u32[]{:S(2)}) collective-permute-start(bf16[384,128]{1,0:T(8,128)(2,1)S(1)} %shard_map.192), channel_id=1, source_target_pairs={{0,8},{1,9},{2,10},{3,11},{4,12},{5,13},{6,14},{7,15},{8,0},{9,1},... | collective-permute-start | bytes 294920 | tf_op jit(solution)/shard_map/ppermute | solution.py:25
  127.3 2.2 %collective-permute-done.37 = bf16[384,128]{1,0:T(8,128)(2,1)S(1)} collective-permute-done((bf16[384,128]{1,0:T(8,128)(2,1)S(1)}, bf16[384,128]{1,0:T(8,128)(2,1)S(1)}, u32[]{:S(2)}, u32[]{:S(2)}) %collective-permute-start.37) | collective-permute-done | bytes 98336 | tf_op jit(solution)/shard_map/ppermute | solution.py:25
  129.6 3.3 %collective-permute-start.38 = (bf16[384,128]{1,0:T(8,128)(2,1)S(1)}, bf16[384,128]{1,0:T(8,128)(2,1)S(1)}, u32[]{:S(2)}, u32[]{:S(2)}) collective-permute-start(bf16[384,128]{1,0:T(8,128)(2,1)S(1)} %add_convert_fusion), channel_id=1, source_target_pairs={{0,16},{1,17},{2,18},{3,19},{4,20},{5,21},{6,22},{7,23},{8,24},{9,... | collective-permute-start | bytes 294920 | tf_op jit(solution)/shard_map/ppermute | solution.py:25
  132.9 2.6 %collective-permute-done.38 = bf16[384,128]{1,0:T(8,128)(2,1)S(1)} collective-permute-done((bf16[384,128]{1,0:T(8,128)(2,1)S(1)}, bf16[384,128]{1,0:T(8,128)(2,1)S(1)}, u32[]{:S(2)}, u32[]{:S(2)}) %collective-permute-start.38) | collective-permute-done | bytes 98336 | tf_op jit(solution)/shard_map/ppermute | solution.py:25
  135.8 1.8 %collective-permute-start.42 = (bf16[768,128]{1,0:T(8,128)(2,1)S(1)}, bf16[768,128]{1,0:T(8,128)(2,1)S(1)}, u32[]{:S(2)}, u32[]{:S(2)}) collective-permute-start(bf16[768,128]{1,0:T(8,128)(2,1)S(1)} %constant_dynamic-update-slice_fusion.4.refs_0_), channel_id=1, source_target_pairs={{0,4},{1,5},{2,6},{3,7},{4,0},{5,1},{6,2},{7,3},{8,12},{9,13},{10,... | collective-permute-start | bytes 589832 | tf_op jit(solution)/shard_map/ppermute | solution.py:25
  139.1 4.2 %collective-permute-done.41.refs_1_ = bf16[768,128]{1,0:T(8,128)(2,1)S(1)} collective-permute-done((bf16[768,128]{1,0:T(8,128)(2,1)S(1)}, bf16[768,128]{1,0:T(8,128)(2,1)S(1)}, u32[]{:S(2)}, u32[]{:S(2)}) %collective-permute-start.41) | collective-permute-done | bytes 196640 | tf_op jit(solution)/shard_map/ppermute | solution.py:25
  143.5 1.9 %collective-permute-done.43.refs_3_ = bf16[768,128]{1,0:T(8,128)(2,1)S(1)} collective-permute-done((bf16[768,128]{1,0:T(8,128)(2,1)S(1)}, bf16[768,128]{1,0:T(8,128)(2,1)S(1)}, u32[]{:S(2)}, u32[]{:S(2)}) %collective-permute-start.43) | collective-permute-done | bytes 196640 | tf_op jit(solution)/shard_map/ppermute | solution.py:25
  145.4 5.7 %shard_map.193 = (bf16[1536,128]{1,0:T(8,128)(2,1)}, bf16[192,128]{1,0:T(8,128)(2,1)S(1)}, bf16[192,128]{1,0:T(8,128)(2,1)S(1)}) custom-call(s32[111]{0:T(128)S(1)} %concatenate.19.scalars, bf16[768,128]{1,0:T(8,128)(2,1)S(1)} %constant_dynamic-update-slice_fusion.4.refs_0_, bf16[768,128]{1,0:T(8,128)(2,1)S(1)} %collective-permute-done.41.refs_1_, ...), custom_call_target="tpu_custom_call" | custom-call | flops 1 | bytes 1 | tf_op jit(solution)/shard_map/pallas_call | solution.py:38
  151.1 6.3 %all-to-all-start = ((bf16[16,96,128]{2,1,0:T(8,128)(2,1)}), bf16[16,96,128]{2,1,0:T(8,128)(2,1)S(1)}, u32[]{:S(2)}, u32[]{:S(2)}) async-start(bf16[16,96,128]{2,1,0:T(8,128)(2,1)} %bitcast.41), calls=%async_computation | async-start | bytes 786432 | tf_op jit(solution)/shard_map/all_to_all | solution.py:634
  160.0 7.0 %all-to-all-done = bf16[16,96,128]{2,1,0:T(8,128)(2,1)S(1)} async-done(((bf16[16,96,128]{2,1,0:T(8,128)(2,1)}), bf16[16,96,128]{2,1,0:T(8,128)(2,1)S(1)}, u32[]{:S(2)}, u32[]{:S(2)}) %all-to-all-start) | async-done | bytes 393248 | tf_op jit(solution)/shard_map/all_to_all | solution.py:634
  (138 shorter events, 47.8 us)
Async XLA Ops:
  4.2 22.7 %collective-permute-start.6 = (bf16[384,6144]{1,0:T(8,128)(2,1)}, bf16[384,6144]{1,0:T(8,128)(2,1)S(1)}, u32[]{:S(2)}, u32[]{:S(2)}) collective-permute-start(bf16[384,6144]{1,0:T(8,128)(2,1)} %refs_8_), channel_id=1, source_target_pairs={{0,1},{1,0},{2,3},{3,2},{4,5},{5,4},{6,7},{7,6},{8,9},{9,8},{10,11... | collective-permute-start | bytes 14155784 | tf_op jit(solution)/shard_map/ppermute | solution.py:25
  4.7 22.2 %collective-permute-start.2 = (bf16[1536,256]{1,0:T(8,128)(2,1)}, bf16[1536,256]{1,0:T(8,128)(2,1)S(1)}, u32[]{:S(2)}, u32[]{:S(2)}) collective-permute-start(bf16[1536,256]{1,0:T(8,128)(2,1)} %b0.1), channel_id=1, source_target_pairs={{0,2},{1,3},{4,6},{5,7},{8,10},{9,11},{12,14},{13,15},{16,18},{17,... | collective-permute-start | bytes 2359304 | tf_op jit(solution)/shard_map/ppermute | solution.py:25
  9.9 17.0 %collective-permute-start.5 = (bf16[1536,128]{1,0:T(8,128)(2,1)S(1)}, bf16[1536,128]{1,0:T(8,128)(2,1)S(1)}, u32[]{:S(2)}, u32[]{:S(2)}) collective-permute-start(bf16[1536,128]{1,0:T(8,128)(2,1)S(1)} %get-tuple-element.183.refs_0_), channel_id=1, source_target_pairs={{0,4},{1,5},{2,6},{3,7},{4,0},{5,1},{6,2},{7,3},{8,12},{9,13},{10,... | collective-permute-start | bytes 1179656 | tf_op jit(solution)/shard_map/ppermute | solution.py:25
  11.4 13.8 %collective-permute-start.3 = (bf16[768,128]{1,0:T(8,128)(2,1)S(1)}, bf16[768,128]{1,0:T(8,128)(2,1)S(1)}, u32[]{:S(2)}, u32[]{:S(2)}) collective-permute-start(bf16[768,128]{1,0:T(8,128)(2,1)S(1)} %get-tuple-element.144), channel_id=1, source_target_pairs={{0,8},{1,9},{2,10},{3,11},{4,12},{5,13},{6,14},{7,15},{8,0},{9,1},... | collective-permute-start | bytes 589832 | tf_op jit(solution)/shard_map/ppermute | solution.py:25
  13.0 12.2 %collective-permute-start.4 = (bf16[384,128]{1,0:T(8,128)(2,1)S(1)}, bf16[384,128]{1,0:T(8,128)(2,1)S(1)}, u32[]{:S(2)}, u32[]{:S(2)}) collective-permute-start(bf16[384,128]{1,0:T(8,128)(2,1)S(1)} %get-tuple-element.145), channel_id=1, source_target_pairs={{0,16},{1,17},{2,18},{3,19},{4,20},{5,21},{6,22},{7,23},{8,24},{9,... | collective-permute-start | bytes 294920 | tf_op jit(solution)/shard_map/ppermute | solution.py:25
  27.1 11.6 %collective-permute-start.10 = (bf16[1536,128]{1,0:T(8,128)(2,1)S(1)}, bf16[1536,128]{1,0:T(8,128)(2,1)S(1)}, u32[]{:S(2)}, u32[]{:S(2)}) collective-permute-start(bf16[1536,128]{1,0:T(8,128)(2,1)S(1)} %constant_dynamic-update-slice_fusion.refs_8_), channel_id=1, source_target_pairs={{0,4},{1,5},{2,6},{3,7},{4,0},{5,1},{6,2},{7,3},{8,12},{9,13},{10,... | collective-permute-start | bytes 1179656 | tf_op jit(solution)/shard_map/ppermute | solution.py:25
  28.6 11.9 %collective-permute-start.8 = (bf16[1536,128]{1,0:T(8,128)(2,1)S(1)}, bf16[1536,128]{1,0:T(8,128)(2,1)S(1)}, u32[]{:S(2)}, u32[]{:S(2)}) collective-permute-start(bf16[1536,128]{1,0:T(8,128)(2,1)S(1)} %get-tuple-element.183.refs_0_), channel_id=1, source_target_pairs={{0,2},{1,3},{2,0},{3,1},{4,6},{5,7},{6,4},{7,5},{8,10},{9,11},{10,... | collective-permute-start | bytes 1179656 | tf_op jit(solution)/shard_map/ppermute | solution.py:25
  31.0 6.9 %collective-permute-start.9 = (bf16[768,128]{1,0:T(8,128)(2,1)S(1)}, bf16[768,128]{1,0:T(8,128)(2,1)S(1)}, u32[]{:S(2)}, u32[]{:S(2)}) collective-permute-start(bf16[768,128]{1,0:T(8,128)(2,1)S(1)} %pad_maximum_fusion.1), channel_id=1, source_target_pairs={{0,8},{1,9},{2,10},{3,11},{4,12},{5,13},{6,14},{7,15},{8,0},{9,1},... | collective-permute-start | bytes 589832 | tf_op jit(solution)/shard_map/ppermute | solution.py:25
  40.5 10.0 %collective-permute-start.14 = (bf16[1536,128]{1,0:T(8,128)(2,1)S(1)}, bf16[1536,128]{1,0:T(8,128)(2,1)S(1)}, u32[]{:S(2)}, u32[]{:S(2)}) collective-permute-start(bf16[1536,128]{1,0:T(8,128)(2,1)S(1)} %get-tuple-element.183.refs_0_), channel_id=1, source_target_pairs={{0,1},{1,0},{2,3},{3,2},{4,5},{5,4},{6,7},{7,6},{8,9},{9,8},{10,11... | collective-permute-start | bytes 1179656 | tf_op jit(solution)/shard_map/ppermute | solution.py:25
  41.0 9.5 %collective-permute-start.15 = (bf16[1536,128]{1,0:T(8,128)(2,1)S(1)}, bf16[1536,128]{1,0:T(8,128)(2,1)S(1)}, u32[]{:S(2)}, u32[]{:S(2)}) collective-permute-start(bf16[1536,128]{1,0:T(8,128)(2,1)S(1)} %collective-permute-done.5.refs_1_), channel_id=1, source_target_pairs={{0,1},{1,0},{2,3},{3,2},{4,5},{5,4},{6,7},{7,6},{8,9},{9,8},{10,11... | collective-permute-start | bytes 1179656 | tf_op jit(solution)/shard_map/ppermute | solution.py:25
  41.1 11.5 %collective-permute-start.13 = (bf16[1536,128]{1,0:T(8,128)(2,1)S(1)}, bf16[1536,128]{1,0:T(8,128)(2,1)S(1)}, u32[]{:S(2)}, u32[]{:S(2)}) collective-permute-start(bf16[1536,128]{1,0:T(8,128)(2,1)S(1)} %collective-permute-done.8.refs_2_), channel_id=1, source_target_pairs={{0,4},{1,5},{2,6},{3,7},{4,0},{5,1},{6,2},{7,3},{8,12},{9,13},{10,... | collective-permute-start | bytes 1179656 | tf_op jit(solution)/shard_map/ppermute | solution.py:25
  41.6 10.9 %collective-permute-start.16 = (bf16[1536,128]{1,0:T(8,128)(2,1)S(1)}, bf16[1536,128]{1,0:T(8,128)(2,1)S(1)}, u32[]{:S(2)}, u32[]{:S(2)}) collective-permute-start(bf16[1536,128]{1,0:T(8,128)(2,1)S(1)} %collective-permute-done.8.refs_2_), channel_id=1, source_target_pairs={{0,1},{1,0},{2,3},{3,2},{4,5},{5,4},{6,7},{7,6},{8,9},{9,8},{10,11... | collective-permute-start | bytes 1179656 | tf_op jit(solution)/shard_map/ppermute | solution.py:25
  42.9 7.0 %collective-permute-start.12 = (bf16[768,128]{1,0:T(8,128)(2,1)S(1)}, bf16[768,128]{1,0:T(8,128)(2,1)S(1)}, u32[]{:S(2)}, u32[]{:S(2)}) collective-permute-start(bf16[768,128]{1,0:T(8,128)(2,1)S(1)} %get-tuple-element.166), channel_id=1, source_target_pairs={{0,2},{1,3},{2,0},{3,1},{4,6},{5,7},{6,4},{7,5},{8,10},{9,11},{10,... | collective-permute-start | bytes 589832 | tf_op jit(solution)/shard_map/ppermute | solution.py:25
  52.6 12.9 %collective-permute-start.17 = (bf16[1536,128]{1,0:T(8,128)(2,1)S(1)}, bf16[1536,128]{1,0:T(8,128)(2,1)S(1)}, u32[]{:S(2)}, u32[]{:S(2)}) collective-permute-start(bf16[1536,128]{1,0:T(8,128)(2,1)S(1)} %collective-permute-done.13.refs_3_), channel_id=1, source_target_pairs={{0,1},{1,0},{2,3},{3,2},{4,5},{5,4},{6,7},{7,6},{8,9},{9,8},{10,11... | collective-permute-start | bytes 1179656 | tf_op jit(solution)/shard_map/ppermute | solution.py:25
  52.6 15.0 %collective-permute-start.19 = (bf16[1536,384]{1,0:T(8,128)(2,1)S(1)}, bf16[1536,384]{1,0:T(8,128)(2,1)S(1)}, u32[]{:S(2)}, u32[]{:S(2)}) collective-permute-start(bf16[1536,384]{1,0:T(8,128)(2,1)S(1)} %copy-done.6), channel_id=1, source_target_pairs={{0,1},{1,0},{2,3},{3,2},{4,5},{5,4},{6,7},{7,6},{8,9},{9,8},{10,11... | collective-permute-start | bytes 3538952 | tf_op jit(solution)/shard_map/ppermute | solution.py:25
  65.6 11.5 %collective-permute-start.20 = (bf16[1536,128]{1,0:T(8,128)(2,1)S(1)}, bf16[1536,128]{1,0:T(8,128)(2,1)S(1)}, u32[]{:S(2)}, u32[]{:S(2)}) collective-permute-start(bf16[1536,128]{1,0:T(8,128)(2,1)S(1)} %pad_maximum_fusion.refs_8_), channel_id=1, source_target_pairs={{0,4},{1,5},{2,6},{3,7},{4,0},{5,1},{6,2},{7,3},{8,12},{9,13},{10,... | collective-permute-start | bytes 1179656 | tf_op jit(solution)/shard_map/ppermute | solution.py:25
  66.2 11.2 %collective-permute-start.21 = (bf16[1536,128]{1,0:T(8,128)(2,1)S(1)}, bf16[1536,128]{1,0:T(8,128)(2,1)S(1)}, u32[]{:S(2)}, u32[]{:S(2)}) collective-permute-start(bf16[1536,128]{1,0:T(8,128)(2,1)S(1)} %constant_dynamic-update-slice_fusion.refs_8_), channel_id=1, source_target_pairs={{0,2},{1,3},{2,0},{3,1},{4,6},{5,7},{6,4},{7,5},{8,10},{9,11},{10,... | collective-permute-start | bytes 1179656 | tf_op jit(solution)/shard_map/ppermute | solution.py:25
  79.8 19.6 %collective-permute-start.28 = (bf16[192,6144]{1,0:T(8,128)(2,1)S(1)}, bf16[192,6144]{1,0:T(8,128)(2,1)S(1)}, u32[]{:S(2)}, u32[]{:S(2)}) collective-permute-start(bf16[192,6144]{1,0:T(8,128)(2,1)S(1)} %copy-done.3), channel_id=1, source_target_pairs={{0,1},{1,0},{2,3},{3,2},{4,5},{5,4},{6,7},{7,6},{8,9},{9,8},{10,11... | collective-permute-start | bytes 7077896 | tf_op jit(solution)/shard_map/ppermute | solution.py:25
  80.0 19.4 %collective-permute-start.29 = (bf16[192,1536]{1,0:T(8,128)(2,1)S(1)}, bf16[192,1536]{1,0:T(8,128)(2,1)S(1)}, u32[]{:S(2)}, u32[]{:S(2)}) collective-permute-start(bf16[192,1536]{1,0:T(8,128)(2,1)S(1)} %bitcast.51), channel_id=1, source_target_pairs={{0,1},{1,0},{2,3},{3,2},{4,5},{5,4},{6,7},{7,6},{8,9},{9,8},{10,11... | collective-permute-start | bytes 1769480 | tf_op jit(solution)/shard_map/ppermute | solution.py:25
  82.4 6.6 %collective-permute-start.25 = (bf16[384,128]{1,0:T(8,128)(2,1)S(1)}, bf16[384,128]{1,0:T(8,128)(2,1)S(1)}, u32[]{:S(2)}, u32[]{:S(2)}) collective-permute-start(bf16[384,128]{1,0:T(8,128)(2,1)S(1)} %get-tuple-element.208), channel_id=1, source_target_pairs={{0,6},{1,7},{2,4},{3,5},{4,2},{5,3},{6,0},{7,1},{8,14},{9,15},{10,... | collective-permute-start | bytes 294920 | tf_op jit(solution)/shard_map/ppermute | solution.py:25
  85.2 11.8 %collective-permute-start.27 = (bf16[1536,128]{1,0:T(8,128)(2,1)S(1)}, bf16[1536,128]{1,0:T(8,128)(2,1)S(1)}, u32[]{:S(2)}, u32[]{:S(2)}) collective-permute-start(bf16[1536,128]{1,0:T(8,128)(2,1)S(1)} %collective-permute-done.21.refs_10_), channel_id=1, source_target_pairs={{0,4},{1,5},{2,6},{3,7},{4,0},{5,1},{6,2},{7,3},{8,12},{9,13},{10,... | collective-permute-start | bytes 1179656 | tf_op jit(solution)/shard_map/ppermute | solution.py:25
  89.6 9.8 %collective-permute-start.30 = (bf16[1536,128]{1,0:T(8,128)(2,1)S(1)}, bf16[1536,128]{1,0:T(8,128)(2,1)S(1)}, u32[]{:S(2)}, u32[]{:S(2)}) collective-permute-start(bf16[1536,128]{1,0:T(8,128)(2,1)S(1)} %pad_maximum_fusion.refs_8_), channel_id=1, source_target_pairs={{0,2},{1,3},{2,0},{3,1},{4,6},{5,7},{6,4},{7,5},{8,10},{9,11},{10,... | collective-permute-start | bytes 1179656 | tf_op jit(solution)/shard_map/ppermute | solution.py:25
  99.4 7.8 %collective-permute-start.31 = (bf16[768,128]{1,0:T(8,128)(2,1)S(1)}, bf16[768,128]{1,0:T(8,128)(2,1)S(1)}, u32[]{:S(2)}, u32[]{:S(2)}) collective-permute-start(bf16[768,128]{1,0:T(8,128)(2,1)S(1)} %constant_dynamic-update-slice_fusion.2.refs_0_), channel_id=1, source_target_pairs={{0,2},{1,3},{2,0},{3,1},{4,6},{5,7},{6,4},{7,5},{8,10},{9,11},{10,... | collective-permute-start | bytes 589832 | tf_op jit(solution)/shard_map/ppermute | solution.py:25
  101.0 6.3 %collective-permute-start.32 = (bf16[768,128]{1,0:T(8,128)(2,1)S(1)}, bf16[768,128]{1,0:T(8,128)(2,1)S(1)}, u32[]{:S(2)}, u32[]{:S(2)}) collective-permute-start(bf16[768,128]{1,0:T(8,128)(2,1)S(1)} %constant_dynamic-update-slice_fusion.2.refs_0_), channel_id=1, source_target_pairs={{0,4},{1,5},{2,6},{3,7},{4,0},{5,1},{6,2},{7,3},{8,12},{9,13},{10,... | collective-permute-start | bytes 589832 | tf_op jit(solution)/shard_map/ppermute | solution.py:25
  101.5 8.0 %collective-permute-start.33 = (bf16[768,128]{1,0:T(8,128)(2,1)S(1)}, bf16[768,128]{1,0:T(8,128)(2,1)S(1)}, u32[]{:S(2)}, u32[]{:S(2)}) collective-permute-start(bf16[768,128]{1,0:T(8,128)(2,1)S(1)} %constant_dynamic-update-slice_fusion.2.refs_0_), channel_id=1, source_target_pairs={{0,6},{1,7},{2,4},{3,5},{4,2},{5,3},{6,0},{7,1},{8,14},{9,15},{10,... | collective-permute-start | bytes 589832 | tf_op jit(solution)/shard_map/ppermute | solution.py:25
  117.7 6.6 %collective-permute-start.36 = (bf16[384,128]{1,0:T(8,128)(2,1)S(1)}, bf16[384,128]{1,0:T(8,128)(2,1)S(1)}, u32[]{:S(2)}, u32[]{:S(2)}) collective-permute-start(bf16[384,128]{1,0:T(8,128)(2,1)S(1)} %get-tuple-element.238), channel_id=1, source_target_pairs={{0,6},{1,7},{2,4},{3,5},{4,2},{5,3},{6,0},{7,1},{8,14},{9,15},{10,... | collective-permute-start | bytes 294920 | tf_op jit(solution)/shard_map/ppermute | solution.py:25
  126.8 8.7 %collective-permute-start.39 = (bf16[1536,128]{1,0:T(8,128)(2,1)S(1)}, bf16[1536,128]{1,0:T(8,128)(2,1)S(1)}, u32[]{:S(2)}, u32[]{:S(2)}) collective-permute-start(bf16[1536,128]{1,0:T(8,128)(2,1)S(1)} %collective-permute-done.30.refs_10_), channel_id=1, source_target_pairs={{0,4},{1,5},{2,6},{3,7},{4,0},{5,1},{6,2},{7,3},{8,12},{9,13},{10,... | collective-permute-start | bytes 1179656 | tf_op jit(solution)/shard_map/ppermute | solution.py:25
  129.6 5.9 %collective-permute-start.38 = (bf16[384,128]{1,0:T(8,128)(2,1)S(1)}, bf16[384,128]{1,0:T(8,128)(2,1)S(1)}, u32[]{:S(2)}, u32[]{:S(2)}) collective-permute-start(bf16[384,128]{1,0:T(8,128)(2,1)S(1)} %add_convert_fusion), channel_id=1, source_target_pairs={{0,16},{1,17},{2,18},{3,19},{4,20},{5,21},{6,22},{7,23},{8,24},{9,... | collective-permute-start | bytes 294920 | tf_op jit(solution)/shard_map/ppermute | solution.py:25
  135.5 7.8 %collective-permute-start.41 = (bf16[768,128]{1,0:T(8,128)(2,1)S(1)}, bf16[768,128]{1,0:T(8,128)(2,1)S(1)}, u32[]{:S(2)}, u32[]{:S(2)}) collective-permute-start(bf16[768,128]{1,0:T(8,128)(2,1)S(1)} %constant_dynamic-update-slice_fusion.4.refs_0_), channel_id=1, source_target_pairs={{0,2},{1,3},{2,0},{3,1},{4,6},{5,7},{6,4},{7,5},{8,10},{9,11},{10,... | collective-permute-start | bytes 589832 | tf_op jit(solution)/shard_map/ppermute | solution.py:25
  135.8 7.8 %collective-permute-start.42 = (bf16[768,128]{1,0:T(8,128)(2,1)S(1)}, bf16[768,128]{1,0:T(8,128)(2,1)S(1)}, u32[]{:S(2)}, u32[]{:S(2)}) collective-permute-start(bf16[768,128]{1,0:T(8,128)(2,1)S(1)} %constant_dynamic-update-slice_fusion.4.refs_0_), channel_id=1, source_target_pairs={{0,4},{1,5},{2,6},{3,7},{4,0},{5,1},{6,2},{7,3},{8,12},{9,13},{10,... | collective-permute-start | bytes 589832 | tf_op jit(solution)/shard_map/ppermute | solution.py:25
  137.6 7.8 %collective-permute-start.43 = (bf16[768,128]{1,0:T(8,128)(2,1)S(1)}, bf16[768,128]{1,0:T(8,128)(2,1)S(1)}, u32[]{:S(2)}, u32[]{:S(2)}) collective-permute-start(bf16[768,128]{1,0:T(8,128)(2,1)S(1)} %constant_dynamic-update-slice_fusion.4.refs_0_), channel_id=1, source_target_pairs={{0,6},{1,7},{2,4},{3,5},{4,2},{5,3},{6,0},{7,1},{8,14},{9,15},{10,... | collective-permute-start | bytes 589832 | tf_op jit(solution)/shard_map/ppermute | solution.py:25
  151.1 15.9 %all-to-all-start = ((bf16[16,96,128]{2,1,0:T(8,128)(2,1)}), bf16[16,96,128]{2,1,0:T(8,128)(2,1)S(1)}, u32[]{:S(2)}, u32[]{:S(2)}) async-start(bf16[16,96,128]{2,1,0:T(8,128)(2,1)} %bitcast.41), calls=%async_computation | async-start | bytes 786432 | tf_op jit(solution)/shard_map/all_to_all | solution.py:634
  (39 other events, 506.7 us)

commit v8 on v7

--- a/solution.py
+++ b/solution.py
@@ -609,7 +609,7 @@
     chunks, keep, send = tie((chunks, keep, send))
 
     part = reduce_chunks(chunks, plane, scalars)
-    part, keep, send, y_fourth = tie((part, keep, send, y_fourth))
+    part, keep, send = tie((part, keep, send))
     pieces_fourth = with_x(x_fourth, own_fourth, y_fourth)
     halves_third = keep, permute(send, 1)
     part = (part.astype(F32) + permute(part, mask_z1).astype(F32)).astype(BF16)

time: 171 us -> 171 us (level)
  transfers between devices with their start and end apart: 47 -> 47, of which waited for: 28 -> 29; matrix products, arithmetic and copies ran while one was open for 1% -> 1% of each run, Pallas kernels for 15% -> 15%
where the time goes in v8:
time: 171 us; the launch traced here: 170 us
  waiting for transfers between devices  57 us (33%)
  starting transfers between devices  55 us (32%)
  Pallas kernels  40.8 us (24%)
  blocking collectives  12.3 us (7%)
  local copies, waits for them, and re-layouts  3.84 us (2%)
    ppermute x46, waiting for transfers between devices, permute(): return lax.ppermute(value, AXES, pairs)  49.9 us
    ppermute x46, starting transfers between devices, permute(): return lax.ppermute(value, AXES, pairs)  48.7 us
    pallas_call x15, Pallas kernels, kernel_call(): pl.pallas_call(kernel, out_shape=[pltpu.VMEM(o.shape, o.dtype) if inside...  40.8 us
    all_gather x1, blocking collectives, spread(): return lax.all_gather(value, PLANE, axis=0, tiled=True)  12.3 us
    all_to_all x1, waiting for transfers between devices, per_device(): arrived = lax.all_to_all(update, everywhere, 0, 0, tiled=True)  7.04 us
    all_to_all x1, starting transfers between devices, per_device(): arrived = lax.all_to_all(update, everywhere, 0, 0, tiled=True)  6.3 us
  transfers between devices with their start and end apart: 47, of which 29 were waited for; matrix products, arithmetic and copies ran while one was open for 1% of the time, Pallas kernels for 15%

profile of v8, /device:TPU:0, one launch (start us, length us, event | category | flops | bytes accessed | tf_op | source)
XLA Modules:
  0.0 170.1 jit_solution(9429970281550035896)
XLA Ops:
  4.7 4.5 %collective-permute-start.2 = (bf16[1536,256]{1,0:T(8,128)(2,1)}, bf16[1536,256]{1,0:T(8,128)(2,1)S(1)}, u32[]{:S(2)}, u32[]{:S(2)}) collective-permute-start(bf16[1536,256]{1,0:T(8,128)(2,1)} %b0.1), channel_id=1, source_target_pairs={{0,2},{1,3},{4,6},{5,7},{8,10},{9,11},{12,14},{13,15},{16,18},{17,... | collective-permute-start | bytes 2359304 | tf_op jit(solution)/shard_map/ppermute | solution.py:25
  11.4 1.6 collective-permute-start.3
  13.0 2.6 %collective-permute-start.4 = (bf16[384,128]{1,0:T(8,128)(2,1)S(1)}, bf16[384,128]{1,0:T(8,128)(2,1)S(1)}, u32[]{:S(2)}, u32[]{:S(2)}) collective-permute-start(bf16[384,128]{1,0:T(8,128)(2,1)S(1)} %get-tuple-element.144), channel_id=1, source_target_pairs={{0,16},{1,17},{2,18},{3,19},{4,20},{5,21},{6,22},{7,23},{8,24},{9,... | collective-permute-start | bytes 294920 | tf_op jit(solution)/shard_map/ppermute | solution.py:25
  16.7 8.5 %shard_map.183 = (f32[1536,256]{1,0:T(8,128)S(1)}, bf16[1536,3072]{1,0:T(8,128)(2,1)S(1)}, bf16[1536,1536]{1,0:T(8,128)(2,1)S(1)}) custom-call(s32[111]{0:T(128)S(1)} %concatenate.19.scalars, bf16[1536,256]{1,0:T(8,128)(2,1)S(1)} %copy-done, bf16[1536,256]{1,0:T(8,128)(2,1)S(1)} %collective-permute-done.1.b1, bf16[1536,6144]{1,0:T(8,128)(2,1)} %inverse.1, ...), custom_call_target="tpu_custom_call" | custom-call | flops 1 | bytes 1 | tf_op jit(solution)/shard_map/pallas_call | solution.py:38
  25.2 1.7 collective-permute-done.2.refs_0_
  28.6 2.4 %collective-permute-start.8 = (bf16[1536,128]{1,0:T(8,128)(2,1)S(1)}, bf16[1536,128]{1,0:T(8,128)(2,1)S(1)}, u32[]{:S(2)}, u32[]{:S(2)}) collective-permute-start(bf16[1536,128]{1,0:T(8,128)(2,1)S(1)} %get-tuple-element.182.refs_0_), channel_id=1, source_target_pairs={{0,2},{1,3},{2,0},{3,1},{4,6},{5,7},{6,4},{7,5},{8,10},{9,11},{10,... | collective-permute-start | bytes 1179656 | tf_op jit(solution)/shard_map/ppermute | solution.py:25
  31.0 1.6 collective-permute-start.9
  32.7 5.2 %shard_map.185 = (bf16[1536,256]{1,0:T(8,128)(2,1)}, f32[1536,128]{1,0:T(8,128)S(1)}, bf16[1536,128]{1,0:T(8,128)(2,1)S(1)}, bf16[768,6144]{1,0:T(8,128)(2,1)S(1)}, bf16[1536,768]{1,0:T(8,128)(2,1)S(1)}) custom-call(s32[111]{0:T(128)S(1)} %concatenate.19.scalars, f32[1536,256]{1,0:T(8,128)S(1)} %get-tuple-element.150.acc, ...), custom_call_target="tpu_custom_call" | custom-call | flops 1 | bytes 1 | tf_op jit(solution)/shard_map/pallas_call | solution.py:38
  38.7 1.8 %collective-permute-done.8.refs_2_ = bf16[1536,128]{1,0:T(8,128)(2,1)S(1)} collective-permute-done((bf16[1536,128]{1,0:T(8,128)(2,1)S(1)}, bf16[1536,128]{1,0:T(8,128)(2,1)S(1)}, u32[]{:S(2)}, u32[]{:S(2)}) %collective-permute-start.8) | collective-permute-done | bytes 393248 | tf_op jit(solution)/shard_map/ppermute | solution.py:25
  42.9 1.8 %collective-permute-start.12 = (bf16[768,128]{1,0:T(8,128)(2,1)S(1)}, bf16[768,128]{1,0:T(8,128)(2,1)S(1)}, u32[]{:S(2)}, u32[]{:S(2)}) collective-permute-start(bf16[768,128]{1,0:T(8,128)(2,1)S(1)} %get-tuple-element.165), channel_id=1, source_target_pairs={{0,2},{1,3},{2,0},{3,1},{4,6},{5,7},{6,4},{7,5},{8,10},{9,11},{10,... | collective-permute-start | bytes 589832 | tf_op jit(solution)/shard_map/ppermute | solution.py:25
  44.8 5.2 %collective-permute-done.12.rest_0_ = bf16[768,128]{1,0:T(8,128)(2,1)S(1)} collective-permute-done((bf16[768,128]{1,0:T(8,128)(2,1)S(1)}, bf16[768,128]{1,0:T(8,128)(2,1)S(1)}, u32[]{:S(2)}, u32[]{:S(2)}) %collective-permute-start.12) | collective-permute-done | bytes 196640 | tf_op jit(solution)/shard_map/ppermute | solution.py:25
  50.6 2.0 %collective-permute-done.13.refs_3_ = bf16[1536,128]{1,0:T(8,128)(2,1)S(1)} collective-permute-done((bf16[1536,128]{1,0:T(8,128)(2,1)S(1)}, bf16[1536,128]{1,0:T(8,128)(2,1)S(1)}, u32[]{:S(2)}, u32[]{:S(2)}) %collective-permute-start.13) | collective-permute-done | bytes 393248 | tf_op jit(solution)/shard_map/ppermute | solution.py:25
  53.1 12.3 %all_gather.3.mine = bf16[3072,128]{1,0:T(8,128)(2,1)S(1)} all-gather(bf16[768,128]{1,0:T(8,128)(2,1)S(1)} %shard_map.187), channel_id=1, replica_groups=mesh['hi'=1,'z2'=2,'z1'=2,'x'=2,'y'=2,'core'=2] {'x','y'}, dimensions={0}, use_global_device_ids=true | all-gather | bytes 983040 | tf_op jit(solution)/shard_map/all_gather | solution.py:541
  68.7 7.3 %shard_map.188 = (bf16[768,256]{1,0:T(8,128)(2,1)}, f32[1536,128]{1,0:T(8,128)S(1)}, bf16[1536,128]{1,0:T(8,128)(2,1)S(1)}, bf16[384,6144]{1,0:T(8,128)(2,1)S(1)...) custom-call(s32[111]{0:T(128)S(1)} %concatenate.19.scalars, ...), custom_call_target="tpu_custom_call" | custom-call | flops 1 | bytes 1 | tf_op jit(solution)/shard_map/pallas_call | solution.py:38
  77.4 1.7 %collective-permute-done.22.received = bf16[1536,128]{1,0:T(8,128)(2,1)S(1)} collective-permute-done((bf16[1536,128]{1,0:T(8,128)(2,1)S(1)}, bf16[1536,128]{1,0:T(8,128)(2,1)S(1)}, u32[]{:S(2)}, u32[]{:S(2)}) %collective-permute-start.22) | collective-permute-done | bytes 393248 | tf_op jit(solution)/shard_map/ppermute | solution.py:25
  89.6 2.1 %collective-permute-start.30 = (bf16[1536,128]{1,0:T(8,128)(2,1)S(1)}, bf16[1536,128]{1,0:T(8,128)(2,1)S(1)}, u32[]{:S(2)}, u32[]{:S(2)}) collective-permute-start(bf16[1536,128]{1,0:T(8,128)(2,1)S(1)} %pad_maximum_fusion.refs_8_), channel_id=1, source_target_pairs={{0,2},{1,3},{2,0},{3,1},{4,6},{5,7},{6,4},{7,5},{8,10},{9,11},{10,... | collective-permute-start | bytes 1179656 | tf_op jit(solution)/shard_map/ppermute | solution.py:25
  93.2 3.7 %collective-permute-done.27.refs_11_ = bf16[1536,128]{1,0:T(8,128)(2,1)S(1)} collective-permute-done((bf16[1536,128]{1,0:T(8,128)(2,1)S(1)}, bf16[1536,128]{1,0:T(8,128)(2,1)S(1)}, u32[]{:S(2)}, u32[]{:S(2)}) %collective-permute-start.27) | collective-permute-done | bytes 393248 | tf_op jit(solution)/shard_map/ppermute | solution.py:25
  97.0 2.4 %collective-permute-done.30.refs_10_ = bf16[1536,128]{1,0:T(8,128)(2,1)S(1)} collective-permute-done((bf16[1536,128]{1,0:T(8,128)(2,1)S(1)}, bf16[1536,128]{1,0:T(8,128)(2,1)S(1)}, u32[]{:S(2)}, u32[]{:S(2)}) %collective-permute-start.30) | collective-permute-done | bytes 393248 | tf_op jit(solution)/shard_map/ppermute | solution.py:25
  103.0 4.3 %collective-permute-done.31.refs_1_ = bf16[768,128]{1,0:T(8,128)(2,1)S(1)} collective-permute-done((bf16[768,128]{1,0:T(8,128)(2,1)S(1)}, bf16[768,128]{1,0:T(8,128)(2,1)S(1)}, u32[]{:S(2)}, u32[]{:S(2)}) %collective-permute-start.31) | collective-permute-done | bytes 196640 | tf_op jit(solution)/shard_map/ppermute | solution.py:25
  107.3 2.2 %collective-permute-done.33.refs_3_ = bf16[768,128]{1,0:T(8,128)(2,1)S(1)} collective-permute-done((bf16[768,128]{1,0:T(8,128)(2,1)S(1)}, bf16[768,128]{1,0:T(8,128)(2,1)S(1)}, u32[]{:S(2)}, u32[]{:S(2)}) %collective-permute-start.33) | collective-permute-done | bytes 196640 | tf_op jit(solution)/shard_map/ppermute | solution.py:25
  109.5 6.1 %shard_map.191 = (f32[384,128]{1,0:T(8,128)S(1)}, bf16[384,128]{1,0:T(8,128)(2,1)S(1)}, bf16[384,128]{1,0:T(8,128)(2,1)S(1)}, bf16[384,128]{1,0:T(8,128)(2,1)S(1...) custom-call(s32[111]{0:T(128)S(1)} %concatenate.19.scalars, ...), custom_call_target="tpu_custom_call" | custom-call | flops 1 | bytes 1 | tf_op jit(solution)/shard_map/pallas_call | solution.py:38
  121.2 3.1 %collective-permute-done.36.rest_2_ = bf16[384,128]{1,0:T(8,128)(2,1)S(1)} collective-permute-done((bf16[384,128]{1,0:T(8,128)(2,1)S(1)}, bf16[384,128]{1,0:T(8,128)(2,1)S(1)}, u32[]{:S(2)}, u32[]{:S(2)}) %collective-permute-start.36) | collective-permute-done | bytes 98336 | tf_op jit(solution)/shard_map/ppermute | solution.py:25
  124.8 1.9 %collective-permute-start.37 = (bf16[384,128]{1,0:T(8,128)(2,1)S(1)}, bf16[384,128]{1,0:T(8,128)(2,1)S(1)}, u32[]{:S(2)}, u32[]{:S(2)}) collective-permute-start(bf16[384,128]{1,0:T(8,128)(2,1)S(1)} %shard_map.192), channel_id=1, source_target_pairs={{0,8},{1,9},{2,10},{3,11},{4,12},{5,13},{6,14},{7,15},{8,0},{9,1},... | collective-permute-start | bytes 294920 | tf_op jit(solution)/shard_map/ppermute | solution.py:25
  127.3 2.2 %collective-permute-done.37 = bf16[384,128]{1,0:T(8,128)(2,1)S(1)} collective-permute-done((bf16[384,128]{1,0:T(8,128)(2,1)S(1)}, bf16[384,128]{1,0:T(8,128)(2,1)S(1)}, u32[]{:S(2)}, u32[]{:S(2)}) %collective-permute-start.37) | collective-permute-done | bytes 98336 | tf_op jit(solution)/shard_map/ppermute | solution.py:25
  129.6 3.3 %collective-permute-start.38 = (bf16[384,128]{1,0:T(8,128)(2,1)S(1)}, bf16[384,128]{1,0:T(8,128)(2,1)S(1)}, u32[]{:S(2)}, u32[]{:S(2)}) collective-permute-start(bf16[384,128]{1,0:T(8,128)(2,1)S(1)} %add_convert_fusion), channel_id=1, source_target_pairs={{0,16},{1,17},{2,18},{3,19},{4,20},{5,21},{6,22},{7,23},{8,24},{9,... | collective-permute-start | bytes 294920 | tf_op jit(solution)/shard_map/ppermute | solution.py:25
  132.9 1.7 collective-permute-done.39.refs_11_
  135.8 1.8 %collective-permute-start.42 = (bf16[768,128]{1,0:T(8,128)(2,1)S(1)}, bf16[768,128]{1,0:T(8,128)(2,1)S(1)}, u32[]{:S(2)}, u32[]{:S(2)}) collective-permute-start(bf16[768,128]{1,0:T(8,128)(2,1)S(1)} %constant_dynamic-update-slice_fusion.4.refs_0_), channel_id=1, source_target_pairs={{0,4},{1,5},{2,6},{3,7},{4,0},{5,1},{6,2},{7,3},{8,12},{9,13},{10,... | collective-permute-start | bytes 589832 | tf_op jit(solution)/shard_map/ppermute | solution.py:25
  139.1 4.2 %collective-permute-done.41.refs_1_ = bf16[768,128]{1,0:T(8,128)(2,1)S(1)} collective-permute-done((bf16[768,128]{1,0:T(8,128)(2,1)S(1)}, bf16[768,128]{1,0:T(8,128)(2,1)S(1)}, u32[]{:S(2)}, u32[]{:S(2)}) %collective-permute-start.41) | collective-permute-done | bytes 196640 | tf_op jit(solution)/shard_map/ppermute | solution.py:25
  143.5 1.9 %collective-permute-done.43.refs_3_ = bf16[768,128]{1,0:T(8,128)(2,1)S(1)} collective-permute-done((bf16[768,128]{1,0:T(8,128)(2,1)S(1)}, bf16[768,128]{1,0:T(8,128)(2,1)S(1)}, u32[]{:S(2)}, u32[]{:S(2)}) %collective-permute-start.43) | collective-permute-done | bytes 196640 | tf_op jit(solution)/shard_map/ppermute | solution.py:25
  145.4 5.7 %shard_map.193 = (bf16[1536,128]{1,0:T(8,128)(2,1)}, bf16[192,128]{1,0:T(8,128)(2,1)S(1)}, bf16[192,128]{1,0:T(8,128)(2,1)S(1)}) custom-call(s32[111]{0:T(128)S(1)} %concatenate.19.scalars, bf16[768,128]{1,0:T(8,128)(2,1)S(1)} %constant_dynamic-update-slice_fusion.4.refs_0_, bf16[768,128]{1,0:T(8,128)(2,1)S(1)} %collective-permute-done.41.refs_1_, ...), custom_call_target="tpu_custom_call" | custom-call | flops 1 | bytes 1 | tf_op jit(solution)/shard_map/pallas_call | solution.py:38
  151.1 6.3 %all-to-all-start = ((bf16[16,96,128]{2,1,0:T(8,128)(2,1)}), bf16[16,96,128]{2,1,0:T(8,128)(2,1)S(1)}, u32[]{:S(2)}, u32[]{:S(2)}) async-start(bf16[16,96,128]{2,1,0:T(8,128)(2,1)} %bitcast.41), calls=%async_computation | async-start | bytes 786432 | tf_op jit(solution)/shard_map/all_to_all | solution.py:634
  160.0 7.0 %all-to-all-done = bf16[16,96,128]{2,1,0:T(8,128)(2,1)S(1)} async-done(((bf16[16,96,128]{2,1,0:T(8,128)(2,1)}), bf16[16,96,128]{2,1,0:T(8,128)(2,1)S(1)}, u32[]{:S(2)}, u32[]{:S(2)}) %all-to-all-start) | async-done | bytes 393248 | tf_op jit(solution)/shard_map/all_to_all | solution.py:634
  (138 shorter events, 48.7 us)
Async XLA Ops:
  4.2 22.7 %collective-permute-start.6 = (bf16[384,6144]{1,0:T(8,128)(2,1)}, bf16[384,6144]{1,0:T(8,128)(2,1)S(1)}, u32[]{:S(2)}, u32[]{:S(2)}) collective-permute-start(bf16[384,6144]{1,0:T(8,128)(2,1)} %refs_8_), channel_id=1, source_target_pairs={{0,1},{1,0},{2,3},{3,2},{4,5},{5,4},{6,7},{7,6},{8,9},{9,8},{10,11... | collective-permute-start | bytes 14155784 | tf_op jit(solution)/shard_map/ppermute | solution.py:25
  4.7 22.2 %collective-permute-start.2 = (bf16[1536,256]{1,0:T(8,128)(2,1)}, bf16[1536,256]{1,0:T(8,128)(2,1)S(1)}, u32[]{:S(2)}, u32[]{:S(2)}) collective-permute-start(bf16[1536,256]{1,0:T(8,128)(2,1)} %b0.1), channel_id=1, source_target_pairs={{0,2},{1,3},{4,6},{5,7},{8,10},{9,11},{12,14},{13,15},{16,18},{17,... | collective-permute-start | bytes 2359304 | tf_op jit(solution)/shard_map/ppermute | solution.py:25
  9.9 17.0 %collective-permute-start.5 = (bf16[1536,128]{1,0:T(8,128)(2,1)S(1)}, bf16[1536,128]{1,0:T(8,128)(2,1)S(1)}, u32[]{:S(2)}, u32[]{:S(2)}) collective-permute-start(bf16[1536,128]{1,0:T(8,128)(2,1)S(1)} %get-tuple-element.182.refs_0_), channel_id=1, source_target_pairs={{0,4},{1,5},{2,6},{3,7},{4,0},{5,1},{6,2},{7,3},{8,12},{9,13},{10,... | collective-permute-start | bytes 1179656 | tf_op jit(solution)/shard_map/ppermute | solution.py:25
  11.4 13.8 %collective-permute-start.3 = (bf16[768,128]{1,0:T(8,128)(2,1)S(1)}, bf16[768,128]{1,0:T(8,128)(2,1)S(1)}, u32[]{:S(2)}, u32[]{:S(2)}) collective-permute-start(bf16[768,128]{1,0:T(8,128)(2,1)S(1)} %get-tuple-element.143), channel_id=1, source_target_pairs={{0,8},{1,9},{2,10},{3,11},{4,12},{5,13},{6,14},{7,15},{8,0},{9,1},... | collective-permute-start | bytes 589832 | tf_op jit(solution)/shard_map/ppermute | solution.py:25
  13.0 12.2 %collective-permute-start.4 = (bf16[384,128]{1,0:T(8,128)(2,1)S(1)}, bf16[384,128]{1,0:T(8,128)(2,1)S(1)}, u32[]{:S(2)}, u32[]{:S(2)}) collective-permute-start(bf16[384,128]{1,0:T(8,128)(2,1)S(1)} %get-tuple-element.144), channel_id=1, source_target_pairs={{0,16},{1,17},{2,18},{3,19},{4,20},{5,21},{6,22},{7,23},{8,24},{9,... | collective-permute-start | bytes 294920 | tf_op jit(solution)/shard_map/ppermute | solution.py:25
  27.1 11.6 %collective-permute-start.10 = (bf16[1536,128]{1,0:T(8,128)(2,1)S(1)}, bf16[1536,128]{1,0:T(8,128)(2,1)S(1)}, u32[]{:S(2)}, u32[]{:S(2)}) collective-permute-start(bf16[1536,128]{1,0:T(8,128)(2,1)S(1)} %constant_dynamic-update-slice_fusion.refs_8_), channel_id=1, source_target_pairs={{0,4},{1,5},{2,6},{3,7},{4,0},{5,1},{6,2},{7,3},{8,12},{9,13},{10,... | collective-permute-start | bytes 1179656 | tf_op jit(solution)/shard_map/ppermute | solution.py:25
  28.6 11.9 %collective-permute-start.8 = (bf16[1536,128]{1,0:T(8,128)(2,1)S(1)}, bf16[1536,128]{1,0:T(8,128)(2,1)S(1)}, u32[]{:S(2)}, u32[]{:S(2)}) collective-permute-start(bf16[1536,128]{1,0:T(8,128)(2,1)S(1)} %get-tuple-element.182.refs_0_), channel_id=1, source_target_pairs={{0,2},{1,3},{2,0},{3,1},{4,6},{5,7},{6,4},{7,5},{8,10},{9,11},{10,... | collective-permute-start | bytes 1179656 | tf_op jit(solution)/shard_map/ppermute | solution.py:25
  31.0 6.9 %collective-permute-start.9 = (bf16[768,128]{1,0:T(8,128)(2,1)S(1)}, bf16[768,128]{1,0:T(8,128)(2,1)S(1)}, u32[]{:S(2)}, u32[]{:S(2)}) collective-permute-start(bf16[768,128]{1,0:T(8,128)(2,1)S(1)} %pad_maximum_fusion.1), channel_id=1, source_target_pairs={{0,8},{1,9},{2,10},{3,11},{4,12},{5,13},{6,14},{7,15},{8,0},{9,1},... | collective-permute-start | bytes 589832 | tf_op jit(solution)/shard_map/ppermute | solution.py:25
  40.5 10.0 %collective-permute-start.14 = (bf16[1536,128]{1,0:T(8,128)(2,1)S(1)}, bf16[1536,128]{1,0:T(8,128)(2,1)S(1)}, u32[]{:S(2)}, u32[]{:S(2)}) collective-permute-start(bf16[1536,128]{1,0:T(8,128)(2,1)S(1)} %get-tuple-element.182.refs_0_), channel_id=1, source_target_pairs={{0,1},{1,0},{2,3},{3,2},{4,5},{5,4},{6,7},{7,6},{8,9},{9,8},{10,11... | collective-permute-start | bytes 1179656 | tf_op jit(solution)/shard_map/ppermute | solution.py:25
  41.0 9.5 %collective-permute-start.15 = (bf16[1536,128]{1,0:T(8,128)(2,1)S(1)}, bf16[1536,128]{1,0:T(8,128)(2,1)S(1)}, u32[]{:S(2)}, u32[]{:S(2)}) collective-permute-start(bf16[1536,128]{1,0:T(8,128)(2,1)S(1)} %collective-permute-done.5.refs_1_), channel_id=1, source_target_pairs={{0,1},{1,0},{2,3},{3,2},{4,5},{5,4},{6,7},{7,6},{8,9},{9,8},{10,11... | collective-permute-start | bytes 1179656 | tf_op jit(solution)/shard_map/ppermute | solution.py:25
  41.1 11.5 %collective-permute-start.13 = (bf16[1536,128]{1,0:T(8,128)(2,1)S(1)}, bf16[1536,128]{1,0:T(8,128)(2,1)S(1)}, u32[]{:S(2)}, u32[]{:S(2)}) collective-permute-start(bf16[1536,128]{1,0:T(8,128)(2,1)S(1)} %collective-permute-done.8.refs_2_), channel_id=1, source_target_pairs={{0,4},{1,5},{2,6},{3,7},{4,0},{5,1},{6,2},{7,3},{8,12},{9,13},{10,... | collective-permute-start | bytes 1179656 | tf_op jit(solution)/shard_map/ppermute | solution.py:25
  41.6 10.9 %collective-permute-start.16 = (bf16[1536,128]{1,0:T(8,128)(2,1)S(1)}, bf16[1536,128]{1,0:T(8,128)(2,1)S(1)}, u32[]{:S(2)}, u32[]{:S(2)}) collective-permute-start(bf16[1536,128]{1,0:T(8,128)(2,1)S(1)} %collective-permute-done.8.refs_2_), channel_id=1, source_target_pairs={{0,1},{1,0},{2,3},{3,2},{4,5},{5,4},{6,7},{7,6},{8,9},{9,8},{10,11... | collective-permute-start | bytes 1179656 | tf_op jit(solution)/shard_map/ppermute | solution.py:25
  42.9 7.0 %collective-permute-start.12 = (bf16[768,128]{1,0:T(8,128)(2,1)S(1)}, bf16[768,128]{1,0:T(8,128)(2,1)S(1)}, u32[]{:S(2)}, u32[]{:S(2)}) collective-permute-start(bf16[768,128]{1,0:T(8,128)(2,1)S(1)} %get-tuple-element.165), channel_id=1, source_target_pairs={{0,2},{1,3},{2,0},{3,1},{4,6},{5,7},{6,4},{7,5},{8,10},{9,11},{10,... | collective-permute-start | bytes 589832 | tf_op jit(solution)/shard_map/ppermute | solution.py:25
  52.6 12.9 %collective-permute-start.17 = (bf16[1536,128]{1,0:T(8,128)(2,1)S(1)}, bf16[1536,128]{1,0:T(8,128)(2,1)S(1)}, u32[]{:S(2)}, u32[]{:S(2)}) collective-permute-start(bf16[1536,128]{1,0:T(8,128)(2,1)S(1)} %collective-permute-done.13.refs_3_), channel_id=1, source_target_pairs={{0,1},{1,0},{2,3},{3,2},{4,5},{5,4},{6,7},{7,6},{8,9},{9,8},{10,11... | collective-permute-start | bytes 1179656 | tf_op jit(solution)/shard_map/ppermute | solution.py:25
  52.6 15.0 %collective-permute-start.19 = (bf16[1536,384]{1,0:T(8,128)(2,1)S(1)}, bf16[1536,384]{1,0:T(8,128)(2,1)S(1)}, u32[]{:S(2)}, u32[]{:S(2)}) collective-permute-start(bf16[1536,384]{1,0:T(8,128)(2,1)S(1)} %copy-done.6), channel_id=1, source_target_pairs={{0,1},{1,0},{2,3},{3,2},{4,5},{5,4},{6,7},{7,6},{8,9},{9,8},{10,11... | collective-permute-start | bytes 3538952 | tf_op jit(solution)/shard_map/ppermute | solution.py:25
  65.6 11.5 %collective-permute-start.20 = (bf16[1536,128]{1,0:T(8,128)(2,1)S(1)}, bf16[1536,128]{1,0:T(8,128)(2,1)S(1)}, u32[]{:S(2)}, u32[]{:S(2)}) collective-permute-start(bf16[1536,128]{1,0:T(8,128)(2,1)S(1)} %pad_maximum_fusion.refs_8_), channel_id=1, source_target_pairs={{0,4},{1,5},{2,6},{3,7},{4,0},{5,1},{6,2},{7,3},{8,12},{9,13},{10,... | collective-permute-start | bytes 1179656 | tf_op jit(solution)/shard_map/ppermute | solution.py:25
  66.2 11.2 %collective-permute-start.21 = (bf16[1536,128]{1,0:T(8,128)(2,1)S(1)}, bf16[1536,128]{1,0:T(8,128)(2,1)S(1)}, u32[]{:S(2)}, u32[]{:S(2)}) collective-permute-start(bf16[1536,128]{1,0:T(8,128)(2,1)S(1)} %constant_dynamic-update-slice_fusion.refs_8_), channel_id=1, source_target_pairs={{0,2},{1,3},{2,0},{3,1},{4,6},{5,7},{6,4},{7,5},{8,10},{9,11},{10,... | collective-permute-start | bytes 1179656 | tf_op jit(solution)/shard_map/ppermute | solution.py:25
  79.8 19.6 %collective-permute-start.28 = (bf16[192,6144]{1,0:T(8,128)(2,1)S(1)}, bf16[192,6144]{1,0:T(8,128)(2,1)S(1)}, u32[]{:S(2)}, u32[]{:S(2)}) collective-permute-start(bf16[192,6144]{1,0:T(8,128)(2,1)S(1)} %copy-done.3), channel_id=1, source_target_pairs={{0,1},{1,0},{2,3},{3,2},{4,5},{5,4},{6,7},{7,6},{8,9},{9,8},{10,11... | collective-permute-start | bytes 7077896 | tf_op jit(solution)/shard_map/ppermute | solution.py:25
  80.0 19.4 %collective-permute-start.29 = (bf16[192,1536]{1,0:T(8,128)(2,1)S(1)}, bf16[192,1536]{1,0:T(8,128)(2,1)S(1)}, u32[]{:S(2)}, u32[]{:S(2)}) collective-permute-start(bf16[192,1536]{1,0:T(8,128)(2,1)S(1)} %bitcast.51), channel_id=1, source_target_pairs={{0,1},{1,0},{2,3},{3,2},{4,5},{5,4},{6,7},{7,6},{8,9},{9,8},{10,11... | collective-permute-start | bytes 1769480 | tf_op jit(solution)/shard_map/ppermute | solution.py:25
  82.4 6.6 %collective-permute-start.25 = (bf16[384,128]{1,0:T(8,128)(2,1)S(1)}, bf16[384,128]{1,0:T(8,128)(2,1)S(1)}, u32[]{:S(2)}, u32[]{:S(2)}) collective-permute-start(bf16[384,128]{1,0:T(8,128)(2,1)S(1)} %get-tuple-element.207), channel_id=1, source_target_pairs={{0,6},{1,7},{2,4},{3,5},{4,2},{5,3},{6,0},{7,1},{8,14},{9,15},{10,... | collective-permute-start | bytes 294920 | tf_op jit(solution)/shard_map/ppermute | solution.py:25
  85.2 11.8 %collective-permute-start.27 = (bf16[1536,128]{1,0:T(8,128)(2,1)S(1)}, bf16[1536,128]{1,0:T(8,128)(2,1)S(1)}, u32[]{:S(2)}, u32[]{:S(2)}) collective-permute-start(bf16[1536,128]{1,0:T(8,128)(2,1)S(1)} %collective-permute-done.21.refs_10_), channel_id=1, source_target_pairs={{0,4},{1,5},{2,6},{3,7},{4,0},{5,1},{6,2},{7,3},{8,12},{9,13},{10,... | collective-permute-start | bytes 1179656 | tf_op jit(solution)/shard_map/ppermute | solution.py:25
  89.6 9.8 %collective-permute-start.30 = (bf16[1536,128]{1,0:T(8,128)(2,1)S(1)}, bf16[1536,128]{1,0:T(8,128)(2,1)S(1)}, u32[]{:S(2)}, u32[]{:S(2)}) collective-permute-start(bf16[1536,128]{1,0:T(8,128)(2,1)S(1)} %pad_maximum_fusion.refs_8_), channel_id=1, source_target_pairs={{0,2},{1,3},{2,0},{3,1},{4,6},{5,7},{6,4},{7,5},{8,10},{9,11},{10,... | collective-permute-start | bytes 1179656 | tf_op jit(solution)/shard_map/ppermute | solution.py:25
  99.4 7.8 %collective-permute-start.31 = (bf16[768,128]{1,0:T(8,128)(2,1)S(1)}, bf16[768,128]{1,0:T(8,128)(2,1)S(1)}, u32[]{:S(2)}, u32[]{:S(2)}) collective-permute-start(bf16[768,128]{1,0:T(8,128)(2,1)S(1)} %constant_dynamic-update-slice_fusion.2.refs_0_), channel_id=1, source_target_pairs={{0,2},{1,3},{2,0},{3,1},{4,6},{5,7},{6,4},{7,5},{8,10},{9,11},{10,... | collective-permute-start | bytes 589832 | tf_op jit(solution)/shard_map/ppermute | solution.py:25
  101.0 6.3 %collective-permute-start.32 = (bf16[768,128]{1,0:T(8,128)(2,1)S(1)}, bf16[768,128]{1,0:T(8,128)(2,1)S(1)}, u32[]{:S(2)}, u32[]{:S(2)}) collective-permute-start(bf16[768,128]{1,0:T(8,128)(2,1)S(1)} %constant_dynamic-update-slice_fusion.2.refs_0_), channel_id=1, source_target_pairs={{0,4},{1,5},{2,6},{3,7},{4,0},{5,1},{6,2},{7,3},{8,12},{9,13},{10,... | collective-permute-start | bytes 589832 | tf_op jit(solution)/shard_map/ppermute | solution.py:25
  101.5 8.0 %collective-permute-start.33 = (bf16[768,128]{1,0:T(8,128)(2,1)S(1)}, bf16[768,128]{1,0:T(8,128)(2,1)S(1)}, u32[]{:S(2)}, u32[]{:S(2)}) collective-permute-start(bf16[768,128]{1,0:T(8,128)(2,1)S(1)} %constant_dynamic-update-slice_fusion.2.refs_0_), channel_id=1, source_target_pairs={{0,6},{1,7},{2,4},{3,5},{4,2},{5,3},{6,0},{7,1},{8,14},{9,15},{10,... | collective-permute-start | bytes 589832 | tf_op jit(solution)/shard_map/ppermute | solution.py:25
  117.7 6.6 %collective-permute-start.36 = (bf16[384,128]{1,0:T(8,128)(2,1)S(1)}, bf16[384,128]{1,0:T(8,128)(2,1)S(1)}, u32[]{:S(2)}, u32[]{:S(2)}) collective-permute-start(bf16[384,128]{1,0:T(8,128)(2,1)S(1)} %get-tuple-element.237), channel_id=1, source_target_pairs={{0,6},{1,7},{2,4},{3,5},{4,2},{5,3},{6,0},{7,1},{8,14},{9,15},{10,... | collective-permute-start | bytes 294920 | tf_op jit(solution)/shard_map/ppermute | solution.py:25
  126.8 7.8 %collective-permute-start.39 = (bf16[1536,128]{1,0:T(8,128)(2,1)S(1)}, bf16[1536,128]{1,0:T(8,128)(2,1)S(1)}, u32[]{:S(2)}, u32[]{:S(2)}) collective-permute-start(bf16[1536,128]{1,0:T(8,128)(2,1)S(1)} %collective-permute-done.30.refs_10_), channel_id=1, source_target_pairs={{0,4},{1,5},{2,6},{3,7},{4,0},{5,1},{6,2},{7,3},{8,12},{9,13},{10,... | collective-permute-start | bytes 1179656 | tf_op jit(solution)/shard_map/ppermute | solution.py:25
  129.6 5.9 %collective-permute-start.38 = (bf16[384,128]{1,0:T(8,128)(2,1)S(1)}, bf16[384,128]{1,0:T(8,128)(2,1)S(1)}, u32[]{:S(2)}, u32[]{:S(2)}) collective-permute-start(bf16[384,128]{1,0:T(8,128)(2,1)S(1)} %add_convert_fusion), channel_id=1, source_target_pairs={{0,16},{1,17},{2,18},{3,19},{4,20},{5,21},{6,22},{7,23},{8,24},{9,... | collective-permute-start | bytes 294920 | tf_op jit(solution)/shard_map/ppermute | solution.py:25
  135.5 7.8 %collective-permute-start.41 = (bf16[768,128]{1,0:T(8,128)(2,1)S(1)}, bf16[768,128]{1,0:T(8,128)(2,1)S(1)}, u32[]{:S(2)}, u32[]{:S(2)}) collective-permute-start(bf16[768,128]{1,0:T(8,128)(2,1)S(1)} %constant_dynamic-update-slice_fusion.4.refs_0_), channel_id=1, source_target_pairs={{0,2},{1,3},{2,0},{3,1},{4,6},{5,7},{6,4},{7,5},{8,10},{9,11},{10,... | collective-permute-start | bytes 589832 | tf_op jit(solution)/shard_map/ppermute | solution.py:25
  135.8 7.8 %collective-permute-start.42 = (bf16[768,128]{1,0:T(8,128)(2,1)S(1)}, bf16[768,128]{1,0:T(8,128)(2,1)S(1)}, u32[]{:S(2)}, u32[]{:S(2)}) collective-permute-start(bf16[768,128]{1,0:T(8,128)(2,1)S(1)} %constant_dynamic-update-slice_fusion.4.refs_0_), channel_id=1, source_target_pairs={{0,4},{1,5},{2,6},{3,7},{4,0},{5,1},{6,2},{7,3},{8,12},{9,13},{10,... | collective-permute-start | bytes 589832 | tf_op jit(solution)/shard_map/ppermute | solution.py:25
  137.6 7.8 %collective-permute-start.43 = (bf16[768,128]{1,0:T(8,128)(2,1)S(1)}, bf16[768,128]{1,0:T(8,128)(2,1)S(1)}, u32[]{:S(2)}, u32[]{:S(2)}) collective-permute-start(bf16[768,128]{1,0:T(8,128)(2,1)S(1)} %constant_dynamic-update-slice_fusion.4.refs_0_), channel_id=1, source_target_pairs={{0,6},{1,7},{2,4},{3,5},{4,2},{5,3},{6,0},{7,1},{8,14},{9,15},{10,... | collective-permute-start | bytes 589832 | tf_op jit(solution)/shard_map/ppermute | solution.py:25
  151.1 15.9 %all-to-all-start = ((bf16[16,96,128]{2,1,0:T(8,128)(2,1)}), bf16[16,96,128]{2,1,0:T(8,128)(2,1)S(1)}, u32[]{:S(2)}, u32[]{:S(2)}) async-start(bf16[16,96,128]{2,1,0:T(8,128)(2,1)} %bitcast.41), calls=%async_computation | async-start | bytes 786432 | tf_op jit(solution)/shard_map/all_to_all | solution.py:634
  (39 other events, 507.6 us)
